TPU v7x, 32 devices: a whole 2x2x4 slice. The times are simulated.
32 devices in a mesh: seq: 4 (over y, x), mp: 8 (over z, core).
Axes of the slice: x: 2, y: 2, z: 4, core: 2. Of those that a mesh axis runs over, the one named last changes fastest.
Arguments:
- queries: bfloat16 [4096, 1024], P(('seq', 'mp')), may hold values from -6 to 6
- keys: bfloat16 [4096, 1024], P(('seq', 'mp')), may hold values from -6 to 6
- values: bfloat16 [4096, 1024], P(('seq', 'mp')), may hold values from -6 to 6
- out_weight: bfloat16 [1024, 1024], P('mp'), may hold values from -0.1875 to 0.1875
- upstream: bfloat16 [4096, 1024], P(('seq', 'mp')), may hold values from -6 to 6
- adjacency: int32 [32, 4], P(('seq', 'mp')), may hold values 0 or 1
- counts: int32 [32], P(('seq', 'mp')), may hold values from 32 to 128, as said below
Outputs:
- mixed_out: bfloat16 [4096, 1024], P(('seq', 'mp'))
- grad_queries: bfloat16 [4096, 1024], P(('seq', 'mp'))
- grad_keys: bfloat16 [4096, 1024], P(('seq', 'mp'))
- grad_values: bfloat16 [4096, 1024], P(('seq', 'mp'))
Inputs may be any that keep to these rules, and one draw needn't show every extreme that they name: `counts`: each block has between 32 and 128 valid slots; some block has exactly 128 and some exactly 32.
All inputs are finite; a program needn't handle non-finite values. No bound on the sum of `adjacency` on one device may be relied on, other than what follows from the above.
Results may differ from a plain program's by a relative error of at most 0.023.
Values may be sent and summed in bfloat16 or wider, within the bound.
No kernel may reach another device: no remote copies, remote signals or barrier semaphores. Data moves between devices by JAX's collectives and lax.ppermute only.
A program may use at most 64 MiB of HBM per device.

v0:
```python
import jax
import jax.numpy as jnp
from jax import lax
from jax.sharding import PartitionSpec as P

HEADS = 16
HEAD_DIM = 64


score_scale = 0.125
cycle_offsets = (1, -1, 2, -2)


def passed_along(value, axis, steps):
    count = lax.axis_size(axis)
    pairs = [(source, (source + steps) % count) for source in range(count)]
    return lax.ppermute(value, axis, pairs)


def split_heads(matrix):
    return matrix.reshape(matrix.shape[0], HEADS, HEAD_DIM)


def masked_scores(query_heads, key_block, key_count):
    scores = (
        jnp.einsum(
            "qhd,khd->hqk", query_heads, split_heads(key_block), preferred_element_type=jnp.float32
        )
        * score_scale
    )
    positions = jnp.arange(key_block.shape[0], dtype=jnp.int32)
    return jnp.where((positions < key_count)[None, None, :], scores, -jnp.inf)


def local(queries, keys, values, out_weight, upstream, adjacency, counts):
    row_count = queries.shape[0]
    model_width = queries.shape[1]
    query_heads = split_heads(queries)
    own_pair = jnp.stack([keys, values])
    own_entry = (own_pair, counts)
    remote = [passed_along((own_entry[0], own_entry[1]), "seq", offset) for offset in cycle_offsets]
    present = [adjacency[0, column] > 0 for column in range(4)]

    def live_scores(pair_block, key_count):
        return masked_scores(query_heads, pair_block[0], key_count)

    def dead_scores(pair_block, key_count):
        return jnp.full((HEADS, row_count, pair_block.shape[1]), -jnp.inf, jnp.float32)

    own_scores = masked_scores(query_heads, keys, counts[0])
    remote_scores = []
    for column in range(4):
        pair_block, key_count = remote[column]
        remote_scores.append(
            lax.cond(present[column], live_scores, dead_scores, pair_block, key_count[0])
        )
    maxima = jnp.max(own_scores, axis=2)
    for scores in remote_scores:
        maxima = jnp.maximum(maxima, jnp.max(scores, axis=2))
    own_expo = jnp.exp(own_scores - maxima[:, :, None])
    remote_expo = [jnp.exp(scores - maxima[:, :, None]) for scores in remote_scores]
    totals = jnp.sum(own_expo, axis=2)
    for expo in remote_expo:
        totals = totals + jnp.sum(expo, axis=2)
    own_probs = own_expo / totals[:, :, None]
    remote_probs = [expo / totals[:, :, None] for expo in remote_expo]

    def weighted(pair_block, probabilities):
        return jnp.einsum(
            "hqk,khd->qhd",
            probabilities.astype(jnp.bfloat16),
            split_heads(pair_block[1]),
            preferred_element_type=jnp.float32,
        )

    def skip_weighted(pair_block, probabilities):
        return jnp.zeros((row_count, HEADS, HEAD_DIM), jnp.float32)

    attended = weighted(own_pair, own_probs)
    for column in range(4):
        pair_block, key_count = remote[column]
        attended = attended + lax.cond(
            present[column], weighted, skip_weighted, pair_block, remote_probs[column]
        )
    attended = attended.reshape(row_count, model_width).astype(jnp.bfloat16)
    contract_rows = (((1,), (1,)), ((), ()))
    mixed_out = jnp.dot(
        attended,
        lax.all_gather(out_weight, "mp", axis=0, tiled=True),
        preferred_element_type=jnp.float32,
    )
    grad_attended = lax.dot_general(
        upstream,
        lax.all_gather(out_weight, "mp", axis=0, tiled=True),
        contract_rows,
        preferred_element_type=jnp.float32,
    )
    mixed_out = mixed_out.astype(jnp.bfloat16)
    grad_attended = grad_attended.astype(jnp.bfloat16)
    grad_heads = split_heads(grad_attended)
    row_delta = jnp.einsum(
        "qhd,qhd->hq", grad_heads, split_heads(attended), preferred_element_type=jnp.float32
    )

    def pair_grads(pair_block, probabilities):
        grad_probs = jnp.einsum(
            "qhd,khd->hqk",
            grad_heads,
            split_heads(pair_block[1]),
            preferred_element_type=jnp.float32,
        )
        grad_scores = (probabilities * (grad_probs - row_delta[:, :, None])).astype(jnp.bfloat16)
        query_term = score_scale * jnp.einsum(
            "hqk,khd->qhd",
            grad_scores,
            split_heads(pair_block[0]),
            preferred_element_type=jnp.float32,
        )
        key_term = score_scale * jnp.einsum(
            "hqk,qhd->khd", grad_scores, query_heads, preferred_element_type=jnp.float32
        )
        value_term = jnp.einsum(
            "hqk,qhd->khd",
            probabilities.astype(jnp.bfloat16),
            grad_heads,
            preferred_element_type=jnp.float32,
        )
        pair_terms = jnp.stack(
            [key_term.reshape(row_count, model_width), value_term.reshape(row_count, model_width)]
        )
        return (query_term, pair_terms)

    def remote_grads(pair_block, probabilities):
        query_term, pair_terms = pair_grads(pair_block, probabilities)
        return (query_term, pair_terms.astype(jnp.bfloat16))

    def skip_grads(pair_block, probabilities):
        return (
            jnp.zeros((row_count, HEADS, HEAD_DIM), jnp.float32),
            jnp.zeros((2, row_count, model_width), jnp.bfloat16),
        )

    query_grad, own_terms = pair_grads(own_pair, own_probs)
    partials = []
    for column in range(4):
        pair_block, key_count = remote[column]
        query_term, pair_terms = lax.cond(
            present[column], remote_grads, skip_grads, pair_block, remote_probs[column]
        )
        query_grad = query_grad + query_term
        partials.append(pair_terms)
    returned = [
        passed_along(partials[column], "seq", -cycle_offsets[column]) for column in range(4)
    ]
    combined = own_terms
    for landed in returned:
        combined = combined + landed.astype(jnp.float32)
    grad_keys = combined[0].astype(jnp.bfloat16)
    grad_values = combined[1].astype(jnp.bfloat16)
    grad_queries = query_grad.reshape(row_count, model_width).astype(jnp.bfloat16)
    return (mixed_out, grad_queries, grad_keys, grad_values)


def solution(mesh):
    return jax.shard_map(
        local,
        mesh=mesh,
        in_specs=(
            P(("seq", "mp"), None),
            P(("seq", "mp"), None),
            P(("seq", "mp"), None),
            P("mp", None),
            P(("seq", "mp"), None),
            P(("seq", "mp"), None),
            P(("seq", "mp")),
        ),
        out_specs=(
            P(("seq", "mp"), None),
            P(("seq", "mp"), None),
            P(("seq", "mp"), None),
            P(("seq", "mp"), None),
        ),
        check_vma=False,
    )
```

profile of v0, /device:TPU:0, one launch (start us, length us, event | category | flops | bytes accessed | tf_op | source)
XLA Modules:
  0.0 142.8 jit_solution(10058304975665000070)
XLA Ops:
  11.2 3.0 %collective-permute-start.5 = (bf16[2,128,1024]{1,2,0:T(8,128)(2,1)}, bf16[2,128,1024]{1,2,0:T(8,128)(2,1)S(1)}, u32[]{:S(2)}, u32[]{:S(2)}) collective-permute-start(bf16[2,128,1024]{1,2,0:T(8,128)(2,1)} %pad_maximum_fusion.4), channel_id=1, source_target_pairs={{0,16},{8,24},{16,0},{24,8},{1,17},{9,25},{17,1},{25,9},{2,18},{10... | collective-permute-start | bytes 1572872 | tf_op jit(solution)/shard_map/ppermute | solution.py:17
  22.5 15.2 %collective-permute-done.4 = s32[1]{0:T(128)} collective-permute-done((s32[1]{0:T(128)}, s32[1]{0:T(128)}, u32[]{:S(2)}, u32[]{:S(2)}) %collective-permute-start.4) | collective-permute-done | bytes 36 | tf_op jit(solution)/shard_map/ppermute | solution.py:17
  43.0 3.3 %fusion.39 = (f32[16,128]{1,0:T(8,128)S(1)}, f32[16,128]{1,0:T(8,128)S(1)}, f32[16,128]{1,0:T(8,128)S(1)}, f32[16,128]{1,0:T(8,128)S(1)}, f32[16,128]{1,0:T(8,128)S(1)}) fusion(f32[16,128,128]{1,2,0:T(8,128)} %copy-done.3, f32[16,128]{1,0:T(8,128)S(1)} %fusion.51, f32[16,128,128]{1,2,0:T(8,128)} %get-tuple-element.167, ...), kind=kLoop, calls=%fused_computation.84 | loop fusion | flops 2611200 | bytes 5292032 | tf_op jit(solution)/shard_map/reduce_sum | solution.py:64
  46.4 3.6 %fusion.38 = (f32[16,128,128]{1,2,0:T(8,128)}, f32[16,128,128]{1,2,0:T(8,128)}, f32[16,128,128]{1,2,0:T(8,128)}, f32[16,128,128]{1,2,0:T(8,128)}, bf16[16,128,128]{1,2,0:T(8,128)(2,1)}) fusion(f32[16,128,128]{1,2,0:T(8,128)S(1)} %copy-done.4, f32[16,128]{1,0:T(8,128)S(1)} %add_add_fusion, f32[16,128]{1,0:T(8,128)S(1)} %fusion.51, ...), kind=kLoop, calls=%fused_computation.83 | loop fusion | flops 2883584 | bytes 9977856 | tf_op jit(solution)/shard_map/div | solution.py:66
  52.3 4.6 %conditional.18 = (f32[128,16,64]{0,2,1:T(8,128)}) conditional(s32[]{:T(128)} %bitcast.56, () %tuple.115, (bf16[2,128,1024]{1,2,0:T(8,128)(2,1)S(1)}, f32[16,128,128]{1,2,0:T(8,128)}) %tuple.116), branch_computations={%region_22.23_spmd, %region_23.24_spmd} | conditional | flops 33554432 | bytes 3407880 | solution.py:82
  52.3 2.3 %copy.52 = bf16[16,128,128]{2,1,0:T(8,128)(2,1)} copy(f32[16,128,128]{1,2,0:T(8,128)} %get-tuple-element.215) | data formatting | bytes 1572864 | tf_op jit(solution)/shard_map
  54.6 2.3 %convolution_bitcast_fusion.2 = f32[128,16,64]{0,2,1:T(8,128)} fusion(bf16[128,16,64]{0,2,1:T(8,128)(2,1)S(1)} %bitcast.197, bf16[16,128,128]{2,1,0:T(8,128)(2,1)} %copy.52), kind=kOutput, calls=%fused_computation.16 | convolution fusion | flops 33554432 | bytes 1310720 | tf_op jit(solution)/shard_map/cond/branch_1_fun/hqk,khd->qhd/dot_general | solution.py:69
  56.9 3.3 %conditional.19 = (f32[128,16,64]{0,2,1:T(8,128)}) conditional(s32[]{:T(128)} %bitcast.58, () %tuple.117, (bf16[2,128,1024]{1,2,0:T(8,128)(2,1)S(1)}, f32[16,128,128]{1,2,0:T(8,128)S(1)}) %tuple.206), branch_computations={%region_24.25_spmd, %region_25.26_spmd} | conditional | flops 33554432 | bytes 3407880 | solution.py:82
  57.9 2.3 %convolution_bitcast_fusion.3 = f32[128,16,64]{0,2,1:T(8,128)} fusion(bf16[128,16,64]{0,2,1:T(8,128)(2,1)S(1)} %bitcast.198, bf16[16,128,128]{2,1,0:T(8,128)(2,1)} %copy.53), kind=kOutput, calls=%fused_computation.18 | convolution fusion | flops 33554432 | bytes 1310720 | tf_op jit(solution)/shard_map/cond/branch_1_fun/hqk,khd->qhd/dot_general | solution.py:69
  60.2 2.1 %convolution_bitcast_fusion.4 = f32[128,16,64]{0,2,1:T(8,128)} fusion(bf16[128,16,64]{0,2,1:T(8,128)(2,1)S(1)} %bitcast.190, bf16[16,128,128]{1,2,0:T(8,128)(2,1)} %get-tuple-element.271), kind=kOutput, calls=%fused_computation.65 | convolution fusion | flops 33554432 | bytes 1310720 | tf_op jit(solution)/shard_map/hqk,khd->qhd/dot_general | solution.py:69
  62.4 3.1 %convolution_convert_fusion.4 = bf16[128,1024]{1,0:T(8,128)(2,1)} fusion(bf16[128,1024]{1,0:T(8,128)(2,1)S(1)} %copy-done, bf16[1024,1024]{1,0:T(8,128)(2,1)} %all-gather.2.cloned.1.call-done), kind=kOutput, calls=%fused_computation.69 | convolution fusion | flops 268566528 | bytes 2621440 | tf_op jit(solution)/shard_map/dot_general | solution.py:92
  66.6 2.3 %fusion.62 = f32[16,64,128]{2,1,0:T(8,128)} fusion(bf16[128,16,64]{0,2,1:T(8,128)(2,1)S(1)} %bitcast.180, bf16[16,128,128]{1,2,0:T(8,128)(2,1)} %get-tuple-element.271), kind=kOutput, calls=%fused_computation.116 | convolution fusion | flops 33554432 | bytes 1310720 | tf_op jit(solution)/shard_map/hqk,qhd->khd/dot_general | solution.py:122
  68.9 2.7 %fusion.46 = (f32[16,128]{1,0:T(8,128)S(1)}, bf16[128,16,64]{0,2,1:T(8,128)(2,1)}) fusion(bf16[128,1024]{0,1:T(8,128)(2,1)S(1)} %copy.54, f32[128,16,64]{0,2,1:T(8,128)} %get-tuple-element.313, f32[128,16,64]{0,2,1:T(8,128)} %get-tuple-element.312, f32[128,16,64]{0,2,1:T(8,128)} %get-tuple-element.311, f32[128,16,64]{0,2,1:T(8,128)} %convolution_bitcast_fusion.4, ...), kind=kLoop, calls=%fused_computation.93 | loop fusion | flops 1177600 | bytes 3153920 | tf_op jit(solution)/shard_map/qhd,qhd->hq/dot_general | solution.py:101
  76.2 2.1 %copy.65 = bf16[2,128,1024]{2,1,0:T(8,128)(2,1)} copy(bf16[2,128,1024]{1,2,0:T(8,128)(2,1)} %get-tuple-element.174) | data formatting | bytes 1048576 | tf_op jit(solution)/shard_map/cond | solution.py:147
  82.9 2.0 %copy.66 = bf16[2,128,1024]{2,1,0:T(8,128)(2,1)} copy(bf16[2,128,1024]{1,2,0:T(8,128)(2,1)} %get-tuple-element.175) | data formatting | bytes 1048576 | tf_op jit(solution)/shard_map/cond | solution.py:147
  84.9 12.3 %collective-permute-start.7 = (bf16[2,128,1024]{2,1,0:T(8,128)(2,1)}, bf16[2,128,1024]{2,1,0:T(8,128)(2,1)}, u32[]{:S(2)}, u32[]{:S(2)}) collective-permute-start(bf16[2,128,1024]{2,1,0:T(8,128)(2,1)} %copy.66), channel_id=1, source_target_pairs={{0,8},{8,16},{16,24},{24,0},{1,9},{9,17},{17,25},{25,1},{2,10},{10... | collective-permute-start | bytes 1572872 | tf_op jit(solution)/shard_map/ppermute | solution.py:17
  97.2 5.9 %conditional.22 = (f32[128,16,64]{0,2,1:T(8,128)}, bf16[2,128,1024]{1,2,0:T(8,128)(2,1)}) conditional(s32[]{:T(128)} %bitcast.56, () %tuple.123, (bf16[2,128,1024]{1,2,0:T(8,128)(2,1)S(1)}, bf16[128,16,64]{0,2,1:T(8,128)(2,1)S(1)}, f32[16,128]{1,0:T(8,128)S(1)}, f32[16,128,128]{1,2,0:T(8,128)S(1)}, bf16[128,16,64]{0,2,1:T(8,128)(2,1)S(1)}) %tuple.208), branch_computations={%region_30.31_spmd, %region_31.32_spmd} | conditional | flops 136052736 | bytes 14426156 | solution.py:147
  103.1 2.0 %copy.67 = bf16[2,128,1024]{2,1,0:T(8,128)(2,1)} copy(bf16[2,128,1024]{1,2,0:T(8,128)(2,1)} %get-tuple-element.176) | data formatting | bytes 1048576 | tf_op jit(solution)/shard_map/cond | solution.py:147
  105.1 3.6 %conditional.23 = (f32[128,16,64]{0,2,1:T(8,128)}, bf16[2,128,1024]{1,2,0:T(8,128)(2,1)}) conditional(s32[]{:T(128)} %bitcast.58, () %tuple.125, (bf16[2,128,1024]{1,2,0:T(8,128)(2,1)S(1)}, bf16[128,16,64]{0,2,1:T(8,128)(2,1)S(1)}, f32[16,128]{1,0:T(8,128)S(1)}, f32[16,128,128]{1,2,0:T(8,128)S(1)}, bf16[128,16,64]{0,2,1:T(8,128)(2,1)S(1)}) %tuple.207), branch_computations={%region_32.33_spmd, %region_33.34_spmd} | conditional | flops 136052736 | bytes 10231824 | solution.py:147
  108.7 2.1 %copy.68 = bf16[2,128,1024]{2,1,0:T(8,128)(2,1)} copy(bf16[2,128,1024]{1,2,0:T(8,128)(2,1)} %get-tuple-element.177) | data formatting | bytes 1048576 | tf_op jit(solution)/shard_map/cond | solution.py:147
  111.1 2.2 %copy.64 = f32[1,128,1024]{2,1,0:T(8,128)} copy(f32[1,128,1024]{1,2,0:T(8,128)} %bitcast.192) | data formatting | bytes 1048576 | tf_op jit(solution)/shard_map/stack;reshape | solution.py:128
  117.0 4.8 %collective-permute-done.8 = bf16[2,128,1024]{2,1,0:T(8,128)(2,1)} collective-permute-done((bf16[2,128,1024]{2,1,0:T(8,128)(2,1)}, bf16[2,128,1024]{2,1,0:T(8,128)(2,1)}, u32[]{:S(2)}, u32[]{:S(2)}) %collective-permute-start.8) | collective-permute-done | bytes 524320 | tf_op jit(solution)/shard_map/ppermute | solution.py:17
  121.9 11.1 %collective-permute-done.9 = bf16[2,128,1024]{2,1,0:T(8,128)(2,1)} collective-permute-done((bf16[2,128,1024]{2,1,0:T(8,128)(2,1)}, bf16[2,128,1024]{2,1,0:T(8,128)(2,1)}, u32[]{:S(2)}, u32[]{:S(2)}) %collective-permute-start.9) | collective-permute-done | bytes 524320 | tf_op jit(solution)/shard_map/ppermute | solution.py:17
  133.0 2.1 %fusion.35 = bf16[2,128,1024]{2,1,0:T(8,128)(2,1)S(1)} fusion(f32[1,128,1024]{2,1,0:T(8,128)} %copy.64, f32[1,128,1024]{2,1,0:T(8,128)S(1)} %copy-done.18, bf16[2,128,1024]{2,1,0:T(8,128)(2,1)} %collective-permute-done.9, bf16[2,128,1024]{2,1,0:T(8,128)(2,1)} %collective-permute-done.8, bf16[2,128,1024]{2,1,0:T(8,128)(2,1)} %collective-permute-done.7, ...), kind=kLoop, calls=%fused_computation.75 | loop fusion | flops 2621440 | bytes 3670016 | tf_op jit(solution)/shard_map/convert.29
  (119 shorter events, 50.6 us)
Async XLA Ops:
  7.2 55.2 %copy-start = (bf16[128,1024]{1,0:T(8,128)(2,1)S(1)}, bf16[128,1024]{1,0:T(8,128)(2,1)}, u32[]{:S(2)}) copy-start(bf16[128,1024]{1,0:T(8,128)(2,1)} %param.35) | copy-start | bytes 786436
  7.2 11.7 %copy-start.21 = (bf16[128,1024]{1,0:T(8,128)(2,1)S(1)}, bf16[128,1024]{1,0:T(8,128)(2,1)}, u32[]{:S(2)}) copy-start(bf16[128,1024]{1,0:T(8,128)(2,1)} %param.31) | copy-start | bytes 786436
  7.2 11.9 %copy-start.22 = (s32[1,4]{1,0:T(1,128)S(1)}, s32[1,4]{1,0:T(1,128)}, u32[]{:S(2)}) copy-start(s32[1,4]{1,0:T(1,128)} %param.36) | copy-start | bytes 52
  7.2 55.2 %all-gather.2.cloned.1.call-start = ((), (), s32[]{:S(2)}) async-start(), calls=%async_computation | async-start | bytes 2359296 | tf_op jit(solution)/shard_map/all_gather | solution.py:89
  9.1 28.6 %copy-start.13 = (bf16[128,1024]{0,1:T(8,128)(2,1)}, bf16[128,1024]{0,1:T(8,128)(2,1)S(1)}, u32[]{:S(2)}) copy-start(bf16[128,1024]{0,1:T(8,128)(2,1)S(1)} %copy.45) | copy-start | bytes 786436
  10.3 8.6 %copy-start.15 = (bf16[128,1024]{0,1:T(8,128)(2,1)}, bf16[128,1024]{0,1:T(8,128)(2,1)S(1)}, u32[]{:S(2)}) copy-start(bf16[128,1024]{0,1:T(8,128)(2,1)S(1)} %copy.47) | copy-start | bytes 786436
  11.2 26.5 %collective-permute-start.5 = (bf16[2,128,1024]{1,2,0:T(8,128)(2,1)}, bf16[2,128,1024]{1,2,0:T(8,128)(2,1)S(1)}, u32[]{:S(2)}, u32[]{:S(2)}) collective-permute-start(bf16[2,128,1024]{1,2,0:T(8,128)(2,1)} %pad_maximum_fusion.4), channel_id=1, source_target_pairs={{0,16},{8,24},{16,0},{24,8},{1,17},{9,25},{17,1},{25,9},{2,18},{10... | collective-permute-start | bytes 1572872 | tf_op jit(solution)/shard_map/ppermute | solution.py:17
  14.1 25.9 %collective-permute-start.1 = (bf16[2,128,1024]{1,2,0:T(8,128)(2,1)}, bf16[2,128,1024]{1,2,0:T(8,128)(2,1)}, u32[]{:S(2)}, u32[]{:S(2)}) collective-permute-start(bf16[2,128,1024]{1,2,0:T(8,128)(2,1)} %pad_maximum_fusion.4), channel_id=1, source_target_pairs={{0,8},{8,16},{16,24},{24,0},{1,9},{9,17},{17,25},{25,1},{2,10},{10... | collective-permute-start | bytes 1572872 | tf_op jit(solution)/shard_map/ppermute | solution.py:17
  15.6 25.8 %collective-permute-start.3 = (bf16[2,128,1024]{1,2,0:T(8,128)(2,1)}, bf16[2,128,1024]{1,2,0:T(8,128)(2,1)}, u32[]{:S(2)}, u32[]{:S(2)}) collective-permute-start(bf16[2,128,1024]{1,2,0:T(8,128)(2,1)} %pad_maximum_fusion.4), channel_id=1, source_target_pairs={{0,24},{8,0},{16,8},{24,16},{1,25},{9,1},{17,9},{25,17},{2,26},{10... | collective-permute-start | bytes 1572872 | tf_op jit(solution)/shard_map/ppermute | solution.py:17
  17.1 20.6 %collective-permute-start.4 = (s32[1]{0:T(128)}, s32[1]{0:T(128)}, u32[]{:S(2)}, u32[]{:S(2)}) collective-permute-start(s32[1]{0:T(128)} %param.37), channel_id=1, source_target_pairs={{0,16},{8,24},{16,0},{24,8},{1,17},{9,25},{17,1},{25,9},{2,18},{10... | collective-permute-start | bytes 20 | tf_op jit(solution)/shard_map/ppermute | solution.py:17
  17.1 22.9 %collective-permute-start = (s32[1]{0:T(128)}, s32[1]{0:T(128)}, u32[]{:S(2)}, u32[]{:S(2)}) collective-permute-start(s32[1]{0:T(128)} %param.37), channel_id=1, source_target_pairs={{0,8},{8,16},{16,24},{24,0},{1,9},{9,17},{17,25},{25,1},{2,10},{10... | collective-permute-start | bytes 20 | tf_op jit(solution)/shard_map/ppermute | solution.py:17
  37.7 3.8 %collective-permute-start.2 = (s32[1]{0:T(128)}, s32[1]{0:T(128)}, u32[]{:S(2)}, u32[]{:S(2)}) collective-permute-start(s32[1]{0:T(128)} %param.37), channel_id=1, source_target_pairs={{0,24},{8,0},{16,8},{24,16},{1,25},{9,1},{17,9},{25,17},{2,26},{10... | collective-permute-start | bytes 20 | tf_op jit(solution)/shard_map/ppermute | solution.py:17
  43.0 3.4 %copy-start.4 = (f32[16,128,128]{1,2,0:T(8,128)S(1)}, f32[16,128,128]{1,2,0:T(8,128)}, u32[]{:S(2)}) copy-start(f32[16,128,128]{1,2,0:T(8,128)} %copy-done.3) | copy-start | bytes 3145732
  52.3 4.6 %copy-start.5 = (f32[16,128,128]{1,2,0:T(8,128)S(1)}, f32[16,128,128]{1,2,0:T(8,128)}, u32[]{:S(2)}) copy-start(f32[16,128,128]{1,2,0:T(8,128)} %get-tuple-element.270) | copy-start | bytes 3145732
  66.6 5.0 %copy-start.17 = (bf16[128,1024]{0,1:T(8,128)(2,1)S(1)}, bf16[128,1024]{0,1:T(8,128)(2,1)}, u32[]{:S(2)}) copy-start(bf16[128,1024]{0,1:T(8,128)(2,1)} %copy-done.15) | copy-start | bytes 786436
  78.3 38.8 %collective-permute-start.6 = (bf16[2,128,1024]{2,1,0:T(8,128)(2,1)}, bf16[2,128,1024]{2,1,0:T(8,128)(2,1)}, u32[]{:S(2)}, u32[]{:S(2)}) collective-permute-start(bf16[2,128,1024]{2,1,0:T(8,128)(2,1)} %copy.65), channel_id=1, source_target_pairs={{0,24},{8,0},{16,8},{24,16},{1,25},{9,1},{17,9},{25,17},{2,26},{10... | collective-permute-start | bytes 1572872 | tf_op jit(solution)/shard_map/ppermute | solution.py:17
  81.2 16.1 %copy-start.6 = (f32[16,128,128]{1,2,0:T(8,128)S(1)}, f32[16,128,128]{1,2,0:T(8,128)}, u32[]{:S(2)}) copy-start(f32[16,128,128]{1,2,0:T(8,128)} %get-tuple-element.269) | copy-start | bytes 3145732
  84.9 32.1 %collective-permute-start.7 = (bf16[2,128,1024]{2,1,0:T(8,128)(2,1)}, bf16[2,128,1024]{2,1,0:T(8,128)(2,1)}, u32[]{:S(2)}, u32[]{:S(2)}) collective-permute-start(bf16[2,128,1024]{2,1,0:T(8,128)(2,1)} %copy.66), channel_id=1, source_target_pairs={{0,8},{8,16},{16,24},{24,0},{1,9},{9,17},{17,25},{25,1},{2,10},{10... | collective-permute-start | bytes 1572872 | tf_op jit(solution)/shard_map/ppermute | solution.py:17
  105.1 16.7 %collective-permute-start.8 = (bf16[2,128,1024]{2,1,0:T(8,128)(2,1)}, bf16[2,128,1024]{2,1,0:T(8,128)(2,1)}, u32[]{:S(2)}, u32[]{:S(2)}) collective-permute-start(bf16[2,128,1024]{2,1,0:T(8,128)(2,1)} %copy.67), channel_id=1, source_target_pairs={{0,16},{8,24},{16,0},{24,8},{1,17},{9,25},{17,1},{25,9},{2,18},{10... | collective-permute-start | bytes 1572872 | tf_op jit(solution)/shard_map/ppermute | solution.py:17
  108.7 4.5 %copy-start.19 = (f32[128,16,64]{0,2,1:T(8,128)S(1)}, f32[128,16,64]{0,2,1:T(8,128)}, u32[]{:S(2)}) copy-start(f32[128,16,64]{0,2,1:T(8,128)} %fusion.31) | copy-start | bytes 1572868
  110.9 22.1 %collective-permute-start.9 = (bf16[2,128,1024]{2,1,0:T(8,128)(2,1)}, bf16[2,128,1024]{2,1,0:T(8,128)(2,1)}, u32[]{:S(2)}, u32[]{:S(2)}) collective-permute-start(bf16[2,128,1024]{2,1,0:T(8,128)(2,1)} %copy.68), channel_id=1, source_target_pairs={{0,16},{8,24},{16,0},{24,8},{1,17},{9,25},{17,1},{25,9},{2,18},{10... | collective-permute-start | bytes 1572872 | tf_op jit(solution)/shard_map/ppermute | solution.py:17
  111.0 4.8 %copy-start.12 = (bf16[1024,1024]{1,0:T(8,128)(2,1)S(1)}, bf16[1024,1024]{1,0:T(8,128)(2,1)}, u32[]{:S(2)}) copy-start(bf16[1024,1024]{1,0:T(8,128)(2,1)} %all-gather.2.cloned.1.call-done) | copy-start | bytes 6291460
  111.1 4.8 %copy-start.20 = (bf16[128,16,64]{0,2,1:T(8,128)(2,1)S(1)}, bf16[128,16,64]{0,2,1:T(8,128)(2,1)}, u32[]{:S(2)}) copy-start(bf16[128,16,64]{0,2,1:T(8,128)(2,1)} %get-tuple-element.248) | copy-start | bytes 786436
  115.0 18.0 %copy-start.18 = (f32[1,128,1024]{2,1,0:T(8,128)S(1)}, f32[1,128,1024]{2,1,0:T(8,128)}, u32[]{:S(2)}) copy-start(f32[1,128,1024]{2,1,0:T(8,128)} %copy.63) | copy-start | bytes 1572868
  (8 other events, 16.4 us)
Sparse Core Ops, SparseCore 0:
  9.6 31.7 all-gather.1
where the time goes:
time: 145 us; the launch traced here: 143 us
  waiting for transfers between devices  32.5 us (22%)
  local copies, waits for them, and re-layouts  31.8 us (22%)
  matrix products  23.2 us (16%)
  starting transfers between devices  20.4 us (14%)
  between operations  17.4 us (12%)
  other arithmetic  17.3 us (12%)
    ppermute x10, waiting for transfers between devices, passed_along(): return lax.ppermute(value, axis, pairs)  31.8 us
    ppermute x10, starting transfers between devices, passed_along(): return lax.ppermute(value, axis, pairs)  20.3 us
    another operation x12, local copies, waits for them, and re-layouts  11.3 us
    cond x4, local copies, waits for them, and re-layouts, local(): lax.cond(present[column], remote_grads, skip_grads, pair_block, remote_pr...  8.3 us
    dot_general x3, matrix products, weighted(): jnp.einsum('hqk,khd->qhd', probabilities.astype(jnp.bfloat16), split_head...  6.72 us
    unnamed x44, local copies, waits for them, and re-layouts  5.28 us
    another operation x2, local copies, waits for them, and re-layouts, pair_grads(): jnp.stack([key_term.reshape(row_count, model_width), value_term.reshape(r...  4.23 us
    dot_general x3, matrix products, pair_grads(): jnp.einsum('hqk,khd->qhd', grad_scores, split_heads(pair_block[0]), prefe...  3.61 us
  transfers between devices with their start and end apart: 11, of which 5 were waited for; matrix products, arithmetic and copies ran while one was open for 36% of the time, Pallas kernels for 0%

commit v1 on v0

v1 whole, which is shorter than its diff:
```python
import functools

import jax
import jax.numpy as jnp
from jax import lax
from jax.experimental import pallas as pl
from jax.experimental.pallas import tpu as pltpu
from jax.sharding import PartitionSpec as P

HEADS = 16
HEAD_DIM = 64
META = 32

score_scale = 0.125
log2_scale = 0.125 * 1.4426950408889634
cycle_offsets = (1, -1, 2, -2)
absent = -1e30
bf16 = jnp.bfloat16
f32 = jnp.float32


def dot_nn(a, b):
    return lax.dot_general(a, b, (((1,), (0,)), ((), ())), preferred_element_type=f32)


def dot_nt(a, b):
    return lax.dot_general(a, b, (((1,), (1,)), ((), ())), preferred_element_type=f32)


def vmem():
    return pl.BlockSpec(memory_space=pltpu.VMEM)


def params(mib):
    return pltpu.CompilerParams(vmem_limit_bytes=mib * 1024 * 1024)


def exchange(value, axis, distance):
    count = lax.axis_size(axis)
    return lax.ppermute(value, axis, [(i, i ^ distance) for i in range(count)])


def pack_kernel(cycle, q_ref, k_ref, v_ref, adj_ref, cnt_ref, *outs):
    rows = q_ref.shape[0]
    width = q_ref.shape[1] // cycle
    own = lax.axis_index("seq")
    lines = lax.broadcasted_iota(jnp.int32, (META, width), 0)
    meta = jnp.where(lines == 0, 1, 0)
    for column, offset in enumerate(cycle_offsets):
        named = lax.rem(own - offset + 2 * cycle, cycle)
        meta = meta + jnp.where(
            (lines == lax.bitwise_xor(own, named)) & (adj_ref[0, column] > 0), 1, 0
        )
    meta = jnp.where(lines == META - 1, cnt_ref[0], meta).astype(f32).astype(bf16)
    for place in range(cycle):
        target = lax.bitwise_xor(own, place)
        if width % 128 == 0:
            columns = pl.ds(pl.multiple_of(target * width, width), width)
            for at, ref in enumerate((q_ref, k_ref, v_ref)):
                outs[place][at * rows:(at + 1) * rows, :] = ref[:, columns]
        else:
            for other in range(cycle):
                @pl.when(target == other)
                def _():
                    for at, ref in enumerate((q_ref, k_ref, v_ref)):
                        outs[place][at * rows:(at + 1) * rows, :] = ref[
                            :, other * width:(other + 1) * width
                        ]
        outs[place][3 * rows:, :] = meta


def pack(cycle, queries, keys, values, adjacency, counts):
    rows, model = queries.shape
    width = model // cycle
    smem = pl.BlockSpec(memory_space=pltpu.SMEM)
    return pl.pallas_call(
        functools.partial(pack_kernel, cycle),
        out_shape=[jax.ShapeDtypeStruct((3 * rows + META, width), bf16)] * cycle,
        in_specs=[vmem()] * 3 + [smem] * 2,
        out_specs=[vmem()] * cycle,
        compiler_params=params(32),
        name="pack",
    )(queries, keys, values, adjacency, counts)


def fill(cycle, rows, chunks, bias, *parts):
    for place in range(cycle):
        for at, part in parts:
            part[place * rows:(place + 1) * rows, :] = chunks[place][at * rows:(at + 1) * rows, :]
    lines = lax.broadcasted_iota(jnp.int32, (rows, rows), 0).astype(f32)
    lists = [chunks[place][3 * rows:, :].astype(f32) for place in range(cycle)]
    for key_place in range(cycle):
        count = lists[key_place][META - 1:, :1]
        valid = lines < count
        for query_place in range(cycle):
            way = key_place ^ query_place
            times = lists[query_place][way:way + 1, :1]
            term = jnp.where(times > 0, jnp.log2(jnp.maximum(times, 1.0)), absent)
            bias[
                key_place * rows:(key_place + 1) * rows,
                query_place * rows:(query_place + 1) * rows,
            ] = jnp.where(valid, term, absent)


def head_tile(width):
    return min(128, width)


def only_head(tile, which):
    lanes = lax.broadcasted_iota(jnp.int32, tile.shape, 1)
    inside = (lanes >= which * HEAD_DIM) & (lanes < (which + 1) * HEAD_DIM)
    return jnp.where(inside, tile, jnp.zeros_like(tile))


def forward_kernel(cycle, query_tile, *refs):
    chunks = refs[:cycle]
    outs = refs[cycle:2 * cycle]
    att_t, lse, q_all, k_all, v_all, bias = refs[2 * cycle:]
    width = q_all.shape[1]
    tokens = q_all.shape[0]
    rows = tokens // cycle
    fill(cycle, rows, chunks, bias, (0, q_all), (1, k_all), (2, v_all))
    tile = head_tile(width)
    v_t = v_all[...].astype(f32).T.astype(bf16)
    for start in range(0, tokens, query_tile):
        span = slice(start, start + query_tile)
        for head in range(width // HEAD_DIM):
            at = head * HEAD_DIM // tile * tile
            which = (head * HEAD_DIM - at) // HEAD_DIM
            scores = dot_nt(
                k_all[:, at:at + tile], only_head(q_all[span, at:at + tile], which)
            )
            scores = scores * log2_scale + bias[:, span]
            largest = jnp.max(scores, axis=0, keepdims=True)
            expo = jnp.exp2(scores - largest)
            total = jnp.sum(expo, axis=0, keepdims=True)
            probs = (expo * (1.0 / total)).astype(bf16)
            lse[head:head + 1, span] = largest + jnp.log2(total)
            att_t[head * HEAD_DIM:(head + 1) * HEAD_DIM, span] = dot_nn(
                v_t[head * HEAD_DIM:(head + 1) * HEAD_DIM, :], probs
            )
    attended = att_t[...].T.astype(bf16)
    for place in range(cycle):
        outs[place][...] = attended[place * rows:(place + 1) * rows, :]


def forward(cycle, chunks):
    width = chunks[0].shape[1]
    rows = (chunks[0].shape[0] - META) // 3
    tokens = rows * cycle
    outs = pl.pallas_call(
        functools.partial(forward_kernel, cycle, min(tokens, 512)),
        out_shape=[jax.ShapeDtypeStruct((rows, width), bf16)] * cycle
        + [
            jax.ShapeDtypeStruct((width, tokens), f32),
            jax.ShapeDtypeStruct((8, tokens), f32),
        ],
        in_specs=[vmem()] * cycle,
        out_specs=[vmem()] * (cycle + 2),
        scratch_shapes=[pltpu.VMEM((tokens, width), bf16)] * 3
        + [pltpu.VMEM((tokens, tokens), f32)],
        compiler_params=params(60),
        name="forward",
    )(*chunks)
    return outs[:cycle], outs[cycle], outs[cycle + 1]


def backward_kernel(cycle, query_tile, *refs):
    chunks = refs[:cycle]
    grads = refs[cycle:2 * cycle]
    att_t, lse = refs[2 * cycle:2 * cycle + 2]
    outs = refs[2 * cycle + 2:3 * cycle + 2]
    q_all, k_all, v_all, g_all, dq_t, dk, dv, bias = refs[3 * cycle + 2:]
    width = q_all.shape[1]
    tokens = q_all.shape[0]
    rows = tokens // cycle
    fill(cycle, rows, chunks, bias, (0, q_all), (1, k_all), (2, v_all))
    for place in range(cycle):
        g_all[place * rows:(place + 1) * rows, :] = grads[place][...]
    tile = head_tile(width)
    k_t = k_all[...].astype(f32).T.astype(bf16)
    g_t = g_all[...].astype(f32).T
    product = g_t * att_t[...].astype(bf16).astype(f32)
    for start in range(0, tokens, query_tile):
        span = slice(start, start + query_tile)
        for at in range(0, width, tile):
            dk_tile = dv_tile = None
            for which in range(tile // HEAD_DIM):
                low = at + which * HEAD_DIM
                head = low // HEAD_DIM
                delta = jnp.sum(product[low:low + HEAD_DIM, span], axis=0, keepdims=True)
                q_head = only_head(q_all[span, at:at + tile], which)
                g_head = only_head(g_all[span, at:at + tile], which)
                scores = dot_nt(k_all[:, at:at + tile], q_head)
                probs = jnp.exp2(
                    scores * log2_scale + bias[:, span] - lse[head:head + 1, span]
                )
                grad_probs = dot_nt(v_all[:, at:at + tile], g_head)
                grad_scores = (probs * (grad_probs - delta)).astype(bf16)
                dk_head = dot_nn(grad_scores, q_head)
                dv_head = dot_nn(probs.astype(bf16), g_head)
                dk_tile = dk_head if dk_tile is None else dk_tile + dk_head
                dv_tile = dv_head if dv_tile is None else dv_tile + dv_head
                dq_t[low:low + HEAD_DIM, span] = dot_nn(k_t[low:low + HEAD_DIM, :], grad_scores)
            if start == 0:
                dk[:, at:at + tile] = dk_tile
                dv[:, at:at + tile] = dv_tile
            else:
                dk[:, at:at + tile] += dk_tile
                dv[:, at:at + tile] += dv_tile
    dq = (dq_t[...] * score_scale).T.astype(bf16)
    for place in range(cycle):
        span = slice(place * rows, (place + 1) * rows)
        outs[place][:rows, :] = dq[span, :]
        outs[place][rows:2 * rows, :] = (dk[span, :] * score_scale).astype(bf16)
        outs[place][2 * rows:, :] = dv[span, :].astype(bf16)


def backward(cycle, chunks, grads, att_t, lse):
    rows, width = grads[0].shape
    tokens = rows * cycle
    return pl.pallas_call(
        functools.partial(backward_kernel, cycle, min(tokens, 512)),
        out_shape=[jax.ShapeDtypeStruct((3 * rows, width), bf16)] * cycle,
        in_specs=[vmem()] * (2 * cycle + 2),
        out_specs=[vmem()] * cycle,
        scratch_shapes=[pltpu.VMEM((tokens, width), bf16)] * 4
        + [pltpu.VMEM((width, tokens), f32)]
        + [pltpu.VMEM((tokens, width), f32)] * 2
        + [pltpu.VMEM((tokens, tokens), f32)],
        compiler_params=params(60),
        name="backward",
    )(*chunks, *grads, att_t, lse)


def gather_rows(out_weight):
    count = lax.axis_size("mp")
    chips = count // 2
    pieces = []
    for step in range(chips):
        if step == 0:
            piece = out_weight
        else:
            piece = lax.ppermute(
                out_weight, "mp", [(i, (i - 2 * step) % count) for i in range(count)]
            )
        pieces.append(piece)
    return pieces + [exchange(piece, "mp", 1) for piece in pieces]


def load_rows(pieces, weight, sems):
    rows = pieces[0].shape[0]
    chips = len(pieces) // 2
    own = lax.axis_index("mp")
    chip, core = own // 2, lax.rem(own, 2)
    copies = []
    for at, piece in enumerate(pieces):
        owner = 2 * lax.rem(chip + at % chips, chips) + (core if at < chips else 1 - core)
        first = pl.multiple_of(owner * rows, rows)
        copies.append(
            pltpu.make_async_copy(piece, weight.at[pl.ds(first, rows), :], sems.at[at])
        )
    for copy in copies:
        copy.start()
    for copy in copies:
        copy.wait()


def grad_kernel(cycle, count, up_ref, *refs):
    pieces = refs[:count]
    outs = refs[count:count + cycle]
    weight, sems = refs[count + cycle:]
    load_rows(pieces, weight, sems)
    width = weight.shape[0] // cycle
    own = lax.axis_index("seq")
    for place in range(cycle):
        first = pl.multiple_of(lax.bitwise_xor(own, place) * width, width)
        outs[place][...] = dot_nt(up_ref[...], weight[pl.ds(first, width), :]).astype(bf16)


def project_grad(cycle, upstream, pieces):
    rows, model = upstream.shape
    count = len(pieces)
    return pl.pallas_call(
        functools.partial(grad_kernel, cycle, count),
        out_shape=[jax.ShapeDtypeStruct((rows, model // cycle), bf16)] * cycle,
        in_specs=[vmem()] + [pl.BlockSpec(memory_space=pl.ANY)] * count,
        out_specs=[vmem()] * cycle,
        scratch_shapes=[pltpu.VMEM((model, model), bf16), pltpu.SemaphoreType.DMA((count,))],
        compiler_params=params(32),
        name="project_grad",
    )(upstream, *pieces)


def mixed_kernel(cycle, count, *refs):
    attended = refs[:cycle]
    pieces = refs[cycle:cycle + count]
    out, weight, sems = refs[cycle + count:]
    load_rows(pieces, weight, sems)
    width = weight.shape[0] // cycle
    own = lax.axis_index("seq")
    total = None
    for place in range(cycle):
        first = pl.multiple_of(lax.bitwise_xor(own, place) * width, width)
        term = dot_nn(attended[place][...], weight[pl.ds(first, width), :])
        total = term if total is None else total + term
    out[...] = total.astype(bf16)


def project(cycle, attended, pieces):
    rows = attended[0].shape[0]
    model = attended[0].shape[1] * cycle
    count = len(pieces)
    return pl.pallas_call(
        functools.partial(mixed_kernel, cycle, count),
        out_shape=jax.ShapeDtypeStruct((rows, model), bf16),
        in_specs=[vmem()] * cycle + [pl.BlockSpec(memory_space=pl.ANY)] * count,
        out_specs=vmem(),
        scratch_shapes=[pltpu.VMEM((model, model), bf16), pltpu.SemaphoreType.DMA((count,))],
        compiler_params=params(32),
        name="project",
    )(*attended, *pieces)


def unpack_kernel(cycle, *refs):
    chunks = refs[:cycle]
    outs = refs[cycle:]
    rows = outs[0].shape[0]
    width = outs[0].shape[1] // cycle
    own = lax.axis_index("seq")
    for place in range(cycle):
        source = lax.bitwise_xor(own, place)
        if width % 128 == 0:
            columns = pl.ds(pl.multiple_of(source * width, width), width)
            for at, out in enumerate(outs):
                out[:, columns] = chunks[place][at * rows:(at + 1) * rows, :]
        else:
            for other in range(cycle):
                @pl.when(source == other)
                def _():
                    for at, out in enumerate(outs):
                        out[:, other * width:(other + 1) * width] = chunks[place][
                            at * rows:(at + 1) * rows, :
                        ]


def unpack(cycle, chunks):
    rows = chunks[0].shape[0] // 3
    model = chunks[0].shape[1] * cycle
    return pl.pallas_call(
        functools.partial(unpack_kernel, cycle),
        out_shape=[jax.ShapeDtypeStruct((rows, model), bf16)] * 3,
        in_specs=[vmem()] * cycle,
        out_specs=[vmem()] * 3,
        compiler_params=params(32),
        name="unpack",
    )(*chunks)


def swapped(chunks):
    return [chunks[0]] + [exchange(chunks[k], "seq", k) for k in range(1, len(chunks))]


def local(queries, keys, values, out_weight, upstream, adjacency, counts):
    cycle = lax.axis_size("seq")
    pieces = gather_rows(out_weight)
    chunks = swapped(pack(cycle, queries, keys, values, adjacency, counts))
    attended, att_t, lse = forward(cycle, chunks)
    grads = swapped(project_grad(cycle, upstream, pieces))
    attended = swapped(attended)
    terms = swapped(backward(cycle, chunks, grads, att_t, lse))
    mixed_out = project(cycle, attended, pieces)
    grad_queries, grad_keys, grad_values = unpack(cycle, terms)
    return (mixed_out, grad_queries, grad_keys, grad_values)


def solution(mesh):
    tokens = P(("seq", "mp"), None)
    return jax.shard_map(
        local,
        mesh=mesh,
        in_specs=(tokens, tokens, tokens, P("mp", None), tokens, tokens, P(("seq", "mp"))),
        out_specs=(tokens,) * 4,
        check_vma=False,
    )
```

time: 145 us -> 78 us (0.54); the launches traced: 143 us -> 77.7 us
  local copies, waits for them, and re-layouts: 31.8 us -> 4.88 us
  matrix products: 23.2 us -> 0 us
  other arithmetic: 17.3 us -> 0 us
  between operations: 17.4 us -> 1.47 us
  Pallas kernels: 0 us -> 14.4 us
  waiting for transfers between devices: 32.5 us -> 34.9 us
  starting transfers between devices: 20.4 us -> 22.1 us
    dot_general x20 -> x0, matrix products: 23.2 us -> none  [the longest x3 6.72 us: weighted(): jnp.einsum('hqk,khd->qhd', probabilities.astype(jnp.bfloat16), split_head...]
    another operation x14 -> x0, local copies, waits for them, and re-layouts: 15.5 us -> none
    pallas_call x0 -> x6, Pallas kernels: none -> 14.4 us  [the longest x1 5.67 us: backward(): pl.pallas_call(functools.partial(backward_kernel, cycle, min(tokens, 512)...]
    cond x6 -> x0, local copies, waits for them, and re-layouts: 8.3 us -> none  [the longest x4 8.3 us: local(): lax.cond(present[column], remote_grads, skip_grads, pair_block, remote_pr...]
    another operation x4 -> x0, other arithmetic: 4.68 us -> none
    div x1 -> x0, other arithmetic: 3.6 us -> none  [local(): remote_probs = [expo / totals[:, :, None] for expo in remote_expo]]
    reduce_sum x1 -> x0, other arithmetic: 3.32 us -> none  [local(): totals = totals + jnp.sum(expo, axis=2)]
    ppermute x10 -> x19, waiting for transfers between devices: 31.8 us -> 34.9 us  [the longest x3 21.5 us: gather_rows(): lax.ppermute(out_weight, 'mp', [(i, (i - 2 * step) % count) for i in rang...]
  transfers between devices with their start and end apart: 11 -> 19, of which waited for: 5 -> 6; matrix products, arithmetic and copies ran while one was open for 36% -> 0% of each run, Pallas kernels for 0% -> 10%
where the time goes in v1:
time: 78 us; the launch traced here: 77.7 us
  waiting for transfers between devices  34.9 us (45%)
  starting transfers between devices  22.1 us (28%)
  Pallas kernels  14.4 us (18%)
  local copies, waits for them, and re-layouts  4.88 us (6%)
  between operations  1.47 us (2%)
    ppermute x3, waiting for transfers between devices, gather_rows(): lax.ppermute(out_weight, 'mp', [(i, (i - 2 * step) % count) for i in rang...  21.5 us
    ppermute x16, starting transfers between devices, exchange(): return lax.ppermute(value, axis, [(i, i ^ distance) for i in range(count)])  16 us
    ppermute x16, waiting for transfers between devices, exchange(): return lax.ppermute(value, axis, [(i, i ^ distance) for i in range(count)])  13.4 us
    ppermute x3, starting transfers between devices, gather_rows(): lax.ppermute(out_weight, 'mp', [(i, (i - 2 * step) % count) for i in rang...  6.11 us
    pallas_call x1, Pallas kernels, backward(): pl.pallas_call(functools.partial(backward_kernel, cycle, min(tokens, 512)...  5.67 us
    unnamed x38, local copies, waits for them, and re-layouts  4.88 us
    pallas_call x1, Pallas kernels, forward(): pl.pallas_call(functools.partial(forward_kernel, cycle, min(tokens, 512))...  4.56 us
  transfers between devices with their start and end apart: 19, of which 6 were waited for; matrix products, arithmetic and copies ran while one was open for 0% of the time, Pallas kernels for 10%

profile of v1, /device:TPU:0, one launch (start us, length us, event | category | flops | bytes accessed | tf_op | source)
XLA Modules:
  0.0 77.7 jit_solution(12080115729613809581)
XLA Ops:
  0.6 5.1 %collective-permute-start.6 = (bf16[128,1024]{1,0:T(8,128)(2,1)}, bf16[128,1024]{1,0:T(8,128)(2,1)S(1)}, u32[]{:S(2)}, u32[]{:S(2)}) collective-permute-start(bf16[128,1024]{1,0:T(8,128)(2,1)} %refs_0_.1), channel_id=1, source_target_pairs={{0,6},{1,7},{2,0},{3,1},{4,2},{5,3},{6,4},{7,5},{8,14},{9,15},{10,... | collective-permute-start | bytes 786440 | tf_op jit(solution)/shard_map/ppermute | solution.py:244
  5.7 1.0 %collective-permute-start.8 = (bf16[128,1024]{1,0:T(8,128)(2,1)}, bf16[128,1024]{1,0:T(8,128)(2,1)S(1)}, u32[]{:S(2)}, u32[]{:S(2)}) collective-permute-start(bf16[128,1024]{1,0:T(8,128)(2,1)} %refs_0_.1), channel_id=1, source_target_pairs={{0,2},{1,3},{2,4},{3,5},{4,6},{5,7},{6,0},{7,1},{8,10},{9,11},{10,... | collective-permute-start | bytes 786440 | tf_op jit(solution)/shard_map/ppermute | solution.py:244
  6.8 6.1 %collective-permute-done.6.refs_5_.refs_1_ = bf16[128,1024]{1,0:T(8,128)(2,1)S(1)} collective-permute-done((bf16[128,1024]{1,0:T(8,128)(2,1)}, bf16[128,1024]{1,0:T(8,128)(2,1)S(1)}, u32[]{:S(2)}, u32[]{:S(2)}) %collective-permute-start.6) | collective-permute-done | bytes 262176 | tf_op jit(solution)/shard_map/ppermute | solution.py:244
  12.8 15.4 %collective-permute-done.7.refs_6_.refs_2_ = bf16[128,1024]{1,0:T(8,128)(2,1)S(1)} collective-permute-done((bf16[128,1024]{1,0:T(8,128)(2,1)}, bf16[128,1024]{1,0:T(8,128)(2,1)S(1)}, u32[]{:S(2)}, u32[]{:S(2)}) %collective-permute-start.7) | collective-permute-done | bytes 262176 | tf_op jit(solution)/shard_map/ppermute | solution.py:244
  29.5 0.9 %copy-done.3 = bf16[128,1024]{1,0:T(8,128)(2,1)S(1)} copy-done((bf16[128,1024]{1,0:T(8,128)(2,1)S(1)}, bf16[128,1024]{1,0:T(8,128)(2,1)}, u32[]{:S(2)}) %copy-start.3) | copy-done | bytes 262168
  30.4 0.9 %copy-done.4 = bf16[128,1024]{1,0:T(8,128)(2,1)S(1)} copy-done((bf16[128,1024]{1,0:T(8,128)(2,1)S(1)}, bf16[128,1024]{1,0:T(8,128)(2,1)}, u32[]{:S(2)}) %copy-start.4) | copy-done | bytes 262168
  31.3 0.9 %copy-done.5 = bf16[128,1024]{1,0:T(8,128)(2,1)S(1)} copy-done((bf16[128,1024]{1,0:T(8,128)(2,1)S(1)}, bf16[128,1024]{1,0:T(8,128)(2,1)}, u32[]{:S(2)}) %copy-start.5) | copy-done | bytes 262168
  33.0 1.6 %collective-permute-start = (bf16[416,256]{1,0:T(8,128)(2,1)S(1)}, bf16[416,256]{1,0:T(8,128)(2,1)S(1)}, u32[]{:S(2)}, u32[]{:S(2)}) collective-permute-start(bf16[416,256]{1,0:T(8,128)(2,1)S(1)} %get-tuple-element.26), channel_id=1, source_target_pairs={{0,8},{8,0},{16,24},{24,16},{1,9},{9,1},{17,25},{25,17},{2,10},{10... | collective-permute-start | bytes 638984 | tf_op jit(solution)/shard_map/ppermute | solution.py:40
  34.5 1.5 %collective-permute-start.1 = (bf16[416,256]{1,0:T(8,128)(2,1)S(1)}, bf16[416,256]{1,0:T(8,128)(2,1)S(1)}, u32[]{:S(2)}, u32[]{:S(2)}) collective-permute-start(bf16[416,256]{1,0:T(8,128)(2,1)S(1)} %get-tuple-element.27), channel_id=1, source_target_pairs={{0,16},{8,24},{16,0},{24,8},{1,17},{9,25},{17,1},{25,9},{2,18},{10... | collective-permute-start | bytes 638984 | tf_op jit(solution)/shard_map/ppermute | solution.py:40
  36.6 1.1 %project_grad.1 = (bf16[128,256]{1,0:T(8,128)(2,1)S(1)}, bf16[128,256]{1,0:T(8,128)(2,1)S(1)}, bf16[128,256]{1,0:T(8,128)(2,1)S(1)}, bf16[128,256]{1,0:T(8,128)(2,1)S(1)}) custom-call(bf16[128,1024]{1,0:T(8,128)(2,1)S(1)} %copy-done.2, bf16[128,1024]{1,0:T(8,128)(2,1)S(1)} %copy-done, bf16[128,1024]{1,0:T(8,128)(2,1)S(1)} %collective-permute-done.6.refs_5_.refs_1_, ...), custom_call_target="tpu_custom_call" | custom-call | tf_op jit(solution)/shard_map/project_grad/pallas_call | solution.py:284
  38.3 1.5 %collective-permute-start.13 = (bf16[128,256]{1,0:T(8,128)(2,1)S(1)}, bf16[128,256]{1,0:T(8,128)(2,1)S(1)}, u32[]{:S(2)}, u32[]{:S(2)}) collective-permute-start(bf16[128,256]{1,0:T(8,128)(2,1)S(1)} %get-tuple-element.34), channel_id=1, source_target_pairs={{0,8},{8,0},{16,24},{24,16},{1,9},{9,1},{17,25},{25,17},{2,10},{10... | collective-permute-start | bytes 196616 | tf_op jit(solution)/shard_map/ppermute | solution.py:40
  39.8 1.5 %collective-permute-start.14 = (bf16[128,256]{1,0:T(8,128)(2,1)S(1)}, bf16[128,256]{1,0:T(8,128)(2,1)S(1)}, u32[]{:S(2)}, u32[]{:S(2)}) collective-permute-start(bf16[128,256]{1,0:T(8,128)(2,1)S(1)} %get-tuple-element.35), channel_id=1, source_target_pairs={{0,16},{8,24},{16,0},{24,8},{1,17},{9,25},{17,1},{25,9},{2,18},{10... | collective-permute-start | bytes 196616 | tf_op jit(solution)/shard_map/ppermute | solution.py:40
  41.3 2.3 %collective-permute-start.15 = (bf16[128,256]{1,0:T(8,128)(2,1)S(1)}, bf16[128,256]{1,0:T(8,128)(2,1)S(1)}, u32[]{:S(2)}, u32[]{:S(2)}) collective-permute-start(bf16[128,256]{1,0:T(8,128)(2,1)S(1)} %get-tuple-element.36), channel_id=1, source_target_pairs={{0,24},{8,16},{16,8},{24,0},{1,25},{9,17},{17,9},{25,1},{2,26},{10... | collective-permute-start | bytes 196616 | tf_op jit(solution)/shard_map/ppermute | solution.py:40
  43.6 3.5 %collective-permute-done.1.refs_2_ = bf16[416,256]{1,0:T(8,128)(2,1)S(1)} collective-permute-done((bf16[416,256]{1,0:T(8,128)(2,1)S(1)}, bf16[416,256]{1,0:T(8,128)(2,1)S(1)}, u32[]{:S(2)}, u32[]{:S(2)}) %collective-permute-start.1) | collective-permute-done | bytes 213024 | tf_op jit(solution)/shard_map/ppermute | solution.py:40
  47.9 4.6 %forward.1 = (bf16[128,256]{1,0:T(8,128)(2,1)}, bf16[128,256]{1,0:T(8,128)(2,1)}, bf16[128,256]{1,0:T(8,128)(2,1)}, bf16[128,256]{1,0:T(8,128)(2,1)}, f32[256,512]{1,0:T(8,128)}, /*index=5*/f32[8,512]{1,0:T(8,128)}) custom-call(bf16[416,256]{1,0:T(8,128)(2,1)} %copy-done.1, bf16[416,256]{1,0:T(8,128)(2,1)} %copy-done.10, bf16[416,256]{1,0:T(8,128)(2,1)} %copy-done.11, ...), custom_call_target="tpu_custom_call" | custom-call | tf_op jit(solution)/shard_map/forward/pallas_call | solution.py:151
  53.2 5.7 %backward.1 = (bf16[384,256]{1,0:T(8,128)(2,1)}, bf16[384,256]{1,0:T(8,128)(2,1)}, bf16[384,256]{1,0:T(8,128)(2,1)}, bf16[384,256]{1,0:T(8,128)(2,1)}) custom-call(bf16[416,256]{1,0:T(8,128)(2,1)} %copy-done.1, bf16[416,256]{1,0:T(8,128)(2,1)} %copy-done.10, bf16[416,256]{1,0:T(8,128)(2,1)} %copy-done.11, bf16[416,256]{1,0:T(8,128)(2,1)} %copy-done.12, ...), custom_call_target="tpu_custom_call" | custom-call | tf_op jit(solution)/shard_map/backward/pallas_call | solution.py:222
  58.8 1.0 %collective-permute-start.16 = (bf16[384,256]{1,0:T(8,128)(2,1)}, bf16[384,256]{1,0:T(8,128)(2,1)S(1)}, u32[]{:S(2)}, u32[]{:S(2)}) collective-permute-start(bf16[384,256]{1,0:T(8,128)(2,1)} %get-tuple-element.40), channel_id=1, source_target_pairs={{0,8},{8,0},{16,24},{24,16},{1,9},{9,1},{17,25},{25,17},{2,10},{10... | collective-permute-start | bytes 589832 | tf_op jit(solution)/shard_map/ppermute | solution.py:40
  59.8 1.5 %collective-permute-start.17 = (bf16[384,256]{1,0:T(8,128)(2,1)}, bf16[384,256]{1,0:T(8,128)(2,1)S(1)}, u32[]{:S(2)}, u32[]{:S(2)}) collective-permute-start(bf16[384,256]{1,0:T(8,128)(2,1)} %get-tuple-element.41), channel_id=1, source_target_pairs={{0,16},{8,24},{16,0},{24,8},{1,17},{9,25},{17,1},{25,9},{2,18},{10... | collective-permute-start | bytes 589832 | tf_op jit(solution)/shard_map/ppermute | solution.py:40
  61.3 1.4 %collective-permute-start.18 = (bf16[384,256]{1,0:T(8,128)(2,1)}, bf16[384,256]{1,0:T(8,128)(2,1)S(1)}, u32[]{:S(2)}, u32[]{:S(2)}) collective-permute-start(bf16[384,256]{1,0:T(8,128)(2,1)} %get-tuple-element.42), channel_id=1, source_target_pairs={{0,24},{8,16},{16,8},{24,0},{1,25},{9,17},{17,9},{25,1},{2,26},{10... | collective-permute-start | bytes 589832 | tf_op jit(solution)/shard_map/ppermute | solution.py:40
  63.3 1.5 %collective-permute-start.4 = (bf16[128,256]{1,0:T(8,128)(2,1)S(1)}, bf16[128,256]{1,0:T(8,128)(2,1)S(1)}, u32[]{:S(2)}, u32[]{:S(2)}) collective-permute-start(bf16[128,256]{1,0:T(8,128)(2,1)S(1)} %copy-done.17), channel_id=1, source_target_pairs={{0,16},{8,24},{16,0},{24,8},{1,17},{9,25},{17,1},{25,9},{2,18},{10... | collective-permute-start | bytes 196616 | tf_op jit(solution)/shard_map/ppermute | solution.py:40
  64.8 5.3 %collective-permute-done.3.refs_1_ = bf16[128,256]{1,0:T(8,128)(2,1)S(1)} collective-permute-done((bf16[128,256]{1,0:T(8,128)(2,1)S(1)}, bf16[128,256]{1,0:T(8,128)(2,1)S(1)}, u32[]{:S(2)}, u32[]{:S(2)}) %collective-permute-start.3) | collective-permute-done | bytes 65568 | tf_op jit(solution)/shard_map/ppermute | solution.py:40
  71.1 4.2 %collective-permute-done.5.refs_3_ = bf16[128,256]{1,0:T(8,128)(2,1)S(1)} collective-permute-done((bf16[128,256]{1,0:T(8,128)(2,1)S(1)}, bf16[128,256]{1,0:T(8,128)(2,1)S(1)}, u32[]{:S(2)}, u32[]{:S(2)}) %collective-permute-start.5) | collective-permute-done | bytes 65568 | tf_op jit(solution)/shard_map/ppermute | solution.py:40
  75.3 1.4 %project.1 = bf16[128,1024]{1,0:T(8,128)(2,1)} custom-call(bf16[128,256]{1,0:T(8,128)(2,1)S(1)} %copy-done.7, bf16[128,256]{1,0:T(8,128)(2,1)S(1)} %collective-permute-done.3.refs_1_, bf16[128,256]{1,0:T(8,128)(2,1)S(1)} %collective-permute-done.4.refs_2_, bf16[128,256]{1,0:T(8,128)(2,1)S(1)} %collective-permute-done.5.refs_3_, ...), custom_call_target="tpu_custom_call" | custom-call | tf_op jit(solution)/shard_map/project/pallas_call | solution.py:314
  76.7 1.0 %unpack.1 = (bf16[128,1024]{1,0:T(8,128)(2,1)}, bf16[128,1024]{1,0:T(8,128)(2,1)}, bf16[128,1024]{1,0:T(8,128)(2,1)}) custom-call(bf16[384,256]{1,0:T(8,128)(2,1)S(1)} %copy-done.6, bf16[384,256]{1,0:T(8,128)(2,1)S(1)} %collective-permute-done.16.refs_1_, bf16[384,256]{1,0:T(8,128)(2,1)S(1)} %collective-permute-done.17.refs_2_, ...), custom_call_target="tpu_custom_call" | custom-call | tf_op jit(solution)/shard_map/unpack/pallas_call | solution.py:350
  (58 shorter events, 5.3 us)
Async XLA Ops:
  0.6 28.8 %copy-start.9 = (s32[1,4]{1,0:T(1,128)S(1)}, s32[1,4]{1,0:T(1,128)}, u32[]{:S(2)}) copy-start(s32[1,4]{1,0:T(1,128)} %adj_ref.1) | copy-start | bytes 52
  0.6 12.2 %collective-permute-start.6 = (bf16[128,1024]{1,0:T(8,128)(2,1)}, bf16[128,1024]{1,0:T(8,128)(2,1)S(1)}, u32[]{:S(2)}, u32[]{:S(2)}) collective-permute-start(bf16[128,1024]{1,0:T(8,128)(2,1)} %refs_0_.1), channel_id=1, source_target_pairs={{0,6},{1,7},{2,0},{3,1},{4,2},{5,3},{6,4},{7,5},{8,14},{9,15},{10,... | collective-permute-start | bytes 786440 | tf_op jit(solution)/shard_map/ppermute | solution.py:244
  5.7 22.5 %collective-permute-start.7 = (bf16[128,1024]{1,0:T(8,128)(2,1)}, bf16[128,1024]{1,0:T(8,128)(2,1)S(1)}, u32[]{:S(2)}, u32[]{:S(2)}) collective-permute-start(bf16[128,1024]{1,0:T(8,128)(2,1)} %refs_0_.1), channel_id=1, source_target_pairs={{0,4},{1,5},{2,6},{3,7},{4,0},{5,1},{6,2},{7,3},{8,12},{9,13},{10,... | collective-permute-start | bytes 786440 | tf_op jit(solution)/shard_map/ppermute | solution.py:244
  5.7 22.5 %collective-permute-start.8 = (bf16[128,1024]{1,0:T(8,128)(2,1)}, bf16[128,1024]{1,0:T(8,128)(2,1)S(1)}, u32[]{:S(2)}, u32[]{:S(2)}) collective-permute-start(bf16[128,1024]{1,0:T(8,128)(2,1)} %refs_0_.1), channel_id=1, source_target_pairs={{0,2},{1,3},{2,4},{3,5},{4,6},{5,7},{6,0},{7,1},{8,10},{9,11},{10,... | collective-permute-start | bytes 786440 | tf_op jit(solution)/shard_map/ppermute | solution.py:244
  6.8 27.8 %collective-permute-start.9 = (bf16[128,1024]{1,0:T(8,128)(2,1)}, bf16[128,1024]{1,0:T(8,128)(2,1)S(1)}, u32[]{:S(2)}, u32[]{:S(2)}) collective-permute-start(bf16[128,1024]{1,0:T(8,128)(2,1)} %refs_0_.1), channel_id=1, source_target_pairs={{0,1},{1,0},{2,3},{3,2},{4,5},{5,4},{6,7},{7,6},{8,9},{9,8},{10,11... | collective-permute-start | bytes 786440 | tf_op jit(solution)/shard_map/ppermute | solution.py:40
  12.8 23.2 %collective-permute-start.10 = (bf16[128,1024]{1,0:T(8,128)(2,1)S(1)}, bf16[128,1024]{1,0:T(8,128)(2,1)S(1)}, u32[]{:S(2)}, u32[]{:S(2)}) collective-permute-start(bf16[128,1024]{1,0:T(8,128)(2,1)S(1)} %collective-permute-done.6.refs_5_.refs_1_), channel_id=1, source_target_pairs={{0,1},{1,0},{2,3},{3,2},{4,5},{5,4},{6,7},{7,6},{8,9},{9,8},{10,11... | collective-permute-start | bytes 786440 | tf_op jit(solution)/shard_map/ppermute | solution.py:40
  28.3 8.3 %collective-permute-start.11 = (bf16[128,1024]{1,0:T(8,128)(2,1)S(1)}, bf16[128,1024]{1,0:T(8,128)(2,1)S(1)}, u32[]{:S(2)}, u32[]{:S(2)}) collective-permute-start(bf16[128,1024]{1,0:T(8,128)(2,1)S(1)} %collective-permute-done.7.refs_6_.refs_2_), channel_id=1, source_target_pairs={{0,1},{1,0},{2,3},{3,2},{4,5},{5,4},{6,7},{7,6},{8,9},{9,8},{10,11... | collective-permute-start | bytes 786440 | tf_op jit(solution)/shard_map/ppermute | solution.py:40
  28.3 8.3 %collective-permute-start.12 = (bf16[128,1024]{1,0:T(8,128)(2,1)S(1)}, bf16[128,1024]{1,0:T(8,128)(2,1)S(1)}, u32[]{:S(2)}, u32[]{:S(2)}) collective-permute-start(bf16[128,1024]{1,0:T(8,128)(2,1)S(1)} %collective-permute-done.8.refs_7_.refs_3_), channel_id=1, source_target_pairs={{0,1},{1,0},{2,3},{3,2},{4,5},{5,4},{6,7},{7,6},{8,9},{9,8},{10,11... | collective-permute-start | bytes 786440 | tf_op jit(solution)/shard_map/ppermute | solution.py:40
  33.0 8.4 %collective-permute-start = (bf16[416,256]{1,0:T(8,128)(2,1)S(1)}, bf16[416,256]{1,0:T(8,128)(2,1)S(1)}, u32[]{:S(2)}, u32[]{:S(2)}) collective-permute-start(bf16[416,256]{1,0:T(8,128)(2,1)S(1)} %get-tuple-element.26), channel_id=1, source_target_pairs={{0,8},{8,0},{16,24},{24,16},{1,9},{9,1},{17,25},{25,17},{2,10},{10... | collective-permute-start | bytes 638984 | tf_op jit(solution)/shard_map/ppermute | solution.py:40
  34.5 12.6 %collective-permute-start.1 = (bf16[416,256]{1,0:T(8,128)(2,1)S(1)}, bf16[416,256]{1,0:T(8,128)(2,1)S(1)}, u32[]{:S(2)}, u32[]{:S(2)}) collective-permute-start(bf16[416,256]{1,0:T(8,128)(2,1)S(1)} %get-tuple-element.27), channel_id=1, source_target_pairs={{0,16},{8,24},{16,0},{24,8},{1,17},{9,25},{17,1},{25,9},{2,18},{10... | collective-permute-start | bytes 638984 | tf_op jit(solution)/shard_map/ppermute | solution.py:40
  36.1 11.1 %collective-permute-start.2 = (bf16[416,256]{1,0:T(8,128)(2,1)S(1)}, bf16[416,256]{1,0:T(8,128)(2,1)S(1)}, u32[]{:S(2)}, u32[]{:S(2)}) collective-permute-start(bf16[416,256]{1,0:T(8,128)(2,1)S(1)} %get-tuple-element.28), channel_id=1, source_target_pairs={{0,24},{8,16},{16,8},{24,0},{1,25},{9,17},{17,9},{25,1},{2,26},{10... | collective-permute-start | bytes 638984 | tf_op jit(solution)/shard_map/ppermute | solution.py:40
  38.3 14.2 %collective-permute-start.13 = (bf16[128,256]{1,0:T(8,128)(2,1)S(1)}, bf16[128,256]{1,0:T(8,128)(2,1)S(1)}, u32[]{:S(2)}, u32[]{:S(2)}) collective-permute-start(bf16[128,256]{1,0:T(8,128)(2,1)S(1)} %get-tuple-element.34), channel_id=1, source_target_pairs={{0,8},{8,0},{16,24},{24,16},{1,9},{9,1},{17,25},{25,17},{2,10},{10... | collective-permute-start | bytes 196616 | tf_op jit(solution)/shard_map/ppermute | solution.py:40
  39.8 12.7 %collective-permute-start.14 = (bf16[128,256]{1,0:T(8,128)(2,1)S(1)}, bf16[128,256]{1,0:T(8,128)(2,1)S(1)}, u32[]{:S(2)}, u32[]{:S(2)}) collective-permute-start(bf16[128,256]{1,0:T(8,128)(2,1)S(1)} %get-tuple-element.35), channel_id=1, source_target_pairs={{0,16},{8,24},{16,0},{24,8},{1,17},{9,25},{17,1},{25,9},{2,18},{10... | collective-permute-start | bytes 196616 | tf_op jit(solution)/shard_map/ppermute | solution.py:40
  41.3 11.2 %collective-permute-start.15 = (bf16[128,256]{1,0:T(8,128)(2,1)S(1)}, bf16[128,256]{1,0:T(8,128)(2,1)S(1)}, u32[]{:S(2)}, u32[]{:S(2)}) collective-permute-start(bf16[128,256]{1,0:T(8,128)(2,1)S(1)} %get-tuple-element.36), channel_id=1, source_target_pairs={{0,24},{8,16},{16,8},{24,0},{1,25},{9,17},{17,9},{25,1},{2,26},{10... | collective-permute-start | bytes 196616 | tf_op jit(solution)/shard_map/ppermute | solution.py:40
  53.1 9.6 %copy-start.18 = (bf16[128,256]{1,0:T(8,128)(2,1)S(1)}, bf16[128,256]{1,0:T(8,128)(2,1)}, u32[]{:S(2)}) copy-start(bf16[128,256]{1,0:T(8,128)(2,1)} %get-tuple-element.30) | copy-start | bytes 196612
  53.1 10.2 %copy-start.17 = (bf16[128,256]{1,0:T(8,128)(2,1)S(1)}, bf16[128,256]{1,0:T(8,128)(2,1)}, u32[]{:S(2)}) copy-start(bf16[128,256]{1,0:T(8,128)(2,1)} %get-tuple-element.31) | copy-start | bytes 196612
  53.1 17.0 %copy-start.16 = (bf16[128,256]{1,0:T(8,128)(2,1)S(1)}, bf16[128,256]{1,0:T(8,128)(2,1)}, u32[]{:S(2)}) copy-start(bf16[128,256]{1,0:T(8,128)(2,1)} %get-tuple-element.32) | copy-start | bytes 196612
  53.2 22.1 %copy-start.7 = (bf16[128,256]{1,0:T(8,128)(2,1)S(1)}, bf16[128,256]{1,0:T(8,128)(2,1)}, u32[]{:S(2)}) copy-start(bf16[128,256]{1,0:T(8,128)(2,1)} %get-tuple-element.29.refs_0_) | copy-start | bytes 196612
  58.8 17.9 %collective-permute-start.16 = (bf16[384,256]{1,0:T(8,128)(2,1)}, bf16[384,256]{1,0:T(8,128)(2,1)S(1)}, u32[]{:S(2)}, u32[]{:S(2)}) collective-permute-start(bf16[384,256]{1,0:T(8,128)(2,1)} %get-tuple-element.40), channel_id=1, source_target_pairs={{0,8},{8,0},{16,24},{24,16},{1,9},{9,1},{17,25},{25,17},{2,10},{10... | collective-permute-start | bytes 589832 | tf_op jit(solution)/shard_map/ppermute | solution.py:40
  59.8 16.9 %collective-permute-start.17 = (bf16[384,256]{1,0:T(8,128)(2,1)}, bf16[384,256]{1,0:T(8,128)(2,1)S(1)}, u32[]{:S(2)}, u32[]{:S(2)}) collective-permute-start(bf16[384,256]{1,0:T(8,128)(2,1)} %get-tuple-element.41), channel_id=1, source_target_pairs={{0,16},{8,24},{16,0},{24,8},{1,17},{9,25},{17,1},{25,9},{2,18},{10... | collective-permute-start | bytes 589832 | tf_op jit(solution)/shard_map/ppermute | solution.py:40
  61.3 15.4 %collective-permute-start.18 = (bf16[384,256]{1,0:T(8,128)(2,1)}, bf16[384,256]{1,0:T(8,128)(2,1)S(1)}, u32[]{:S(2)}, u32[]{:S(2)}) collective-permute-start(bf16[384,256]{1,0:T(8,128)(2,1)} %get-tuple-element.42), channel_id=1, source_target_pairs={{0,24},{8,16},{16,8},{24,0},{1,25},{9,17},{17,9},{25,1},{2,26},{10... | collective-permute-start | bytes 589832 | tf_op jit(solution)/shard_map/ppermute | solution.py:40
  62.7 7.4 %collective-permute-start.3 = (bf16[128,256]{1,0:T(8,128)(2,1)S(1)}, bf16[128,256]{1,0:T(8,128)(2,1)S(1)}, u32[]{:S(2)}, u32[]{:S(2)}) collective-permute-start(bf16[128,256]{1,0:T(8,128)(2,1)S(1)} %copy-done.18), channel_id=1, source_target_pairs={{0,8},{8,0},{16,24},{24,16},{1,9},{9,1},{17,25},{25,17},{2,10},{10... | collective-permute-start | bytes 196616 | tf_op jit(solution)/shard_map/ppermute | solution.py:40
  63.3 7.7 %collective-permute-start.4 = (bf16[128,256]{1,0:T(8,128)(2,1)S(1)}, bf16[128,256]{1,0:T(8,128)(2,1)S(1)}, u32[]{:S(2)}, u32[]{:S(2)}) collective-permute-start(bf16[128,256]{1,0:T(8,128)(2,1)S(1)} %copy-done.17), channel_id=1, source_target_pairs={{0,16},{8,24},{16,0},{24,8},{1,17},{9,25},{17,1},{25,9},{2,18},{10... | collective-permute-start | bytes 196616 | tf_op jit(solution)/shard_map/ppermute | solution.py:40
  70.1 5.2 %collective-permute-start.5 = (bf16[128,256]{1,0:T(8,128)(2,1)S(1)}, bf16[128,256]{1,0:T(8,128)(2,1)S(1)}, u32[]{:S(2)}, u32[]{:S(2)}) collective-permute-start(bf16[128,256]{1,0:T(8,128)(2,1)S(1)} %copy-done.16), channel_id=1, source_target_pairs={{0,24},{8,16},{16,8},{24,0},{1,25},{9,17},{17,9},{25,1},{2,26},{10... | collective-permute-start | bytes 196616 | tf_op jit(solution)/shard_map/ppermute | solution.py:40
  (14 other events, 27.3 us)

commit v2 on v1

v2 whole, which is shorter than its diff:
```python
import functools

import jax
import jax.numpy as jnp
from jax import lax
from jax.experimental import pallas as pl
from jax.experimental.pallas import tpu as pltpu
from jax.sharding import PartitionSpec as P

HEADS = 16
HEAD_DIM = 64
META = 32

score_scale = 0.125
log2_scale = 0.125 * 1.4426950408889634
cycle_offsets = (1, -1, 2, -2)
absent = -1e30
bf16 = jnp.bfloat16
f32 = jnp.float32


def dot_nn(a, b):
    return lax.dot_general(a, b, (((1,), (0,)), ((), ())), preferred_element_type=f32)


def dot_nt(a, b):
    return lax.dot_general(a, b, (((1,), (1,)), ((), ())), preferred_element_type=f32)


def vmem():
    return pl.BlockSpec(memory_space=pltpu.VMEM)


def params(mib):
    return pltpu.CompilerParams(vmem_limit_bytes=mib * 1024 * 1024)


def anywhere():
    return pl.BlockSpec(memory_space=pltpu.HBM)


def exchange(value, axis, distance):
    count = lax.axis_size(axis)
    return lax.ppermute(value, axis, [(i, i ^ distance) for i in range(count)])


def swapped(chunks):
    return [chunks[0]] + [exchange(chunks[k], "seq", k) for k in range(1, len(chunks))]


def group_of(cycle, member, chip):
    turn = (member + chip) % cycle
    if cycle == 4:
        return turn ^ (((turn ^ (turn >> 1)) & 1) * 3)
    return turn


def my_place():
    rank = lax.axis_index("mp")
    return lax.axis_index("seq"), rank // 2, lax.rem(rank, 2)


def columns_at(first, width):
    return pl.ds(pl.multiple_of(first, width), width)


def pack_kernel(cycle, square, q_ref, k_ref, v_ref, w_ref, up_ref, adj_ref, cnt_ref, *refs):
    outs = refs[:cycle]
    sems, w_sem = refs[cycle + 1:]
    rows, model = q_ref.shape
    width = model // cycle
    own, chip, _ = my_place()
    copies = []
    if width % 128 == 0:
        for place in range(cycle):
            group = group_of(cycle, lax.bitwise_xor(own, place), chip)
            for at, ref in enumerate((q_ref, k_ref, v_ref)):
                copies.append(
                    pltpu.make_async_copy(
                        ref.at[:, columns_at(group * width, width)],
                        outs[place].at[at * rows:(at + 1) * rows, :],
                        sems.at[place, at],
                    )
                )
                copies[-1].start()
    copies.append(pltpu.make_async_copy(w_ref, refs[cycle], w_sem))
    copies[-1].start()
    if square:
        for part in range(cycle):
            first = 3 * rows + META + part * rows
            copies.append(
                pltpu.make_async_copy(
                    up_ref.at[:, part * width:(part + 1) * width],
                    outs[1].at[first:first + rows, :],
                    sems.at[part, 3],
                )
            )
            copies[-1].start()
    lines = lax.broadcasted_iota(jnp.int32, (META, width), 0)
    meta = jnp.where(lines == 0, 1, 0)
    for column, offset in enumerate(cycle_offsets):
        named = lax.rem(own - offset + 2 * cycle, cycle)
        meta = meta + jnp.where(
            (lines == lax.bitwise_xor(own, named)) & (adj_ref[0, column] > 0), 1, 0
        )
    meta = jnp.where(lines == META - 1, cnt_ref[0], meta).astype(f32).astype(bf16)
    for place in range(cycle):
        outs[place][3 * rows:3 * rows + META, :] = meta
        if width % 128:
            group = group_of(cycle, lax.bitwise_xor(own, place), chip)
            for other in range(cycle):
                @pl.when(group == other)
                def _():
                    for at, ref in enumerate((q_ref, k_ref, v_ref)):
                        outs[place][at * rows:(at + 1) * rows, :] = ref[
                            :, other * width:(other + 1) * width
                        ]
    for copy in copies:
        copy.wait()


def pack(cycle, square, queries, keys, values, out_weight, upstream, adjacency, counts):
    rows, model = queries.shape
    width = model // cycle
    smem = pl.BlockSpec(memory_space=pltpu.SMEM)
    return pl.pallas_call(
        functools.partial(pack_kernel, cycle, square),
        out_shape=[
            jax.ShapeDtypeStruct(
                (3 * rows + META + (model if square and place == 1 else 0) * rows // width, width), bf16
            )
            for place in range(cycle)
        ]
        + [jax.ShapeDtypeStruct(out_weight.shape, bf16)],
        in_specs=[anywhere() if width % 128 == 0 else vmem()] * 3
        + [anywhere()] * 2
        + [smem] * 2,
        out_specs=[vmem()] * (cycle + 1),
        scratch_shapes=[pltpu.SemaphoreType.DMA((cycle, 4)), pltpu.SemaphoreType.DMA],
        compiler_params=params(62),
        name="pack",
    )(queries, keys, values, out_weight, upstream, adjacency, counts)


def fill(cycle, rows, chunks, bias, *parts):
    for place in range(cycle):
        for at, part in parts:
            part[place * rows:(place + 1) * rows, :] = chunks[place][at * rows:(at + 1) * rows, :]
    lines = lax.broadcasted_iota(jnp.int32, (rows, rows), 0).astype(f32)
    lists = [chunks[place][3 * rows:3 * rows + META, :].astype(f32) for place in range(cycle)]
    for key_place in range(cycle):
        count = lists[key_place][META - 1:, :1]
        valid = lines < count
        for query_place in range(cycle):
            way = key_place ^ query_place
            times = lists[query_place][way:way + 1, :1]
            term = jnp.where(times > 0, jnp.log2(jnp.maximum(times, 1.0)), absent)
            bias[
                key_place * rows:(key_place + 1) * rows,
                query_place * rows:(query_place + 1) * rows,
            ] = jnp.where(valid, term, absent)


def head_tile(width):
    return min(128, width)


def only_head(tile, which):
    lanes = lax.broadcasted_iota(jnp.int32, tile.shape, 1)
    inside = (lanes >= which * HEAD_DIM) & (lanes < (which + 1) * HEAD_DIM)
    return jnp.where(inside, tile, jnp.zeros_like(tile))


def forward_kernel(cycle, query_tile, *refs):
    chunks = refs[:cycle]
    outs = refs[cycle:2 * cycle]
    att_t, lse, q_all, k_all, v_all, bias = refs[2 * cycle:]
    width = q_all.shape[1]
    tokens = q_all.shape[0]
    rows = tokens // cycle
    fill(cycle, rows, chunks, bias, (0, q_all), (1, k_all), (2, v_all))
    tile = head_tile(width)
    v_t = v_all[...].astype(f32).T.astype(bf16)
    for start in range(0, tokens, query_tile):
        span = slice(start, start + query_tile)
        for head in range(width // HEAD_DIM):
            at = head * HEAD_DIM // tile * tile
            which = (head * HEAD_DIM - at) // HEAD_DIM
            scores = dot_nt(
                k_all[:, at:at + tile], only_head(q_all[span, at:at + tile], which)
            )
            scores = scores * log2_scale + bias[:, span]
            largest = jnp.max(scores, axis=0, keepdims=True)
            expo = jnp.exp2(scores - largest)
            total = jnp.sum(expo, axis=0, keepdims=True)
            probs = (expo * (1.0 / total)).astype(bf16)
            lse[head:head + 1, span] = largest + jnp.log2(total)
            att_t[head * HEAD_DIM:(head + 1) * HEAD_DIM, span] = dot_nn(
                v_t[head * HEAD_DIM:(head + 1) * HEAD_DIM, :], probs
            )
    attended = att_t[...].T.astype(bf16)
    for place in range(cycle):
        outs[place][...] = attended[place * rows:(place + 1) * rows, :]


def forward(cycle, chunks):
    width = chunks[0].shape[1]
    rows = (chunks[0].shape[0] - META) // 3
    tokens = rows * cycle
    outs = pl.pallas_call(
        functools.partial(forward_kernel, cycle, min(tokens, 512)),
        out_shape=[jax.ShapeDtypeStruct((rows, width), bf16)] * cycle
        + [
            jax.ShapeDtypeStruct((width, tokens), f32),
            jax.ShapeDtypeStruct((8, tokens), f32),
        ],
        in_specs=[vmem()] * cycle,
        out_specs=[vmem()] * (cycle + 2),
        scratch_shapes=[pltpu.VMEM((tokens, width), bf16)] * 3
        + [pltpu.VMEM((tokens, tokens), f32)],
        compiler_params=params(16 if tokens <= 512 else 60),
        name="forward",
    )(*chunks)
    return outs[:cycle], outs[cycle], outs[cycle + 1]


def backward_kernel(cycle, query_tile, grad_count, *refs):
    chunks = refs[:cycle]
    refs = refs[cycle:]
    grads = refs[:grad_count]
    attended = refs[grad_count:grad_count + cycle]
    refs = refs[grad_count + cycle:]
    att_t, lse = refs[:2]
    outs = refs[2:cycle + 2]
    q_all, k_all, v_all, g_all, dq_t, dk, dv, bias = refs[cycle + 2:]
    width = q_all.shape[1]
    tokens = q_all.shape[0]
    rows = tokens // cycle
    fill(cycle, rows, chunks, bias, (0, q_all), (1, k_all), (2, v_all))
    filled = 0
    for grad in grads:
        g_all[filled:filled + grad.shape[0], :] = grad[...]
        filled += grad.shape[0]
    tile = head_tile(width)
    k_t = k_all[...].astype(f32).T.astype(bf16)
    g_t = g_all[...].astype(f32).T
    product = g_t * att_t[...].astype(bf16).astype(f32)
    for start in range(0, tokens, query_tile):
        span = slice(start, start + query_tile)
        for at in range(0, width, tile):
            dk_tile = dv_tile = None
            for which in range(tile // HEAD_DIM):
                low = at + which * HEAD_DIM
                head = low // HEAD_DIM
                delta = jnp.sum(product[low:low + HEAD_DIM, span], axis=0, keepdims=True)
                q_head = only_head(q_all[span, at:at + tile], which)
                g_head = only_head(g_all[span, at:at + tile], which)
                scores = dot_nt(k_all[:, at:at + tile], q_head)
                probs = jnp.exp2(
                    scores * log2_scale + bias[:, span] - lse[head:head + 1, span]
                )
                grad_probs = dot_nt(v_all[:, at:at + tile], g_head)
                grad_scores = (probs * (grad_probs - delta)).astype(bf16)
                dk_head = dot_nn(grad_scores, q_head)
                dv_head = dot_nn(probs.astype(bf16), g_head)
                dk_tile = dk_head if dk_tile is None else dk_tile + dk_head
                dv_tile = dv_head if dv_tile is None else dv_tile + dv_head
                dq_t[low:low + HEAD_DIM, span] = dot_nn(k_t[low:low + HEAD_DIM, :], grad_scores)
            if start == 0:
                dk[:, at:at + tile] = dk_tile
                dv[:, at:at + tile] = dv_tile
            else:
                dk[:, at:at + tile] += dk_tile
                dv[:, at:at + tile] += dv_tile
    dq = (dq_t[...] * score_scale).T.astype(bf16)
    for place in range(cycle):
        span = slice(place * rows, (place + 1) * rows)
        outs[place][:rows, :] = dq[span, :]
        outs[place][rows:2 * rows, :] = (dk[span, :] * score_scale).astype(bf16)
        outs[place][2 * rows:3 * rows, :] = dv[span, :].astype(bf16)
        outs[place][3 * rows:, :] = attended[place][...]


def backward(cycle, chunks, grads, attended, att_t, lse):
    rows, width = attended[0].shape
    tokens = rows * cycle
    return pl.pallas_call(
        functools.partial(backward_kernel, cycle, min(tokens, 512), len(grads)),
        out_shape=[jax.ShapeDtypeStruct((4 * rows, width), bf16)] * cycle,
        in_specs=[vmem()] * (2 * cycle + len(grads) + 2),
        out_specs=[vmem()] * cycle,
        scratch_shapes=[pltpu.VMEM((tokens, width), bf16)] * 4
        + [pltpu.VMEM((width, tokens), f32)]
        + [pltpu.VMEM((tokens, width), f32)] * 2
        + [pltpu.VMEM((tokens, tokens), f32)],
        compiler_params=params(16 if tokens <= 512 else 60),
        name="backward",
    )(*chunks, *grads, *attended, att_t, lse)


def fetch_rows(out_weight, place):
    cycle, count = lax.axis_size("seq"), lax.axis_size("mp")
    pairs = []
    for member in range(cycle):
        for rank in range(count):
            owner = 2 * group_of(cycle, member ^ place, rank // 2) + rank % 2
            pairs.append((member * count + owner, member * count + rank))
    half = lax.ppermute(out_weight, ("seq", "mp"), pairs)
    return [half, exchange(half, "mp", 1)]


def both_halves(halves, core):
    mine, other = halves[0][...], halves[1][...]
    first = core == 0
    return jnp.concatenate([jnp.where(first, mine, other), jnp.where(first, other, mine)], axis=0)


def near_kernel(up_ref, next_ref, *refs):
    halves = refs[:4]
    near, far, both, sem = refs[-4:]
    rows, model = up_ref.shape
    width = next_ref.shape[1]
    copy = pltpu.make_async_copy(up_ref, both.at[:rows, :], sem)
    copy.start()
    first = next_ref.shape[0] - model // width * rows
    for part in range(model // width):
        both[rows:, part * width:(part + 1) * width] = next_ref[
            first + part * rows:first + (part + 1) * rows, :
        ]
    copy.wait()
    _, _, core = my_place()
    half = halves[0].shape[0]
    for group, out in enumerate((near, far)):
        for side in range(2):
            at = columns_at((core if side == 0 else 1 - core) * half, half)
            out[:, at] = dot_nt(both[...], halves[2 * group + side][...]).astype(bf16)


def near_grads(upstream, neighbour, halves, after):
    rows, width = upstream.shape[0], 2 * halves[0].shape[0]
    return pl.pallas_call(
        near_kernel,
        out_shape=[jax.ShapeDtypeStruct((2 * rows, width), bf16)] * 2,
        in_specs=[anywhere()] + [vmem()] * 5 + [pl.BlockSpec(memory_space=pl.ANY)] * len(after),
        out_specs=[vmem()] * 2,
        scratch_shapes=[
            pltpu.VMEM((2 * rows, upstream.shape[1]), bf16),
            pltpu.SemaphoreType.DMA,
        ],
        compiler_params=params(8),
        name="near_grads",
    )(upstream, neighbour, *halves, *after)


def grad_kernel(cycle, up_ref, *refs):
    _, _, core = my_place()
    outs = refs[2 * cycle:]
    for place in range(cycle):
        rows = both_halves(refs[2 * place:2 * place + 2], core)
        outs[place][...] = dot_nt(up_ref[...], rows).astype(bf16)


def project_grad(cycle, upstream, halves):
    rows, model = upstream.shape
    return pl.pallas_call(
        functools.partial(grad_kernel, cycle),
        out_shape=[jax.ShapeDtypeStruct((rows, model // cycle), bf16)] * cycle,
        in_specs=[vmem()] * (1 + 2 * cycle),
        out_specs=[vmem()] * cycle,
        compiler_params=params(8),
        name="project_grad",
    )(upstream, *halves)


def finish_kernel(cycle, *refs):
    chunks = refs[:cycle]
    halves = refs[cycle:3 * cycle]
    mixed, *outs = refs[3 * cycle:3 * cycle + 4]
    rows, model = mixed.shape
    width = model // cycle
    own, chip, core = my_place()
    copies = []
    total = None
    for place in range(cycle):
        group = group_of(cycle, lax.bitwise_xor(own, place), chip)
        if width % 128 == 0:
            for at, out in enumerate(outs):
                copies.append(
                    pltpu.make_async_copy(
                        chunks[place].at[at * rows:(at + 1) * rows, :],
                        out.at[:, columns_at(group * width, width)],
                        refs[-1].at[place, at],
                    )
                )
                copies[-1].start()
        else:
            for other in range(cycle):
                @pl.when(group == other)
                def _():
                    for at, out in enumerate(outs):
                        out[:, other * width:(other + 1) * width] = chunks[place][
                            at * rows:(at + 1) * rows, :
                        ]
    for place in range(cycle):
        pair = halves[2 * place:2 * place + 2]
        if width % 256 == 0:
            half = width // 2
            terms = [
                dot_nn(
                    chunks[place][3 * rows:, columns_at((core if side == 0 else 1 - core) * half, half)],
                    pair[side][...],
                )
                for side in range(2)
            ]
        else:
            terms = [dot_nn(chunks[place][3 * rows:, :], both_halves(pair, core))]
        for term in terms:
            total = term if total is None else total + term
    mixed[...] = total.astype(bf16)
    for copy in copies:
        copy.wait()


def finish(cycle, chunks, halves):
    rows = chunks[0].shape[0] // 4
    model = chunks[0].shape[1] * cycle
    aligned = model // cycle % 128 == 0
    return pl.pallas_call(
        functools.partial(finish_kernel, cycle),
        out_shape=[jax.ShapeDtypeStruct((rows, model), bf16)] * 4,
        in_specs=[vmem()] * (3 * cycle),
        out_specs=[vmem()] + [anywhere() if aligned else vmem()] * 3,
        scratch_shapes=[pltpu.SemaphoreType.DMA((cycle, 3))],
        compiler_params=params(8),
        name="finish",
    )(*chunks, *halves)


def local(queries, keys, values, out_weight, upstream, adjacency, counts):
    cycle = lax.axis_size("seq")
    square = cycle == 4 and lax.axis_size("mp") == 8
    *chunks, out_weight = pack(
        cycle, square, queries, keys, values, out_weight, upstream, adjacency, counts
    )
    chunks = swapped(chunks)
    halves = {}
    for place in (0, 2, 1, 3) if square else range(cycle):
        halves[place] = fetch_rows(out_weight, place)
    if square:
        near, far = near_grads(upstream, chunks[1], halves[0] + halves[2], chunks[2:])
        grads = [near, exchange(far, "seq", 2)]
    else:
        grads = swapped(project_grad(cycle, upstream, sum((halves[k] for k in range(cycle)), [])))
    attended, att_t, lse = forward(cycle, chunks)
    terms = swapped(backward(cycle, chunks, grads, attended, att_t, lse))
    return tuple(finish(cycle, terms, sum((halves[k] for k in range(cycle)), [])))


def solution(mesh):
    tokens = P(("seq", "mp"), None)
    return jax.shard_map(
        local,
        mesh=mesh,
        in_specs=(tokens, tokens, tokens, P("mp", None), tokens, tokens, P(("seq", "mp"))),
        out_specs=(tokens,) * 4,
        check_vma=False,
    )
```

time: 78 us -> 65.8 us (0.84)
  waiting for transfers between devices: 34.9 us -> 24.8 us
  starting transfers between devices: 22.1 us -> 27.2 us
  local copies, waits for them, and re-layouts: 4.88 us -> 0.01 us
  Pallas kernels: 14.4 us -> 12.1 us
    ppermute x3 -> x4, waiting for transfers between devices: 21.5 us -> 6.38 us  [fetch_rows(): half = lax.ppermute(out_weight, ('seq', 'mp'), pairs)]
    ppermute x3 -> x4, starting transfers between devices: 6.11 us -> 16.7 us  [fetch_rows(): half = lax.ppermute(out_weight, ('seq', 'mp'), pairs)]
    ppermute x16 -> x11, starting transfers between devices: 16 us -> 10.5 us  [exchange(): return lax.ppermute(value, axis, [(i, i ^ distance) for i in range(count)])]
    ppermute x16 -> x11, waiting for transfers between devices: 13.4 us -> 18.4 us  [exchange(): return lax.ppermute(value, axis, [(i, i ^ distance) for i in range(count)])]
    unnamed x38 -> x4, local copies, waits for them, and re-layouts: 4.88 us -> 0.01 us
    pallas_call x1, Pallas kernels: 5.67 us -> 3.19 us  [backward(): pl.pallas_call(functools.partial(backward_kernel, cycle, min(tokens, 512)...]
    pallas_call x4 -> x3, Pallas kernels: 4.13 us -> 6.41 us  [the longest x1 3.45 us: pack(): pl.pallas_call(functools.partial(pack_kernel, cycle, square), out_shape=[...]
    pallas_call x1, Pallas kernels: 4.56 us -> 2.45 us  [forward(): pl.pallas_call(functools.partial(forward_kernel, cycle, min(tokens, 512))...]
  transfers between devices with their start and end apart: 19 -> 15, of which waited for: 6 -> 7; matrix products, arithmetic and copies ran while one was open for 0% -> 0% of each run, Pallas kernels for 10% -> 10%
where the time goes in v2:
time: 65.8 us; the launch traced here: 65.5 us
  starting transfers between devices  27.2 us (41%)
  waiting for transfers between devices  24.8 us (38%)
  Pallas kernels  12.1 us (18%)
  between operations  1.41 us (2%)
    ppermute x11, waiting for transfers between devices, exchange(): return lax.ppermute(value, axis, [(i, i ^ distance) for i in range(count)])  18.4 us
    ppermute x4, starting transfers between devices, fetch_rows(): half = lax.ppermute(out_weight, ('seq', 'mp'), pairs)  16.7 us
    ppermute x11, starting transfers between devices, exchange(): return lax.ppermute(value, axis, [(i, i ^ distance) for i in range(count)])  10.5 us
    ppermute x4, waiting for transfers between devices, fetch_rows(): half = lax.ppermute(out_weight, ('seq', 'mp'), pairs)  6.38 us
    pallas_call x1, Pallas kernels, pack(): pl.pallas_call(functools.partial(pack_kernel, cycle, square), out_shape=[...  3.45 us
    pallas_call x1, Pallas kernels, backward(): pl.pallas_call(functools.partial(backward_kernel, cycle, min(tokens, 512)...  3.19 us
    pallas_call x1, Pallas kernels, forward(): pl.pallas_call(functools.partial(forward_kernel, cycle, min(tokens, 512))...  2.45 us
    pallas_call x1, Pallas kernels, finish(): pl.pallas_call(functools.partial(finish_kernel, cycle), out_shape=[jax.Sh...  2.19 us
  transfers between devices with their start and end apart: 15, of which 7 were waited for; matrix products, arithmetic and copies ran while one was open for 0% of the time, Pallas kernels for 10%

profile of v2, /device:TPU:0, one launch (start us, length us, event | category | flops | bytes accessed | tf_op | source)
XLA Modules:
  0.0 65.5 jit_solution(12658873501467118326)
XLA Ops:
  1.3 3.4 %pack.1 = (bf16[416,256]{1,0:T(8,128)(2,1)}, bf16[928,256]{1,0:T(8,128)(2,1)}, bf16[416,256]{1,0:T(8,128)(2,1)}, bf16[416,256]{1,0:T(8,128)(2,1)}, bf16[128,1024]{1,0:T(8,128)(2,1)}) custom-call(bf16[128,1024]{1,0:T(8,128)(2,1)} %q_ref.1, bf16[128,1024]{1,0:T(8,128)(2,1)} %k_ref.1, bf16[128,1024]{1,0:T(8,128)(2,1)} %v_ref.1, bf16[128,1024]{1,0:T(8,128)(2,1)} %w_ref.1, ...), custom_call_target="tpu_custom_call" | custom-call | tf_op jit(solution)/shard_map/pack/pallas_call | solution.py:126
  4.7 1.6 %collective-permute-start.3 = (bf16[128,1024]{1,0:T(8,128)(2,1)}, bf16[128,1024]{1,0:T(8,128)(2,1)S(1)}, u32[]{:S(2)}, u32[]{:S(2)}) collective-permute-start(bf16[128,1024]{1,0:T(8,128)(2,1)} %get-tuple-element.25), channel_id=1, source_target_pairs={{0,0},{1,1},{4,2},{5,3},{2,4},{3,5},{6,6},{7,7},{12,8},{13,9},{10,... | collective-permute-start | bytes 786440 | tf_op jit(solution)/shard_map/ppermute | solution.py:308
  6.4 6.7 %collective-permute-start.5 = (bf16[128,1024]{1,0:T(8,128)(2,1)}, bf16[128,1024]{1,0:T(8,128)(2,1)S(1)}, u32[]{:S(2)}, u32[]{:S(2)}) collective-permute-start(bf16[128,1024]{1,0:T(8,128)(2,1)} %get-tuple-element.25), channel_id=1, source_target_pairs={{2,0},{3,1},{6,2},{7,3},{0,4},{1,5},{4,6},{5,7},{14,8},{15,9},{8,1... | collective-permute-start | bytes 786440 | tf_op jit(solution)/shard_map/ppermute | solution.py:308
  13.1 2.1 %collective-permute-start = (bf16[928,256]{1,0:T(8,128)(2,1)}, bf16[928,256]{1,0:T(8,128)(2,1)S(1)}, u32[]{:S(2)}, u32[]{:S(2)}) collective-permute-start(bf16[928,256]{1,0:T(8,128)(2,1)} %get-tuple-element.22), channel_id=1, source_target_pairs={{0,8},{8,0},{16,24},{24,16},{1,9},{9,1},{17,25},{25,17},{2,10},{10... | collective-permute-start | bytes 1425416 | tf_op jit(solution)/shard_map/ppermute | solution.py:44
  15.2 1.7 %collective-permute-start.1 = (bf16[416,256]{1,0:T(8,128)(2,1)}, bf16[416,256]{1,0:T(8,128)(2,1)S(1)}, u32[]{:S(2)}, u32[]{:S(2)}) collective-permute-start(bf16[416,256]{1,0:T(8,128)(2,1)} %get-tuple-element.23), channel_id=1, source_target_pairs={{0,16},{8,24},{16,0},{24,8},{1,17},{9,25},{17,1},{25,9},{2,18},{10... | collective-permute-start | bytes 638984 | tf_op jit(solution)/shard_map/ppermute | solution.py:44
  16.9 0.1 collective-permute-start.4
  17.0 2.4 %collective-permute-done.5.refs_2_.refs_8_ = bf16[128,1024]{1,0:T(8,128)(2,1)S(1)} collective-permute-done((bf16[128,1024]{1,0:T(8,128)(2,1)}, bf16[128,1024]{1,0:T(8,128)(2,1)S(1)}, u32[]{:S(2)}, u32[]{:S(2)}) %collective-permute-start.5) | collective-permute-done | bytes 262176 | tf_op jit(solution)/shard_map/ppermute | solution.py:308
  19.4 0.0 collective-permute-start.6
  19.4 2.4 %collective-permute-done.1.refs_4_.refs_2_ = bf16[416,256]{1,0:T(8,128)(2,1)S(1)} collective-permute-done((bf16[416,256]{1,0:T(8,128)(2,1)}, bf16[416,256]{1,0:T(8,128)(2,1)S(1)}, u32[]{:S(2)}, u32[]{:S(2)}) %collective-permute-start.1) | collective-permute-done | bytes 213024 | tf_op jit(solution)/shard_map/ppermute | solution.py:44
  21.8 5.4 %collective-permute-start.11 = (bf16[128,1024]{1,0:T(8,128)(2,1)}, bf16[128,1024]{1,0:T(8,128)(2,1)S(1)}, u32[]{:S(2)}, u32[]{:S(2)}) collective-permute-start(bf16[128,1024]{1,0:T(8,128)(2,1)} %get-tuple-element.25), channel_id=1, source_target_pairs={{4,0},{5,1},{2,2},{3,3},{6,4},{7,5},{0,6},{1,7},{8,8},{9,9},{12,10... | collective-permute-start | bytes 786440 | tf_op jit(solution)/shard_map/ppermute | solution.py:308
  27.3 4.2 %collective-permute-done.2.refs_5_.refs_3_ = bf16[416,256]{1,0:T(8,128)(2,1)S(1)} collective-permute-done((bf16[416,256]{1,0:T(8,128)(2,1)}, bf16[416,256]{1,0:T(8,128)(2,1)S(1)}, u32[]{:S(2)}, u32[]{:S(2)}) %collective-permute-start.2) | collective-permute-done | bytes 213024 | tf_op jit(solution)/shard_map/ppermute | solution.py:44
  31.5 3.0 %collective-permute-start.13 = (bf16[128,1024]{1,0:T(8,128)(2,1)}, bf16[128,1024]{1,0:T(8,128)(2,1)S(1)}, u32[]{:S(2)}, u32[]{:S(2)}) collective-permute-start(bf16[128,1024]{1,0:T(8,128)(2,1)} %get-tuple-element.25), channel_id=1, source_target_pairs={{6,0},{7,1},{0,2},{1,3},{4,4},{5,5},{2,6},{3,7},{10,8},{11,9},{14,... | collective-permute-start | bytes 786440 | tf_op jit(solution)/shard_map/ppermute | solution.py:308
  34.5 0.8 %near_grads.1 = (bf16[256,256]{1,0:T(8,128)(2,1)S(1)}, bf16[256,256]{1,0:T(8,128)(2,1)S(1)}) custom-call(bf16[128,1024]{1,0:T(8,128)(2,1)S(1)} %copy-done, bf16[928,256]{1,0:T(8,128)(2,1)S(1)} %collective-permute-done.next_ref.refs_1_, bf16[128,1024]{1,0:T(8,128)(2,1)S(1)} %collective-permute-done.3.refs_0_.refs_4_, ...), custom_call_target="tpu_custom_call" | custom-call | tf_op jit(solution)/shard_map/near_grads/pallas_call | solution.py:341
  35.3 3.0 %collective-permute-start.7 = (bf16[256,256]{1,0:T(8,128)(2,1)S(1)}, bf16[256,256]{1,0:T(8,128)(2,1)S(1)}, u32[]{:S(2)}, u32[]{:S(2)}) collective-permute-start(bf16[256,256]{1,0:T(8,128)(2,1)S(1)} %get-tuple-element.27), channel_id=1, source_target_pairs={{0,16},{8,24},{16,0},{24,8},{1,17},{9,25},{17,1},{25,9},{2,18},{10... | collective-permute-start | bytes 393224 | tf_op jit(solution)/shard_map/ppermute | solution.py:44
  38.3 4.0 %collective-permute-done.13.refs_10_ = bf16[128,1024]{1,0:T(8,128)(2,1)S(1)} collective-permute-done((bf16[128,1024]{1,0:T(8,128)(2,1)}, bf16[128,1024]{1,0:T(8,128)(2,1)S(1)}, u32[]{:S(2)}, u32[]{:S(2)}) %collective-permute-start.13) | collective-permute-done | bytes 262176 | tf_op jit(solution)/shard_map/ppermute | solution.py:308
  42.3 2.5 %forward.1 = (bf16[128,256]{1,0:T(8,128)(2,1)S(1)}, bf16[128,256]{1,0:T(8,128)(2,1)S(1)}, bf16[128,256]{1,0:T(8,128)(2,1)S(1)}, bf16[128,256]{1,0:T(8,128)(2,1)S...) custom-call(bf16[416,256]{1,0:T(8,128)(2,1)S(1)} %copy-done.1, ...), custom_call_target="tpu_custom_call" | custom-call | tf_op jit(solution)/shard_map/forward/pallas_call | solution.py:210
  44.8 3.2 %backward.1 = (bf16[512,256]{1,0:T(8,128)(2,1)S(1)}, bf16[512,256]{1,0:T(8,128)(2,1)S(1)}, bf16[512,256]{1,0:T(8,128)(2,1)S(1)}, bf16[512,256]{1,0:T(8,128)(2,1)S(1)}) custom-call(bf16[416,256]{1,0:T(8,128)(2,1)S(1)} %copy-done.1, bf16[928,256]{1,0:T(8,128)(2,1)S(1)} %collective-permute-done.next_ref.refs_1_, ...), custom_call_target="tpu_custom_call" | custom-call | tf_op jit(solution)/shard_map/backward/pallas_call | solution.py:287
  48.0 0.1 collective-permute-start.10
  48.1 1.3 %collective-permute-start.8 = (bf16[512,256]{1,0:T(8,128)(2,1)S(1)}, bf16[512,256]{1,0:T(8,128)(2,1)S(1)}, u32[]{:S(2)}, u32[]{:S(2)}) collective-permute-start(bf16[512,256]{1,0:T(8,128)(2,1)S(1)} %get-tuple-element.35), channel_id=1, source_target_pairs={{0,8},{8,0},{16,24},{24,16},{1,9},{9,1},{17,25},{25,17},{2,10},{10... | collective-permute-start | bytes 786440 | tf_op jit(solution)/shard_map/ppermute | solution.py:44
  49.4 2.2 %collective-permute-start.9 = (bf16[512,256]{1,0:T(8,128)(2,1)S(1)}, bf16[512,256]{1,0:T(8,128)(2,1)S(1)}, u32[]{:S(2)}, u32[]{:S(2)}) collective-permute-start(bf16[512,256]{1,0:T(8,128)(2,1)S(1)} %get-tuple-element.36), channel_id=1, source_target_pairs={{0,16},{8,24},{16,0},{24,8},{1,17},{9,25},{17,1},{25,9},{2,18},{10... | collective-permute-start | bytes 786440 | tf_op jit(solution)/shard_map/ppermute | solution.py:44
  51.6 6.5 %collective-permute-done.10.refs_3_ = bf16[512,256]{1,0:T(8,128)(2,1)S(1)} collective-permute-done((bf16[512,256]{1,0:T(8,128)(2,1)S(1)}, bf16[512,256]{1,0:T(8,128)(2,1)S(1)}, u32[]{:S(2)}, u32[]{:S(2)}) %collective-permute-start.10) | collective-permute-done | bytes 262176 | tf_op jit(solution)/shard_map/ppermute | solution.py:44
  58.1 3.6 %collective-permute-done.8.refs_1_ = bf16[512,256]{1,0:T(8,128)(2,1)S(1)} collective-permute-done((bf16[512,256]{1,0:T(8,128)(2,1)S(1)}, bf16[512,256]{1,0:T(8,128)(2,1)S(1)}, u32[]{:S(2)}, u32[]{:S(2)}) %collective-permute-start.8) | collective-permute-done | bytes 262176 | tf_op jit(solution)/shard_map/ppermute | solution.py:44
  61.7 1.6 %collective-permute-done.9.refs_2_ = bf16[512,256]{1,0:T(8,128)(2,1)S(1)} collective-permute-done((bf16[512,256]{1,0:T(8,128)(2,1)S(1)}, bf16[512,256]{1,0:T(8,128)(2,1)S(1)}, u32[]{:S(2)}, u32[]{:S(2)}) %collective-permute-start.9) | collective-permute-done | bytes 262176 | tf_op jit(solution)/shard_map/ppermute | solution.py:44
  63.3 2.2 %finish.1 = (bf16[128,1024]{1,0:T(8,128)(2,1)}, bf16[128,1024]{1,0:T(8,128)(2,1)}, bf16[128,1024]{1,0:T(8,128)(2,1)}, bf16[128,1024]{1,0:T(8,128)(2,1)}) custom-call(bf16[512,256]{1,0:T(8,128)(2,1)S(1)} %get-tuple-element.34.refs_0_, bf16[512,256]{1,0:T(8,128)(2,1)S(1)} %collective-permute-done.8.refs_1_, ...), custom_call_target="tpu_custom_call" | custom-call | tf_op jit(solution)/shard_map/finish/pallas_call | solution.py:428
  (15 shorter events, 0.0 us)
Async XLA Ops:
  1.3 33.3 %copy-start = (bf16[128,1024]{1,0:T(8,128)(2,1)S(1)}, bf16[128,1024]{1,0:T(8,128)(2,1)}, u32[]{:S(2)}) copy-start(bf16[128,1024]{1,0:T(8,128)(2,1)} %up_ref.3) | copy-start | bytes 786436
  4.7 12.2 %collective-permute-start.3 = (bf16[128,1024]{1,0:T(8,128)(2,1)}, bf16[128,1024]{1,0:T(8,128)(2,1)S(1)}, u32[]{:S(2)}, u32[]{:S(2)}) collective-permute-start(bf16[128,1024]{1,0:T(8,128)(2,1)} %get-tuple-element.25), channel_id=1, source_target_pairs={{0,0},{1,1},{4,2},{5,3},{2,4},{3,5},{6,6},{7,7},{12,8},{13,9},{10,... | collective-permute-start | bytes 786440 | tf_op jit(solution)/shard_map/ppermute | solution.py:308
  6.4 13.0 %collective-permute-start.5 = (bf16[128,1024]{1,0:T(8,128)(2,1)}, bf16[128,1024]{1,0:T(8,128)(2,1)S(1)}, u32[]{:S(2)}, u32[]{:S(2)}) collective-permute-start(bf16[128,1024]{1,0:T(8,128)(2,1)} %get-tuple-element.25), channel_id=1, source_target_pairs={{2,0},{3,1},{6,2},{7,3},{0,4},{1,5},{4,6},{5,7},{14,8},{15,9},{8,1... | collective-permute-start | bytes 786440 | tf_op jit(solution)/shard_map/ppermute | solution.py:308
  13.1 21.4 %collective-permute-start = (bf16[928,256]{1,0:T(8,128)(2,1)}, bf16[928,256]{1,0:T(8,128)(2,1)S(1)}, u32[]{:S(2)}, u32[]{:S(2)}) collective-permute-start(bf16[928,256]{1,0:T(8,128)(2,1)} %get-tuple-element.22), channel_id=1, source_target_pairs={{0,8},{8,0},{16,24},{24,16},{1,9},{9,1},{17,25},{25,17},{2,10},{10... | collective-permute-start | bytes 1425416 | tf_op jit(solution)/shard_map/ppermute | solution.py:44
  15.2 6.6 %collective-permute-start.1 = (bf16[416,256]{1,0:T(8,128)(2,1)}, bf16[416,256]{1,0:T(8,128)(2,1)S(1)}, u32[]{:S(2)}, u32[]{:S(2)}) collective-permute-start(bf16[416,256]{1,0:T(8,128)(2,1)} %get-tuple-element.23), channel_id=1, source_target_pairs={{0,16},{8,24},{16,0},{24,8},{1,17},{9,25},{17,1},{25,9},{2,18},{10... | collective-permute-start | bytes 638984 | tf_op jit(solution)/shard_map/ppermute | solution.py:44
  16.9 25.4 %copy-start.1 = (bf16[416,256]{1,0:T(8,128)(2,1)S(1)}, bf16[416,256]{1,0:T(8,128)(2,1)}, u32[]{:S(2)}) copy-start(bf16[416,256]{1,0:T(8,128)(2,1)} %get-tuple-element.21.refs_0_) | copy-start | bytes 638980
  16.9 14.6 %collective-permute-start.2 = (bf16[416,256]{1,0:T(8,128)(2,1)}, bf16[416,256]{1,0:T(8,128)(2,1)S(1)}, u32[]{:S(2)}, u32[]{:S(2)}) collective-permute-start(bf16[416,256]{1,0:T(8,128)(2,1)} %get-tuple-element.24), channel_id=1, source_target_pairs={{0,24},{8,16},{16,8},{24,0},{1,25},{9,17},{17,9},{25,1},{2,26},{10... | collective-permute-start | bytes 638984 | tf_op jit(solution)/shard_map/ppermute | solution.py:44
  16.9 17.6 %collective-permute-start.4 = (bf16[128,1024]{1,0:T(8,128)(2,1)S(1)}, bf16[128,1024]{1,0:T(8,128)(2,1)S(1)}, u32[]{:S(2)}, u32[]{:S(2)}) collective-permute-start(bf16[128,1024]{1,0:T(8,128)(2,1)S(1)} %collective-permute-done.3.refs_0_.refs_4_), channel_id=1, source_target_pairs={{0,1},{1,0},{2,3},{3,2},{4,5},{5,4},{6,7},{7,6},{8,9},{9,8},{10,11... | collective-permute-start | bytes 786440 | tf_op jit(solution)/shard_map/ppermute | solution.py:44
  19.4 15.1 %collective-permute-start.6 = (bf16[128,1024]{1,0:T(8,128)(2,1)S(1)}, bf16[128,1024]{1,0:T(8,128)(2,1)S(1)}, u32[]{:S(2)}, u32[]{:S(2)}) collective-permute-start(bf16[128,1024]{1,0:T(8,128)(2,1)S(1)} %collective-permute-done.5.refs_2_.refs_8_), channel_id=1, source_target_pairs={{0,1},{1,0},{2,3},{3,2},{4,5},{5,4},{6,7},{7,6},{8,9},{9,8},{10,11... | collective-permute-start | bytes 786440 | tf_op jit(solution)/shard_map/ppermute | solution.py:44
  21.8 16.5 %collective-permute-start.11 = (bf16[128,1024]{1,0:T(8,128)(2,1)}, bf16[128,1024]{1,0:T(8,128)(2,1)S(1)}, u32[]{:S(2)}, u32[]{:S(2)}) collective-permute-start(bf16[128,1024]{1,0:T(8,128)(2,1)} %get-tuple-element.25), channel_id=1, source_target_pairs={{4,0},{5,1},{2,2},{3,3},{6,4},{7,5},{0,6},{1,7},{8,8},{9,9},{12,10... | collective-permute-start | bytes 786440 | tf_op jit(solution)/shard_map/ppermute | solution.py:308
  31.5 10.8 %collective-permute-start.13 = (bf16[128,1024]{1,0:T(8,128)(2,1)}, bf16[128,1024]{1,0:T(8,128)(2,1)S(1)}, u32[]{:S(2)}, u32[]{:S(2)}) collective-permute-start(bf16[128,1024]{1,0:T(8,128)(2,1)} %get-tuple-element.25), channel_id=1, source_target_pairs={{6,0},{7,1},{0,2},{1,3},{4,4},{5,5},{2,6},{3,7},{10,8},{11,9},{14,... | collective-permute-start | bytes 786440 | tf_op jit(solution)/shard_map/ppermute | solution.py:308
  35.3 9.5 %collective-permute-start.7 = (bf16[256,256]{1,0:T(8,128)(2,1)S(1)}, bf16[256,256]{1,0:T(8,128)(2,1)S(1)}, u32[]{:S(2)}, u32[]{:S(2)}) collective-permute-start(bf16[256,256]{1,0:T(8,128)(2,1)S(1)} %get-tuple-element.27), channel_id=1, source_target_pairs={{0,16},{8,24},{16,0},{24,8},{1,17},{9,25},{17,1},{25,9},{2,18},{10... | collective-permute-start | bytes 393224 | tf_op jit(solution)/shard_map/ppermute | solution.py:44
  38.3 13.2 %collective-permute-start.12 = (bf16[128,1024]{1,0:T(8,128)(2,1)S(1)}, bf16[128,1024]{1,0:T(8,128)(2,1)S(1)}, u32[]{:S(2)}, u32[]{:S(2)}) collective-permute-start(bf16[128,1024]{1,0:T(8,128)(2,1)S(1)} %collective-permute-done.11.refs_6_), channel_id=1, source_target_pairs={{0,1},{1,0},{2,3},{3,2},{4,5},{5,4},{6,7},{7,6},{8,9},{9,8},{10,11... | collective-permute-start | bytes 786440 | tf_op jit(solution)/shard_map/ppermute | solution.py:44
  42.3 9.2 %collective-permute-start.14 = (bf16[128,1024]{1,0:T(8,128)(2,1)S(1)}, bf16[128,1024]{1,0:T(8,128)(2,1)S(1)}, u32[]{:S(2)}, u32[]{:S(2)}) collective-permute-start(bf16[128,1024]{1,0:T(8,128)(2,1)S(1)} %collective-permute-done.13.refs_10_), channel_id=1, source_target_pairs={{0,1},{1,0},{2,3},{3,2},{4,5},{5,4},{6,7},{7,6},{8,9},{9,8},{10,11... | collective-permute-start | bytes 786440 | tf_op jit(solution)/shard_map/ppermute | solution.py:44
  48.0 10.1 %collective-permute-start.10 = (bf16[512,256]{1,0:T(8,128)(2,1)S(1)}, bf16[512,256]{1,0:T(8,128)(2,1)S(1)}, u32[]{:S(2)}, u32[]{:S(2)}) collective-permute-start(bf16[512,256]{1,0:T(8,128)(2,1)S(1)} %get-tuple-element.37), channel_id=1, source_target_pairs={{0,24},{8,16},{16,8},{24,0},{1,25},{9,17},{17,9},{25,1},{2,26},{10... | collective-permute-start | bytes 786440 | tf_op jit(solution)/shard_map/ppermute | solution.py:44
  48.1 13.6 %collective-permute-start.8 = (bf16[512,256]{1,0:T(8,128)(2,1)S(1)}, bf16[512,256]{1,0:T(8,128)(2,1)S(1)}, u32[]{:S(2)}, u32[]{:S(2)}) collective-permute-start(bf16[512,256]{1,0:T(8,128)(2,1)S(1)} %get-tuple-element.35), channel_id=1, source_target_pairs={{0,8},{8,0},{16,24},{24,16},{1,9},{9,1},{17,25},{25,17},{2,10},{10... | collective-permute-start | bytes 786440 | tf_op jit(solution)/shard_map/ppermute | solution.py:44
  49.4 13.9 %collective-permute-start.9 = (bf16[512,256]{1,0:T(8,128)(2,1)S(1)}, bf16[512,256]{1,0:T(8,128)(2,1)S(1)}, u32[]{:S(2)}, u32[]{:S(2)}) collective-permute-start(bf16[512,256]{1,0:T(8,128)(2,1)S(1)} %get-tuple-element.36), channel_id=1, source_target_pairs={{0,16},{8,24},{16,0},{24,8},{1,17},{9,25},{17,1},{25,9},{2,18},{10... | collective-permute-start | bytes 786440 | tf_op jit(solution)/shard_map/ppermute | solution.py:44

commit v3 on v2

v3 whole, which is shorter than its diff:
```python
import functools

import jax
import jax.numpy as jnp
from jax import lax
from jax.experimental import pallas as pl
from jax.experimental.pallas import tpu as pltpu
from jax.sharding import PartitionSpec as P

HEADS = 16
HEAD_DIM = 64
META = 32

score_scale = 0.125
log2_scale = 0.125 * 1.4426950408889634
cycle_offsets = (1, -1, 2, -2)
absent = -1e30
bf16 = jnp.bfloat16
f32 = jnp.float32


def dot_nn(a, b):
    return lax.dot_general(a, b, (((1,), (0,)), ((), ())), preferred_element_type=f32)


def dot_nt(a, b):
    return lax.dot_general(a, b, (((1,), (1,)), ((), ())), preferred_element_type=f32)


def vmem():
    return pl.BlockSpec(memory_space=pltpu.VMEM)


def params(mib):
    return pltpu.CompilerParams(vmem_limit_bytes=mib * 1024 * 1024)


def unread():
    return pl.BlockSpec(memory_space=pl.ANY)


def anywhere():
    return pl.BlockSpec(memory_space=pltpu.HBM)


def cost(micros):
    return pl.CostEstimate(flops=int(micros * 1e9), bytes_accessed=0, transcendentals=0)


def exchange(value, axis, distance):
    count = lax.axis_size(axis)
    return lax.ppermute(value, axis, [(i, i ^ distance) for i in range(count)])


def swapped(chunks):
    return [chunks[0]] + [exchange(chunks[k], "seq", k) for k in range(1, len(chunks))]


def group_of(cycle, member, chip):
    turn = (member + chip) % cycle
    if cycle == 4:
        return turn ^ (((turn ^ (turn >> 1)) & 1) * 3)
    return turn


def my_place():
    rank = lax.axis_index("mp")
    return lax.axis_index("seq"), rank // 2, lax.rem(rank, 2)


def columns_at(first, width):
    return pl.ds(pl.multiple_of(first, width), width)


def pack_kernel(cycle, places, extra, q_ref, k_ref, v_ref, adj_ref, cnt_ref, *refs):
    refs, (sems, more_sems) = refs[:-2], refs[-2:]
    outs = refs[-len(places) - extra:]
    rows, model = q_ref.shape
    width = model // cycle
    own, chip, _ = my_place()
    copies = []
    if width % 128 == 0:
        for place, out in zip(places, outs):
            group = group_of(cycle, lax.bitwise_xor(own, place), chip)
            for at, ref in enumerate((q_ref, k_ref, v_ref)):
                copies.append(
                    pltpu.make_async_copy(
                        ref.at[:, columns_at(group * width, width)],
                        out.at[at * rows:(at + 1) * rows, :],
                        sems.at[place, at],
                    )
                )
                copies[-1].start()
    for at in range(extra):
        copies.append(
            pltpu.make_async_copy(refs[at], outs[len(places) + at], more_sems.at[at])
        )
        copies[-1].start()
    lines = lax.broadcasted_iota(jnp.int32, (META, width), 0)
    meta = jnp.where(lines == 0, 1, 0)
    for column, offset in enumerate(cycle_offsets):
        named = lax.rem(own - offset + 2 * cycle, cycle)
        meta = meta + jnp.where(
            (lines == lax.bitwise_xor(own, named)) & (adj_ref[0, column] > 0), 1, 0
        )
    meta = jnp.where(lines == META - 1, cnt_ref[0], meta).astype(f32).astype(bf16)
    for place, out in zip(places, outs):
        out[3 * rows:, :] = meta
        if width % 128:
            group = group_of(cycle, lax.bitwise_xor(own, place), chip)
            for other in range(cycle):
                @pl.when(group == other)
                def _():
                    for at, ref in enumerate((q_ref, k_ref, v_ref)):
                        out[at * rows:(at + 1) * rows, :] = ref[
                            :, other * width:(other + 1) * width
                        ]
    for copy in copies:
        copy.wait()


def pack(cycle, places, tensors, extra=(), after=()):
    rows, model = tensors[0].shape
    width = model // cycle
    smem = pl.BlockSpec(memory_space=pltpu.SMEM)
    return pl.pallas_call(
        functools.partial(pack_kernel, cycle, places, len(extra)),
        out_shape=[jax.ShapeDtypeStruct((3 * rows + META, width), bf16)] * len(places)
        + [jax.ShapeDtypeStruct(array.shape, bf16) for array in extra],
        in_specs=[anywhere() if width % 128 == 0 else vmem()] * 3
        + [smem] * 2
        + [anywhere()] * len(extra)
        + [unread()] * len(after),
        out_specs=[vmem()] * (len(places) + len(extra)),
        scratch_shapes=[pltpu.SemaphoreType.DMA((cycle, 3)), pltpu.SemaphoreType.DMA((2,))],
        compiler_params=params(8 if extra else 62),
        cost_estimate=cost(5),
        name="pack",
    )(*tensors, *extra, *after)


def gather_kernel(cycle, *refs):
    chunks = refs[:cycle]
    q_all, k_all, v_all, k_t, v_t, bias = refs[cycle:]
    rows = q_all.shape[0] // cycle
    for place in range(cycle):
        for at, part in enumerate((q_all, k_all, v_all)):
            part[place * rows:(place + 1) * rows, :] = chunks[place][at * rows:(at + 1) * rows, :]
    k_t[...] = k_all[...].astype(f32).T.astype(bf16)
    v_t[...] = v_all[...].astype(f32).T.astype(bf16)
    lines = lax.broadcasted_iota(jnp.int32, (rows, rows), 0).astype(f32)
    lists = [chunks[place][3 * rows:, :].astype(f32) for place in range(cycle)]
    for key_place in range(cycle):
        count = lists[key_place][META - 1:, :1]
        valid = lines < count
        for query_place in range(cycle):
            way = key_place ^ query_place
            times = lists[query_place][way:way + 1, :1]
            term = jnp.where(times > 0, jnp.log2(jnp.maximum(times, 1.0)), absent)
            bias[
                key_place * rows:(key_place + 1) * rows,
                query_place * rows:(query_place + 1) * rows,
            ] = jnp.where(valid, term, absent)


def gather(cycle, chunks):
    width = chunks[0].shape[1]
    rows = (chunks[0].shape[0] - META) // 3
    tokens = rows * cycle
    return pl.pallas_call(
        functools.partial(gather_kernel, cycle),
        out_shape=[jax.ShapeDtypeStruct((tokens, width), bf16)] * 3
        + [jax.ShapeDtypeStruct((width, tokens), bf16)] * 2
        + [jax.ShapeDtypeStruct((tokens, tokens), f32)],
        in_specs=[vmem()] * cycle,
        out_specs=[vmem()] * 6,
        compiler_params=params(8 if tokens <= 512 else 40),
        cost_estimate=cost(5),
        name="gather",
    )(*chunks)


def head_tile(width):
    return min(128, width)


def only_head(tile, which):
    lanes = lax.broadcasted_iota(jnp.int32, tile.shape, 1)
    inside = (lanes >= which * HEAD_DIM) & (lanes < (which + 1) * HEAD_DIM)
    return jnp.where(inside, tile, jnp.zeros_like(tile))


def forward_kernel(query_tile, q_all, k_all, v_t, bias, *refs):
    outs = refs[:-2]
    att_t, lse = refs[-2:]
    tokens, width = q_all.shape
    tile = head_tile(width)
    for start in range(0, tokens, query_tile):
        span = slice(start, start + query_tile)
        for head in range(width // HEAD_DIM):
            at = head * HEAD_DIM // tile * tile
            which = (head * HEAD_DIM - at) // HEAD_DIM
            scores = dot_nt(
                k_all[:, at:at + tile], only_head(q_all[span, at:at + tile], which)
            )
            scores = scores * log2_scale + bias[:, span]
            largest = jnp.max(scores, axis=0, keepdims=True)
            expo = jnp.exp2(scores - largest)
            total = jnp.sum(expo, axis=0, keepdims=True)
            probs = (expo * (1.0 / total)).astype(bf16)
            lse[head:head + 1, span] = largest + jnp.log2(total)
            att_t[head * HEAD_DIM:(head + 1) * HEAD_DIM, span] = dot_nn(
                v_t[head * HEAD_DIM:(head + 1) * HEAD_DIM, :], probs
            )
    attended = att_t[...].T.astype(bf16)
    filled = 0
    for out in outs:
        out[...] = attended[filled:filled + out.shape[0], :]
        filled += out.shape[0]


def forward(cycle, together, q_all, k_all, v_t, bias):
    tokens, width = q_all.shape
    rows = tokens // cycle
    parts = cycle // together
    outs = pl.pallas_call(
        functools.partial(forward_kernel, min(tokens, 512)),
        out_shape=[jax.ShapeDtypeStruct((together * rows, width), bf16)] * parts
        + [
            jax.ShapeDtypeStruct((width, tokens), f32),
            jax.ShapeDtypeStruct((8, tokens), f32),
        ],
        in_specs=[vmem()] * 4,
        out_specs=[vmem()] * (parts + 2),
        compiler_params=params(16 if tokens <= 512 else 60),
        cost_estimate=cost(3),
        name="forward",
    )(q_all, k_all, v_t, bias)
    return outs[:parts], outs[parts], outs[parts + 1]


def backward_kernel(cycle, query_tile, grad_count, att_count, *refs):
    q_all, k_all, v_all, k_t, bias, att_t, lse = refs[:7]
    refs = refs[7:]
    grads = refs[:grad_count]
    attended = refs[grad_count:grad_count + att_count]
    outs = refs[-4 - cycle:-4]
    g_all, dq_t, dk, dv = refs[-4:]
    width = q_all.shape[1]
    tokens = q_all.shape[0]
    rows = tokens // cycle
    filled = 0
    for grad in grads:
        g_all[filled:filled + grad.shape[0], :] = grad[...]
        filled += grad.shape[0]
    tile = head_tile(width)
    g_t = g_all[...].astype(f32).T
    product = g_t * att_t[...].astype(bf16).astype(f32)
    for start in range(0, tokens, query_tile):
        span = slice(start, start + query_tile)
        for at in range(0, width, tile):
            dk_tile = dv_tile = None
            for which in range(tile // HEAD_DIM):
                low = at + which * HEAD_DIM
                head = low // HEAD_DIM
                delta = jnp.sum(product[low:low + HEAD_DIM, span], axis=0, keepdims=True)
                q_head = only_head(q_all[span, at:at + tile], which)
                g_head = only_head(g_all[span, at:at + tile], which)
                scores = dot_nt(k_all[:, at:at + tile], q_head)
                probs = jnp.exp2(
                    scores * log2_scale + bias[:, span] - lse[head:head + 1, span]
                )
                grad_probs = dot_nt(v_all[:, at:at + tile], g_head)
                grad_scores = (probs * (grad_probs - delta)).astype(bf16)
                dk_head = dot_nn(grad_scores, q_head)
                dv_head = dot_nn(probs.astype(bf16), g_head)
                dk_tile = dk_head if dk_tile is None else dk_tile + dk_head
                dv_tile = dv_head if dv_tile is None else dv_tile + dv_head
                dq_t[low:low + HEAD_DIM, span] = dot_nn(k_t[low:low + HEAD_DIM, :], grad_scores)
            if start == 0:
                dk[:, at:at + tile] = dk_tile
                dv[:, at:at + tile] = dv_tile
            else:
                dk[:, at:at + tile] += dk_tile
                dv[:, at:at + tile] += dv_tile
    dq = (dq_t[...] * score_scale).T.astype(bf16)
    for place in range(cycle):
        span = slice(place * rows, (place + 1) * rows)
        outs[place][:rows, :] = dq[span, :]
        outs[place][rows:2 * rows, :] = (dk[span, :] * score_scale).astype(bf16)
        outs[place][2 * rows:3 * rows, :] = dv[span, :].astype(bf16)
        if attended:
            outs[place][3 * rows:, :] = attended[place][...]


def backward(cycle, inputs, grads, attended, after):
    tokens, width = inputs[0].shape
    rows = tokens // cycle
    return pl.pallas_call(
        functools.partial(backward_kernel, cycle, min(tokens, 512), len(grads), len(attended)),
        out_shape=[jax.ShapeDtypeStruct(((4 if attended else 3) * rows, width), bf16)] * cycle,
        in_specs=[vmem()] * (len(inputs) + len(grads) + len(attended)) + [unread()] * len(after),
        out_specs=[vmem()] * cycle,
        scratch_shapes=[
            pltpu.VMEM((tokens, width), bf16),
            pltpu.VMEM((width, tokens), f32),
            pltpu.VMEM((tokens, width), f32),
            pltpu.VMEM((tokens, width), f32),
        ],
        compiler_params=params(16 if tokens <= 512 else 60),
        cost_estimate=cost(3),
        name="backward",
    )(*inputs, *grads, *attended, *after)


def fetch_rows(out_weight, place):
    cycle, count = lax.axis_size("seq"), lax.axis_size("mp")
    pairs = []
    for member in range(cycle):
        for rank in range(count):
            owner = 2 * group_of(cycle, member ^ place, rank // 2) + rank % 2
            pairs.append((member * count + owner, member * count + rank))
    return lax.ppermute(out_weight, ("seq", "mp"), pairs)


def with_other_core(half):
    return [half, exchange(half, "mp", 1)]


def both_halves(halves, core):
    mine, other = halves[0][...], halves[1][...]
    first = core == 0
    return jnp.concatenate([jnp.where(first, mine, other), jnp.where(first, other, mine)], axis=0)


def half_columns(halves, core, side):
    half = halves[0].shape[0]
    return columns_at((core if side == 0 else 1 - core) * half, half)


def near_kernel(up_ref, next_ref, *refs):
    halves = refs[:4]
    near, far = refs[-2:]
    rows = up_ref.shape[0]
    _, _, core = my_place()
    for group, out in enumerate((far, near)):
        for side in range(2):
            weight = halves[2 * (1 - group) + side]
            for block, ref in enumerate((up_ref, next_ref)):
                out[block * rows:(block + 1) * rows, half_columns(halves, core, side)] = dot_nt(
                    ref[...], weight[...]
                ).astype(bf16)


def near_grads(upstream, next_upstream, halves, after):
    rows, width = upstream.shape[0], 2 * halves[0].shape[0]
    return pl.pallas_call(
        near_kernel,
        out_shape=[jax.ShapeDtypeStruct((2 * rows, width), bf16)] * 2,
        in_specs=[vmem()] * 6 + [unread()] * len(after),
        out_specs=[vmem()] * 2,
        compiler_params=params(8),
        cost_estimate=cost(1),
        name="near_grads",
    )(upstream, next_upstream, *halves, *after)


def mix_kernel(near_ref, far_ref, *refs):
    halves = refs[:4]
    own, other = refs[-2:]
    rows = own.shape[0]
    _, _, core = my_place()
    total = None
    for group, ref in enumerate((near_ref, far_ref)):
        for side in range(2):
            term = dot_nn(
                ref[:, half_columns(halves, core, side)], halves[2 * group + side][...]
            )
            total = term if total is None else total + term
    own[...] = total[:rows, :]
    other[...] = total[rows:, :].astype(bf16)


def mix(near, far, halves, after):
    rows, model = near.shape[0] // 2, halves[0].shape[1]
    return pl.pallas_call(
        mix_kernel,
        out_shape=[
            jax.ShapeDtypeStruct((rows, model), f32),
            jax.ShapeDtypeStruct((rows, model), bf16),
        ],
        in_specs=[vmem()] * 6 + [unread()] * len(after),
        out_specs=[vmem()] * 2,
        compiler_params=params(8),
        cost_estimate=cost(1),
        name="mix",
    )(near, far, *halves, *after)


def grad_kernel(cycle, up_ref, *refs):
    _, _, core = my_place()
    outs = refs[2 * cycle:]
    for place in range(cycle):
        rows = both_halves(refs[2 * place:2 * place + 2], core)
        outs[place][...] = dot_nt(up_ref[...], rows).astype(bf16)


def project_grad(cycle, upstream, halves):
    rows, model = upstream.shape
    return pl.pallas_call(
        functools.partial(grad_kernel, cycle),
        out_shape=[jax.ShapeDtypeStruct((rows, model // cycle), bf16)] * cycle,
        in_specs=[vmem()] * (1 + 2 * cycle),
        out_specs=[vmem()] * cycle,
        compiler_params=params(8),
        name="project_grad",
    )(upstream, *halves)


def place_columns(chunks, outs, sems):
    cycle = len(chunks)
    rows, model = outs[0].shape
    width = model // cycle
    own, chip, _ = my_place()
    copies = []
    for place in range(cycle):
        group = group_of(cycle, lax.bitwise_xor(own, place), chip)
        if width % 128 == 0:
            for at, out in enumerate(outs):
                copies.append(
                    pltpu.make_async_copy(
                        chunks[place].at[at * rows:(at + 1) * rows, :],
                        out.at[:, columns_at(group * width, width)],
                        sems.at[place, at],
                    )
                )
                copies[-1].start()
        else:
            for other in range(cycle):
                @pl.when(group == other)
                def _():
                    for at, out in enumerate(outs):
                        out[:, other * width:(other + 1) * width] = chunks[place][
                            at * rows:(at + 1) * rows, :
                        ]
    return copies


def finish_kernel(cycle, *refs):
    chunks = refs[:cycle]
    mixed, *outs = refs[-5:-1]
    copies = place_columns(chunks, outs, refs[-1])
    rows = mixed.shape[0]
    if len(refs) == cycle + 7:
        mine, landed = refs[cycle:cycle + 2]
        mixed[...] = (mine[...] + landed[...].astype(f32)).astype(bf16)
    else:
        halves = refs[cycle:3 * cycle]
        _, _, core = my_place()
        total = None
        for place in range(cycle):
            weight = both_halves(halves[2 * place:2 * place + 2], core)
            term = dot_nn(chunks[place][3 * rows:, :], weight)
            total = term if total is None else total + term
        mixed[...] = total.astype(bf16)
    for copy in copies:
        copy.wait()


def finish(cycle, rows, chunks, others):
    model = chunks[0].shape[1] * cycle
    aligned = model // cycle % 128 == 0
    return pl.pallas_call(
        functools.partial(finish_kernel, cycle),
        out_shape=[jax.ShapeDtypeStruct((rows, model), bf16)] * 4,
        in_specs=[vmem()] * (cycle + len(others)),
        out_specs=[vmem()] + [anywhere() if aligned else vmem()] * 3,
        scratch_shapes=[pltpu.SemaphoreType.DMA((cycle, 3))],
        compiler_params=params(8),
        name="finish",
    )(*chunks, *others)


def local(queries, keys, values, out_weight, upstream, adjacency, counts):
    cycle = lax.axis_size("seq")
    rows = queries.shape[0]
    tensors = (queries, keys, values, adjacency, counts)
    if cycle == 4 and lax.axis_size("mp") == 8:
        return square(cycle, rows, tensors, out_weight, upstream)
    chunks = swapped(pack(cycle, range(cycle), tensors))
    halves = []
    for place in range(cycle):
        halves += with_other_core(fetch_rows(out_weight, place))
    q_all, k_all, v_all, k_t, v_t, bias = gather(cycle, chunks)
    attended, att_t, lse = forward(cycle, 1, q_all, k_all, v_t, bias)
    grads = swapped(project_grad(cycle, upstream, halves))
    inputs = (q_all, k_all, v_all, k_t, bias, att_t, lse)
    terms = swapped(backward(cycle, inputs, grads, attended, []))
    return tuple(finish(cycle, rows, terms, halves))


def square(cycle, rows, tensors, out_weight, upstream):
    first = fetch_rows(out_weight, 0)
    sent = list(pack(cycle, range(1, cycle), tensors))
    own_chunk, out_weight, upstream = pack(cycle, [0], tensors, (out_weight, upstream), [first])
    chunks = swapped([own_chunk] + sent)
    second = fetch_rows(out_weight, 2)
    next_upstream = exchange(upstream, "seq", 1)
    halves = with_other_core(first) + with_other_core(second)
    q_all, k_all, v_all, k_t, v_t, bias = gather(cycle, chunks)
    (near_att, far_att), att_t, lse = forward(cycle, 2, q_all, k_all, v_t, bias)
    far_att = exchange(far_att, "seq", 2)
    near, far = near_grads(upstream, next_upstream, halves, [lse])
    grads = [near, exchange(far, "seq", 2)]
    own_mixed, next_mixed = mix(near_att, far_att, halves, [far])
    inputs = (q_all, k_all, v_all, k_t, bias, att_t, lse)
    terms = backward(cycle, inputs, grads, [], [next_mixed])
    next_mixed = exchange(next_mixed, "seq", 1)
    return tuple(finish(cycle, rows, swapped(terms), [own_mixed, next_mixed]))


def solution(mesh):
    tokens = P(("seq", "mp"), None)
    return jax.shard_map(
        local,
        mesh=mesh,
        in_specs=(tokens, tokens, tokens, P("mp", None), tokens, tokens, P(("seq", "mp"))),
        out_specs=(tokens,) * 4,
        check_vma=False,
    )
```

time: 65.8 us -> 54.4 us (0.83)
  waiting for transfers between devices: 24.8 us -> 17 us
  starting transfers between devices: 27.2 us -> 23.2 us
    ppermute x4 -> x2, starting transfers between devices: 16.7 us -> 4.04 us  [fetch_rows(): return lax.ppermute(out_weight, ('seq', 'mp'), pairs)]
    ppermute x11 -> x12, starting transfers between devices: 10.5 us -> 19.1 us  [exchange(): return lax.ppermute(value, axis, [(i, i ^ distance) for i in range(count)])]
    ppermute x4 -> x2, waiting for transfers between devices: 6.38 us -> 0.01 us  [fetch_rows(): return lax.ppermute(out_weight, ('seq', 'mp'), pairs)]
    ppermute x11 -> x12, waiting for transfers between devices: 18.4 us -> 17 us  [exchange(): return lax.ppermute(value, axis, [(i, i ^ distance) for i in range(count)])]
    pallas_call x2 -> x5, Pallas kernels: 5.9 us -> 7.03 us  [the longest x2 3.67 us: pack(): pl.pallas_call(functools.partial(pack_kernel, cycle, places, len(extra)),...]
  transfers between devices with their start and end apart: 15 -> 14, of which waited for: 7 -> 5; matrix products, arithmetic and copies ran while one was open for 0% -> 0% of each run, Pallas kernels for 10% -> 20%
where the time goes in v3:
time: 54.4 us; the launch traced here: 54.2 us
  starting transfers between devices  23.2 us (43%)
  waiting for transfers between devices  17 us (31%)
  Pallas kernels  12.5 us (23%)
  between operations  1.45 us (3%)
    ppermute x12, starting transfers between devices, exchange(): return lax.ppermute(value, axis, [(i, i ^ distance) for i in range(count)])  19.1 us
    ppermute x12, waiting for transfers between devices, exchange(): return lax.ppermute(value, axis, [(i, i ^ distance) for i in range(count)])  17 us
    ppermute x2, starting transfers between devices, fetch_rows(): return lax.ppermute(out_weight, ('seq', 'mp'), pairs)  4.04 us
    pallas_call x2, Pallas kernels, pack(): pl.pallas_call(functools.partial(pack_kernel, cycle, places, len(extra)),...  3.67 us
    pallas_call x1, Pallas kernels, backward(): pl.pallas_call(functools.partial(backward_kernel, cycle, min(tokens, 512)...  3.06 us
    pallas_call x1, Pallas kernels, forward(): pl.pallas_call(functools.partial(forward_kernel, min(tokens, 512)), out_s...  2.4 us
    pallas_call x1, Pallas kernels, finish(): pl.pallas_call(functools.partial(finish_kernel, cycle), out_shape=[jax.Sh...  1.69 us
  transfers between devices with their start and end apart: 14, of which 5 were waited for; matrix products, arithmetic and copies ran while one was open for 0% of the time, Pallas kernels for 20%

profile of v3, /device:TPU:0, one launch (start us, length us, event | category | flops | bytes accessed | tf_op | source)
XLA Modules:
  0.0 54.2 jit_solution(12849960756207388857)
XLA Ops:
  0.6 1.6 %collective-permute-start = (bf16[128,1024]{1,0:T(8,128)(2,1)}, bf16[128,1024]{1,0:T(8,128)(2,1)S(1)}, u32[]{:S(2)}, u32[]{:S(2)}) collective-permute-start(bf16[128,1024]{1,0:T(8,128)(2,1)} %refs_0_.1), channel_id=1, source_target_pairs={{0,0},{1,1},{4,2},{5,3},{2,4},{3,5},{6,6},{7,7},{12,8},{13,9},{10,... | collective-permute-start | bytes 786440 | tf_op jit(solution)/shard_map/ppermute | solution.py:323
  2.9 2.9 %pack.3 = (bf16[416,256]{1,0:T(8,128)(2,1)}, bf16[416,256]{1,0:T(8,128)(2,1)}, bf16[416,256]{1,0:T(8,128)(2,1)}) custom-call(bf16[128,1024]{1,0:T(8,128)(2,1)} %q_ref.3, bf16[128,1024]{1,0:T(8,128)(2,1)} %k_ref.3, bf16[128,1024]{1,0:T(8,128)(2,1)} %v_ref.3, s32[1,4]{1,0:T(1,128)} %adj_ref.3, s32[1]{0:T(128)S(6)} %copy.11.cnt_ref), custom_call_target="tpu_custom_call" | custom-call | flops 5000000000 | tf_op jit(solution)/shard_map/pack/pallas_call | solution.py:126
  5.8 6.9 %collective-permute-start.1 = (bf16[416,256]{1,0:T(8,128)(2,1)}, bf16[416,256]{1,0:T(8,128)(2,1)S(1)}, u32[]{:S(2)}, u32[]{:S(2)}) collective-permute-start(bf16[416,256]{1,0:T(8,128)(2,1)} %get-tuple-element.29), channel_id=1, source_target_pairs={{0,8},{8,0},{16,24},{24,16},{1,9},{9,1},{17,25},{25,17},{2,10},{10... | collective-permute-start | bytes 638984 | tf_op jit(solution)/shard_map/ppermute | solution.py:52
  12.7 1.5 %collective-permute-start.3 = (bf16[416,256]{1,0:T(8,128)(2,1)}, bf16[416,256]{1,0:T(8,128)(2,1)S(1)}, u32[]{:S(2)}, u32[]{:S(2)}) collective-permute-start(bf16[416,256]{1,0:T(8,128)(2,1)} %get-tuple-element.31), channel_id=1, source_target_pairs={{0,24},{8,16},{16,8},{24,0},{1,25},{9,17},{17,9},{25,1},{2,26},{10... | collective-permute-start | bytes 638984 | tf_op jit(solution)/shard_map/ppermute | solution.py:52
  14.3 0.8 %pack.2 = (bf16[416,256]{1,0:T(8,128)(2,1)S(1)}, bf16[128,1024]{1,0:T(8,128)(2,1)S(1)}, bf16[128,1024]{1,0:T(8,128)(2,1)S(1)}) custom-call(bf16[128,1024]{1,0:T(8,128)(2,1)S(1)} %copy-done, bf16[128,1024]{1,0:T(8,128)(2,1)S(1)} %copy-done.1, bf16[128,1024]{1,0:T(8,128)(2,1)S(1)} %copy-done.2, s32[1,4]{1,0:T(1,128)S(1)} %copy-done.5, s32[1]{0:T(128)S(6)} %copy.11.cnt_ref, ...), custom_call_target="tpu_custom_call" | custom-call | flops 5000000000 | tf_op jit(solution)/shard_map/pack/pallas_call | solution.py:126
  15.1 2.4 %collective-permute-start.6 = (bf16[128,1024]{1,0:T(8,128)(2,1)S(1)}, bf16[128,1024]{1,0:T(8,128)(2,1)S(1)}, u32[]{:S(2)}, u32[]{:S(2)}) collective-permute-start(bf16[128,1024]{1,0:T(8,128)(2,1)S(1)} %get-tuple-element.41), channel_id=1, source_target_pairs={{2,0},{3,1},{6,2},{7,3},{0,4},{1,5},{4,6},{5,7},{14,8},{15,9},{8,1... | collective-permute-start | bytes 786440 | tf_op jit(solution)/shard_map/ppermute | solution.py:323
  17.6 1.5 %collective-permute-start.4 = (bf16[128,1024]{1,0:T(8,128)(2,1)S(1)}, bf16[128,1024]{1,0:T(8,128)(2,1)S(1)}, u32[]{:S(2)}, u32[]{:S(2)}) collective-permute-start(bf16[128,1024]{1,0:T(8,128)(2,1)S(1)} %get-tuple-element.40.up_ref), channel_id=1, source_target_pairs={{0,8},{8,0},{16,24},{24,16},{1,9},{9,1},{17,25},{25,17},{2,10},{10... | collective-permute-start | bytes 786440 | tf_op jit(solution)/shard_map/ppermute | solution.py:52
  19.1 4.8 %collective-permute-done.2.refs_2_ = bf16[416,256]{1,0:T(8,128)(2,1)S(1)} collective-permute-done((bf16[416,256]{1,0:T(8,128)(2,1)}, bf16[416,256]{1,0:T(8,128)(2,1)S(1)}, u32[]{:S(2)}, u32[]{:S(2)}) %collective-permute-start.2) | collective-permute-done | bytes 213024 | tf_op jit(solution)/shard_map/ppermute | solution.py:52
  23.9 0.3 gather.1
  24.3 2.4 %forward.1 = (bf16[256,256]{1,0:T(8,128)(2,1)S(1)}, bf16[256,256]{1,0:T(8,128)(2,1)S(1)}, f32[256,512]{1,0:T(8,128)S(1)}, f32[8,512]{1,0:T(8,128)S(1)}) custom-call(bf16[512,256]{1,0:T(8,128)(2,1)S(1)} %get-tuple-element.32.q_all.refs_0_, bf16[512,256]{1,0:T(8,128)(2,1)S(1)} %get-tuple-element.33.k_all.refs_1_, bf16[256,512]{1,0:T(8,128)(2,1)S(1)} %get-tuple-element.37.v_t, ...), custom_call_target="tpu_custom_call" | custom-call | flops 3000000000 | tf_op jit(solution)/shard_map/forward/pallas_call | solution.py:226
  26.7 1.3 %collective-permute-start.9 = (bf16[256,256]{1,0:T(8,128)(2,1)S(1)}, bf16[256,256]{1,0:T(8,128)(2,1)S(1)}, u32[]{:S(2)}, u32[]{:S(2)}) collective-permute-start(bf16[256,256]{1,0:T(8,128)(2,1)S(1)} %get-tuple-element.45), channel_id=1, source_target_pairs={{0,16},{8,24},{16,0},{24,8},{1,17},{9,25},{17,1},{25,9},{2,18},{10... | collective-permute-start | bytes 393224 | tf_op jit(solution)/shard_map/ppermute | solution.py:52
  28.0 0.2 collective-permute-done.4.next_ref
  28.1 0.7 %near_grads.1 = (bf16[256,256]{1,0:T(8,128)(2,1)S(1)}, bf16[256,256]{1,0:T(8,128)(2,1)S(1)}) custom-call(bf16[128,1024]{1,0:T(8,128)(2,1)S(1)} %get-tuple-element.40.up_ref, bf16[128,1024]{1,0:T(8,128)(2,1)S(1)} %collective-permute-done.4.next_ref, bf16[128,1024]{1,0:T(8,128)(2,1)S(1)} %collective-permute-done.refs_2_.refs_0_, ...), custom_call_target="tpu_custom_call" | custom-call | flops 1000000000 | tf_op jit(solution)/shard_map/near_grads/pallas_call | solution.py:357
  28.9 0.8 %collective-permute-start.8 = (bf16[256,256]{1,0:T(8,128)(2,1)S(1)}, bf16[256,256]{1,0:T(8,128)(2,1)S(1)}, u32[]{:S(2)}, u32[]{:S(2)}) collective-permute-start(bf16[256,256]{1,0:T(8,128)(2,1)S(1)} %get-tuple-element.43.refs_4_), channel_id=1, source_target_pairs={{0,16},{8,24},{16,0},{24,8},{1,17},{9,25},{17,1},{25,9},{2,18},{10... | collective-permute-start | bytes 393224 | tf_op jit(solution)/shard_map/ppermute | solution.py:52
  29.7 3.4 %collective-permute-done.9.far_ref = bf16[256,256]{1,0:T(8,128)(2,1)S(1)} collective-permute-done((bf16[256,256]{1,0:T(8,128)(2,1)S(1)}, bf16[256,256]{1,0:T(8,128)(2,1)S(1)}, u32[]{:S(2)}, u32[]{:S(2)}) %collective-permute-start.9) | collective-permute-done | bytes 131104 | tf_op jit(solution)/shard_map/ppermute | solution.py:52
  33.1 0.7 %mix.1 = (f32[128,1024]{1,0:T(8,128)S(1)}, bf16[128,1024]{1,0:T(8,128)(2,1)S(1)}) custom-call(bf16[256,256]{1,0:T(8,128)(2,1)S(1)} %get-tuple-element.44.near_ref, bf16[256,256]{1,0:T(8,128)(2,1)S(1)} %collective-permute-done.9.far_ref, bf16[128,1024]{1,0:T(8,128)(2,1)S(1)} %collective-permute-done.refs_2_.refs_0_, ...), custom_call_target="tpu_custom_call" | custom-call | flops 1000000000 | tf_op jit(solution)/shard_map/mix/pallas_call | solution.py:386
  33.8 3.4 %collective-permute-start.13 = (bf16[128,1024]{1,0:T(8,128)(2,1)S(1)}, bf16[128,1024]{1,0:T(8,128)(2,1)S(1)}, u32[]{:S(2)}, u32[]{:S(2)}) collective-permute-start(bf16[128,1024]{1,0:T(8,128)(2,1)S(1)} %get-tuple-element.46.refs_9_), channel_id=1, source_target_pairs={{0,8},{8,0},{16,24},{24,16},{1,9},{9,1},{17,25},{25,17},{2,10},{10... | collective-permute-start | bytes 786440 | tf_op jit(solution)/shard_map/ppermute | solution.py:52
  37.2 3.1 %backward.1 = (bf16[384,256]{1,0:T(8,128)(2,1)S(1)}, bf16[384,256]{1,0:T(8,128)(2,1)S(1)}, bf16[384,256]{1,0:T(8,128)(2,1)S(1)}, bf16[384,256]{1,0:T(8,128)(2,1)S(1)}) custom-call(bf16[512,256]{1,0:T(8,128)(2,1)S(1)} %get-tuple-element.32.q_all.refs_0_, bf16[512,256]{1,0:T(8,128)(2,1)S(1)} %get-tuple-element.33.k_all.refs_1_, ...), custom_call_target="tpu_custom_call" | custom-call | flops 3000000000 | tf_op jit(solution)/shard_map/backward/pallas_call | solution.py:299
  40.3 1.7 %collective-permute-start.10 = (bf16[384,256]{1,0:T(8,128)(2,1)S(1)}, bf16[384,256]{1,0:T(8,128)(2,1)S(1)}, u32[]{:S(2)}, u32[]{:S(2)}) collective-permute-start(bf16[384,256]{1,0:T(8,128)(2,1)S(1)} %get-tuple-element.48), channel_id=1, source_target_pairs={{0,8},{8,0},{16,24},{24,16},{1,9},{9,1},{17,25},{25,17},{2,10},{10... | collective-permute-start | bytes 589832 | tf_op jit(solution)/shard_map/ppermute | solution.py:52
  42.0 0.3 collective-permute-start.11
  42.3 1.5 %collective-permute-start.12 = (bf16[384,256]{1,0:T(8,128)(2,1)S(1)}, bf16[384,256]{1,0:T(8,128)(2,1)S(1)}, u32[]{:S(2)}, u32[]{:S(2)}) collective-permute-start(bf16[384,256]{1,0:T(8,128)(2,1)S(1)} %get-tuple-element.50), channel_id=1, source_target_pairs={{0,24},{8,16},{16,8},{24,0},{1,25},{9,17},{17,9},{25,1},{2,26},{10... | collective-permute-start | bytes 589832 | tf_op jit(solution)/shard_map/ppermute | solution.py:52
  43.8 4.3 %collective-permute-done.10.refs_1_ = bf16[384,256]{1,0:T(8,128)(2,1)S(1)} collective-permute-done((bf16[384,256]{1,0:T(8,128)(2,1)S(1)}, bf16[384,256]{1,0:T(8,128)(2,1)S(1)}, u32[]{:S(2)}, u32[]{:S(2)}) %collective-permute-start.10) | collective-permute-done | bytes 196640 | tf_op jit(solution)/shard_map/ppermute | solution.py:52
  48.2 4.3 %collective-permute-done.11.refs_2_ = bf16[384,256]{1,0:T(8,128)(2,1)S(1)} collective-permute-done((bf16[384,256]{1,0:T(8,128)(2,1)S(1)}, bf16[384,256]{1,0:T(8,128)(2,1)S(1)}, u32[]{:S(2)}, u32[]{:S(2)}) %collective-permute-start.11) | collective-permute-done | bytes 196640 | tf_op jit(solution)/shard_map/ppermute | solution.py:52
  52.5 1.7 %finish.1 = (bf16[128,1024]{1,0:T(8,128)(2,1)}, bf16[128,1024]{1,0:T(8,128)(2,1)}, bf16[128,1024]{1,0:T(8,128)(2,1)}, bf16[128,1024]{1,0:T(8,128)(2,1)}) custom-call(bf16[384,256]{1,0:T(8,128)(2,1)S(1)} %get-tuple-element.47.refs_0_, bf16[384,256]{1,0:T(8,128)(2,1)S(1)} %collective-permute-done.10.refs_1_, ...), custom_call_target="tpu_custom_call" | custom-call | tf_op jit(solution)/shard_map/finish/pallas_call | solution.py:473
  (24 shorter events, 0.1 us)
Async XLA Ops:
  0.6 13.7 %collective-permute-start = (bf16[128,1024]{1,0:T(8,128)(2,1)}, bf16[128,1024]{1,0:T(8,128)(2,1)S(1)}, u32[]{:S(2)}, u32[]{:S(2)}) collective-permute-start(bf16[128,1024]{1,0:T(8,128)(2,1)} %refs_0_.1), channel_id=1, source_target_pairs={{0,0},{1,1},{4,2},{5,3},{2,4},{3,5},{6,6},{7,7},{12,8},{13,9},{10,... | collective-permute-start | bytes 786440 | tf_op jit(solution)/shard_map/ppermute | solution.py:323
  2.9 11.4 %copy-start = (bf16[128,1024]{1,0:T(8,128)(2,1)S(1)}, bf16[128,1024]{1,0:T(8,128)(2,1)}, u32[]{:S(2)}) copy-start(bf16[128,1024]{1,0:T(8,128)(2,1)} %q_ref.3) | copy-start | bytes 786436
  2.9 11.4 %copy-start.1 = (bf16[128,1024]{1,0:T(8,128)(2,1)S(1)}, bf16[128,1024]{1,0:T(8,128)(2,1)}, u32[]{:S(2)}) copy-start(bf16[128,1024]{1,0:T(8,128)(2,1)} %k_ref.3) | copy-start | bytes 786436
  2.9 11.4 %copy-start.2 = (bf16[128,1024]{1,0:T(8,128)(2,1)S(1)}, bf16[128,1024]{1,0:T(8,128)(2,1)}, u32[]{:S(2)}) copy-start(bf16[128,1024]{1,0:T(8,128)(2,1)} %v_ref.3) | copy-start | bytes 786436
  2.9 11.4 %copy-start.3 = (bf16[128,1024]{1,0:T(8,128)(2,1)S(1)}, bf16[128,1024]{1,0:T(8,128)(2,1)}, u32[]{:S(2)}) copy-start(bf16[128,1024]{1,0:T(8,128)(2,1)} %refs_0_.1) | copy-start | bytes 786436
  2.9 11.4 %copy-start.4 = (bf16[128,1024]{1,0:T(8,128)(2,1)S(1)}, bf16[128,1024]{1,0:T(8,128)(2,1)}, u32[]{:S(2)}) copy-start(bf16[128,1024]{1,0:T(8,128)(2,1)} %refs_1_.1) | copy-start | bytes 786436
  5.8 13.3 %collective-permute-start.1 = (bf16[416,256]{1,0:T(8,128)(2,1)}, bf16[416,256]{1,0:T(8,128)(2,1)S(1)}, u32[]{:S(2)}, u32[]{:S(2)}) collective-permute-start(bf16[416,256]{1,0:T(8,128)(2,1)} %get-tuple-element.29), channel_id=1, source_target_pairs={{0,8},{8,0},{16,24},{24,16},{1,9},{9,1},{17,25},{25,17},{2,10},{10... | collective-permute-start | bytes 638984 | tf_op jit(solution)/shard_map/ppermute | solution.py:52
  12.7 1.6 %copy-start.5 = (s32[1,4]{1,0:T(1,128)S(1)}, s32[1,4]{1,0:T(1,128)}, u32[]{:S(2)}) copy-start(s32[1,4]{1,0:T(1,128)} %adj_ref.3) | copy-start | bytes 52
  12.7 11.2 %collective-permute-start.2 = (bf16[416,256]{1,0:T(8,128)(2,1)}, bf16[416,256]{1,0:T(8,128)(2,1)S(1)}, u32[]{:S(2)}, u32[]{:S(2)}) collective-permute-start(bf16[416,256]{1,0:T(8,128)(2,1)} %get-tuple-element.30), channel_id=1, source_target_pairs={{0,16},{8,24},{16,0},{24,8},{1,17},{9,25},{17,1},{25,9},{2,18},{10... | collective-permute-start | bytes 638984 | tf_op jit(solution)/shard_map/ppermute | solution.py:52
  12.7 11.2 %collective-permute-start.3 = (bf16[416,256]{1,0:T(8,128)(2,1)}, bf16[416,256]{1,0:T(8,128)(2,1)S(1)}, u32[]{:S(2)}, u32[]{:S(2)}) collective-permute-start(bf16[416,256]{1,0:T(8,128)(2,1)} %get-tuple-element.31), channel_id=1, source_target_pairs={{0,24},{8,16},{16,8},{24,0},{1,25},{9,17},{17,9},{25,1},{2,26},{10... | collective-permute-start | bytes 638984 | tf_op jit(solution)/shard_map/ppermute | solution.py:52
  15.1 9.1 %collective-permute-start.6 = (bf16[128,1024]{1,0:T(8,128)(2,1)S(1)}, bf16[128,1024]{1,0:T(8,128)(2,1)S(1)}, u32[]{:S(2)}, u32[]{:S(2)}) collective-permute-start(bf16[128,1024]{1,0:T(8,128)(2,1)S(1)} %get-tuple-element.41), channel_id=1, source_target_pairs={{2,0},{3,1},{6,2},{7,3},{0,4},{1,5},{4,6},{5,7},{14,8},{15,9},{8,1... | collective-permute-start | bytes 786440 | tf_op jit(solution)/shard_map/ppermute | solution.py:323
  17.6 10.6 %collective-permute-start.4 = (bf16[128,1024]{1,0:T(8,128)(2,1)S(1)}, bf16[128,1024]{1,0:T(8,128)(2,1)S(1)}, u32[]{:S(2)}, u32[]{:S(2)}) collective-permute-start(bf16[128,1024]{1,0:T(8,128)(2,1)S(1)} %get-tuple-element.40.up_ref), channel_id=1, source_target_pairs={{0,8},{8,0},{16,24},{24,16},{1,9},{9,1},{17,25},{25,17},{2,10},{10... | collective-permute-start | bytes 786440 | tf_op jit(solution)/shard_map/ppermute | solution.py:52
  19.1 8.9 %collective-permute-start.5 = (bf16[128,1024]{1,0:T(8,128)(2,1)S(1)}, bf16[128,1024]{1,0:T(8,128)(2,1)S(1)}, u32[]{:S(2)}, u32[]{:S(2)}) collective-permute-start(bf16[128,1024]{1,0:T(8,128)(2,1)S(1)} %collective-permute-done.refs_2_.refs_0_), channel_id=1, source_target_pairs={{0,1},{1,0},{2,3},{3,2},{4,5},{5,4},{6,7},{7,6},{8,9},{9,8},{10,11... | collective-permute-start | bytes 786440 | tf_op jit(solution)/shard_map/ppermute | solution.py:52
  24.2 3.9 %collective-permute-start.7 = (bf16[128,1024]{1,0:T(8,128)(2,1)S(1)}, bf16[128,1024]{1,0:T(8,128)(2,1)S(1)}, u32[]{:S(2)}, u32[]{:S(2)}) collective-permute-start(bf16[128,1024]{1,0:T(8,128)(2,1)S(1)} %collective-permute-done.6.refs_2_), channel_id=1, source_target_pairs={{0,1},{1,0},{2,3},{3,2},{4,5},{5,4},{6,7},{7,6},{8,9},{9,8},{10,11... | collective-permute-start | bytes 786440 | tf_op jit(solution)/shard_map/ppermute | solution.py:52
  26.7 6.4 %collective-permute-start.9 = (bf16[256,256]{1,0:T(8,128)(2,1)S(1)}, bf16[256,256]{1,0:T(8,128)(2,1)S(1)}, u32[]{:S(2)}, u32[]{:S(2)}) collective-permute-start(bf16[256,256]{1,0:T(8,128)(2,1)S(1)} %get-tuple-element.45), channel_id=1, source_target_pairs={{0,16},{8,24},{16,0},{24,8},{1,17},{9,25},{17,1},{25,9},{2,18},{10... | collective-permute-start | bytes 393224 | tf_op jit(solution)/shard_map/ppermute | solution.py:52
  28.9 8.4 %collective-permute-start.8 = (bf16[256,256]{1,0:T(8,128)(2,1)S(1)}, bf16[256,256]{1,0:T(8,128)(2,1)S(1)}, u32[]{:S(2)}, u32[]{:S(2)}) collective-permute-start(bf16[256,256]{1,0:T(8,128)(2,1)S(1)} %get-tuple-element.43.refs_4_), channel_id=1, source_target_pairs={{0,16},{8,24},{16,0},{24,8},{1,17},{9,25},{17,1},{25,9},{2,18},{10... | collective-permute-start | bytes 393224 | tf_op jit(solution)/shard_map/ppermute | solution.py:52
  33.8 10.1 %collective-permute-start.13 = (bf16[128,1024]{1,0:T(8,128)(2,1)S(1)}, bf16[128,1024]{1,0:T(8,128)(2,1)S(1)}, u32[]{:S(2)}, u32[]{:S(2)}) collective-permute-start(bf16[128,1024]{1,0:T(8,128)(2,1)S(1)} %get-tuple-element.46.refs_9_), channel_id=1, source_target_pairs={{0,8},{8,0},{16,24},{24,16},{1,9},{9,1},{17,25},{25,17},{2,10},{10... | collective-permute-start | bytes 786440 | tf_op jit(solution)/shard_map/ppermute | solution.py:52
  40.3 7.9 %collective-permute-start.10 = (bf16[384,256]{1,0:T(8,128)(2,1)S(1)}, bf16[384,256]{1,0:T(8,128)(2,1)S(1)}, u32[]{:S(2)}, u32[]{:S(2)}) collective-permute-start(bf16[384,256]{1,0:T(8,128)(2,1)S(1)} %get-tuple-element.48), channel_id=1, source_target_pairs={{0,8},{8,0},{16,24},{24,16},{1,9},{9,1},{17,25},{25,17},{2,10},{10... | collective-permute-start | bytes 589832 | tf_op jit(solution)/shard_map/ppermute | solution.py:52
  42.0 10.5 %collective-permute-start.11 = (bf16[384,256]{1,0:T(8,128)(2,1)S(1)}, bf16[384,256]{1,0:T(8,128)(2,1)S(1)}, u32[]{:S(2)}, u32[]{:S(2)}) collective-permute-start(bf16[384,256]{1,0:T(8,128)(2,1)S(1)} %get-tuple-element.49), channel_id=1, source_target_pairs={{0,16},{8,24},{16,0},{24,8},{1,17},{9,25},{17,1},{25,9},{2,18},{10... | collective-permute-start | bytes 589832 | tf_op jit(solution)/shard_map/ppermute | solution.py:52
  42.3 10.2 %collective-permute-start.12 = (bf16[384,256]{1,0:T(8,128)(2,1)S(1)}, bf16[384,256]{1,0:T(8,128)(2,1)S(1)}, u32[]{:S(2)}, u32[]{:S(2)}) collective-permute-start(bf16[384,256]{1,0:T(8,128)(2,1)S(1)} %get-tuple-element.50), channel_id=1, source_target_pairs={{0,24},{8,16},{16,8},{24,0},{1,25},{9,17},{17,9},{25,1},{2,26},{10... | collective-permute-start | bytes 589832 | tf_op jit(solution)/shard_map/ppermute | solution.py:52

commit v4 on v3

--- a/solution.py
+++ b/solution.py
@@ -32,7 +32,7 @@
 
 
 def params(mib):
-    return pltpu.CompilerParams(vmem_limit_bytes=mib * 1024 * 1024)
+    return pltpu.CompilerParams(vmem_limit_bytes=int(mib * 1024) * 1024)
 
 
 def unread():
@@ -52,15 +52,42 @@
     return lax.ppermute(value, axis, [(i, i ^ distance) for i in range(count)])
 
 
-def swapped(chunks):
-    return [chunks[0]] + [exchange(chunks[k], "seq", k) for k in range(1, len(chunks))]
+def exchange_seq(value, distance):
+    return exchange(value, "seq", distance)
+
+
+def turned(distance):
+    return distance ^ (((distance ^ (distance >> 1)) & 1) * 3)
+
+
+def exchange_slot(value, slot):
+    count = lax.axis_size("mp")
+    pairs = []
+    for member in range(lax.axis_size("seq")):
+        for rank in range(count):
+            partner = member ^ (turned(slot) if rank % 2 else slot)
+            pairs.append((member * count + rank, partner * count + rank))
+    return lax.ppermute(value, ("seq", "mp"), pairs)
+
+
+def is_square():
+    return lax.axis_size("seq") == 4 and lax.axis_size("mp") == 8
+
+
+def distance_of(slot):
+    if is_square():
+        core = lax.rem(lax.axis_index("mp"), 2)
+        return jnp.where(core == 0, slot, turned(slot))
+    return slot
+
+
+def swapped(chunks, swap=exchange_seq):
+    return [chunks[0]] + [swap(chunks[k], k) for k in range(1, len(chunks))]
 
 
 def group_of(cycle, member, chip):
     turn = (member + chip) % cycle
-    if cycle == 4:
-        return turn ^ (((turn ^ (turn >> 1)) & 1) * 3)
-    return turn
+    return turned(turn) if cycle == 4 else turn
 
 
 def my_place():
@@ -72,16 +99,22 @@
     return pl.ds(pl.multiple_of(first, width), width)
 
 
-def pack_kernel(cycle, places, extra, q_ref, k_ref, v_ref, adj_ref, cnt_ref, *refs):
-    refs, (sems, more_sems) = refs[:-2], refs[-2:]
+def pack_kernel(cycle, places, extra, q_ref, k_ref, v_ref, adj_any, cnt_any, *refs):
+    refs, (adj_ref, cnt_ref, sems, more_sems) = refs[:-4], refs[-4:]
     outs = refs[-len(places) - extra:]
     rows, model = q_ref.shape
     width = model // cycle
     own, chip, _ = my_place()
+    lists = [
+        pltpu.make_async_copy(adj_any, adj_ref, more_sems.at[2]),
+        pltpu.make_async_copy(cnt_any, cnt_ref, more_sems.at[3]),
+    ]
+    for copy in lists:
+        copy.start()
     copies = []
     if width % 128 == 0:
         for place, out in zip(places, outs):
-            group = group_of(cycle, lax.bitwise_xor(own, place), chip)
+            group = group_of(cycle, lax.bitwise_xor(own, distance_of(place)), chip)
             for at, ref in enumerate((q_ref, k_ref, v_ref)):
                 copies.append(
                     pltpu.make_async_copy(
@@ -96,18 +129,20 @@
             pltpu.make_async_copy(refs[at], outs[len(places) + at], more_sems.at[at])
         )
         copies[-1].start()
+    for copy in lists:
+        copy.wait()
     lines = lax.broadcasted_iota(jnp.int32, (META, width), 0)
     meta = jnp.where(lines == 0, 1, 0)
     for column, offset in enumerate(cycle_offsets):
         named = lax.rem(own - offset + 2 * cycle, cycle)
         meta = meta + jnp.where(
-            (lines == lax.bitwise_xor(own, named)) & (adj_ref[0, column] > 0), 1, 0
+            (lines == distance_of(lax.bitwise_xor(own, named))) & (adj_ref[0, column] > 0), 1, 0
         )
-    meta = jnp.where(lines == META - 1, cnt_ref[0], meta).astype(f32).astype(bf16)
+    meta = jnp.where(lines == META - 1, cnt_ref[0, 0], meta).astype(f32).astype(bf16)
     for place, out in zip(places, outs):
         out[3 * rows:, :] = meta
         if width % 128:
-            group = group_of(cycle, lax.bitwise_xor(own, place), chip)
+            group = group_of(cycle, lax.bitwise_xor(own, distance_of(place)), chip)
             for other in range(cycle):
                 @pl.when(group == other)
                 def _():
@@ -119,29 +154,55 @@
         copy.wait()
 
 
-def pack(cycle, places, tensors, extra=(), after=()):
+def hold_kernel(count, *refs):
+    outs, sems = refs[-count - 1:-1], refs[-1]
+    copies = [pltpu.make_async_copy(refs[at], outs[at], sems.at[at]) for at in range(count)]
+    for copy in copies:
+        copy.start()
+    for copy in copies:
+        copy.wait()
+
+
+def hold(arrays, after):
+    count = len(arrays)
+    return pl.pallas_call(
+        functools.partial(hold_kernel, count),
+        out_shape=[jax.ShapeDtypeStruct(array.shape, array.dtype) for array in arrays],
+        in_specs=[unread()] * (count + len(after)),
+        out_specs=[vmem()] * count,
+        scratch_shapes=[pltpu.SemaphoreType.DMA((count,))],
+        compiler_params=params(2),
+        cost_estimate=cost(1),
+        name="hold",
+    )(*arrays, *after)
+
+
+def pack(cycle, places, tensors, extra=()):
     rows, model = tensors[0].shape
     width = model // cycle
-    smem = pl.BlockSpec(memory_space=pltpu.SMEM)
     return pl.pallas_call(
         functools.partial(pack_kernel, cycle, places, len(extra)),
         out_shape=[jax.ShapeDtypeStruct((3 * rows + META, width), bf16)] * len(places)
         + [jax.ShapeDtypeStruct(array.shape, bf16) for array in extra],
         in_specs=[anywhere() if width % 128 == 0 else vmem()] * 3
-        + [smem] * 2
-        + [anywhere()] * len(extra)
-        + [unread()] * len(after),
+        + [unread()] * 2
+        + [anywhere()] * len(extra),
         out_specs=[vmem()] * (len(places) + len(extra)),
-        scratch_shapes=[pltpu.SemaphoreType.DMA((cycle, 3)), pltpu.SemaphoreType.DMA((2,))],
-        compiler_params=params(8 if extra else 62),
+        scratch_shapes=[
+            pltpu.SMEM(tensors[3].shape, jnp.int32),
+            pltpu.SMEM(tensors[4].shape, jnp.int32),
+            pltpu.SemaphoreType.DMA((cycle, 3)),
+            pltpu.SemaphoreType.DMA((4,)),
+        ],
+        compiler_params=params(62),
         cost_estimate=cost(5),
         name="pack",
-    )(*tensors, *extra, *after)
+    )(*tensors, *extra)
 
 
 def gather_kernel(cycle, *refs):
     chunks = refs[:cycle]
-    q_all, k_all, v_all, k_t, v_t, bias = refs[cycle:]
+    q_all, k_all, v_all, k_t, v_t, bias = refs[-6:]
     rows = q_all.shape[0] // cycle
     for place in range(cycle):
         for at, part in enumerate((q_all, k_all, v_all)):
@@ -163,7 +224,7 @@
             ] = jnp.where(valid, term, absent)
 
 
-def gather(cycle, chunks):
+def gather(cycle, chunks, after=()):
     width = chunks[0].shape[1]
     rows = (chunks[0].shape[0] - META) // 3
     tokens = rows * cycle
@@ -172,12 +233,12 @@
         out_shape=[jax.ShapeDtypeStruct((tokens, width), bf16)] * 3
         + [jax.ShapeDtypeStruct((width, tokens), bf16)] * 2
         + [jax.ShapeDtypeStruct((tokens, tokens), f32)],
-        in_specs=[vmem()] * cycle,
+        in_specs=[vmem()] * cycle + [unread()] * len(after),
         out_specs=[vmem()] * 6,
         compiler_params=params(8 if tokens <= 512 else 40),
         cost_estimate=cost(5),
         name="gather",
-    )(*chunks)
+    )(*chunks, *after)
 
 
 def head_tile(width):
@@ -313,12 +374,13 @@
     )(*inputs, *grads, *attended, *after)
 
 
-def fetch_rows(out_weight, place):
+def fetch_rows(out_weight, distance, flip=False):
     cycle, count = lax.axis_size("seq"), lax.axis_size("mp")
     pairs = []
     for member in range(cycle):
         for rank in range(count):
-            owner = 2 * group_of(cycle, member ^ place, rank // 2) + rank % 2
+            owner = 2 * group_of(cycle, member ^ distance(rank % 2), rank // 2)
+            owner += (rank + flip) % 2
             pairs.append((member * count + owner, member * count + rank))
     return lax.ppermute(out_weight, ("seq", "mp"), pairs)
 
@@ -424,7 +486,7 @@
     own, chip, _ = my_place()
     copies = []
     for place in range(cycle):
-        group = group_of(cycle, lax.bitwise_xor(own, place), chip)
+        group = group_of(cycle, lax.bitwise_xor(own, distance_of(place)), chip)
         if width % 128 == 0:
             for at, out in enumerate(outs):
                 copies.append(
@@ -484,13 +546,13 @@
 def local(queries, keys, values, out_weight, upstream, adjacency, counts):
     cycle = lax.axis_size("seq")
     rows = queries.shape[0]
-    tensors = (queries, keys, values, adjacency, counts)
-    if cycle == 4 and lax.axis_size("mp") == 8:
+    tensors = (queries, keys, values, adjacency, counts.reshape(1, 1))
+    if is_square():
         return square(cycle, rows, tensors, out_weight, upstream)
     chunks = swapped(pack(cycle, range(cycle), tensors))
     halves = []
     for place in range(cycle):
-        halves += with_other_core(fetch_rows(out_weight, place))
+        halves += with_other_core(fetch_rows(out_weight, lambda core: place))
     q_all, k_all, v_all, k_t, v_t, bias = gather(cycle, chunks)
     attended, att_t, lse = forward(cycle, 1, q_all, k_all, v_t, bias)
     grads = swapped(project_grad(cycle, upstream, halves))
@@ -500,23 +562,27 @@
 
 
 def square(cycle, rows, tensors, out_weight, upstream):
-    first = fetch_rows(out_weight, 0)
-    sent = list(pack(cycle, range(1, cycle), tensors))
-    own_chunk, out_weight, upstream = pack(cycle, [0], tensors, (out_weight, upstream), [first])
-    chunks = swapped([own_chunk] + sent)
-    second = fetch_rows(out_weight, 2)
-    next_upstream = exchange(upstream, "seq", 1)
-    halves = with_other_core(first) + with_other_core(second)
-    q_all, k_all, v_all, k_t, v_t, bias = gather(cycle, chunks)
+    *chunks, out_weight = pack(cycle, range(cycle), tensors, (out_weight,))
+    first = fetch_rows(out_weight, lambda core: 0)
+    out_weight, upstream = hold((out_weight, upstream), [first])
+    chunks = swapped(chunks, exchange_slot)
+    next_upstream = exchange_slot(upstream, 1)
+    second = [
+        fetch_rows(out_weight, lambda core: turned(2) if core else 2, flip) for flip in (False, True)
+    ]
+    halves = with_other_core(first) + second
+    q_all, k_all, v_all, k_t, v_t, bias = gather(cycle, chunks, [upstream])
     (near_att, far_att), att_t, lse = forward(cycle, 2, q_all, k_all, v_t, bias)
-    far_att = exchange(far_att, "seq", 2)
+    far_att = exchange_slot(far_att, 2)
     near, far = near_grads(upstream, next_upstream, halves, [lse])
-    grads = [near, exchange(far, "seq", 2)]
+    grads = [near, exchange_slot(far, 2)]
     own_mixed, next_mixed = mix(near_att, far_att, halves, [far])
     inputs = (q_all, k_all, v_all, k_t, bias, att_t, lse)
     terms = backward(cycle, inputs, grads, [], [next_mixed])
-    next_mixed = exchange(next_mixed, "seq", 1)
-    return tuple(finish(cycle, rows, swapped(terms), [own_mixed, next_mixed]))
+    next_mixed = exchange_slot(next_mixed, 1)
+    return tuple(
+        finish(cycle, rows, swapped(terms, exchange_slot), [own_mixed, next_mixed])
+    )
 
 
 def solution(mesh):

time: 54.4 us -> 54.5 us (level)
  starting transfers between devices: 23.2 us -> 33.7 us
  waiting for transfers between devices: 17 us -> 6.85 us
  Pallas kernels: 12.5 us -> 11.4 us
  local copies, waits for them, and re-layouts: 0.02 us -> 0.96 us
    ppermute x0 -> x10, starting transfers between devices: none -> 24.1 us  [exchange_slot(): return lax.ppermute(value, ('seq', 'mp'), pairs)]
    ppermute x12 -> x1, starting transfers between devices: 19.1 us -> 1.92 us  [exchange(): return lax.ppermute(value, axis, [(i, i ^ distance) for i in range(count)])]
    ppermute x12 -> x1, waiting for transfers between devices: 17 us -> 0.01 us  [exchange(): return lax.ppermute(value, axis, [(i, i ^ distance) for i in range(count)])]
    ppermute x0 -> x10, waiting for transfers between devices: none -> 6.84 us  [exchange_slot(): return lax.ppermute(value, ('seq', 'mp'), pairs)]
    ppermute x2 -> x3, starting transfers between devices: 4.04 us -> 7.7 us  [fetch_rows(): return lax.ppermute(out_weight, ('seq', 'mp'), pairs)]
    pallas_call x2 -> x1, Pallas kernels: 3.67 us -> 2.5 us  [pack(): pl.pallas_call(functools.partial(pack_kernel, cycle, places, len(extra)),...]
    unnamed x12 -> x6, local copies, waits for them, and re-layouts: 0.02 us -> 0.96 us
  transfers between devices with their start and end apart: 14 -> 14, of which waited for: 5 -> 3; matrix products, arithmetic and copies ran while one was open for 0% -> 0% of each run, Pallas kernels for 20% -> 13%
where the time goes in v4:
time: 54.5 us; the launch traced here: 54.3 us
  starting transfers between devices  33.7 us (62%)
  Pallas kernels  11.4 us (21%)
  waiting for transfers between devices  6.85 us (13%)
  between operations  1.39 us (3%)
  local copies, waits for them, and re-layouts  0.96 us (2%)
    ppermute x10, starting transfers between devices, exchange_slot(): return lax.ppermute(value, ('seq', 'mp'), pairs)  24.1 us
    ppermute x3, starting transfers between devices, fetch_rows(): return lax.ppermute(out_weight, ('seq', 'mp'), pairs)  7.7 us
    ppermute x10, waiting for transfers between devices, exchange_slot(): return lax.ppermute(value, ('seq', 'mp'), pairs)  6.84 us
    pallas_call x1, Pallas kernels, backward(): pl.pallas_call(functools.partial(backward_kernel, cycle, min(tokens, 512)...  3.06 us
    pallas_call x1, Pallas kernels, pack(): pl.pallas_call(functools.partial(pack_kernel, cycle, places, len(extra)),...  2.5 us
    pallas_call x1, Pallas kernels, forward(): pl.pallas_call(functools.partial(forward_kernel, min(tokens, 512)), out_s...  2.41 us
    ppermute x1, starting transfers between devices, exchange(): return lax.ppermute(value, axis, [(i, i ^ distance) for i in range(count)])  1.92 us
    pallas_call x1, Pallas kernels, finish(): pl.pallas_call(functools.partial(finish_kernel, cycle), out_shape=[jax.Sh...  1.69 us
  transfers between devices with their start and end apart: 14, of which 3 were waited for; matrix products, arithmetic and copies ran while one was open for 0% of the time, Pallas kernels for 13%

profile of v4, /device:TPU:0, one launch (start us, length us, event | category | flops | bytes accessed | tf_op | source)
XLA Modules:
  0.0 54.3 jit_solution(16488584633141959627)
XLA Ops:
  1.3 2.5 %pack.1 = (bf16[416,256]{1,0:T(8,128)(2,1)}, bf16[416,256]{1,0:T(8,128)(2,1)}, bf16[416,256]{1,0:T(8,128)(2,1)}, bf16[416,256]{1,0:T(8,128)(2,1)}, bf16[128,1024]{1,0:T(8,128)(2,1)}) custom-call(bf16[128,1024]{1,0:T(8,128)(2,1)} %q_ref.1, bf16[128,1024]{1,0:T(8,128)(2,1)} %k_ref.1, bf16[128,1024]{1,0:T(8,128)(2,1)} %v_ref.1, s32[1,4]{1,0:T(1,128)} %adj_any.1, ...), custom_call_target="tpu_custom_call" | custom-call | flops 5000000000 | tf_op jit(solution)/shard_map/pack/pallas_call | solution.py:183
  3.8 1.6 %collective-permute-start.3 = (bf16[128,1024]{1,0:T(8,128)(2,1)}, bf16[128,1024]{1,0:T(8,128)(2,1)S(1)}, u32[]{:S(2)}, u32[]{:S(2)}) collective-permute-start(bf16[128,1024]{1,0:T(8,128)(2,1)} %get-tuple-element.33.refs_0_), channel_id=1, source_target_pairs={{0,0},{1,1},{4,2},{5,3},{2,4},{3,5},{6,6},{7,7},{12,8},{13,9},{10,... | collective-permute-start | bytes 786440 | tf_op jit(solution)/shard_map/ppermute | solution.py:385
  5.4 6.9 %collective-permute-start = (bf16[416,256]{1,0:T(8,128)(2,1)}, bf16[416,256]{1,0:T(8,128)(2,1)S(1)}, u32[]{:S(2)}, u32[]{:S(2)}) collective-permute-start(bf16[416,256]{1,0:T(8,128)(2,1)} %get-tuple-element.30), channel_id=1, source_target_pairs={{0,8},{1,17},{2,10},{3,19},{4,12},{5,21},{6,14},{7,23},{8,0},{9,25... | collective-permute-start | bytes 638984 | tf_op jit(solution)/shard_map/ppermute | solution.py:70
  12.3 1.5 %collective-permute-start.2 = (bf16[416,256]{1,0:T(8,128)(2,1)}, bf16[416,256]{1,0:T(8,128)(2,1)S(1)}, u32[]{:S(2)}, u32[]{:S(2)}) collective-permute-start(bf16[416,256]{1,0:T(8,128)(2,1)} %get-tuple-element.32), channel_id=1, source_target_pairs={{0,24},{1,25},{2,26},{3,27},{4,28},{5,29},{6,30},{7,31},{8,16},{9,... | collective-permute-start | bytes 638984 | tf_op jit(solution)/shard_map/ppermute | solution.py:70
  13.9 0.9 %copy-done.1 = bf16[128,1024]{1,0:T(8,128)(2,1)S(1)} copy-done((bf16[128,1024]{1,0:T(8,128)(2,1)S(1)}, bf16[128,1024]{1,0:T(8,128)(2,1)}, u32[]{:S(2)}) %copy-start.1) | copy-done | bytes 262168
  14.9 0.1 collective-permute-start.7
  14.9 6.0 %collective-permute-start.6 = (bf16[128,1024]{1,0:T(8,128)(2,1)S(1)}, bf16[128,1024]{1,0:T(8,128)(2,1)S(1)}, u32[]{:S(2)}, u32[]{:S(2)}) collective-permute-start(bf16[128,1024]{1,0:T(8,128)(2,1)S(1)} %get-tuple-element.43), channel_id=1, source_target_pairs={{2,0},{5,1},{6,2},{3,3},{0,4},{7,5},{4,6},{1,7},{14,8},{9,9},{8,10... | collective-permute-start | bytes 786440 | tf_op jit(solution)/shard_map/ppermute | solution.py:385
  21.0 0.7 %collective-permute-start.4 = (bf16[128,1024]{1,0:T(8,128)(2,1)S(1)}, bf16[128,1024]{1,0:T(8,128)(2,1)S(1)}, u32[]{:S(2)}, u32[]{:S(2)}) collective-permute-start(bf16[128,1024]{1,0:T(8,128)(2,1)S(1)} %get-tuple-element.34.refs_4_.up_ref), channel_id=1, source_target_pairs={{0,8},{1,17},{2,10},{3,19},{4,12},{5,21},{6,14},{7,23},{8,0},{9,25... | collective-permute-start | bytes 786440 | tf_op jit(solution)/shard_map/ppermute | solution.py:70
  21.7 1.9 %collective-permute-start.5 = (bf16[128,1024]{1,0:T(8,128)(2,1)S(1)}, bf16[128,1024]{1,0:T(8,128)(2,1)S(1)}, u32[]{:S(2)}, u32[]{:S(2)}) collective-permute-start(bf16[128,1024]{1,0:T(8,128)(2,1)S(1)} %collective-permute-done.3.refs_2_.refs_0_), channel_id=1, source_target_pairs={{0,1},{1,0},{2,3},{3,2},{4,5},{5,4},{6,7},{7,6},{8,9},{9,8},{10,11... | collective-permute-start | bytes 786440 | tf_op jit(solution)/shard_map/ppermute | solution.py:52
  23.6 0.3 gather.1
  23.9 2.4 %forward.1 = (bf16[256,256]{1,0:T(8,128)(2,1)S(1)}, bf16[256,256]{1,0:T(8,128)(2,1)S(1)}, f32[256,512]{1,0:T(8,128)S(1)}, f32[8,512]{1,0:T(8,128)S(1)}) custom-call(bf16[512,256]{1,0:T(8,128)(2,1)S(1)} %get-tuple-element.35.q_all.refs_0_, bf16[512,256]{1,0:T(8,128)(2,1)S(1)} %get-tuple-element.36.k_all.refs_1_, bf16[256,512]{1,0:T(8,128)(2,1)S(1)} %get-tuple-element.40.v_t, ...), custom_call_target="tpu_custom_call" | custom-call | flops 3000000000 | tf_op jit(solution)/shard_map/forward/pallas_call | solution.py:287
  26.3 2.5 %collective-permute-start.9 = (bf16[256,256]{1,0:T(8,128)(2,1)S(1)}, bf16[256,256]{1,0:T(8,128)(2,1)S(1)}, u32[]{:S(2)}, u32[]{:S(2)}) collective-permute-start(bf16[256,256]{1,0:T(8,128)(2,1)S(1)} %get-tuple-element.47), channel_id=1, source_target_pairs={{0,16},{1,9},{2,18},{3,11},{4,20},{5,13},{6,22},{7,15},{8,24},{9,1... | collective-permute-start | bytes 393224 | tf_op jit(solution)/shard_map/ppermute | solution.py:70
  28.8 0.7 %near_grads.1 = (bf16[256,256]{1,0:T(8,128)(2,1)S(1)}, bf16[256,256]{1,0:T(8,128)(2,1)S(1)}) custom-call(bf16[128,1024]{1,0:T(8,128)(2,1)S(1)} %get-tuple-element.34.refs_4_.up_ref, bf16[128,1024]{1,0:T(8,128)(2,1)S(1)} %collective-permute-done.4.next_ref, bf16[128,1024]{1,0:T(8,128)(2,1)S(1)} %collective-permute-done.3.refs_2_.refs_0_, ...), custom_call_target="tpu_custom_call" | custom-call | flops 1000000000 | tf_op jit(solution)/shard_map/near_grads/pallas_call | solution.py:419
  29.5 1.6 %collective-permute-start.8 = (bf16[256,256]{1,0:T(8,128)(2,1)S(1)}, bf16[256,256]{1,0:T(8,128)(2,1)S(1)}, u32[]{:S(2)}, u32[]{:S(2)}) collective-permute-start(bf16[256,256]{1,0:T(8,128)(2,1)S(1)} %get-tuple-element.45.refs_4_), channel_id=1, source_target_pairs={{0,16},{1,9},{2,18},{3,11},{4,20},{5,13},{6,22},{7,15},{8,24},{9,1... | collective-permute-start | bytes 393224 | tf_op jit(solution)/shard_map/ppermute | solution.py:70
  31.1 0.6 %collective-permute-done.9.far_ref = bf16[256,256]{1,0:T(8,128)(2,1)S(1)} collective-permute-done((bf16[256,256]{1,0:T(8,128)(2,1)S(1)}, bf16[256,256]{1,0:T(8,128)(2,1)S(1)}, u32[]{:S(2)}, u32[]{:S(2)}) %collective-permute-start.9) | collective-permute-done | bytes 131104 | tf_op jit(solution)/shard_map/ppermute | solution.py:70
  31.7 0.7 %mix.1 = (f32[128,1024]{1,0:T(8,128)S(1)}, bf16[128,1024]{1,0:T(8,128)(2,1)S(1)}) custom-call(bf16[256,256]{1,0:T(8,128)(2,1)S(1)} %get-tuple-element.46.near_ref, bf16[256,256]{1,0:T(8,128)(2,1)S(1)} %collective-permute-done.9.far_ref, bf16[128,1024]{1,0:T(8,128)(2,1)S(1)} %collective-permute-done.3.refs_2_.refs_0_, ...), custom_call_target="tpu_custom_call" | custom-call | flops 1000000000 | tf_op jit(solution)/shard_map/mix/pallas_call | solution.py:448
  32.4 5.6 %collective-permute-start.13 = (bf16[128,1024]{1,0:T(8,128)(2,1)S(1)}, bf16[128,1024]{1,0:T(8,128)(2,1)S(1)}, u32[]{:S(2)}, u32[]{:S(2)}) collective-permute-start(bf16[128,1024]{1,0:T(8,128)(2,1)S(1)} %get-tuple-element.48.refs_9_), channel_id=1, source_target_pairs={{0,8},{1,17},{2,10},{3,19},{4,12},{5,21},{6,14},{7,23},{8,0},{9,25... | collective-permute-start | bytes 786440 | tf_op jit(solution)/shard_map/ppermute | solution.py:70
  38.0 3.1 %backward.1 = (bf16[384,256]{1,0:T(8,128)(2,1)S(1)}, bf16[384,256]{1,0:T(8,128)(2,1)S(1)}, bf16[384,256]{1,0:T(8,128)(2,1)S(1)}, bf16[384,256]{1,0:T(8,128)(2,1)S(1)}) custom-call(bf16[512,256]{1,0:T(8,128)(2,1)S(1)} %get-tuple-element.35.q_all.refs_0_, bf16[512,256]{1,0:T(8,128)(2,1)S(1)} %get-tuple-element.36.k_all.refs_1_, ...), custom_call_target="tpu_custom_call" | custom-call | flops 3000000000 | tf_op jit(solution)/shard_map/backward/pallas_call | solution.py:360
  41.1 3.7 %collective-permute-start.10 = (bf16[384,256]{1,0:T(8,128)(2,1)S(1)}, bf16[384,256]{1,0:T(8,128)(2,1)S(1)}, u32[]{:S(2)}, u32[]{:S(2)}) collective-permute-start(bf16[384,256]{1,0:T(8,128)(2,1)S(1)} %get-tuple-element.50), channel_id=1, source_target_pairs={{0,8},{1,17},{2,10},{3,19},{4,12},{5,21},{6,14},{7,23},{8,0},{9,25... | collective-permute-start | bytes 589832 | tf_op jit(solution)/shard_map/ppermute | solution.py:70
  44.8 0.6 %collective-permute-start.11 = (bf16[384,256]{1,0:T(8,128)(2,1)S(1)}, bf16[384,256]{1,0:T(8,128)(2,1)S(1)}, u32[]{:S(2)}, u32[]{:S(2)}) collective-permute-start(bf16[384,256]{1,0:T(8,128)(2,1)S(1)} %get-tuple-element.51), channel_id=1, source_target_pairs={{0,16},{1,9},{2,18},{3,11},{4,20},{5,13},{6,22},{7,15},{8,24},{9,1... | collective-permute-start | bytes 589832 | tf_op jit(solution)/shard_map/ppermute | solution.py:70
  45.4 1.0 %collective-permute-start.12 = (bf16[384,256]{1,0:T(8,128)(2,1)S(1)}, bf16[384,256]{1,0:T(8,128)(2,1)S(1)}, u32[]{:S(2)}, u32[]{:S(2)}) collective-permute-start(bf16[384,256]{1,0:T(8,128)(2,1)S(1)} %get-tuple-element.52), channel_id=1, source_target_pairs={{0,24},{1,25},{2,26},{3,27},{4,28},{5,29},{6,30},{7,31},{8,16},{9,... | collective-permute-start | bytes 589832 | tf_op jit(solution)/shard_map/ppermute | solution.py:70
  46.3 2.4 %collective-permute-done.10.refs_1_ = bf16[384,256]{1,0:T(8,128)(2,1)S(1)} collective-permute-done((bf16[384,256]{1,0:T(8,128)(2,1)S(1)}, bf16[384,256]{1,0:T(8,128)(2,1)S(1)}, u32[]{:S(2)}, u32[]{:S(2)}) %collective-permute-start.10) | collective-permute-done | bytes 196640 | tf_op jit(solution)/shard_map/ppermute | solution.py:70
  48.7 3.9 %collective-permute-done.11.refs_2_ = bf16[384,256]{1,0:T(8,128)(2,1)S(1)} collective-permute-done((bf16[384,256]{1,0:T(8,128)(2,1)S(1)}, bf16[384,256]{1,0:T(8,128)(2,1)S(1)}, u32[]{:S(2)}, u32[]{:S(2)}) %collective-permute-start.11) | collective-permute-done | bytes 196640 | tf_op jit(solution)/shard_map/ppermute | solution.py:70
  52.6 1.7 %finish.1 = (bf16[128,1024]{1,0:T(8,128)(2,1)}, bf16[128,1024]{1,0:T(8,128)(2,1)}, bf16[128,1024]{1,0:T(8,128)(2,1)}, bf16[128,1024]{1,0:T(8,128)(2,1)}) custom-call(bf16[384,256]{1,0:T(8,128)(2,1)S(1)} %get-tuple-element.49.refs_0_, bf16[384,256]{1,0:T(8,128)(2,1)S(1)} %collective-permute-done.10.refs_1_, ...), custom_call_target="tpu_custom_call" | custom-call | tf_op jit(solution)/shard_map/finish/pallas_call | solution.py:535
  (18 shorter events, 0.1 us)
Async XLA Ops:
  1.3 12.6 %copy-start = (bf16[128,1024]{1,0:T(8,128)(2,1)S(1)}, bf16[128,1024]{1,0:T(8,128)(2,1)}, u32[]{:S(2)}) copy-start(bf16[128,1024]{1,0:T(8,128)(2,1)} %refs_1_.1) | copy-start | bytes 786436
  3.8 10.1 %collective-permute-start.3 = (bf16[128,1024]{1,0:T(8,128)(2,1)}, bf16[128,1024]{1,0:T(8,128)(2,1)S(1)}, u32[]{:S(2)}, u32[]{:S(2)}) collective-permute-start(bf16[128,1024]{1,0:T(8,128)(2,1)} %get-tuple-element.33.refs_0_), channel_id=1, source_target_pairs={{0,0},{1,1},{4,2},{5,3},{2,4},{3,5},{6,6},{7,7},{12,8},{13,9},{10,... | collective-permute-start | bytes 786440 | tf_op jit(solution)/shard_map/ppermute | solution.py:385
  5.4 15.6 %collective-permute-start = (bf16[416,256]{1,0:T(8,128)(2,1)}, bf16[416,256]{1,0:T(8,128)(2,1)S(1)}, u32[]{:S(2)}, u32[]{:S(2)}) collective-permute-start(bf16[416,256]{1,0:T(8,128)(2,1)} %get-tuple-element.30), channel_id=1, source_target_pairs={{0,8},{1,17},{2,10},{3,19},{4,12},{5,21},{6,14},{7,23},{8,0},{9,25... | collective-permute-start | bytes 638984 | tf_op jit(solution)/shard_map/ppermute | solution.py:70
  12.3 9.3 %collective-permute-start.1 = (bf16[416,256]{1,0:T(8,128)(2,1)}, bf16[416,256]{1,0:T(8,128)(2,1)S(1)}, u32[]{:S(2)}, u32[]{:S(2)}) collective-permute-start(bf16[416,256]{1,0:T(8,128)(2,1)} %get-tuple-element.31), channel_id=1, source_target_pairs={{0,16},{1,9},{2,18},{3,11},{4,20},{5,13},{6,22},{7,15},{8,24},{9,1... | collective-permute-start | bytes 638984 | tf_op jit(solution)/shard_map/ppermute | solution.py:70
  12.3 11.3 %collective-permute-start.2 = (bf16[416,256]{1,0:T(8,128)(2,1)}, bf16[416,256]{1,0:T(8,128)(2,1)S(1)}, u32[]{:S(2)}, u32[]{:S(2)}) collective-permute-start(bf16[416,256]{1,0:T(8,128)(2,1)} %get-tuple-element.32), channel_id=1, source_target_pairs={{0,24},{1,25},{2,26},{3,27},{4,28},{5,29},{6,30},{7,31},{8,16},{9,... | collective-permute-start | bytes 638984 | tf_op jit(solution)/shard_map/ppermute | solution.py:70
  13.9 1.0 %copy-start.1 = (bf16[128,1024]{1,0:T(8,128)(2,1)S(1)}, bf16[128,1024]{1,0:T(8,128)(2,1)}, u32[]{:S(2)}) copy-start(bf16[128,1024]{1,0:T(8,128)(2,1)} %get-tuple-element.33.refs_0_) | copy-start | bytes 786436
  14.8 8.8 %copy-start.2 = (bf16[416,256]{1,0:T(8,128)(2,1)S(1)}, bf16[416,256]{1,0:T(8,128)(2,1)}, u32[]{:S(2)}) copy-start(bf16[416,256]{1,0:T(8,128)(2,1)} %get-tuple-element.29.refs_0_) | copy-start | bytes 638980
  14.9 13.9 %collective-permute-start.7 = (bf16[128,1024]{1,0:T(8,128)(2,1)S(1)}, bf16[128,1024]{1,0:T(8,128)(2,1)S(1)}, u32[]{:S(2)}, u32[]{:S(2)}) collective-permute-start(bf16[128,1024]{1,0:T(8,128)(2,1)S(1)} %get-tuple-element.43), channel_id=1, source_target_pairs={{3,0},{4,1},{7,2},{2,3},{1,4},{6,5},{5,6},{0,7},{15,8},{8,9},{9,10... | collective-permute-start | bytes 786440 | tf_op jit(solution)/shard_map/ppermute | solution.py:385
  14.9 13.8 %collective-permute-start.6 = (bf16[128,1024]{1,0:T(8,128)(2,1)S(1)}, bf16[128,1024]{1,0:T(8,128)(2,1)S(1)}, u32[]{:S(2)}, u32[]{:S(2)}) collective-permute-start(bf16[128,1024]{1,0:T(8,128)(2,1)S(1)} %get-tuple-element.43), channel_id=1, source_target_pairs={{2,0},{5,1},{6,2},{3,3},{0,4},{7,5},{4,6},{1,7},{14,8},{9,9},{8,10... | collective-permute-start | bytes 786440 | tf_op jit(solution)/shard_map/ppermute | solution.py:385
  21.0 7.8 %collective-permute-start.4 = (bf16[128,1024]{1,0:T(8,128)(2,1)S(1)}, bf16[128,1024]{1,0:T(8,128)(2,1)S(1)}, u32[]{:S(2)}, u32[]{:S(2)}) collective-permute-start(bf16[128,1024]{1,0:T(8,128)(2,1)S(1)} %get-tuple-element.34.refs_4_.up_ref), channel_id=1, source_target_pairs={{0,8},{1,17},{2,10},{3,19},{4,12},{5,21},{6,14},{7,23},{8,0},{9,25... | collective-permute-start | bytes 786440 | tf_op jit(solution)/shard_map/ppermute | solution.py:70
  21.7 7.1 %collective-permute-start.5 = (bf16[128,1024]{1,0:T(8,128)(2,1)S(1)}, bf16[128,1024]{1,0:T(8,128)(2,1)S(1)}, u32[]{:S(2)}, u32[]{:S(2)}) collective-permute-start(bf16[128,1024]{1,0:T(8,128)(2,1)S(1)} %collective-permute-done.3.refs_2_.refs_0_), channel_id=1, source_target_pairs={{0,1},{1,0},{2,3},{3,2},{4,5},{5,4},{6,7},{7,6},{8,9},{9,8},{10,11... | collective-permute-start | bytes 786440 | tf_op jit(solution)/shard_map/ppermute | solution.py:52
  26.3 5.4 %collective-permute-start.9 = (bf16[256,256]{1,0:T(8,128)(2,1)S(1)}, bf16[256,256]{1,0:T(8,128)(2,1)S(1)}, u32[]{:S(2)}, u32[]{:S(2)}) collective-permute-start(bf16[256,256]{1,0:T(8,128)(2,1)S(1)} %get-tuple-element.47), channel_id=1, source_target_pairs={{0,16},{1,9},{2,18},{3,11},{4,20},{5,13},{6,22},{7,15},{8,24},{9,1... | collective-permute-start | bytes 393224 | tf_op jit(solution)/shard_map/ppermute | solution.py:70
  29.5 8.5 %collective-permute-start.8 = (bf16[256,256]{1,0:T(8,128)(2,1)S(1)}, bf16[256,256]{1,0:T(8,128)(2,1)S(1)}, u32[]{:S(2)}, u32[]{:S(2)}) collective-permute-start(bf16[256,256]{1,0:T(8,128)(2,1)S(1)} %get-tuple-element.45.refs_4_), channel_id=1, source_target_pairs={{0,16},{1,9},{2,18},{3,11},{4,20},{5,13},{6,22},{7,15},{8,24},{9,1... | collective-permute-start | bytes 393224 | tf_op jit(solution)/shard_map/ppermute | solution.py:70
  32.4 13.9 %collective-permute-start.13 = (bf16[128,1024]{1,0:T(8,128)(2,1)S(1)}, bf16[128,1024]{1,0:T(8,128)(2,1)S(1)}, u32[]{:S(2)}, u32[]{:S(2)}) collective-permute-start(bf16[128,1024]{1,0:T(8,128)(2,1)S(1)} %get-tuple-element.48.refs_9_), channel_id=1, source_target_pairs={{0,8},{1,17},{2,10},{3,19},{4,12},{5,21},{6,14},{7,23},{8,0},{9,25... | collective-permute-start | bytes 786440 | tf_op jit(solution)/shard_map/ppermute | solution.py:70
  41.1 7.6 %collective-permute-start.10 = (bf16[384,256]{1,0:T(8,128)(2,1)S(1)}, bf16[384,256]{1,0:T(8,128)(2,1)S(1)}, u32[]{:S(2)}, u32[]{:S(2)}) collective-permute-start(bf16[384,256]{1,0:T(8,128)(2,1)S(1)} %get-tuple-element.50), channel_id=1, source_target_pairs={{0,8},{1,17},{2,10},{3,19},{4,12},{5,21},{6,14},{7,23},{8,0},{9,25... | collective-permute-start | bytes 589832 | tf_op jit(solution)/shard_map/ppermute | solution.py:70
  44.8 7.8 %collective-permute-start.11 = (bf16[384,256]{1,0:T(8,128)(2,1)S(1)}, bf16[384,256]{1,0:T(8,128)(2,1)S(1)}, u32[]{:S(2)}, u32[]{:S(2)}) collective-permute-start(bf16[384,256]{1,0:T(8,128)(2,1)S(1)} %get-tuple-element.51), channel_id=1, source_target_pairs={{0,16},{1,9},{2,18},{3,11},{4,20},{5,13},{6,22},{7,15},{8,24},{9,1... | collective-permute-start | bytes 589832 | tf_op jit(solution)/shard_map/ppermute | solution.py:70
  45.4 7.2 %collective-permute-start.12 = (bf16[384,256]{1,0:T(8,128)(2,1)S(1)}, bf16[384,256]{1,0:T(8,128)(2,1)S(1)}, u32[]{:S(2)}, u32[]{:S(2)}) collective-permute-start(bf16[384,256]{1,0:T(8,128)(2,1)S(1)} %get-tuple-element.52), channel_id=1, source_target_pairs={{0,24},{1,25},{2,26},{3,27},{4,28},{5,29},{6,30},{7,31},{8,16},{9,... | collective-permute-start | bytes 589832 | tf_op jit(solution)/shard_map/ppermute | solution.py:70

commit v5 on v4

--- a/solution.py
+++ b/solution.py
@@ -52,37 +52,16 @@
     return lax.ppermute(value, axis, [(i, i ^ distance) for i in range(count)])
 
 
-def exchange_seq(value, distance):
-    return exchange(value, "seq", distance)
-
-
 def turned(distance):
     return distance ^ (((distance ^ (distance >> 1)) & 1) * 3)
 
 
-def exchange_slot(value, slot):
-    count = lax.axis_size("mp")
-    pairs = []
-    for member in range(lax.axis_size("seq")):
-        for rank in range(count):
-            partner = member ^ (turned(slot) if rank % 2 else slot)
-            pairs.append((member * count + rank, partner * count + rank))
-    return lax.ppermute(value, ("seq", "mp"), pairs)
-
-
 def is_square():
     return lax.axis_size("seq") == 4 and lax.axis_size("mp") == 8
 
 
-def distance_of(slot):
-    if is_square():
-        core = lax.rem(lax.axis_index("mp"), 2)
-        return jnp.where(core == 0, slot, turned(slot))
-    return slot
-
-
-def swapped(chunks, swap=exchange_seq):
-    return [chunks[0]] + [swap(chunks[k], k) for k in range(1, len(chunks))]
+def swapped(chunks):
+    return [chunks[0]] + [exchange(chunks[k], "seq", k) for k in range(1, len(chunks))]
 
 
 def group_of(cycle, member, chip):
@@ -99,22 +78,23 @@
     return pl.ds(pl.multiple_of(first, width), width)
 
 
-def pack_kernel(cycle, places, extra, q_ref, k_ref, v_ref, adj_any, cnt_any, *refs):
+def pack_kernel(cycle, places, q_ref, k_ref, v_ref, adj_any, cnt_any, *refs):
     refs, (adj_ref, cnt_ref, sems, more_sems) = refs[:-4], refs[-4:]
-    outs = refs[-len(places) - extra:]
+    *outs, word = refs
+    word[...] = jnp.zeros(word.shape, word.dtype)
     rows, model = q_ref.shape
     width = model // cycle
     own, chip, _ = my_place()
     lists = [
-        pltpu.make_async_copy(adj_any, adj_ref, more_sems.at[2]),
-        pltpu.make_async_copy(cnt_any, cnt_ref, more_sems.at[3]),
+        pltpu.make_async_copy(adj_any, adj_ref, more_sems.at[0]),
+        pltpu.make_async_copy(cnt_any, cnt_ref, more_sems.at[1]),
     ]
     for copy in lists:
         copy.start()
     copies = []
     if width % 128 == 0:
         for place, out in zip(places, outs):
-            group = group_of(cycle, lax.bitwise_xor(own, distance_of(place)), chip)
+            group = group_of(cycle, lax.bitwise_xor(own, place), chip)
             for at, ref in enumerate((q_ref, k_ref, v_ref)):
                 copies.append(
                     pltpu.make_async_copy(
@@ -124,11 +104,6 @@
                     )
                 )
                 copies[-1].start()
-    for at in range(extra):
-        copies.append(
-            pltpu.make_async_copy(refs[at], outs[len(places) + at], more_sems.at[at])
-        )
-        copies[-1].start()
     for copy in lists:
         copy.wait()
     lines = lax.broadcasted_iota(jnp.int32, (META, width), 0)
@@ -136,13 +111,13 @@
     for column, offset in enumerate(cycle_offsets):
         named = lax.rem(own - offset + 2 * cycle, cycle)
         meta = meta + jnp.where(
-            (lines == distance_of(lax.bitwise_xor(own, named))) & (adj_ref[0, column] > 0), 1, 0
+            (lines == lax.bitwise_xor(own, named)) & (adj_ref[0, column] > 0), 1, 0
         )
     meta = jnp.where(lines == META - 1, cnt_ref[0, 0], meta).astype(f32).astype(bf16)
     for place, out in zip(places, outs):
         out[3 * rows:, :] = meta
         if width % 128:
-            group = group_of(cycle, lax.bitwise_xor(own, distance_of(place)), chip)
+            group = group_of(cycle, lax.bitwise_xor(own, place), chip)
             for other in range(cycle):
                 @pl.when(group == other)
                 def _():
@@ -177,27 +152,26 @@
     )(*arrays, *after)
 
 
-def pack(cycle, places, tensors, extra=()):
+def pack(cycle, places, tensors):
     rows, model = tensors[0].shape
     width = model // cycle
     return pl.pallas_call(
-        functools.partial(pack_kernel, cycle, places, len(extra)),
+        functools.partial(pack_kernel, cycle, places),
         out_shape=[jax.ShapeDtypeStruct((3 * rows + META, width), bf16)] * len(places)
-        + [jax.ShapeDtypeStruct(array.shape, bf16) for array in extra],
+        + [jax.ShapeDtypeStruct((16, 128), bf16)],
         in_specs=[anywhere() if width % 128 == 0 else vmem()] * 3
-        + [unread()] * 2
-        + [anywhere()] * len(extra),
-        out_specs=[vmem()] * (len(places) + len(extra)),
+        + [unread()] * 2,
+        out_specs=[vmem()] * (len(places) + 1),
         scratch_shapes=[
             pltpu.SMEM(tensors[3].shape, jnp.int32),
             pltpu.SMEM(tensors[4].shape, jnp.int32),
             pltpu.SemaphoreType.DMA((cycle, 3)),
-            pltpu.SemaphoreType.DMA((4,)),
+            pltpu.SemaphoreType.DMA((2,)),
         ],
         compiler_params=params(62),
         cost_estimate=cost(5),
         name="pack",
-    )(*tensors, *extra)
+    )(*tensors)
 
 
 def gather_kernel(cycle, *refs):
@@ -374,13 +348,12 @@
     )(*inputs, *grads, *attended, *after)
 
 
-def fetch_rows(out_weight, distance, flip=False):
+def fetch_rows(out_weight, place):
     cycle, count = lax.axis_size("seq"), lax.axis_size("mp")
     pairs = []
     for member in range(cycle):
         for rank in range(count):
-            owner = 2 * group_of(cycle, member ^ distance(rank % 2), rank // 2)
-            owner += (rank + flip) % 2
+            owner = 2 * group_of(cycle, member ^ place, rank // 2) + rank % 2
             pairs.append((member * count + owner, member * count + rank))
     return lax.ppermute(out_weight, ("seq", "mp"), pairs)
 
@@ -486,7 +459,7 @@
     own, chip, _ = my_place()
     copies = []
     for place in range(cycle):
-        group = group_of(cycle, lax.bitwise_xor(own, distance_of(place)), chip)
+        group = group_of(cycle, lax.bitwise_xor(own, place), chip)
         if width % 128 == 0:
             for at, out in enumerate(outs):
                 copies.append(
@@ -549,10 +522,10 @@
     tensors = (queries, keys, values, adjacency, counts.reshape(1, 1))
     if is_square():
         return square(cycle, rows, tensors, out_weight, upstream)
-    chunks = swapped(pack(cycle, range(cycle), tensors))
+    chunks = swapped(pack(cycle, range(cycle), tensors)[:cycle])
     halves = []
     for place in range(cycle):
-        halves += with_other_core(fetch_rows(out_weight, lambda core: place))
+        halves += with_other_core(fetch_rows(out_weight, place))
     q_all, k_all, v_all, k_t, v_t, bias = gather(cycle, chunks)
     attended, att_t, lse = forward(cycle, 1, q_all, k_all, v_t, bias)
     grads = swapped(project_grad(cycle, upstream, halves))
@@ -562,27 +535,24 @@
 
 
 def square(cycle, rows, tensors, out_weight, upstream):
-    *chunks, out_weight = pack(cycle, range(cycle), tensors, (out_weight,))
-    first = fetch_rows(out_weight, lambda core: 0)
-    out_weight, upstream = hold((out_weight, upstream), [first])
-    chunks = swapped(chunks, exchange_slot)
-    next_upstream = exchange_slot(upstream, 1)
-    second = [
-        fetch_rows(out_weight, lambda core: turned(2) if core else 2, flip) for flip in (False, True)
-    ]
-    halves = with_other_core(first) + second
+    chunks = list(pack(cycle, range(cycle), tensors))
+    word = exchange(chunks.pop(), "mp", 1)
+    chunks = swapped(chunks)
+    out_weight, upstream = hold((out_weight, upstream), [word])
+    fetched = [fetch_rows(out_weight, place) for place in (0, 2)]
+    next_upstream = exchange(upstream, "seq", 1)
     q_all, k_all, v_all, k_t, v_t, bias = gather(cycle, chunks, [upstream])
     (near_att, far_att), att_t, lse = forward(cycle, 2, q_all, k_all, v_t, bias)
-    far_att = exchange_slot(far_att, 2)
-    near, far = near_grads(upstream, next_upstream, halves, [lse])
-    grads = [near, exchange_slot(far, 2)]
+    far_att = exchange(far_att, "seq", 2)
+    first, second = hold(fetched, [lse])
+    halves = with_other_core(first) + with_other_core(second)
+    near, far = near_grads(upstream, next_upstream, halves, [])
+    grads = [near, exchange(far, "seq", 2)]
     own_mixed, next_mixed = mix(near_att, far_att, halves, [far])
     inputs = (q_all, k_all, v_all, k_t, bias, att_t, lse)
     terms = backward(cycle, inputs, grads, [], [next_mixed])
-    next_mixed = exchange_slot(next_mixed, 1)
-    return tuple(
-        finish(cycle, rows, swapped(terms, exchange_slot), [own_mixed, next_mixed])
-    )
+    next_mixed = exchange(next_mixed, "seq", 1)
+    return tuple(finish(cycle, rows, swapped(terms), [own_mixed, next_mixed]))
 
 
 def solution(mesh):

time: 54.5 us -> 53.3 us (0.978)
  starting transfers between devices: 33.7 us -> 28.9 us
  waiting for transfers between devices: 6.85 us -> 11.5 us
  local copies, waits for them, and re-layouts: 0.96 us -> 0.02 us
    ppermute x10 -> x0, starting transfers between devices: 24.1 us -> none  [exchange_slot(): return lax.ppermute(value, ('seq', 'mp'), pairs)]
    ppermute x1 -> x13, starting transfers between devices: 1.92 us -> 23.3 us  [exchange(): return lax.ppermute(value, axis, [(i, i ^ distance) for i in range(count)])]
    ppermute x1 -> x13, waiting for transfers between devices: 0.01 us -> 11.5 us  [exchange(): return lax.ppermute(value, axis, [(i, i ^ distance) for i in range(count)])]
    ppermute x10 -> x0, waiting for transfers between devices: 6.84 us -> none  [exchange_slot(): return lax.ppermute(value, ('seq', 'mp'), pairs)]
    ppermute x3 -> x2, starting transfers between devices: 7.7 us -> 5.59 us  [fetch_rows(): return lax.ppermute(out_weight, ('seq', 'mp'), pairs)]
    unnamed x6 -> x8, local copies, waits for them, and re-layouts: 0.96 us -> 0.02 us
  transfers between devices with their start and end apart: 14 -> 15, of which waited for: 3 -> 4; matrix products, arithmetic and copies ran while one was open for 0% -> 0% of each run, Pallas kernels for 13% -> 14%
where the time goes in v5:
time: 53.3 us; the launch traced here: 53.1 us
  starting transfers between devices  28.9 us (54%)
  waiting for transfers between devices  11.5 us (22%)
  Pallas kernels  11.2 us (21%)
  between operations  1.44 us (3%)
    ppermute x13, starting transfers between devices, exchange(): return lax.ppermute(value, axis, [(i, i ^ distance) for i in range(count)])  23.3 us
    ppermute x13, waiting for transfers between devices, exchange(): return lax.ppermute(value, axis, [(i, i ^ distance) for i in range(count)])  11.5 us
    ppermute x2, starting transfers between devices, fetch_rows(): return lax.ppermute(out_weight, ('seq', 'mp'), pairs)  5.59 us
    pallas_call x1, Pallas kernels, backward(): pl.pallas_call(functools.partial(backward_kernel, cycle, min(tokens, 512)...  3.06 us
    pallas_call x1, Pallas kernels, forward(): pl.pallas_call(functools.partial(forward_kernel, min(tokens, 512)), out_s...  2.41 us
    pallas_call x1, Pallas kernels, pack(): pl.pallas_call(functools.partial(pack_kernel, cycle, places), out_shape=[...  2.26 us
    pallas_call x1, Pallas kernels, finish(): pl.pallas_call(functools.partial(finish_kernel, cycle), out_shape=[jax.Sh...  1.69 us
  transfers between devices with their start and end apart: 15, of which 4 were waited for; matrix products, arithmetic and copies ran while one was open for 0% of the time, Pallas kernels for 14%

profile of v5, /device:TPU:0, one launch (start us, length us, event | category | flops | bytes accessed | tf_op | source)
XLA Modules:
  0.0 53.1 jit_solution(17395116471116125787)
XLA Ops:
  1.3 2.3 %pack.1 = (bf16[416,256]{1,0:T(8,128)(2,1)}, bf16[416,256]{1,0:T(8,128)(2,1)}, bf16[416,256]{1,0:T(8,128)(2,1)}, bf16[416,256]{1,0:T(8,128)(2,1)}, bf16[16,128]{1,0:T(8,128)(2,1)}) custom-call(bf16[128,1024]{1,0:T(8,128)(2,1)} %q_ref.1, bf16[128,1024]{1,0:T(8,128)(2,1)} %k_ref.1, bf16[128,1024]{1,0:T(8,128)(2,1)} %v_ref.1, s32[1,4]{1,0:T(1,128)} %adj_any.1, ...), custom_call_target="tpu_custom_call" | custom-call | flops 5000000000 | tf_op jit(solution)/shard_map/pack/pallas_call | solution.py:158
  3.6 3.0 %collective-permute-start = (bf16[416,256]{1,0:T(8,128)(2,1)}, bf16[416,256]{1,0:T(8,128)(2,1)S(1)}, u32[]{:S(2)}, u32[]{:S(2)}) collective-permute-start(bf16[416,256]{1,0:T(8,128)(2,1)} %get-tuple-element.32), channel_id=1, source_target_pairs={{0,8},{8,0},{16,24},{24,16},{1,9},{9,1},{17,25},{25,17},{2,10},{10... | collective-permute-start | bytes 638984 | tf_op jit(solution)/shard_map/ppermute | solution.py:52
  6.6 1.5 %collective-permute-start.1 = (bf16[416,256]{1,0:T(8,128)(2,1)}, bf16[416,256]{1,0:T(8,128)(2,1)S(1)}, u32[]{:S(2)}, u32[]{:S(2)}) collective-permute-start(bf16[416,256]{1,0:T(8,128)(2,1)} %get-tuple-element.33), channel_id=1, source_target_pairs={{0,16},{8,24},{16,0},{24,8},{1,17},{9,25},{17,1},{25,9},{2,18},{10... | collective-permute-start | bytes 638984 | tf_op jit(solution)/shard_map/ppermute | solution.py:52
  8.2 1.2 %collective-permute-done.3.refs_2_ = bf16[16,128]{1,0:T(8,128)(2,1)S(1)} collective-permute-done((bf16[16,128]{1,0:T(8,128)(2,1)S(1)}, bf16[16,128]{1,0:T(8,128)(2,1)S(1)}, u32[]{:S(2)}, u32[]{:S(2)}) %collective-permute-start.3) | collective-permute-done | bytes 4128 | tf_op jit(solution)/shard_map/ppermute | solution.py:52
  9.4 4.9 %collective-permute-start.6 = (bf16[128,1024]{1,0:T(8,128)(2,1)S(1)}, bf16[128,1024]{1,0:T(8,128)(2,1)S(1)}, u32[]{:S(2)}, u32[]{:S(2)}) collective-permute-start(bf16[128,1024]{1,0:T(8,128)(2,1)S(1)} %get-tuple-element.45), channel_id=1, source_target_pairs={{2,0},{3,1},{6,2},{7,3},{0,4},{1,5},{4,6},{5,7},{14,8},{15,9},{8,1... | collective-permute-start | bytes 786440 | tf_op jit(solution)/shard_map/ppermute | solution.py:358
  14.3 0.7 %collective-permute-start.5 = (bf16[128,1024]{1,0:T(8,128)(2,1)S(1)}, bf16[128,1024]{1,0:T(8,128)(2,1)S(1)}, u32[]{:S(2)}, u32[]{:S(2)}) collective-permute-start(bf16[128,1024]{1,0:T(8,128)(2,1)S(1)} %get-tuple-element.45), channel_id=1, source_target_pairs={{0,0},{1,1},{4,2},{5,3},{2,4},{3,5},{6,6},{7,7},{12,8},{13,9},{10,... | collective-permute-start | bytes 786440 | tf_op jit(solution)/shard_map/ppermute | solution.py:358
  15.0 4.0 %collective-permute-start.4 = (bf16[128,1024]{1,0:T(8,128)(2,1)S(1)}, bf16[128,1024]{1,0:T(8,128)(2,1)S(1)}, u32[]{:S(2)}, u32[]{:S(2)}) collective-permute-start(bf16[128,1024]{1,0:T(8,128)(2,1)S(1)} %get-tuple-element.36.refs_4_.up_ref), channel_id=1, source_target_pairs={{0,8},{8,0},{16,24},{24,16},{1,9},{9,1},{17,25},{25,17},{2,10},{10... | collective-permute-start | bytes 786440 | tf_op jit(solution)/shard_map/ppermute | solution.py:52
  19.1 0.3 gather.1
  19.3 2.4 %forward.1 = (bf16[256,256]{1,0:T(8,128)(2,1)S(1)}, bf16[256,256]{1,0:T(8,128)(2,1)S(1)}, f32[256,512]{1,0:T(8,128)S(1)}, f32[8,512]{1,0:T(8,128)S(1)}) custom-call(bf16[512,256]{1,0:T(8,128)(2,1)S(1)} %get-tuple-element.37.q_all.refs_0_, bf16[512,256]{1,0:T(8,128)(2,1)S(1)} %get-tuple-element.38.k_all.refs_1_, bf16[256,512]{1,0:T(8,128)(2,1)S(1)} %get-tuple-element.42.v_t, ...), custom_call_target="tpu_custom_call" | custom-call | flops 3000000000 | tf_op jit(solution)/shard_map/forward/pallas_call | solution.py:261
  21.8 0.1 collective-permute-start.7
  21.9 0.5 collective-permute-start.8
  22.4 2.9 %collective-permute-start.10 = (bf16[256,256]{1,0:T(8,128)(2,1)S(1)}, bf16[256,256]{1,0:T(8,128)(2,1)S(1)}, u32[]{:S(2)}, u32[]{:S(2)}) collective-permute-start(bf16[256,256]{1,0:T(8,128)(2,1)S(1)} %get-tuple-element.51), channel_id=1, source_target_pairs={{0,16},{8,24},{16,0},{24,8},{1,17},{9,25},{17,1},{25,9},{2,18},{10... | collective-permute-start | bytes 393224 | tf_op jit(solution)/shard_map/ppermute | solution.py:52
  25.3 0.7 %near_grads.1 = (bf16[256,256]{1,0:T(8,128)(2,1)S(1)}, bf16[256,256]{1,0:T(8,128)(2,1)S(1)}) custom-call(bf16[128,1024]{1,0:T(8,128)(2,1)S(1)} %get-tuple-element.36.refs_4_.up_ref, bf16[128,1024]{1,0:T(8,128)(2,1)S(1)} %collective-permute-done.4.next_ref, bf16[128,1024]{1,0:T(8,128)(2,1)S(1)} %get-tuple-element.46.refs_0_, ...), custom_call_target="tpu_custom_call" | custom-call | flops 1000000000 | tf_op jit(solution)/shard_map/near_grads/pallas_call | solution.py:392
  26.1 1.4 %collective-permute-start.9 = (bf16[256,256]{1,0:T(8,128)(2,1)S(1)}, bf16[256,256]{1,0:T(8,128)(2,1)S(1)}, u32[]{:S(2)}, u32[]{:S(2)}) collective-permute-start(bf16[256,256]{1,0:T(8,128)(2,1)S(1)} %get-tuple-element.49.refs_4_), channel_id=1, source_target_pairs={{0,16},{8,24},{16,0},{24,8},{1,17},{9,25},{17,1},{25,9},{2,18},{10... | collective-permute-start | bytes 393224 | tf_op jit(solution)/shard_map/ppermute | solution.py:52
  27.5 2.0 %collective-permute-done.10.far_ref = bf16[256,256]{1,0:T(8,128)(2,1)S(1)} collective-permute-done((bf16[256,256]{1,0:T(8,128)(2,1)S(1)}, bf16[256,256]{1,0:T(8,128)(2,1)S(1)}, u32[]{:S(2)}, u32[]{:S(2)}) %collective-permute-start.10) | collective-permute-done | bytes 131104 | tf_op jit(solution)/shard_map/ppermute | solution.py:52
  29.5 0.7 %mix.1 = (f32[128,1024]{1,0:T(8,128)S(1)}, bf16[128,1024]{1,0:T(8,128)(2,1)S(1)}) custom-call(bf16[256,256]{1,0:T(8,128)(2,1)S(1)} %get-tuple-element.50.near_ref, bf16[256,256]{1,0:T(8,128)(2,1)S(1)} %collective-permute-done.10.far_ref, bf16[128,1024]{1,0:T(8,128)(2,1)S(1)} %get-tuple-element.46.refs_0_, ...), custom_call_target="tpu_custom_call" | custom-call | flops 1000000000 | tf_op jit(solution)/shard_map/mix/pallas_call | solution.py:421
  30.2 6.2 %collective-permute-start.14 = (bf16[128,1024]{1,0:T(8,128)(2,1)S(1)}, bf16[128,1024]{1,0:T(8,128)(2,1)S(1)}, u32[]{:S(2)}, u32[]{:S(2)}) collective-permute-start(bf16[128,1024]{1,0:T(8,128)(2,1)S(1)} %get-tuple-element.52.refs_9_), channel_id=1, source_target_pairs={{0,8},{8,0},{16,24},{24,16},{1,9},{9,1},{17,25},{25,17},{2,10},{10... | collective-permute-start | bytes 786440 | tf_op jit(solution)/shard_map/ppermute | solution.py:52
  36.5 3.1 %backward.1 = (bf16[384,256]{1,0:T(8,128)(2,1)S(1)}, bf16[384,256]{1,0:T(8,128)(2,1)S(1)}, bf16[384,256]{1,0:T(8,128)(2,1)S(1)}, bf16[384,256]{1,0:T(8,128)(2,1)S(1)}) custom-call(bf16[512,256]{1,0:T(8,128)(2,1)S(1)} %get-tuple-element.37.q_all.refs_0_, bf16[512,256]{1,0:T(8,128)(2,1)S(1)} %get-tuple-element.38.k_all.refs_1_, ...), custom_call_target="tpu_custom_call" | custom-call | flops 3000000000 | tf_op jit(solution)/shard_map/backward/pallas_call | solution.py:334
  39.5 1.6 %collective-permute-start.11 = (bf16[384,256]{1,0:T(8,128)(2,1)S(1)}, bf16[384,256]{1,0:T(8,128)(2,1)S(1)}, u32[]{:S(2)}, u32[]{:S(2)}) collective-permute-start(bf16[384,256]{1,0:T(8,128)(2,1)S(1)} %get-tuple-element.54), channel_id=1, source_target_pairs={{0,8},{8,0},{16,24},{24,16},{1,9},{9,1},{17,25},{25,17},{2,10},{10... | collective-permute-start | bytes 589832 | tf_op jit(solution)/shard_map/ppermute | solution.py:52
  41.1 1.7 %collective-permute-start.12 = (bf16[384,256]{1,0:T(8,128)(2,1)S(1)}, bf16[384,256]{1,0:T(8,128)(2,1)S(1)}, u32[]{:S(2)}, u32[]{:S(2)}) collective-permute-start(bf16[384,256]{1,0:T(8,128)(2,1)S(1)} %get-tuple-element.55), channel_id=1, source_target_pairs={{0,16},{8,24},{16,0},{24,8},{1,17},{9,25},{17,1},{25,9},{2,18},{10... | collective-permute-start | bytes 589832 | tf_op jit(solution)/shard_map/ppermute | solution.py:52
  42.8 0.3 collective-permute-start.13
  43.1 4.3 %collective-permute-done.11.refs_1_ = bf16[384,256]{1,0:T(8,128)(2,1)S(1)} collective-permute-done((bf16[384,256]{1,0:T(8,128)(2,1)S(1)}, bf16[384,256]{1,0:T(8,128)(2,1)S(1)}, u32[]{:S(2)}, u32[]{:S(2)}) %collective-permute-start.11) | collective-permute-done | bytes 196640 | tf_op jit(solution)/shard_map/ppermute | solution.py:52
  47.4 4.0 %collective-permute-done.12.refs_2_ = bf16[384,256]{1,0:T(8,128)(2,1)S(1)} collective-permute-done((bf16[384,256]{1,0:T(8,128)(2,1)S(1)}, bf16[384,256]{1,0:T(8,128)(2,1)S(1)}, u32[]{:S(2)}, u32[]{:S(2)}) %collective-permute-start.12) | collective-permute-done | bytes 196640 | tf_op jit(solution)/shard_map/ppermute | solution.py:52
  51.4 1.7 %finish.1 = (bf16[128,1024]{1,0:T(8,128)(2,1)}, bf16[128,1024]{1,0:T(8,128)(2,1)}, bf16[128,1024]{1,0:T(8,128)(2,1)}, bf16[128,1024]{1,0:T(8,128)(2,1)}) custom-call(bf16[384,256]{1,0:T(8,128)(2,1)S(1)} %get-tuple-element.53.refs_0_, bf16[384,256]{1,0:T(8,128)(2,1)S(1)} %collective-permute-done.11.refs_1_, ...), custom_call_target="tpu_custom_call" | custom-call | tf_op jit(solution)/shard_map/finish/pallas_call | solution.py:508
  (23 shorter events, 0.2 us)
Async XLA Ops:
  1.3 8.1 %copy-start = (bf16[128,1024]{1,0:T(8,128)(2,1)S(1)}, bf16[128,1024]{1,0:T(8,128)(2,1)}, u32[]{:S(2)}) copy-start(bf16[128,1024]{1,0:T(8,128)(2,1)} %refs_0_.1) | copy-start | bytes 786436
  1.3 8.0 %copy-start.1 = (bf16[128,1024]{1,0:T(8,128)(2,1)S(1)}, bf16[128,1024]{1,0:T(8,128)(2,1)}, u32[]{:S(2)}) copy-start(bf16[128,1024]{1,0:T(8,128)(2,1)} %refs_1_.1) | copy-start | bytes 786436
  3.6 4.6 %copy-start.3 = (bf16[16,128]{1,0:T(8,128)(2,1)S(1)}, bf16[16,128]{1,0:T(8,128)(2,1)}, u32[]{:S(2)}) copy-start(bf16[16,128]{1,0:T(8,128)(2,1)} %get-tuple-element.35) | copy-start | bytes 12292
  3.6 11.4 %collective-permute-start = (bf16[416,256]{1,0:T(8,128)(2,1)}, bf16[416,256]{1,0:T(8,128)(2,1)S(1)}, u32[]{:S(2)}, u32[]{:S(2)}) collective-permute-start(bf16[416,256]{1,0:T(8,128)(2,1)} %get-tuple-element.32), channel_id=1, source_target_pairs={{0,8},{8,0},{16,24},{24,16},{1,9},{9,1},{17,25},{25,17},{2,10},{10... | collective-permute-start | bytes 638984 | tf_op jit(solution)/shard_map/ppermute | solution.py:52
  6.6 12.5 %collective-permute-start.1 = (bf16[416,256]{1,0:T(8,128)(2,1)}, bf16[416,256]{1,0:T(8,128)(2,1)S(1)}, u32[]{:S(2)}, u32[]{:S(2)}) collective-permute-start(bf16[416,256]{1,0:T(8,128)(2,1)} %get-tuple-element.33), channel_id=1, source_target_pairs={{0,16},{8,24},{16,0},{24,8},{1,17},{9,25},{17,1},{25,9},{2,18},{10... | collective-permute-start | bytes 638984 | tf_op jit(solution)/shard_map/ppermute | solution.py:52
  8.1 11.0 %collective-permute-start.2 = (bf16[416,256]{1,0:T(8,128)(2,1)}, bf16[416,256]{1,0:T(8,128)(2,1)S(1)}, u32[]{:S(2)}, u32[]{:S(2)}) collective-permute-start(bf16[416,256]{1,0:T(8,128)(2,1)} %get-tuple-element.34), channel_id=1, source_target_pairs={{0,24},{8,16},{16,8},{24,0},{1,25},{9,17},{17,9},{25,1},{2,26},{10... | collective-permute-start | bytes 638984 | tf_op jit(solution)/shard_map/ppermute | solution.py:52
  8.1 10.9 %copy-start.2 = (bf16[416,256]{1,0:T(8,128)(2,1)S(1)}, bf16[416,256]{1,0:T(8,128)(2,1)}, u32[]{:S(2)}) copy-start(bf16[416,256]{1,0:T(8,128)(2,1)} %get-tuple-element.31.refs_0_) | copy-start | bytes 638980
  8.1 1.2 %collective-permute-start.3 = (bf16[16,128]{1,0:T(8,128)(2,1)S(1)}, bf16[16,128]{1,0:T(8,128)(2,1)S(1)}, u32[]{:S(2)}, u32[]{:S(2)}) collective-permute-start(bf16[16,128]{1,0:T(8,128)(2,1)S(1)} %copy-done.3), channel_id=1, source_target_pairs={{0,1},{1,0},{2,3},{3,2},{4,5},{5,4},{6,7},{7,6},{8,9},{9,8},{10,11... | collective-permute-start | bytes 12296 | tf_op jit(solution)/shard_map/ppermute | solution.py:52
  9.4 12.4 %collective-permute-start.6 = (bf16[128,1024]{1,0:T(8,128)(2,1)S(1)}, bf16[128,1024]{1,0:T(8,128)(2,1)S(1)}, u32[]{:S(2)}, u32[]{:S(2)}) collective-permute-start(bf16[128,1024]{1,0:T(8,128)(2,1)S(1)} %get-tuple-element.45), channel_id=1, source_target_pairs={{2,0},{3,1},{6,2},{7,3},{0,4},{1,5},{4,6},{5,7},{14,8},{15,9},{8,1... | collective-permute-start | bytes 786440 | tf_op jit(solution)/shard_map/ppermute | solution.py:358
  14.3 7.4 %collective-permute-start.5 = (bf16[128,1024]{1,0:T(8,128)(2,1)S(1)}, bf16[128,1024]{1,0:T(8,128)(2,1)S(1)}, u32[]{:S(2)}, u32[]{:S(2)}) collective-permute-start(bf16[128,1024]{1,0:T(8,128)(2,1)S(1)} %get-tuple-element.45), channel_id=1, source_target_pairs={{0,0},{1,1},{4,2},{5,3},{2,4},{3,5},{6,6},{7,7},{12,8},{13,9},{10,... | collective-permute-start | bytes 786440 | tf_op jit(solution)/shard_map/ppermute | solution.py:358
  15.0 10.3 %collective-permute-start.4 = (bf16[128,1024]{1,0:T(8,128)(2,1)S(1)}, bf16[128,1024]{1,0:T(8,128)(2,1)S(1)}, u32[]{:S(2)}, u32[]{:S(2)}) collective-permute-start(bf16[128,1024]{1,0:T(8,128)(2,1)S(1)} %get-tuple-element.36.refs_4_.up_ref), channel_id=1, source_target_pairs={{0,8},{8,0},{16,24},{24,16},{1,9},{9,1},{17,25},{25,17},{2,10},{10... | collective-permute-start | bytes 786440 | tf_op jit(solution)/shard_map/ppermute | solution.py:52
  21.8 3.5 %collective-permute-start.7 = (bf16[128,1024]{1,0:T(8,128)(2,1)S(1)}, bf16[128,1024]{1,0:T(8,128)(2,1)S(1)}, u32[]{:S(2)}, u32[]{:S(2)}) collective-permute-start(bf16[128,1024]{1,0:T(8,128)(2,1)S(1)} %get-tuple-element.46.refs_0_), channel_id=1, source_target_pairs={{0,1},{1,0},{2,3},{3,2},{4,5},{5,4},{6,7},{7,6},{8,9},{9,8},{10,11... | collective-permute-start | bytes 786440 | tf_op jit(solution)/shard_map/ppermute | solution.py:52
  21.9 3.4 %collective-permute-start.8 = (bf16[128,1024]{1,0:T(8,128)(2,1)S(1)}, bf16[128,1024]{1,0:T(8,128)(2,1)S(1)}, u32[]{:S(2)}, u32[]{:S(2)}) collective-permute-start(bf16[128,1024]{1,0:T(8,128)(2,1)S(1)} %get-tuple-element.47.refs_2_), channel_id=1, source_target_pairs={{0,1},{1,0},{2,3},{3,2},{4,5},{5,4},{6,7},{7,6},{8,9},{9,8},{10,11... | collective-permute-start | bytes 786440 | tf_op jit(solution)/shard_map/ppermute | solution.py:52
  22.4 7.1 %collective-permute-start.10 = (bf16[256,256]{1,0:T(8,128)(2,1)S(1)}, bf16[256,256]{1,0:T(8,128)(2,1)S(1)}, u32[]{:S(2)}, u32[]{:S(2)}) collective-permute-start(bf16[256,256]{1,0:T(8,128)(2,1)S(1)} %get-tuple-element.51), channel_id=1, source_target_pairs={{0,16},{8,24},{16,0},{24,8},{1,17},{9,25},{17,1},{25,9},{2,18},{10... | collective-permute-start | bytes 393224 | tf_op jit(solution)/shard_map/ppermute | solution.py:52
  26.1 10.4 %collective-permute-start.9 = (bf16[256,256]{1,0:T(8,128)(2,1)S(1)}, bf16[256,256]{1,0:T(8,128)(2,1)S(1)}, u32[]{:S(2)}, u32[]{:S(2)}) collective-permute-start(bf16[256,256]{1,0:T(8,128)(2,1)S(1)} %get-tuple-element.49.refs_4_), channel_id=1, source_target_pairs={{0,16},{8,24},{16,0},{24,8},{1,17},{9,25},{17,1},{25,9},{2,18},{10... | collective-permute-start | bytes 393224 | tf_op jit(solution)/shard_map/ppermute | solution.py:52
  30.2 12.9 %collective-permute-start.14 = (bf16[128,1024]{1,0:T(8,128)(2,1)S(1)}, bf16[128,1024]{1,0:T(8,128)(2,1)S(1)}, u32[]{:S(2)}, u32[]{:S(2)}) collective-permute-start(bf16[128,1024]{1,0:T(8,128)(2,1)S(1)} %get-tuple-element.52.refs_9_), channel_id=1, source_target_pairs={{0,8},{8,0},{16,24},{24,16},{1,9},{9,1},{17,25},{25,17},{2,10},{10... | collective-permute-start | bytes 786440 | tf_op jit(solution)/shard_map/ppermute | solution.py:52
  39.5 7.9 %collective-permute-start.11 = (bf16[384,256]{1,0:T(8,128)(2,1)S(1)}, bf16[384,256]{1,0:T(8,128)(2,1)S(1)}, u32[]{:S(2)}, u32[]{:S(2)}) collective-permute-start(bf16[384,256]{1,0:T(8,128)(2,1)S(1)} %get-tuple-element.54), channel_id=1, source_target_pairs={{0,8},{8,0},{16,24},{24,16},{1,9},{9,1},{17,25},{25,17},{2,10},{10... | collective-permute-start | bytes 589832 | tf_op jit(solution)/shard_map/ppermute | solution.py:52
  41.1 10.3 %collective-permute-start.12 = (bf16[384,256]{1,0:T(8,128)(2,1)S(1)}, bf16[384,256]{1,0:T(8,128)(2,1)S(1)}, u32[]{:S(2)}, u32[]{:S(2)}) collective-permute-start(bf16[384,256]{1,0:T(8,128)(2,1)S(1)} %get-tuple-element.55), channel_id=1, source_target_pairs={{0,16},{8,24},{16,0},{24,8},{1,17},{9,25},{17,1},{25,9},{2,18},{10... | collective-permute-start | bytes 589832 | tf_op jit(solution)/shard_map/ppermute | solution.py:52
  42.8 8.6 %collective-permute-start.13 = (bf16[384,256]{1,0:T(8,128)(2,1)S(1)}, bf16[384,256]{1,0:T(8,128)(2,1)S(1)}, u32[]{:S(2)}, u32[]{:S(2)}) collective-permute-start(bf16[384,256]{1,0:T(8,128)(2,1)S(1)} %get-tuple-element.56), channel_id=1, source_target_pairs={{0,24},{8,16},{16,8},{24,0},{1,25},{9,17},{17,9},{25,1},{2,26},{10... | collective-permute-start | bytes 589832 | tf_op jit(solution)/shard_map/ppermute | solution.py:52

commit v6 on v4

--- a/solution.py
+++ b/solution.py
@@ -99,15 +99,15 @@
     return pl.ds(pl.multiple_of(first, width), width)
 
 
-def pack_kernel(cycle, places, extra, q_ref, k_ref, v_ref, adj_any, cnt_any, *refs):
+def pack_kernel(cycle, places, q_ref, k_ref, v_ref, adj_any, cnt_any, *refs):
     refs, (adj_ref, cnt_ref, sems, more_sems) = refs[:-4], refs[-4:]
-    outs = refs[-len(places) - extra:]
+    outs = refs
     rows, model = q_ref.shape
     width = model // cycle
     own, chip, _ = my_place()
     lists = [
-        pltpu.make_async_copy(adj_any, adj_ref, more_sems.at[2]),
-        pltpu.make_async_copy(cnt_any, cnt_ref, more_sems.at[3]),
+        pltpu.make_async_copy(adj_any, adj_ref, more_sems.at[0]),
+        pltpu.make_async_copy(cnt_any, cnt_ref, more_sems.at[1]),
     ]
     for copy in lists:
         copy.start()
@@ -124,11 +124,6 @@
                     )
                 )
                 copies[-1].start()
-    for at in range(extra):
-        copies.append(
-            pltpu.make_async_copy(refs[at], outs[len(places) + at], more_sems.at[at])
-        )
-        copies[-1].start()
     for copy in lists:
         copy.wait()
     lines = lax.broadcasted_iota(jnp.int32, (META, width), 0)
@@ -177,27 +172,25 @@
     )(*arrays, *after)
 
 
-def pack(cycle, places, tensors, extra=()):
+def pack(cycle, places, tensors):
     rows, model = tensors[0].shape
     width = model // cycle
     return pl.pallas_call(
-        functools.partial(pack_kernel, cycle, places, len(extra)),
-        out_shape=[jax.ShapeDtypeStruct((3 * rows + META, width), bf16)] * len(places)
-        + [jax.ShapeDtypeStruct(array.shape, bf16) for array in extra],
+        functools.partial(pack_kernel, cycle, places),
+        out_shape=[jax.ShapeDtypeStruct((3 * rows + META, width), bf16)] * len(places),
         in_specs=[anywhere() if width % 128 == 0 else vmem()] * 3
-        + [unread()] * 2
-        + [anywhere()] * len(extra),
-        out_specs=[vmem()] * (len(places) + len(extra)),
+        + [unread()] * 2,
+        out_specs=[vmem()] * len(places),
         scratch_shapes=[
             pltpu.SMEM(tensors[3].shape, jnp.int32),
             pltpu.SMEM(tensors[4].shape, jnp.int32),
             pltpu.SemaphoreType.DMA((cycle, 3)),
-            pltpu.SemaphoreType.DMA((4,)),
+            pltpu.SemaphoreType.DMA((2,)),
         ],
         compiler_params=params(62),
         cost_estimate=cost(5),
         name="pack",
-    )(*tensors, *extra)
+    )(*tensors)
 
 
 def gather_kernel(cycle, *refs):
@@ -251,8 +244,8 @@
     return jnp.where(inside, tile, jnp.zeros_like(tile))
 
 
-def forward_kernel(query_tile, q_all, k_all, v_t, bias, *refs):
-    outs = refs[:-2]
+def forward_kernel(query_tile, parts, q_all, k_all, v_t, bias, *refs):
+    outs = refs[-2 - parts:-2]
     att_t, lse = refs[-2:]
     tokens, width = q_all.shape
     tile = head_tile(width)
@@ -280,23 +273,23 @@
         filled += out.shape[0]
 
 
-def forward(cycle, together, q_all, k_all, v_t, bias):
+def forward(cycle, together, q_all, k_all, v_t, bias, after=()):
     tokens, width = q_all.shape
     rows = tokens // cycle
     parts = cycle // together
     outs = pl.pallas_call(
-        functools.partial(forward_kernel, min(tokens, 512)),
+        functools.partial(forward_kernel, min(tokens, 512), parts),
         out_shape=[jax.ShapeDtypeStruct((together * rows, width), bf16)] * parts
         + [
             jax.ShapeDtypeStruct((width, tokens), f32),
             jax.ShapeDtypeStruct((8, tokens), f32),
         ],
-        in_specs=[vmem()] * 4,
+        in_specs=[vmem()] * 4 + [unread()] * len(after),
         out_specs=[vmem()] * (parts + 2),
         compiler_params=params(16 if tokens <= 512 else 60),
         cost_estimate=cost(3),
         name="forward",
-    )(q_all, k_all, v_t, bias)
+    )(q_all, k_all, v_t, bias, *after)
     return outs[:parts], outs[parts], outs[parts + 1]
 
 
@@ -549,7 +542,7 @@
     tensors = (queries, keys, values, adjacency, counts.reshape(1, 1))
     if is_square():
         return square(cycle, rows, tensors, out_weight, upstream)
-    chunks = swapped(pack(cycle, range(cycle), tensors))
+    chunks = swapped(list(pack(cycle, range(cycle), tensors)))
     halves = []
     for place in range(cycle):
         halves += with_other_core(fetch_rows(out_weight, lambda core: place))
@@ -562,23 +555,21 @@
 
 
 def square(cycle, rows, tensors, out_weight, upstream):
-    *chunks, out_weight = pack(cycle, range(cycle), tensors, (out_weight,))
+    next_upstream = exchange_slot(upstream, 1)
     first = fetch_rows(out_weight, lambda core: 0)
-    out_weight, upstream = hold((out_weight, upstream), [first])
-    chunks = swapped(chunks, exchange_slot)
-    next_upstream = exchange_slot(upstream, 1)
-    second = [
-        fetch_rows(out_weight, lambda core: turned(2) if core else 2, flip) for flip in (False, True)
+    chunks = swapped(pack(cycle, range(cycle), tensors), exchange_slot)
+    (held_weight,) = hold((out_weight,), [first])
+    halves = with_other_core(first) + [
+        fetch_rows(held_weight, lambda core: turned(2) if core else 2, flip) for flip in (False, True)
     ]
-    halves = with_other_core(first) + second
-    q_all, k_all, v_all, k_t, v_t, bias = gather(cycle, chunks, [upstream])
-    (near_att, far_att), att_t, lse = forward(cycle, 2, q_all, k_all, v_t, bias)
+    q_all, k_all, v_all, k_t, v_t, bias = gather(cycle, chunks)
+    near, far = near_grads(upstream, next_upstream, halves, [])
+    grads = [near, exchange_slot(far, 2)]
+    (near_att, far_att), att_t, lse = forward(cycle, 2, q_all, k_all, v_t, bias, [far])
     far_att = exchange_slot(far_att, 2)
-    near, far = near_grads(upstream, next_upstream, halves, [lse])
-    grads = [near, exchange_slot(far, 2)]
-    own_mixed, next_mixed = mix(near_att, far_att, halves, [far])
     inputs = (q_all, k_all, v_all, k_t, bias, att_t, lse)
-    terms = backward(cycle, inputs, grads, [], [next_mixed])
+    terms = backward(cycle, inputs, grads, [], [])
+    own_mixed, next_mixed = mix(near_att, far_att, halves, [terms[0]])
     next_mixed = exchange_slot(next_mixed, 1)
     return tuple(
         finish(cycle, rows, swapped(terms, exchange_slot), [own_mixed, next_mixed])

time: 54.5 us -> 53.2 us (0.976)
  starting transfers between devices: 33.7 us -> 23.9 us
  waiting for transfers between devices: 6.85 us -> 16.5 us
  local copies, waits for them, and re-layouts: 0.96 us -> 0.01 us
    ppermute x10, waiting for transfers between devices: 6.84 us -> 13.3 us  [exchange_slot(): return lax.ppermute(value, ('seq', 'mp'), pairs)]
    ppermute x3, starting transfers between devices: 7.7 us -> 3.57 us  [fetch_rows(): return lax.ppermute(out_weight, ('seq', 'mp'), pairs)]
    ppermute x10, starting transfers between devices: 24.1 us -> 20.3 us  [exchange_slot(): return lax.ppermute(value, ('seq', 'mp'), pairs)]
    ppermute x3, waiting for transfers between devices: 0.01 us -> 3.27 us  [fetch_rows(): return lax.ppermute(out_weight, ('seq', 'mp'), pairs)]
    ppermute x1, starting transfers between devices: 1.92 us -> 0.01 us  [exchange(): return lax.ppermute(value, axis, [(i, i ^ distance) for i in range(count)])]
    unnamed x6, local copies, waits for them, and re-layouts: 0.96 us -> 0.01 us
  transfers between devices with their start and end apart: 14 -> 14, of which waited for: 3 -> 7; matrix products, arithmetic and copies ran while one was open for 0% -> 0% of each run, Pallas kernels for 13% -> 15%
where the time goes in v6:
time: 53.2 us; the launch traced here: 53 us
  starting transfers between devices  23.9 us (45%)
  waiting for transfers between devices  16.5 us (31%)
  Pallas kernels  11.1 us (21%)
  between operations  1.4 us (3%)
    ppermute x10, starting transfers between devices, exchange_slot(): return lax.ppermute(value, ('seq', 'mp'), pairs)  20.3 us
    ppermute x10, waiting for transfers between devices, exchange_slot(): return lax.ppermute(value, ('seq', 'mp'), pairs)  13.3 us
    ppermute x3, starting transfers between devices, fetch_rows(): return lax.ppermute(out_weight, ('seq', 'mp'), pairs)  3.57 us
    ppermute x3, waiting for transfers between devices, fetch_rows(): return lax.ppermute(out_weight, ('seq', 'mp'), pairs)  3.27 us
    pallas_call x1, Pallas kernels, backward(): pl.pallas_call(functools.partial(backward_kernel, cycle, min(tokens, 512)...  3.05 us
    pallas_call x1, Pallas kernels, forward(): pl.pallas_call(functools.partial(forward_kernel, min(tokens, 512), parts)...  2.41 us
    pallas_call x1, Pallas kernels, pack(): pl.pallas_call(functools.partial(pack_kernel, cycle, places), out_shape=[...  2.25 us
    pallas_call x1, Pallas kernels, finish(): pl.pallas_call(functools.partial(finish_kernel, cycle), out_shape=[jax.Sh...  1.69 us
  transfers between devices with their start and end apart: 14, of which 7 were waited for; matrix products, arithmetic and copies ran while one was open for 0% of the time, Pallas kernels for 15%

profile of v6, /device:TPU:0, one launch (start us, length us, event | category | flops | bytes accessed | tf_op | source)
XLA Modules:
  0.0 53.0 jit_solution(6212260285531169090)
XLA Ops:
  0.6 1.6 %collective-permute-start.4 = (bf16[128,1024]{1,0:T(8,128)(2,1)}, bf16[128,1024]{1,0:T(8,128)(2,1)S(1)}, u32[]{:S(2)}, u32[]{:S(2)}) collective-permute-start(bf16[128,1024]{1,0:T(8,128)(2,1)} %refs_0_.1), channel_id=1, source_target_pairs={{0,0},{1,1},{4,2},{5,3},{2,4},{3,5},{6,6},{7,7},{12,8},{13,9},{10,... | collective-permute-start | bytes 786440 | tf_op jit(solution)/shard_map/ppermute | solution.py:378
  2.9 2.3 %pack.1 = (bf16[416,256]{1,0:T(8,128)(2,1)}, bf16[416,256]{1,0:T(8,128)(2,1)}, bf16[416,256]{1,0:T(8,128)(2,1)}, bf16[416,256]{1,0:T(8,128)(2,1)}) custom-call(bf16[128,1024]{1,0:T(8,128)(2,1)} %q_ref.1, bf16[128,1024]{1,0:T(8,128)(2,1)} %k_ref.1, bf16[128,1024]{1,0:T(8,128)(2,1)} %v_ref.1, s32[1,4]{1,0:T(1,128)} %adj_any.1, s32[1,1]{1,0:T(1,128)} %bitcast.1.cnt_any), custom_call_target="tpu_custom_call" | custom-call | flops 5000000000 | tf_op jit(solution)/shard_map/pack/pallas_call | solution.py:178
  5.2 6.9 %collective-permute-start = (bf16[416,256]{1,0:T(8,128)(2,1)}, bf16[416,256]{1,0:T(8,128)(2,1)S(1)}, u32[]{:S(2)}, u32[]{:S(2)}) collective-permute-start(bf16[416,256]{1,0:T(8,128)(2,1)} %get-tuple-element.27), channel_id=1, source_target_pairs={{0,8},{1,17},{2,10},{3,19},{4,12},{5,21},{6,14},{7,23},{8,0},{9,25... | collective-permute-start | bytes 638984 | tf_op jit(solution)/shard_map/ppermute | solution.py:70
  12.1 1.5 %collective-permute-start.2 = (bf16[416,256]{1,0:T(8,128)(2,1)}, bf16[416,256]{1,0:T(8,128)(2,1)S(1)}, u32[]{:S(2)}, u32[]{:S(2)}) collective-permute-start(bf16[416,256]{1,0:T(8,128)(2,1)} %get-tuple-element.29), channel_id=1, source_target_pairs={{0,24},{1,25},{2,26},{3,27},{4,28},{5,29},{6,30},{7,31},{8,16},{9,... | collective-permute-start | bytes 638984 | tf_op jit(solution)/shard_map/ppermute | solution.py:70
  13.6 1.9 %collective-permute-start.3 = (bf16[128,1024]{1,0:T(8,128)(2,1)S(1)}, bf16[128,1024]{1,0:T(8,128)(2,1)S(1)}, u32[]{:S(2)}, u32[]{:S(2)}) collective-permute-start(bf16[128,1024]{1,0:T(8,128)(2,1)S(1)} %copy-done.1), channel_id=1, source_target_pairs={{0,8},{1,17},{2,10},{3,19},{4,12},{5,21},{6,14},{7,23},{8,0},{9,25... | collective-permute-start | bytes 786440 | tf_op jit(solution)/shard_map/ppermute | solution.py:70
  15.7 2.7 %collective-permute-done.refs_1_ = bf16[416,256]{1,0:T(8,128)(2,1)S(1)} collective-permute-done((bf16[416,256]{1,0:T(8,128)(2,1)}, bf16[416,256]{1,0:T(8,128)(2,1)S(1)}, u32[]{:S(2)}, u32[]{:S(2)}) %collective-permute-start) | collective-permute-done | bytes 213024 | tf_op jit(solution)/shard_map/ppermute | solution.py:70
  18.4 1.9 %collective-permute-start.6 = (bf16[128,1024]{1,0:T(8,128)(2,1)S(1)}, bf16[128,1024]{1,0:T(8,128)(2,1)S(1)}, u32[]{:S(2)}, u32[]{:S(2)}) collective-permute-start(bf16[128,1024]{1,0:T(8,128)(2,1)S(1)} %hold.1), channel_id=1, source_target_pairs={{2,0},{5,1},{6,2},{3,3},{0,4},{7,5},{4,6},{1,7},{14,8},{9,9},{8,10... | collective-permute-start | bytes 786440 | tf_op jit(solution)/shard_map/ppermute | solution.py:378
  20.3 4.5 %collective-permute-done.1.refs_2_ = bf16[416,256]{1,0:T(8,128)(2,1)S(1)} collective-permute-done((bf16[416,256]{1,0:T(8,128)(2,1)}, bf16[416,256]{1,0:T(8,128)(2,1)S(1)}, u32[]{:S(2)}, u32[]{:S(2)}) %collective-permute-start.1) | collective-permute-done | bytes 213024 | tf_op jit(solution)/shard_map/ppermute | solution.py:70
  24.8 0.3 gather.1
  25.1 0.1 collective-permute-done.3.next_ref
  25.2 3.3 %collective-permute-done.6.refs_2_ = bf16[128,1024]{1,0:T(8,128)(2,1)S(1)} collective-permute-done((bf16[128,1024]{1,0:T(8,128)(2,1)S(1)}, bf16[128,1024]{1,0:T(8,128)(2,1)S(1)}, u32[]{:S(2)}, u32[]{:S(2)}) %collective-permute-start.6) | collective-permute-done | bytes 262176 | tf_op jit(solution)/shard_map/ppermute | solution.py:378
  28.4 0.7 %near_grads.1 = (bf16[256,256]{1,0:T(8,128)(2,1)S(1)}, bf16[256,256]{1,0:T(8,128)(2,1)S(1)}) custom-call(bf16[128,1024]{1,0:T(8,128)(2,1)S(1)} %copy-done.1, bf16[128,1024]{1,0:T(8,128)(2,1)S(1)} %collective-permute-done.3.next_ref, bf16[128,1024]{1,0:T(8,128)(2,1)S(1)} %collective-permute-done.4.refs_1_.refs_0_, ...), custom_call_target="tpu_custom_call" | custom-call | flops 1000000000 | tf_op jit(solution)/shard_map/near_grads/pallas_call | solution.py:412
  29.1 0.1 collective-permute-start.8
  29.2 2.4 %forward.1 = (bf16[256,256]{1,0:T(8,128)(2,1)S(1)}, bf16[256,256]{1,0:T(8,128)(2,1)S(1)}, f32[256,512]{1,0:T(8,128)S(1)}, f32[8,512]{1,0:T(8,128)S(1)}) custom-call(bf16[512,256]{1,0:T(8,128)(2,1)S(1)} %get-tuple-element.30.q_all.refs_0_, bf16[512,256]{1,0:T(8,128)(2,1)S(1)} %get-tuple-element.31.k_all.refs_1_, bf16[256,512]{1,0:T(8,128)(2,1)S(1)} %get-tuple-element.35.v_t, ...), custom_call_target="tpu_custom_call" | custom-call | flops 3000000000 | tf_op jit(solution)/shard_map/forward/pallas_call | solution.py:280
  31.6 2.1 %collective-permute-start.12 = (bf16[256,256]{1,0:T(8,128)(2,1)S(1)}, bf16[256,256]{1,0:T(8,128)(2,1)S(1)}, u32[]{:S(2)}, u32[]{:S(2)}) collective-permute-start(bf16[256,256]{1,0:T(8,128)(2,1)S(1)} %get-tuple-element.45), channel_id=1, source_target_pairs={{0,16},{1,9},{2,18},{3,11},{4,20},{5,13},{6,22},{7,15},{8,24},{9,1... | collective-permute-start | bytes 393224 | tf_op jit(solution)/shard_map/ppermute | solution.py:70
  33.7 0.5 collective-permute-done.8.refs_8_
  34.2 3.1 %backward.1 = (bf16[384,256]{1,0:T(8,128)(2,1)S(1)}, bf16[384,256]{1,0:T(8,128)(2,1)S(1)}, bf16[384,256]{1,0:T(8,128)(2,1)S(1)}, bf16[384,256]{1,0:T(8,128)(2,1)S(1)}) custom-call(bf16[512,256]{1,0:T(8,128)(2,1)S(1)} %get-tuple-element.30.q_all.refs_0_, bf16[512,256]{1,0:T(8,128)(2,1)S(1)} %get-tuple-element.31.k_all.refs_1_, ...), custom_call_target="tpu_custom_call" | custom-call | flops 3000000000 | tf_op jit(solution)/shard_map/backward/pallas_call | solution.py:353
  37.3 0.7 %mix.1 = (f32[128,1024]{1,0:T(8,128)S(1)}, bf16[128,1024]{1,0:T(8,128)(2,1)S(1)}) custom-call(bf16[256,256]{1,0:T(8,128)(2,1)S(1)} %get-tuple-element.44.near_ref, bf16[256,256]{1,0:T(8,128)(2,1)S(1)} %collective-permute-done.12.far_ref, bf16[128,1024]{1,0:T(8,128)(2,1)S(1)} %collective-permute-done.4.refs_1_.refs_0_, ...), custom_call_target="tpu_custom_call" | custom-call | flops 1000000000 | tf_op jit(solution)/shard_map/mix/pallas_call | solution.py:441
  37.9 4.3 %collective-permute-start.13 = (bf16[128,1024]{1,0:T(8,128)(2,1)S(1)}, bf16[128,1024]{1,0:T(8,128)(2,1)S(1)}, u32[]{:S(2)}, u32[]{:S(2)}) collective-permute-start(bf16[128,1024]{1,0:T(8,128)(2,1)S(1)} %get-tuple-element.47), channel_id=1, source_target_pairs={{0,8},{1,17},{2,10},{3,19},{4,12},{5,21},{6,14},{7,23},{8,0},{9,25... | collective-permute-start | bytes 786440 | tf_op jit(solution)/shard_map/ppermute | solution.py:70
  42.2 0.1 collective-permute-start.9
  42.4 3.4 %collective-permute-start.11 = (bf16[384,256]{1,0:T(8,128)(2,1)S(1)}, bf16[384,256]{1,0:T(8,128)(2,1)S(1)}, u32[]{:S(2)}, u32[]{:S(2)}) collective-permute-start(bf16[384,256]{1,0:T(8,128)(2,1)S(1)} %get-tuple-element.43), channel_id=1, source_target_pairs={{0,24},{1,25},{2,26},{3,27},{4,28},{5,29},{6,30},{7,31},{8,16},{9,... | collective-permute-start | bytes 589832 | tf_op jit(solution)/shard_map/ppermute | solution.py:70
  45.7 3.3 %collective-permute-done.9.refs_1_ = bf16[384,256]{1,0:T(8,128)(2,1)S(1)} collective-permute-done((bf16[384,256]{1,0:T(8,128)(2,1)S(1)}, bf16[384,256]{1,0:T(8,128)(2,1)S(1)}, u32[]{:S(2)}, u32[]{:S(2)}) %collective-permute-start.9) | collective-permute-done | bytes 196640 | tf_op jit(solution)/shard_map/ppermute | solution.py:70
  49.0 2.2 %collective-permute-done.11.refs_3_ = bf16[384,256]{1,0:T(8,128)(2,1)S(1)} collective-permute-done((bf16[384,256]{1,0:T(8,128)(2,1)S(1)}, bf16[384,256]{1,0:T(8,128)(2,1)S(1)}, u32[]{:S(2)}, u32[]{:S(2)}) %collective-permute-start.11) | collective-permute-done | bytes 196640 | tf_op jit(solution)/shard_map/ppermute | solution.py:70
  51.3 1.7 %finish.1 = (bf16[128,1024]{1,0:T(8,128)(2,1)}, bf16[128,1024]{1,0:T(8,128)(2,1)}, bf16[128,1024]{1,0:T(8,128)(2,1)}, bf16[128,1024]{1,0:T(8,128)(2,1)}) custom-call(bf16[384,256]{1,0:T(8,128)(2,1)S(1)} %get-tuple-element.40.refs_4_.refs_0_, bf16[384,256]{1,0:T(8,128)(2,1)S(1)} %collective-permute-done.9.refs_1_, ...), custom_call_target="tpu_custom_call" | custom-call | tf_op jit(solution)/shard_map/finish/pallas_call | solution.py:528
  (18 shorter events, 0.2 us)
Async XLA Ops:
  0.6 14.9 %collective-permute-start.4 = (bf16[128,1024]{1,0:T(8,128)(2,1)}, bf16[128,1024]{1,0:T(8,128)(2,1)S(1)}, u32[]{:S(2)}, u32[]{:S(2)}) collective-permute-start(bf16[128,1024]{1,0:T(8,128)(2,1)} %refs_0_.1), channel_id=1, source_target_pairs={{0,0},{1,1},{4,2},{5,3},{2,4},{3,5},{6,6},{7,7},{12,8},{13,9},{10,... | collective-permute-start | bytes 786440 | tf_op jit(solution)/shard_map/ppermute | solution.py:378
  2.9 10.7 %copy-start.1 = (bf16[128,1024]{1,0:T(8,128)(2,1)S(1)}, bf16[128,1024]{1,0:T(8,128)(2,1)}, u32[]{:S(2)}) copy-start(bf16[128,1024]{1,0:T(8,128)(2,1)} %up_ref.1) | copy-start | bytes 786436
  2.9 12.7 %copy-start = (bf16[128,1024]{1,0:T(8,128)(2,1)S(1)}, bf16[128,1024]{1,0:T(8,128)(2,1)}, u32[]{:S(2)}) copy-start(bf16[128,1024]{1,0:T(8,128)(2,1)} %refs_0_.1) | copy-start | bytes 786436
  5.2 13.2 %collective-permute-start = (bf16[416,256]{1,0:T(8,128)(2,1)}, bf16[416,256]{1,0:T(8,128)(2,1)S(1)}, u32[]{:S(2)}, u32[]{:S(2)}) collective-permute-start(bf16[416,256]{1,0:T(8,128)(2,1)} %get-tuple-element.27), channel_id=1, source_target_pairs={{0,8},{1,17},{2,10},{3,19},{4,12},{5,21},{6,14},{7,23},{8,0},{9,25... | collective-permute-start | bytes 638984 | tf_op jit(solution)/shard_map/ppermute | solution.py:70
  12.1 12.7 %collective-permute-start.1 = (bf16[416,256]{1,0:T(8,128)(2,1)}, bf16[416,256]{1,0:T(8,128)(2,1)S(1)}, u32[]{:S(2)}, u32[]{:S(2)}) collective-permute-start(bf16[416,256]{1,0:T(8,128)(2,1)} %get-tuple-element.28), channel_id=1, source_target_pairs={{0,16},{1,9},{2,18},{3,11},{4,20},{5,13},{6,22},{7,15},{8,24},{9,1... | collective-permute-start | bytes 638984 | tf_op jit(solution)/shard_map/ppermute | solution.py:70
  12.1 12.7 %copy-start.2 = (bf16[416,256]{1,0:T(8,128)(2,1)S(1)}, bf16[416,256]{1,0:T(8,128)(2,1)}, u32[]{:S(2)}) copy-start(bf16[416,256]{1,0:T(8,128)(2,1)} %get-tuple-element.26.refs_0_) | copy-start | bytes 638980
  12.1 12.7 %collective-permute-start.2 = (bf16[416,256]{1,0:T(8,128)(2,1)}, bf16[416,256]{1,0:T(8,128)(2,1)S(1)}, u32[]{:S(2)}, u32[]{:S(2)}) collective-permute-start(bf16[416,256]{1,0:T(8,128)(2,1)} %get-tuple-element.29), channel_id=1, source_target_pairs={{0,24},{1,25},{2,26},{3,27},{4,28},{5,29},{6,30},{7,31},{8,16},{9,... | collective-permute-start | bytes 638984 | tf_op jit(solution)/shard_map/ppermute | solution.py:70
  13.6 11.5 %collective-permute-start.3 = (bf16[128,1024]{1,0:T(8,128)(2,1)S(1)}, bf16[128,1024]{1,0:T(8,128)(2,1)S(1)}, u32[]{:S(2)}, u32[]{:S(2)}) collective-permute-start(bf16[128,1024]{1,0:T(8,128)(2,1)S(1)} %copy-done.1), channel_id=1, source_target_pairs={{0,8},{1,17},{2,10},{3,19},{4,12},{5,21},{6,14},{7,23},{8,0},{9,25... | collective-permute-start | bytes 786440 | tf_op jit(solution)/shard_map/ppermute | solution.py:70
  15.6 9.5 %collective-permute-start.7 = (bf16[128,1024]{1,0:T(8,128)(2,1)S(1)}, bf16[128,1024]{1,0:T(8,128)(2,1)S(1)}, u32[]{:S(2)}, u32[]{:S(2)}) collective-permute-start(bf16[128,1024]{1,0:T(8,128)(2,1)S(1)} %hold.1), channel_id=1, source_target_pairs={{3,0},{4,1},{7,2},{2,3},{1,4},{6,5},{5,6},{0,7},{15,8},{8,9},{9,10... | collective-permute-start | bytes 786440 | tf_op jit(solution)/shard_map/ppermute | solution.py:378
  18.4 10.1 %collective-permute-start.6 = (bf16[128,1024]{1,0:T(8,128)(2,1)S(1)}, bf16[128,1024]{1,0:T(8,128)(2,1)S(1)}, u32[]{:S(2)}, u32[]{:S(2)}) collective-permute-start(bf16[128,1024]{1,0:T(8,128)(2,1)S(1)} %hold.1), channel_id=1, source_target_pairs={{2,0},{5,1},{6,2},{3,3},{0,4},{7,5},{4,6},{1,7},{14,8},{9,9},{8,10... | collective-permute-start | bytes 786440 | tf_op jit(solution)/shard_map/ppermute | solution.py:378
  24.8 3.6 %collective-permute-start.5 = (bf16[128,1024]{1,0:T(8,128)(2,1)S(1)}, bf16[128,1024]{1,0:T(8,128)(2,1)S(1)}, u32[]{:S(2)}, u32[]{:S(2)}) collective-permute-start(bf16[128,1024]{1,0:T(8,128)(2,1)S(1)} %collective-permute-done.4.refs_1_.refs_0_), channel_id=1, source_target_pairs={{0,1},{1,0},{2,3},{3,2},{4,5},{5,4},{6,7},{7,6},{8,9},{9,8},{10,11... | collective-permute-start | bytes 786440 | tf_op jit(solution)/shard_map/ppermute | solution.py:52
  29.1 5.0 %collective-permute-start.8 = (bf16[256,256]{1,0:T(8,128)(2,1)S(1)}, bf16[256,256]{1,0:T(8,128)(2,1)S(1)}, u32[]{:S(2)}, u32[]{:S(2)}) collective-permute-start(bf16[256,256]{1,0:T(8,128)(2,1)S(1)} %get-tuple-element.36.refs_0_), channel_id=1, source_target_pairs={{0,16},{1,9},{2,18},{3,11},{4,20},{5,13},{6,22},{7,15},{8,24},{9,1... | collective-permute-start | bytes 393224 | tf_op jit(solution)/shard_map/ppermute | solution.py:70
  31.6 5.6 %collective-permute-start.12 = (bf16[256,256]{1,0:T(8,128)(2,1)S(1)}, bf16[256,256]{1,0:T(8,128)(2,1)S(1)}, u32[]{:S(2)}, u32[]{:S(2)}) collective-permute-start(bf16[256,256]{1,0:T(8,128)(2,1)S(1)} %get-tuple-element.45), channel_id=1, source_target_pairs={{0,16},{1,9},{2,18},{3,11},{4,20},{5,13},{6,22},{7,15},{8,24},{9,1... | collective-permute-start | bytes 393224 | tf_op jit(solution)/shard_map/ppermute | solution.py:70
  37.9 13.3 %collective-permute-start.13 = (bf16[128,1024]{1,0:T(8,128)(2,1)S(1)}, bf16[128,1024]{1,0:T(8,128)(2,1)S(1)}, u32[]{:S(2)}, u32[]{:S(2)}) collective-permute-start(bf16[128,1024]{1,0:T(8,128)(2,1)S(1)} %get-tuple-element.47), channel_id=1, source_target_pairs={{0,8},{1,17},{2,10},{3,19},{4,12},{5,21},{6,14},{7,23},{8,0},{9,25... | collective-permute-start | bytes 786440 | tf_op jit(solution)/shard_map/ppermute | solution.py:70
  42.2 6.8 %collective-permute-start.9 = (bf16[384,256]{1,0:T(8,128)(2,1)S(1)}, bf16[384,256]{1,0:T(8,128)(2,1)S(1)}, u32[]{:S(2)}, u32[]{:S(2)}) collective-permute-start(bf16[384,256]{1,0:T(8,128)(2,1)S(1)} %get-tuple-element.41), channel_id=1, source_target_pairs={{0,8},{1,17},{2,10},{3,19},{4,12},{5,21},{6,14},{7,23},{8,0},{9,25... | collective-permute-start | bytes 589832 | tf_op jit(solution)/shard_map/ppermute | solution.py:70
  42.3 6.7 %collective-permute-start.10 = (bf16[384,256]{1,0:T(8,128)(2,1)S(1)}, bf16[384,256]{1,0:T(8,128)(2,1)S(1)}, u32[]{:S(2)}, u32[]{:S(2)}) collective-permute-start(bf16[384,256]{1,0:T(8,128)(2,1)S(1)} %get-tuple-element.42), channel_id=1, source_target_pairs={{0,16},{1,9},{2,18},{3,11},{4,20},{5,13},{6,22},{7,15},{8,24},{9,1... | collective-permute-start | bytes 589832 | tf_op jit(solution)/shard_map/ppermute | solution.py:70
  42.4 8.9 %collective-permute-start.11 = (bf16[384,256]{1,0:T(8,128)(2,1)S(1)}, bf16[384,256]{1,0:T(8,128)(2,1)S(1)}, u32[]{:S(2)}, u32[]{:S(2)}) collective-permute-start(bf16[384,256]{1,0:T(8,128)(2,1)S(1)} %get-tuple-element.43), channel_id=1, source_target_pairs={{0,24},{1,25},{2,26},{3,27},{4,28},{5,29},{6,30},{7,31},{8,16},{9,... | collective-permute-start | bytes 589832 | tf_op jit(solution)/shard_map/ppermute | solution.py:70

commit v7 on v5

--- a/solution.py
+++ b/solution.py
@@ -80,8 +80,7 @@
 
 def pack_kernel(cycle, places, q_ref, k_ref, v_ref, adj_any, cnt_any, *refs):
     refs, (adj_ref, cnt_ref, sems, more_sems) = refs[:-4], refs[-4:]
-    *outs, word = refs
-    word[...] = jnp.zeros(word.shape, word.dtype)
+    outs = refs
     rows, model = q_ref.shape
     width = model // cycle
     own, chip, _ = my_place()
@@ -157,11 +156,10 @@
     width = model // cycle
     return pl.pallas_call(
         functools.partial(pack_kernel, cycle, places),
-        out_shape=[jax.ShapeDtypeStruct((3 * rows + META, width), bf16)] * len(places)
-        + [jax.ShapeDtypeStruct((16, 128), bf16)],
+        out_shape=[jax.ShapeDtypeStruct((3 * rows + META, width), bf16)] * len(places),
         in_specs=[anywhere() if width % 128 == 0 else vmem()] * 3
         + [unread()] * 2,
-        out_specs=[vmem()] * (len(places) + 1),
+        out_specs=[vmem()] * len(places),
         scratch_shapes=[
             pltpu.SMEM(tensors[3].shape, jnp.int32),
             pltpu.SMEM(tensors[4].shape, jnp.int32),
@@ -176,7 +174,8 @@
 
 def gather_kernel(cycle, *refs):
     chunks = refs[:cycle]
-    q_all, k_all, v_all, k_t, v_t, bias = refs[-6:]
+    q_all, k_all, v_all, k_t, v_t, bias, word = refs[-7:]
+    word[...] = jnp.zeros(word.shape, word.dtype)
     rows = q_all.shape[0] // cycle
     for place in range(cycle):
         for at, part in enumerate((q_all, k_all, v_all)):
@@ -206,9 +205,9 @@
         functools.partial(gather_kernel, cycle),
         out_shape=[jax.ShapeDtypeStruct((tokens, width), bf16)] * 3
         + [jax.ShapeDtypeStruct((width, tokens), bf16)] * 2
-        + [jax.ShapeDtypeStruct((tokens, tokens), f32)],
+        + [jax.ShapeDtypeStruct((tokens, tokens), f32), jax.ShapeDtypeStruct((16, 128), bf16)],
         in_specs=[vmem()] * cycle + [unread()] * len(after),
-        out_specs=[vmem()] * 6,
+        out_specs=[vmem()] * 7,
         compiler_params=params(8 if tokens <= 512 else 40),
         cost_estimate=cost(5),
         name="gather",
@@ -225,8 +224,8 @@
     return jnp.where(inside, tile, jnp.zeros_like(tile))
 
 
-def forward_kernel(query_tile, q_all, k_all, v_t, bias, *refs):
-    outs = refs[:-2]
+def forward_kernel(query_tile, parts, q_all, k_all, v_t, bias, *refs):
+    outs = refs[-2 - parts:-2]
     att_t, lse = refs[-2:]
     tokens, width = q_all.shape
     tile = head_tile(width)
@@ -254,23 +253,23 @@
         filled += out.shape[0]
 
 
-def forward(cycle, together, q_all, k_all, v_t, bias):
+def forward(cycle, together, q_all, k_all, v_t, bias, after=()):
     tokens, width = q_all.shape
     rows = tokens // cycle
     parts = cycle // together
     outs = pl.pallas_call(
-        functools.partial(forward_kernel, min(tokens, 512)),
+        functools.partial(forward_kernel, min(tokens, 512), parts),
         out_shape=[jax.ShapeDtypeStruct((together * rows, width), bf16)] * parts
         + [
             jax.ShapeDtypeStruct((width, tokens), f32),
             jax.ShapeDtypeStruct((8, tokens), f32),
         ],
-        in_specs=[vmem()] * 4,
+        in_specs=[vmem()] * 4 + [unread()] * len(after),
         out_specs=[vmem()] * (parts + 2),
         compiler_params=params(16 if tokens <= 512 else 60),
         cost_estimate=cost(3),
         name="forward",
-    )(q_all, k_all, v_t, bias)
+    )(q_all, k_all, v_t, bias, *after)
     return outs[:parts], outs[parts], outs[parts + 1]
 
 
@@ -522,11 +521,11 @@
     tensors = (queries, keys, values, adjacency, counts.reshape(1, 1))
     if is_square():
         return square(cycle, rows, tensors, out_weight, upstream)
-    chunks = swapped(pack(cycle, range(cycle), tensors)[:cycle])
+    chunks = swapped(list(pack(cycle, range(cycle), tensors)))
     halves = []
     for place in range(cycle):
         halves += with_other_core(fetch_rows(out_weight, place))
-    q_all, k_all, v_all, k_t, v_t, bias = gather(cycle, chunks)
+    q_all, k_all, v_all, k_t, v_t, bias, _ = gather(cycle, chunks)
     attended, att_t, lse = forward(cycle, 1, q_all, k_all, v_t, bias)
     grads = swapped(project_grad(cycle, upstream, halves))
     inputs = (q_all, k_all, v_all, k_t, bias, att_t, lse)
@@ -535,22 +534,21 @@
 
 
 def square(cycle, rows, tensors, out_weight, upstream):
-    chunks = list(pack(cycle, range(cycle), tensors))
-    word = exchange(chunks.pop(), "mp", 1)
-    chunks = swapped(chunks)
-    out_weight, upstream = hold((out_weight, upstream), [word])
-    fetched = [fetch_rows(out_weight, place) for place in (0, 2)]
     next_upstream = exchange(upstream, "seq", 1)
-    q_all, k_all, v_all, k_t, v_t, bias = gather(cycle, chunks, [upstream])
-    (near_att, far_att), att_t, lse = forward(cycle, 2, q_all, k_all, v_t, bias)
-    far_att = exchange(far_att, "seq", 2)
-    first, second = hold(fetched, [lse])
-    halves = with_other_core(first) + with_other_core(second)
+    first = fetch_rows(out_weight, 0)
+    chunks = swapped(list(pack(cycle, range(cycle), tensors)))
+    (held_weight,) = hold((out_weight,), [first, next_upstream])
+    second = fetch_rows(held_weight, 2)
+    q_all, k_all, v_all, k_t, v_t, bias, word = gather(cycle, chunks)
+    (held_first,) = hold((first,), [word])
+    halves = [first, exchange(held_first, "mp", 1)] + with_other_core(second)
     near, far = near_grads(upstream, next_upstream, halves, [])
     grads = [near, exchange(far, "seq", 2)]
-    own_mixed, next_mixed = mix(near_att, far_att, halves, [far])
+    (near_att, far_att), att_t, lse = forward(cycle, 2, q_all, k_all, v_t, bias, [far])
+    far_att = exchange(far_att, "seq", 2)
     inputs = (q_all, k_all, v_all, k_t, bias, att_t, lse)
-    terms = backward(cycle, inputs, grads, [], [next_mixed])
+    terms = backward(cycle, inputs, grads, [], [])
+    own_mixed, next_mixed = mix(near_att, far_att, halves, [terms[0]])
     next_mixed = exchange(next_mixed, "seq", 1)
     return tuple(finish(cycle, rows, swapped(terms), [own_mixed, next_mixed]))
 

time: 53.3 us -> 56.8 us (1.066)
  waiting for transfers between devices: 11.5 us -> 20.7 us
  starting transfers between devices: 28.9 us -> 23.3 us
    ppermute x13 -> x12, waiting for transfers between devices: 11.5 us -> 20.7 us  [exchange(): return lax.ppermute(value, axis, [(i, i ^ distance) for i in range(count)])]
    ppermute x13 -> x12, starting transfers between devices: 23.3 us -> 19.8 us  [exchange(): return lax.ppermute(value, axis, [(i, i ^ distance) for i in range(count)])]
    ppermute x2, starting transfers between devices: 5.59 us -> 3.53 us  [fetch_rows(): return lax.ppermute(out_weight, ('seq', 'mp'), pairs)]
  transfers between devices with their start and end apart: 15 -> 14, of which waited for: 4 -> 9; matrix products, arithmetic and copies ran while one was open for 0% -> 0% of each run, Pallas kernels for 14% -> 14%
where the time goes in v7:
time: 56.8 us; the launch traced here: 56.5 us
  starting transfers between devices  23.3 us (41%)
  waiting for transfers between devices  20.7 us (36%)
  Pallas kernels  11.1 us (20%)
  between operations  1.4 us (2%)
    ppermute x12, waiting for transfers between devices, exchange(): return lax.ppermute(value, axis, [(i, i ^ distance) for i in range(count)])  20.7 us
    ppermute x12, starting transfers between devices, exchange(): return lax.ppermute(value, axis, [(i, i ^ distance) for i in range(count)])  19.8 us
    ppermute x2, starting transfers between devices, fetch_rows(): return lax.ppermute(out_weight, ('seq', 'mp'), pairs)  3.53 us
    pallas_call x1, Pallas kernels, backward(): pl.pallas_call(functools.partial(backward_kernel, cycle, min(tokens, 512)...  3.06 us
    pallas_call x1, Pallas kernels, forward(): pl.pallas_call(functools.partial(forward_kernel, min(tokens, 512), parts)...  2.4 us
    pallas_call x1, Pallas kernels, pack(): pl.pallas_call(functools.partial(pack_kernel, cycle, places), out_shape=[...  2.24 us
    pallas_call x1, Pallas kernels, finish(): pl.pallas_call(functools.partial(finish_kernel, cycle), out_shape=[jax.Sh...  1.69 us
  transfers between devices with their start and end apart: 14, of which 9 were waited for; matrix products, arithmetic and copies ran while one was open for 0% of the time, Pallas kernels for 14%

profile of v7, /device:TPU:0, one launch (start us, length us, event | category | flops | bytes accessed | tf_op | source)
XLA Modules:
  0.0 56.5 jit_solution(2759985344319214501)
XLA Ops:
  0.6 1.6 %collective-permute-start.4 = (bf16[128,1024]{1,0:T(8,128)(2,1)}, bf16[128,1024]{1,0:T(8,128)(2,1)S(1)}, u32[]{:S(2)}, u32[]{:S(2)}) collective-permute-start(bf16[128,1024]{1,0:T(8,128)(2,1)} %refs_0_.1), channel_id=1, source_target_pairs={{0,0},{1,1},{4,2},{5,3},{2,4},{3,5},{6,6},{7,7},{12,8},{13,9},{10,... | collective-permute-start | bytes 786440 | tf_op jit(solution)/shard_map/ppermute | solution.py:357
  2.2 6.9 %collective-permute-start.3 = (bf16[128,1024]{1,0:T(8,128)(2,1)}, bf16[128,1024]{1,0:T(8,128)(2,1)S(1)}, u32[]{:S(2)}, u32[]{:S(2)}) collective-permute-start(bf16[128,1024]{1,0:T(8,128)(2,1)} %up_ref.1), channel_id=1, source_target_pairs={{0,8},{8,0},{16,24},{24,16},{1,9},{9,1},{17,25},{25,17},{2,10},{10... | collective-permute-start | bytes 786440 | tf_op jit(solution)/shard_map/ppermute | solution.py:52
  9.8 2.2 %pack.1 = (bf16[416,256]{1,0:T(8,128)(2,1)}, bf16[416,256]{1,0:T(8,128)(2,1)}, bf16[416,256]{1,0:T(8,128)(2,1)}, bf16[416,256]{1,0:T(8,128)(2,1)}) custom-call(bf16[128,1024]{1,0:T(8,128)(2,1)} %q_ref.1, bf16[128,1024]{1,0:T(8,128)(2,1)} %k_ref.1, bf16[128,1024]{1,0:T(8,128)(2,1)} %v_ref.1, s32[1,4]{1,0:T(1,128)} %adj_any.1, s32[1,1]{1,0:T(1,128)} %bitcast.1.cnt_any), custom_call_target="tpu_custom_call" | custom-call | flops 5000000000 | tf_op jit(solution)/shard_map/pack/pallas_call | solution.py:157
  12.1 1.0 %collective-permute-start.1 = (bf16[416,256]{1,0:T(8,128)(2,1)}, bf16[416,256]{1,0:T(8,128)(2,1)S(1)}, u32[]{:S(2)}, u32[]{:S(2)}) collective-permute-start(bf16[416,256]{1,0:T(8,128)(2,1)} %get-tuple-element.29), channel_id=1, source_target_pairs={{0,16},{8,24},{16,0},{24,8},{1,17},{9,25},{17,1},{25,9},{2,18},{10... | collective-permute-start | bytes 638984 | tf_op jit(solution)/shard_map/ppermute | solution.py:52
  13.2 2.4 %collective-permute-start.2 = (bf16[416,256]{1,0:T(8,128)(2,1)}, bf16[416,256]{1,0:T(8,128)(2,1)S(1)}, u32[]{:S(2)}, u32[]{:S(2)}) collective-permute-start(bf16[416,256]{1,0:T(8,128)(2,1)} %get-tuple-element.30), channel_id=1, source_target_pairs={{0,24},{8,16},{16,8},{24,0},{1,25},{9,17},{17,9},{25,1},{2,26},{10... | collective-permute-start | bytes 638984 | tf_op jit(solution)/shard_map/ppermute | solution.py:52
  15.6 0.9 %collective-permute-done.3.refs_2_.next_ref = bf16[128,1024]{1,0:T(8,128)(2,1)S(1)} collective-permute-done((bf16[128,1024]{1,0:T(8,128)(2,1)}, bf16[128,1024]{1,0:T(8,128)(2,1)S(1)}, u32[]{:S(2)}, u32[]{:S(2)}) %collective-permute-start.3) | collective-permute-done | bytes 262176 | tf_op jit(solution)/shard_map/ppermute | solution.py:52
  16.6 1.9 %collective-permute-start.6 = (bf16[128,1024]{1,0:T(8,128)(2,1)S(1)}, bf16[128,1024]{1,0:T(8,128)(2,1)S(1)}, u32[]{:S(2)}, u32[]{:S(2)}) collective-permute-start(bf16[128,1024]{1,0:T(8,128)(2,1)S(1)} %hold.3), channel_id=1, source_target_pairs={{2,0},{3,1},{6,2},{7,3},{0,4},{1,5},{4,6},{5,7},{14,8},{15,9},{8,1... | collective-permute-start | bytes 786440 | tf_op jit(solution)/shard_map/ppermute | solution.py:357
  18.5 2.6 %collective-permute-done.refs_1_ = bf16[416,256]{1,0:T(8,128)(2,1)S(1)} collective-permute-done((bf16[416,256]{1,0:T(8,128)(2,1)}, bf16[416,256]{1,0:T(8,128)(2,1)S(1)}, u32[]{:S(2)}, u32[]{:S(2)}) %collective-permute-start) | collective-permute-done | bytes 213024 | tf_op jit(solution)/shard_map/ppermute | solution.py:52
  21.1 3.6 %collective-permute-done.2.refs_3_ = bf16[416,256]{1,0:T(8,128)(2,1)S(1)} collective-permute-done((bf16[416,256]{1,0:T(8,128)(2,1)}, bf16[416,256]{1,0:T(8,128)(2,1)S(1)}, u32[]{:S(2)}, u32[]{:S(2)}) %collective-permute-start.2) | collective-permute-done | bytes 213024 | tf_op jit(solution)/shard_map/ppermute | solution.py:52
  25.1 0.5 collective-permute-start.7
  25.6 1.0 %collective-permute-done.5.refs_1_ = bf16[128,1024]{1,0:T(8,128)(2,1)S(1)} collective-permute-done((bf16[128,1024]{1,0:T(8,128)(2,1)S(1)}, bf16[128,1024]{1,0:T(8,128)(2,1)S(1)}, u32[]{:S(2)}, u32[]{:S(2)}) %collective-permute-start.5) | collective-permute-done | bytes 262176 | tf_op jit(solution)/shard_map/ppermute | solution.py:52
  27.0 0.7 %near_grads.1 = (bf16[256,256]{1,0:T(8,128)(2,1)S(1)}, bf16[256,256]{1,0:T(8,128)(2,1)S(1)}) custom-call(bf16[128,1024]{1,0:T(8,128)(2,1)S(1)} %copy-done.1, bf16[128,1024]{1,0:T(8,128)(2,1)S(1)} %collective-permute-done.3.refs_2_.next_ref, bf16[128,1024]{1,0:T(8,128)(2,1)S(1)} %collective-permute-done.4.refs_0_.refs_1_, ...), custom_call_target="tpu_custom_call" | custom-call | flops 1000000000 | tf_op jit(solution)/shard_map/near_grads/pallas_call | solution.py:391
  27.8 1.3 %collective-permute-start.8 = (bf16[256,256]{1,0:T(8,128)(2,1)S(1)}, bf16[256,256]{1,0:T(8,128)(2,1)S(1)}, u32[]{:S(2)}, u32[]{:S(2)}) collective-permute-start(bf16[256,256]{1,0:T(8,128)(2,1)S(1)} %get-tuple-element.38.refs_0_), channel_id=1, source_target_pairs={{0,16},{8,24},{16,0},{24,8},{1,17},{9,25},{17,1},{25,9},{2,18},{10... | collective-permute-start | bytes 393224 | tf_op jit(solution)/shard_map/ppermute | solution.py:52
  29.1 2.4 %forward.1 = (bf16[256,256]{1,0:T(8,128)(2,1)S(1)}, bf16[256,256]{1,0:T(8,128)(2,1)S(1)}, f32[256,512]{1,0:T(8,128)S(1)}, f32[8,512]{1,0:T(8,128)S(1)}) custom-call(bf16[512,256]{1,0:T(8,128)(2,1)S(1)} %get-tuple-element.31.q_all.refs_0_, bf16[512,256]{1,0:T(8,128)(2,1)S(1)} %get-tuple-element.32.k_all.refs_1_, bf16[256,512]{1,0:T(8,128)(2,1)S(1)} %get-tuple-element.36.v_t, ...), custom_call_target="tpu_custom_call" | custom-call | flops 3000000000 | tf_op jit(solution)/shard_map/forward/pallas_call | solution.py:260
  31.5 0.8 %collective-permute-start.12 = (bf16[256,256]{1,0:T(8,128)(2,1)S(1)}, bf16[256,256]{1,0:T(8,128)(2,1)S(1)}, u32[]{:S(2)}, u32[]{:S(2)}) collective-permute-start(bf16[256,256]{1,0:T(8,128)(2,1)S(1)} %get-tuple-element.47), channel_id=1, source_target_pairs={{0,16},{8,24},{16,0},{24,8},{1,17},{9,25},{17,1},{25,9},{2,18},{10... | collective-permute-start | bytes 393224 | tf_op jit(solution)/shard_map/ppermute | solution.py:52
  32.3 1.0 %collective-permute-done.8.refs_8_ = bf16[256,256]{1,0:T(8,128)(2,1)S(1)} collective-permute-done((bf16[256,256]{1,0:T(8,128)(2,1)S(1)}, bf16[256,256]{1,0:T(8,128)(2,1)S(1)}, u32[]{:S(2)}, u32[]{:S(2)}) %collective-permute-start.8) | collective-permute-done | bytes 131104 | tf_op jit(solution)/shard_map/ppermute | solution.py:52
  33.4 3.1 %backward.1 = (bf16[384,256]{1,0:T(8,128)(2,1)S(1)}, bf16[384,256]{1,0:T(8,128)(2,1)S(1)}, bf16[384,256]{1,0:T(8,128)(2,1)S(1)}, bf16[384,256]{1,0:T(8,128)(2,1)S(1)}) custom-call(bf16[512,256]{1,0:T(8,128)(2,1)S(1)} %get-tuple-element.31.q_all.refs_0_, bf16[512,256]{1,0:T(8,128)(2,1)S(1)} %get-tuple-element.32.k_all.refs_1_, ...), custom_call_target="tpu_custom_call" | custom-call | flops 3000000000 | tf_op jit(solution)/shard_map/backward/pallas_call | solution.py:333
  36.8 0.7 %mix.1 = (f32[128,1024]{1,0:T(8,128)S(1)}, bf16[128,1024]{1,0:T(8,128)(2,1)S(1)}) custom-call(bf16[256,256]{1,0:T(8,128)(2,1)S(1)} %get-tuple-element.46.near_ref, bf16[256,256]{1,0:T(8,128)(2,1)S(1)} %collective-permute-done.12.far_ref, bf16[128,1024]{1,0:T(8,128)(2,1)S(1)} %collective-permute-done.4.refs_0_.refs_1_, ...), custom_call_target="tpu_custom_call" | custom-call | flops 1000000000 | tf_op jit(solution)/shard_map/mix/pallas_call | solution.py:420
  37.5 3.1 %collective-permute-start.13 = (bf16[128,1024]{1,0:T(8,128)(2,1)S(1)}, bf16[128,1024]{1,0:T(8,128)(2,1)S(1)}, u32[]{:S(2)}, u32[]{:S(2)}) collective-permute-start(bf16[128,1024]{1,0:T(8,128)(2,1)S(1)} %get-tuple-element.49), channel_id=1, source_target_pairs={{0,8},{8,0},{16,24},{24,16},{1,9},{9,1},{17,25},{25,17},{2,10},{10... | collective-permute-start | bytes 786440 | tf_op jit(solution)/shard_map/ppermute | solution.py:52
  40.7 0.9 %collective-permute-start.10 = (bf16[384,256]{1,0:T(8,128)(2,1)S(1)}, bf16[384,256]{1,0:T(8,128)(2,1)S(1)}, u32[]{:S(2)}, u32[]{:S(2)}) collective-permute-start(bf16[384,256]{1,0:T(8,128)(2,1)S(1)} %get-tuple-element.44), channel_id=1, source_target_pairs={{0,16},{8,24},{16,0},{24,8},{1,17},{9,25},{17,1},{25,9},{2,18},{10... | collective-permute-start | bytes 589832 | tf_op jit(solution)/shard_map/ppermute | solution.py:52
  41.6 2.5 %collective-permute-start.11 = (bf16[384,256]{1,0:T(8,128)(2,1)S(1)}, bf16[384,256]{1,0:T(8,128)(2,1)S(1)}, u32[]{:S(2)}, u32[]{:S(2)}) collective-permute-start(bf16[384,256]{1,0:T(8,128)(2,1)S(1)} %get-tuple-element.45), channel_id=1, source_target_pairs={{0,24},{8,16},{16,8},{24,0},{1,25},{9,17},{17,9},{25,1},{2,26},{10... | collective-permute-start | bytes 589832 | tf_op jit(solution)/shard_map/ppermute | solution.py:52
  44.1 7.9 %collective-permute-done.9.refs_1_ = bf16[384,256]{1,0:T(8,128)(2,1)S(1)} collective-permute-done((bf16[384,256]{1,0:T(8,128)(2,1)S(1)}, bf16[384,256]{1,0:T(8,128)(2,1)S(1)}, u32[]{:S(2)}, u32[]{:S(2)}) %collective-permute-start.9) | collective-permute-done | bytes 196640 | tf_op jit(solution)/shard_map/ppermute | solution.py:52
  52.1 2.8 %collective-permute-done.11.refs_3_ = bf16[384,256]{1,0:T(8,128)(2,1)S(1)} collective-permute-done((bf16[384,256]{1,0:T(8,128)(2,1)S(1)}, bf16[384,256]{1,0:T(8,128)(2,1)S(1)}, u32[]{:S(2)}, u32[]{:S(2)}) %collective-permute-start.11) | collective-permute-done | bytes 196640 | tf_op jit(solution)/shard_map/ppermute | solution.py:52
  54.9 1.7 %finish.1 = (bf16[128,1024]{1,0:T(8,128)(2,1)}, bf16[128,1024]{1,0:T(8,128)(2,1)}, bf16[128,1024]{1,0:T(8,128)(2,1)}, bf16[128,1024]{1,0:T(8,128)(2,1)}) custom-call(bf16[384,256]{1,0:T(8,128)(2,1)S(1)} %get-tuple-element.42.refs_4_.refs_0_, bf16[384,256]{1,0:T(8,128)(2,1)S(1)} %collective-permute-done.9.refs_1_, ...), custom_call_target="tpu_custom_call" | custom-call | tf_op jit(solution)/shard_map/finish/pallas_call | solution.py:507
  (19 shorter events, 1.4 us)
Async XLA Ops:
  0.6 15.0 %collective-permute-start.4 = (bf16[128,1024]{1,0:T(8,128)(2,1)}, bf16[128,1024]{1,0:T(8,128)(2,1)S(1)}, u32[]{:S(2)}, u32[]{:S(2)}) collective-permute-start(bf16[128,1024]{1,0:T(8,128)(2,1)} %refs_0_.1), channel_id=1, source_target_pairs={{0,0},{1,1},{4,2},{5,3},{2,4},{3,5},{6,6},{7,7},{12,8},{13,9},{10,... | collective-permute-start | bytes 786440 | tf_op jit(solution)/shard_map/ppermute | solution.py:357
  2.2 14.3 %collective-permute-start.3 = (bf16[128,1024]{1,0:T(8,128)(2,1)}, bf16[128,1024]{1,0:T(8,128)(2,1)S(1)}, u32[]{:S(2)}, u32[]{:S(2)}) collective-permute-start(bf16[128,1024]{1,0:T(8,128)(2,1)} %up_ref.1), channel_id=1, source_target_pairs={{0,8},{8,0},{16,24},{24,16},{1,9},{9,1},{17,25},{25,17},{2,10},{10... | collective-permute-start | bytes 786440 | tf_op jit(solution)/shard_map/ppermute | solution.py:52
  9.8 6.7 %copy-start = (bf16[128,1024]{1,0:T(8,128)(2,1)S(1)}, bf16[128,1024]{1,0:T(8,128)(2,1)}, u32[]{:S(2)}) copy-start(bf16[128,1024]{1,0:T(8,128)(2,1)} %refs_0_.1) | copy-start | bytes 786436
  12.1 9.0 %collective-permute-start = (bf16[416,256]{1,0:T(8,128)(2,1)}, bf16[416,256]{1,0:T(8,128)(2,1)S(1)}, u32[]{:S(2)}, u32[]{:S(2)}) collective-permute-start(bf16[416,256]{1,0:T(8,128)(2,1)} %get-tuple-element.28), channel_id=1, source_target_pairs={{0,8},{8,0},{16,24},{24,16},{1,9},{9,1},{17,25},{25,17},{2,10},{10... | collective-permute-start | bytes 638984 | tf_op jit(solution)/shard_map/ppermute | solution.py:52
  12.1 9.0 %collective-permute-start.1 = (bf16[416,256]{1,0:T(8,128)(2,1)}, bf16[416,256]{1,0:T(8,128)(2,1)S(1)}, u32[]{:S(2)}, u32[]{:S(2)}) collective-permute-start(bf16[416,256]{1,0:T(8,128)(2,1)} %get-tuple-element.29), channel_id=1, source_target_pairs={{0,16},{8,24},{16,0},{24,8},{1,17},{9,25},{17,1},{25,9},{2,18},{10... | collective-permute-start | bytes 638984 | tf_op jit(solution)/shard_map/ppermute | solution.py:52
  13.2 11.5 %copy-start.2 = (bf16[416,256]{1,0:T(8,128)(2,1)S(1)}, bf16[416,256]{1,0:T(8,128)(2,1)}, u32[]{:S(2)}) copy-start(bf16[416,256]{1,0:T(8,128)(2,1)} %get-tuple-element.27.refs_0_) | copy-start | bytes 638980
  13.2 11.5 %collective-permute-start.2 = (bf16[416,256]{1,0:T(8,128)(2,1)}, bf16[416,256]{1,0:T(8,128)(2,1)S(1)}, u32[]{:S(2)}, u32[]{:S(2)}) collective-permute-start(bf16[416,256]{1,0:T(8,128)(2,1)} %get-tuple-element.30), channel_id=1, source_target_pairs={{0,24},{8,16},{16,8},{24,0},{1,25},{9,17},{17,9},{25,1},{2,26},{10... | collective-permute-start | bytes 638984 | tf_op jit(solution)/shard_map/ppermute | solution.py:52
  16.6 8.6 %collective-permute-start.6 = (bf16[128,1024]{1,0:T(8,128)(2,1)S(1)}, bf16[128,1024]{1,0:T(8,128)(2,1)S(1)}, u32[]{:S(2)}, u32[]{:S(2)}) collective-permute-start(bf16[128,1024]{1,0:T(8,128)(2,1)S(1)} %hold.3), channel_id=1, source_target_pairs={{2,0},{3,1},{6,2},{7,3},{0,4},{1,5},{4,6},{5,7},{14,8},{15,9},{8,1... | collective-permute-start | bytes 786440 | tf_op jit(solution)/shard_map/ppermute | solution.py:357
  25.0 2.0 %copy-start.1 = (bf16[128,1024]{1,0:T(8,128)(2,1)S(1)}, bf16[128,1024]{1,0:T(8,128)(2,1)}, u32[]{:S(2)}) copy-start(bf16[128,1024]{1,0:T(8,128)(2,1)} %up_ref.1) | copy-start | bytes 786436
  25.1 1.6 %collective-permute-start.5 = (bf16[128,1024]{1,0:T(8,128)(2,1)S(1)}, bf16[128,1024]{1,0:T(8,128)(2,1)S(1)}, u32[]{:S(2)}, u32[]{:S(2)}) collective-permute-start(bf16[128,1024]{1,0:T(8,128)(2,1)S(1)} %hold.2), channel_id=1, source_target_pairs={{0,1},{1,0},{2,3},{3,2},{4,5},{5,4},{6,7},{7,6},{8,9},{9,8},{10,11... | collective-permute-start | bytes 786440 | tf_op jit(solution)/shard_map/ppermute | solution.py:52
  25.1 1.9 %collective-permute-start.7 = (bf16[128,1024]{1,0:T(8,128)(2,1)S(1)}, bf16[128,1024]{1,0:T(8,128)(2,1)S(1)}, u32[]{:S(2)}, u32[]{:S(2)}) collective-permute-start(bf16[128,1024]{1,0:T(8,128)(2,1)S(1)} %collective-permute-done.6.refs_2_), channel_id=1, source_target_pairs={{0,1},{1,0},{2,3},{3,2},{4,5},{5,4},{6,7},{7,6},{8,9},{9,8},{10,11... | collective-permute-start | bytes 786440 | tf_op jit(solution)/shard_map/ppermute | solution.py:52
  27.8 5.6 %collective-permute-start.8 = (bf16[256,256]{1,0:T(8,128)(2,1)S(1)}, bf16[256,256]{1,0:T(8,128)(2,1)S(1)}, u32[]{:S(2)}, u32[]{:S(2)}) collective-permute-start(bf16[256,256]{1,0:T(8,128)(2,1)S(1)} %get-tuple-element.38.refs_0_), channel_id=1, source_target_pairs={{0,16},{8,24},{16,0},{24,8},{1,17},{9,25},{17,1},{25,9},{2,18},{10... | collective-permute-start | bytes 393224 | tf_op jit(solution)/shard_map/ppermute | solution.py:52
  31.5 5.3 %collective-permute-start.12 = (bf16[256,256]{1,0:T(8,128)(2,1)S(1)}, bf16[256,256]{1,0:T(8,128)(2,1)S(1)}, u32[]{:S(2)}, u32[]{:S(2)}) collective-permute-start(bf16[256,256]{1,0:T(8,128)(2,1)S(1)} %get-tuple-element.47), channel_id=1, source_target_pairs={{0,16},{8,24},{16,0},{24,8},{1,17},{9,25},{17,1},{25,9},{2,18},{10... | collective-permute-start | bytes 393224 | tf_op jit(solution)/shard_map/ppermute | solution.py:52
  37.5 17.3 %collective-permute-start.13 = (bf16[128,1024]{1,0:T(8,128)(2,1)S(1)}, bf16[128,1024]{1,0:T(8,128)(2,1)S(1)}, u32[]{:S(2)}, u32[]{:S(2)}) collective-permute-start(bf16[128,1024]{1,0:T(8,128)(2,1)S(1)} %get-tuple-element.49), channel_id=1, source_target_pairs={{0,8},{8,0},{16,24},{24,16},{1,9},{9,1},{17,25},{25,17},{2,10},{10... | collective-permute-start | bytes 786440 | tf_op jit(solution)/shard_map/ppermute | solution.py:52
  40.6 11.4 %collective-permute-start.9 = (bf16[384,256]{1,0:T(8,128)(2,1)S(1)}, bf16[384,256]{1,0:T(8,128)(2,1)S(1)}, u32[]{:S(2)}, u32[]{:S(2)}) collective-permute-start(bf16[384,256]{1,0:T(8,128)(2,1)S(1)} %get-tuple-element.43), channel_id=1, source_target_pairs={{0,8},{8,0},{16,24},{24,16},{1,9},{9,1},{17,25},{25,17},{2,10},{10... | collective-permute-start | bytes 589832 | tf_op jit(solution)/shard_map/ppermute | solution.py:52
  40.7 11.4 %collective-permute-start.10 = (bf16[384,256]{1,0:T(8,128)(2,1)S(1)}, bf16[384,256]{1,0:T(8,128)(2,1)S(1)}, u32[]{:S(2)}, u32[]{:S(2)}) collective-permute-start(bf16[384,256]{1,0:T(8,128)(2,1)S(1)} %get-tuple-element.44), channel_id=1, source_target_pairs={{0,16},{8,24},{16,0},{24,8},{1,17},{9,25},{17,1},{25,9},{2,18},{10... | collective-permute-start | bytes 589832 | tf_op jit(solution)/shard_map/ppermute | solution.py:52
  41.6 13.2 %collective-permute-start.11 = (bf16[384,256]{1,0:T(8,128)(2,1)S(1)}, bf16[384,256]{1,0:T(8,128)(2,1)S(1)}, u32[]{:S(2)}, u32[]{:S(2)}) collective-permute-start(bf16[384,256]{1,0:T(8,128)(2,1)S(1)} %get-tuple-element.45), channel_id=1, source_target_pairs={{0,24},{8,16},{16,8},{24,0},{1,25},{9,17},{17,9},{25,1},{2,26},{10... | collective-permute-start | bytes 589832 | tf_op jit(solution)/shard_map/ppermute | solution.py:52

commit v8 on v7

--- a/solution.py
+++ b/solution.py
@@ -372,31 +372,30 @@
     return columns_at((core if side == 0 else 1 - core) * half, half)
 
 
-def near_kernel(up_ref, next_ref, *refs):
-    halves = refs[:4]
-    near, far = refs[-2:]
-    rows = up_ref.shape[0]
+def group_kernel(count, *refs):
+    ups, halves = refs[:count], refs[count:count + 2]
+    out = refs[-1]
+    rows = ups[0].shape[0]
     _, _, core = my_place()
-    for group, out in enumerate((far, near)):
-        for side in range(2):
-            weight = halves[2 * (1 - group) + side]
-            for block, ref in enumerate((up_ref, next_ref)):
-                out[block * rows:(block + 1) * rows, half_columns(halves, core, side)] = dot_nt(
-                    ref[...], weight[...]
-                ).astype(bf16)
-
-
-def near_grads(upstream, next_upstream, halves, after):
-    rows, width = upstream.shape[0], 2 * halves[0].shape[0]
-    return pl.pallas_call(
-        near_kernel,
-        out_shape=[jax.ShapeDtypeStruct((2 * rows, width), bf16)] * 2,
-        in_specs=[vmem()] * 6 + [unread()] * len(after),
-        out_specs=[vmem()] * 2,
+    for side in range(2):
+        weight = halves[side][...]
+        for block, ref in enumerate(ups):
+            out[block * rows:(block + 1) * rows, half_columns(halves, core, side)] = dot_nt(
+                ref[...], weight
+            ).astype(bf16)
+
+
+def group_grads(upstreams, halves, after):
+    rows, width = upstreams[0].shape[0], 2 * halves[0].shape[0]
+    return pl.pallas_call(
+        functools.partial(group_kernel, len(upstreams)),
+        out_shape=jax.ShapeDtypeStruct((len(upstreams) * rows, width), bf16),
+        in_specs=[vmem()] * (len(upstreams) + 2) + [unread()] * len(after),
+        out_specs=vmem(),
         compiler_params=params(8),
         cost_estimate=cost(1),
-        name="near_grads",
-    )(upstream, next_upstream, *halves, *after)
+        name="group_grads",
+    )(*upstreams, *halves, *after)
 
 
 def mix_kernel(near_ref, far_ref, *refs):
@@ -534,21 +533,22 @@
 
 
 def square(cycle, rows, tensors, out_weight, upstream):
-    next_upstream = exchange(upstream, "seq", 1)
-    first = fetch_rows(out_weight, 0)
+    next_x, next_y = exchange(upstream, "seq", 1), exchange(upstream, "seq", 2)
     chunks = swapped(list(pack(cycle, range(cycle), tensors)))
-    (held_weight,) = hold((out_weight,), [first, next_upstream])
-    second = fetch_rows(held_weight, 2)
+    (held_weight,) = hold((out_weight,), [next_x, next_y])
+    first = fetch_rows(held_weight, 0)
+    own_rows = with_other_core(first)
     q_all, k_all, v_all, k_t, v_t, bias, word = gather(cycle, chunks)
-    (held_first,) = hold((first,), [word])
-    halves = [first, exchange(held_first, "mp", 1)] + with_other_core(second)
-    near, far = near_grads(upstream, next_upstream, halves, [])
-    grads = [near, exchange(far, "seq", 2)]
-    (near_att, far_att), att_t, lse = forward(cycle, 2, q_all, k_all, v_t, bias, [far])
+    (held_y,) = hold((next_y,), [word])
+    across = exchange(held_y, "seq", 1)
+    (near_att, far_att), att_t, lse = forward(cycle, 2, q_all, k_all, v_t, bias)
     far_att = exchange(far_att, "seq", 2)
+    grads = [group_grads((upstream, next_x, next_y, across), own_rows, [lse])]
     inputs = (q_all, k_all, v_all, k_t, bias, att_t, lse)
     terms = backward(cycle, inputs, grads, [], [])
-    own_mixed, next_mixed = mix(near_att, far_att, halves, [terms[0]])
+    (held_weight,) = hold((out_weight,), [first])
+    second = with_other_core(fetch_rows(held_weight, 2))
+    own_mixed, next_mixed = mix(near_att, far_att, own_rows + second, [terms[0]])
     next_mixed = exchange(next_mixed, "seq", 1)
     return tuple(finish(cycle, rows, swapped(terms), [own_mixed, next_mixed]))
 

time: 56.8 us -> 56.5 us (level)
  starting transfers between devices: 23.3 us -> 21.5 us
  waiting for transfers between devices: 20.7 us -> 22.2 us
    ppermute x12 -> x13, starting transfers between devices: 19.8 us -> 16.3 us  [exchange(): return lax.ppermute(value, axis, [(i, i ^ distance) for i in range(count)])]
    ppermute x2, starting transfers between devices: 3.53 us -> 5.17 us  [fetch_rows(): return lax.ppermute(out_weight, ('seq', 'mp'), pairs)]
    ppermute x2, waiting for transfers between devices: 0.01 us -> 1.49 us  [fetch_rows(): return lax.ppermute(out_weight, ('seq', 'mp'), pairs)]
    ppermute x12 -> x13, waiting for transfers between devices: 20.7 us -> 20.8 us  [exchange(): return lax.ppermute(value, axis, [(i, i ^ distance) for i in range(count)])]
  transfers between devices with their start and end apart: 14 -> 15, of which waited for: 9 -> 7; matrix products, arithmetic and copies ran while one was open for 0% -> 0% of each run, Pallas kernels for 14% -> 16%
where the time goes in v8:
time: 56.5 us; the launch traced here: 56.3 us
  waiting for transfers between devices  22.2 us (39%)
  starting transfers between devices  21.5 us (38%)
  Pallas kernels  11.2 us (20%)
  between operations  1.42 us (3%)
    ppermute x13, waiting for transfers between devices, exchange(): return lax.ppermute(value, axis, [(i, i ^ distance) for i in range(count)])  20.8 us
    ppermute x13, starting transfers between devices, exchange(): return lax.ppermute(value, axis, [(i, i ^ distance) for i in range(count)])  16.3 us
    ppermute x2, starting transfers between devices, fetch_rows(): return lax.ppermute(out_weight, ('seq', 'mp'), pairs)  5.17 us
    pallas_call x1, Pallas kernels, backward(): pl.pallas_call(functools.partial(backward_kernel, cycle, min(tokens, 512)...  3.06 us
    pallas_call x1, Pallas kernels, forward(): pl.pallas_call(functools.partial(forward_kernel, min(tokens, 512), parts)...  2.41 us
    pallas_call x1, Pallas kernels, pack(): pl.pallas_call(functools.partial(pack_kernel, cycle, places), out_shape=[...  2.24 us
    pallas_call x1, Pallas kernels, finish(): pl.pallas_call(functools.partial(finish_kernel, cycle), out_shape=[jax.Sh...  1.7 us
    ppermute x2, waiting for transfers between devices, fetch_rows(): return lax.ppermute(out_weight, ('seq', 'mp'), pairs)  1.49 us
  transfers between devices with their start and end apart: 15, of which 7 were waited for; matrix products, arithmetic and copies ran while one was open for 0% of the time, Pallas kernels for 16%

profile of v8, /device:TPU:0, one launch (start us, length us, event | category | flops | bytes accessed | tf_op | source)
XLA Modules:
  0.0 56.3 jit_solution(5280174040827741783)
XLA Ops:
  0.6 3.0 %collective-permute-start.4 = (bf16[128,1024]{1,0:T(8,128)(2,1)}, bf16[128,1024]{1,0:T(8,128)(2,1)S(1)}, u32[]{:S(2)}, u32[]{:S(2)}) collective-permute-start(bf16[128,1024]{1,0:T(8,128)(2,1)} %refs_0_.4), channel_id=1, source_target_pairs={{0,16},{8,24},{16,0},{24,8},{1,17},{9,25},{17,1},{25,9},{2,18},{10... | collective-permute-start | bytes 786440 | tf_op jit(solution)/shard_map/ppermute | solution.py:52
  3.7 1.5 %collective-permute-start.3 = (bf16[128,1024]{1,0:T(8,128)(2,1)}, bf16[128,1024]{1,0:T(8,128)(2,1)S(1)}, u32[]{:S(2)}, u32[]{:S(2)}) collective-permute-start(bf16[128,1024]{1,0:T(8,128)(2,1)} %refs_0_.4), channel_id=1, source_target_pairs={{0,8},{8,0},{16,24},{24,16},{1,9},{9,1},{17,25},{25,17},{2,10},{10... | collective-permute-start | bytes 786440 | tf_op jit(solution)/shard_map/ppermute | solution.py:52
  5.8 2.2 %pack.1 = (bf16[416,256]{1,0:T(8,128)(2,1)}, bf16[416,256]{1,0:T(8,128)(2,1)}, bf16[416,256]{1,0:T(8,128)(2,1)}, bf16[416,256]{1,0:T(8,128)(2,1)}) custom-call(bf16[128,1024]{1,0:T(8,128)(2,1)} %q_ref.1, bf16[128,1024]{1,0:T(8,128)(2,1)} %k_ref.1, bf16[128,1024]{1,0:T(8,128)(2,1)} %v_ref.1, s32[1,4]{1,0:T(1,128)} %adj_any.1, s32[1,1]{1,0:T(1,128)} %bitcast.1.cnt_any), custom_call_target="tpu_custom_call" | custom-call | flops 5000000000 | tf_op jit(solution)/shard_map/pack/pallas_call | solution.py:157
  8.1 0.6 %collective-permute-start = (bf16[416,256]{1,0:T(8,128)(2,1)}, bf16[416,256]{1,0:T(8,128)(2,1)S(1)}, u32[]{:S(2)}, u32[]{:S(2)}) collective-permute-start(bf16[416,256]{1,0:T(8,128)(2,1)} %get-tuple-element.26), channel_id=1, source_target_pairs={{0,8},{8,0},{16,24},{24,16},{1,9},{9,1},{17,25},{25,17},{2,10},{10... | collective-permute-start | bytes 638984 | tf_op jit(solution)/shard_map/ppermute | solution.py:52
  8.8 2.9 %collective-permute-start.2 = (bf16[416,256]{1,0:T(8,128)(2,1)}, bf16[416,256]{1,0:T(8,128)(2,1)S(1)}, u32[]{:S(2)}, u32[]{:S(2)}) collective-permute-start(bf16[416,256]{1,0:T(8,128)(2,1)} %get-tuple-element.28), channel_id=1, source_target_pairs={{0,24},{8,16},{16,8},{24,0},{1,25},{9,17},{17,9},{25,1},{2,26},{10... | collective-permute-start | bytes 638984 | tf_op jit(solution)/shard_map/ppermute | solution.py:52
  11.6 1.4 %collective-permute-done.3.refs_1_ = bf16[128,1024]{1,0:T(8,128)(2,1)S(1)} collective-permute-done((bf16[128,1024]{1,0:T(8,128)(2,1)}, bf16[128,1024]{1,0:T(8,128)(2,1)S(1)}, u32[]{:S(2)}, u32[]{:S(2)}) %collective-permute-start.3) | collective-permute-done | bytes 262176 | tf_op jit(solution)/shard_map/ppermute | solution.py:52
  13.0 0.7 %collective-permute-start.6 = (bf16[128,1024]{1,0:T(8,128)(2,1)S(1)}, bf16[128,1024]{1,0:T(8,128)(2,1)S(1)}, u32[]{:S(2)}, u32[]{:S(2)}) collective-permute-start(bf16[128,1024]{1,0:T(8,128)(2,1)S(1)} %hold.4), channel_id=1, source_target_pairs={{0,0},{1,1},{4,2},{5,3},{2,4},{3,5},{6,6},{7,7},{12,8},{13,9},{10,... | collective-permute-start | bytes 786440 | tf_op jit(solution)/shard_map/ppermute | solution.py:357
  13.7 3.8 %collective-permute-done.refs_1_ = bf16[416,256]{1,0:T(8,128)(2,1)S(1)} collective-permute-done((bf16[416,256]{1,0:T(8,128)(2,1)}, bf16[416,256]{1,0:T(8,128)(2,1)S(1)}, u32[]{:S(2)}, u32[]{:S(2)}) %collective-permute-start) | collective-permute-done | bytes 213024 | tf_op jit(solution)/shard_map/ppermute | solution.py:52
  17.6 3.0 %collective-permute-done.2.refs_3_ = bf16[416,256]{1,0:T(8,128)(2,1)S(1)} collective-permute-done((bf16[416,256]{1,0:T(8,128)(2,1)}, bf16[416,256]{1,0:T(8,128)(2,1)S(1)}, u32[]{:S(2)}, u32[]{:S(2)}) %collective-permute-start.2) | collective-permute-done | bytes 213024 | tf_op jit(solution)/shard_map/ppermute | solution.py:52
  20.6 0.3 gather.1
  20.9 1.7 %collective-permute-start.5 = (bf16[128,1024]{1,0:T(8,128)(2,1)S(1)}, bf16[128,1024]{1,0:T(8,128)(2,1)S(1)}, u32[]{:S(2)}, u32[]{:S(2)}) collective-permute-start(bf16[128,1024]{1,0:T(8,128)(2,1)S(1)} %hold.3), channel_id=1, source_target_pairs={{0,8},{8,0},{16,24},{24,16},{1,9},{9,1},{17,25},{25,17},{2,10},{10... | collective-permute-start | bytes 786440 | tf_op jit(solution)/shard_map/ppermute | solution.py:52
  22.6 4.5 %collective-permute-start.12 = (bf16[128,1024]{1,0:T(8,128)(2,1)S(1)}, bf16[128,1024]{1,0:T(8,128)(2,1)S(1)}, u32[]{:S(2)}, u32[]{:S(2)}) collective-permute-start(bf16[128,1024]{1,0:T(8,128)(2,1)S(1)} %hold.5), channel_id=1, source_target_pairs={{2,0},{3,1},{6,2},{7,3},{0,4},{1,5},{4,6},{5,7},{14,8},{15,9},{8,1... | collective-permute-start | bytes 786440 | tf_op jit(solution)/shard_map/ppermute | solution.py:357
  27.2 2.4 %forward.1 = (bf16[256,256]{1,0:T(8,128)(2,1)S(1)}, bf16[256,256]{1,0:T(8,128)(2,1)S(1)}, f32[256,512]{1,0:T(8,128)S(1)}, f32[8,512]{1,0:T(8,128)S(1)}) custom-call(bf16[512,256]{1,0:T(8,128)(2,1)S(1)} %get-tuple-element.29.q_all.refs_0_, bf16[512,256]{1,0:T(8,128)(2,1)S(1)} %get-tuple-element.30.k_all.refs_1_, bf16[256,512]{1,0:T(8,128)(2,1)S(1)} %get-tuple-element.34.v_t, ...), custom_call_target="tpu_custom_call" | custom-call | flops 3000000000 | tf_op jit(solution)/shard_map/forward/pallas_call | solution.py:260
  29.7 1.5 %collective-permute-done.12.refs_2_ = bf16[128,1024]{1,0:T(8,128)(2,1)S(1)} collective-permute-done((bf16[128,1024]{1,0:T(8,128)(2,1)S(1)}, bf16[128,1024]{1,0:T(8,128)(2,1)S(1)}, u32[]{:S(2)}, u32[]{:S(2)}) %collective-permute-start.12) | collective-permute-done | bytes 262176 | tf_op jit(solution)/shard_map/ppermute | solution.py:357
  31.2 0.7 %group_grads.1.refs_7_ = bf16[512,256]{1,0:T(8,128)(2,1)S(1)} custom-call(bf16[128,1024]{1,0:T(8,128)(2,1)S(1)} %copy-done.1, bf16[128,1024]{1,0:T(8,128)(2,1)S(1)} %collective-permute-done.3.refs_1_, bf16[128,1024]{1,0:T(8,128)(2,1)S(1)} %collective-permute-done.4.refs_0_.refs_2_, bf16[128,1024]{1,0:T(8,128)(2,1)S(1)} %collective-permute-done.5.refs_3_, ...), custom_call_target="tpu_custom_call" | custom-call | flops 1000000000 | tf_op jit(solution)/shard_map/group_grads/pallas_call | solution.py:390
  32.0 3.1 %backward.1 = (bf16[384,256]{1,0:T(8,128)(2,1)S(1)}, bf16[384,256]{1,0:T(8,128)(2,1)S(1)}, bf16[384,256]{1,0:T(8,128)(2,1)S(1)}, bf16[384,256]{1,0:T(8,128)(2,1)S(1)}) custom-call(bf16[512,256]{1,0:T(8,128)(2,1)S(1)} %get-tuple-element.29.q_all.refs_0_, bf16[512,256]{1,0:T(8,128)(2,1)S(1)} %get-tuple-element.30.k_all.refs_1_, ...), custom_call_target="tpu_custom_call" | custom-call | flops 3000000000 | tf_op jit(solution)/shard_map/backward/pallas_call | solution.py:333
  35.0 0.6 %collective-permute-done.11.far_ref = bf16[256,256]{1,0:T(8,128)(2,1)S(1)} collective-permute-done((bf16[256,256]{1,0:T(8,128)(2,1)S(1)}, bf16[256,256]{1,0:T(8,128)(2,1)S(1)}, u32[]{:S(2)}, u32[]{:S(2)}) %collective-permute-start.11) | collective-permute-done | bytes 131104 | tf_op jit(solution)/shard_map/ppermute | solution.py:52
  35.6 0.7 %mix.1 = (f32[128,1024]{1,0:T(8,128)S(1)}, bf16[128,1024]{1,0:T(8,128)(2,1)S(1)}) custom-call(bf16[256,256]{1,0:T(8,128)(2,1)S(1)} %get-tuple-element.42.near_ref, bf16[256,256]{1,0:T(8,128)(2,1)S(1)} %collective-permute-done.11.far_ref, bf16[128,1024]{1,0:T(8,128)(2,1)S(1)} %collective-permute-done.6.refs_4_.refs_1_.refs_0_, ...), custom_call_target="tpu_custom_call" | custom-call | flops 1000000000 | tf_op jit(solution)/shard_map/mix/pallas_call | solution.py:419
  36.3 2.9 %collective-permute-start.14 = (bf16[128,1024]{1,0:T(8,128)(2,1)S(1)}, bf16[128,1024]{1,0:T(8,128)(2,1)S(1)}, u32[]{:S(2)}, u32[]{:S(2)}) collective-permute-start(bf16[128,1024]{1,0:T(8,128)(2,1)S(1)} %get-tuple-element.45), channel_id=1, source_target_pairs={{0,8},{8,0},{16,24},{24,16},{1,9},{9,1},{17,25},{25,17},{2,10},{10... | collective-permute-start | bytes 786440 | tf_op jit(solution)/shard_map/ppermute | solution.py:52
  39.2 1.7 %collective-permute-start.8 = (bf16[384,256]{1,0:T(8,128)(2,1)S(1)}, bf16[384,256]{1,0:T(8,128)(2,1)S(1)}, u32[]{:S(2)}, u32[]{:S(2)}) collective-permute-start(bf16[384,256]{1,0:T(8,128)(2,1)S(1)} %get-tuple-element.39), channel_id=1, source_target_pairs={{0,8},{8,0},{16,24},{24,16},{1,9},{9,1},{17,25},{25,17},{2,10},{10... | collective-permute-start | bytes 589832 | tf_op jit(solution)/shard_map/ppermute | solution.py:52
  40.9 1.8 %collective-permute-start.9 = (bf16[384,256]{1,0:T(8,128)(2,1)S(1)}, bf16[384,256]{1,0:T(8,128)(2,1)S(1)}, u32[]{:S(2)}, u32[]{:S(2)}) collective-permute-start(bf16[384,256]{1,0:T(8,128)(2,1)S(1)} %get-tuple-element.40), channel_id=1, source_target_pairs={{0,16},{8,24},{16,0},{24,8},{1,17},{9,25},{17,1},{25,9},{2,18},{10... | collective-permute-start | bytes 589832 | tf_op jit(solution)/shard_map/ppermute | solution.py:52
  42.7 7.6 %collective-permute-done.10.refs_3_ = bf16[384,256]{1,0:T(8,128)(2,1)S(1)} collective-permute-done((bf16[384,256]{1,0:T(8,128)(2,1)S(1)}, bf16[384,256]{1,0:T(8,128)(2,1)S(1)}, u32[]{:S(2)}, u32[]{:S(2)}) %collective-permute-start.10) | collective-permute-done | bytes 196640 | tf_op jit(solution)/shard_map/ppermute | solution.py:52
  50.2 4.4 %collective-permute-done.8.refs_1_ = bf16[384,256]{1,0:T(8,128)(2,1)S(1)} collective-permute-done((bf16[384,256]{1,0:T(8,128)(2,1)S(1)}, bf16[384,256]{1,0:T(8,128)(2,1)S(1)}, u32[]{:S(2)}, u32[]{:S(2)}) %collective-permute-start.8) | collective-permute-done | bytes 196640 | tf_op jit(solution)/shard_map/ppermute | solution.py:52
  54.6 1.7 %finish.1 = (bf16[128,1024]{1,0:T(8,128)(2,1)}, bf16[128,1024]{1,0:T(8,128)(2,1)}, bf16[128,1024]{1,0:T(8,128)(2,1)}, bf16[128,1024]{1,0:T(8,128)(2,1)}) custom-call(bf16[384,256]{1,0:T(8,128)(2,1)S(1)} %get-tuple-element.38.refs_4_.refs_0_, bf16[384,256]{1,0:T(8,128)(2,1)S(1)} %collective-permute-done.8.refs_1_, ...), custom_call_target="tpu_custom_call" | custom-call | tf_op jit(solution)/shard_map/finish/pallas_call | solution.py:506
  (22 shorter events, 0.4 us)
Async XLA Ops:
  0.6 11.0 %collective-permute-start.4 = (bf16[128,1024]{1,0:T(8,128)(2,1)}, bf16[128,1024]{1,0:T(8,128)(2,1)S(1)}, u32[]{:S(2)}, u32[]{:S(2)}) collective-permute-start(bf16[128,1024]{1,0:T(8,128)(2,1)} %refs_0_.4), channel_id=1, source_target_pairs={{0,16},{8,24},{16,0},{24,8},{1,17},{9,25},{17,1},{25,9},{2,18},{10... | collective-permute-start | bytes 786440 | tf_op jit(solution)/shard_map/ppermute | solution.py:52
  3.7 9.3 %collective-permute-start.3 = (bf16[128,1024]{1,0:T(8,128)(2,1)}, bf16[128,1024]{1,0:T(8,128)(2,1)S(1)}, u32[]{:S(2)}, u32[]{:S(2)}) collective-permute-start(bf16[128,1024]{1,0:T(8,128)(2,1)} %refs_0_.4), channel_id=1, source_target_pairs={{0,8},{8,0},{16,24},{24,16},{1,9},{9,1},{17,25},{25,17},{2,10},{10... | collective-permute-start | bytes 786440 | tf_op jit(solution)/shard_map/ppermute | solution.py:52
  5.8 7.2 %copy-start = (bf16[128,1024]{1,0:T(8,128)(2,1)S(1)}, bf16[128,1024]{1,0:T(8,128)(2,1)}, u32[]{:S(2)}) copy-start(bf16[128,1024]{1,0:T(8,128)(2,1)} %refs_0_.5) | copy-start | bytes 786436
  8.1 9.5 %collective-permute-start = (bf16[416,256]{1,0:T(8,128)(2,1)}, bf16[416,256]{1,0:T(8,128)(2,1)S(1)}, u32[]{:S(2)}, u32[]{:S(2)}) collective-permute-start(bf16[416,256]{1,0:T(8,128)(2,1)} %get-tuple-element.26), channel_id=1, source_target_pairs={{0,8},{8,0},{16,24},{24,16},{1,9},{9,1},{17,25},{25,17},{2,10},{10... | collective-permute-start | bytes 638984 | tf_op jit(solution)/shard_map/ppermute | solution.py:52
  8.7 8.9 %collective-permute-start.1 = (bf16[416,256]{1,0:T(8,128)(2,1)}, bf16[416,256]{1,0:T(8,128)(2,1)S(1)}, u32[]{:S(2)}, u32[]{:S(2)}) collective-permute-start(bf16[416,256]{1,0:T(8,128)(2,1)} %get-tuple-element.27), channel_id=1, source_target_pairs={{0,16},{8,24},{16,0},{24,8},{1,17},{9,25},{17,1},{25,9},{2,18},{10... | collective-permute-start | bytes 638984 | tf_op jit(solution)/shard_map/ppermute | solution.py:52
  8.7 11.8 %copy-start.2 = (bf16[416,256]{1,0:T(8,128)(2,1)S(1)}, bf16[416,256]{1,0:T(8,128)(2,1)}, u32[]{:S(2)}) copy-start(bf16[416,256]{1,0:T(8,128)(2,1)} %get-tuple-element.25.refs_0_) | copy-start | bytes 638980
  8.8 11.8 %collective-permute-start.2 = (bf16[416,256]{1,0:T(8,128)(2,1)}, bf16[416,256]{1,0:T(8,128)(2,1)S(1)}, u32[]{:S(2)}, u32[]{:S(2)}) collective-permute-start(bf16[416,256]{1,0:T(8,128)(2,1)} %get-tuple-element.28), channel_id=1, source_target_pairs={{0,24},{8,16},{16,8},{24,0},{1,25},{9,17},{17,9},{25,1},{2,26},{10... | collective-permute-start | bytes 638984 | tf_op jit(solution)/shard_map/ppermute | solution.py:52
  13.0 9.6 %collective-permute-start.6 = (bf16[128,1024]{1,0:T(8,128)(2,1)S(1)}, bf16[128,1024]{1,0:T(8,128)(2,1)S(1)}, u32[]{:S(2)}, u32[]{:S(2)}) collective-permute-start(bf16[128,1024]{1,0:T(8,128)(2,1)S(1)} %hold.4), channel_id=1, source_target_pairs={{0,0},{1,1},{4,2},{5,3},{2,4},{3,5},{6,6},{7,7},{12,8},{13,9},{10,... | collective-permute-start | bytes 786440 | tf_op jit(solution)/shard_map/ppermute | solution.py:357
  20.9 10.3 %collective-permute-start.5 = (bf16[128,1024]{1,0:T(8,128)(2,1)S(1)}, bf16[128,1024]{1,0:T(8,128)(2,1)S(1)}, u32[]{:S(2)}, u32[]{:S(2)}) collective-permute-start(bf16[128,1024]{1,0:T(8,128)(2,1)S(1)} %hold.3), channel_id=1, source_target_pairs={{0,8},{8,0},{16,24},{24,16},{1,9},{9,1},{17,25},{25,17},{2,10},{10... | collective-permute-start | bytes 786440 | tf_op jit(solution)/shard_map/ppermute | solution.py:52
  22.6 8.6 %collective-permute-start.12 = (bf16[128,1024]{1,0:T(8,128)(2,1)S(1)}, bf16[128,1024]{1,0:T(8,128)(2,1)S(1)}, u32[]{:S(2)}, u32[]{:S(2)}) collective-permute-start(bf16[128,1024]{1,0:T(8,128)(2,1)S(1)} %hold.5), channel_id=1, source_target_pairs={{2,0},{3,1},{6,2},{7,3},{0,4},{1,5},{4,6},{5,7},{14,8},{15,9},{8,1... | collective-permute-start | bytes 786440 | tf_op jit(solution)/shard_map/ppermute | solution.py:357
  27.1 4.1 %collective-permute-start.7 = (bf16[128,1024]{1,0:T(8,128)(2,1)S(1)}, bf16[128,1024]{1,0:T(8,128)(2,1)S(1)}, u32[]{:S(2)}, u32[]{:S(2)}) collective-permute-start(bf16[128,1024]{1,0:T(8,128)(2,1)S(1)} %collective-permute-done.6.refs_4_.refs_1_.refs_0_), channel_id=1, source_target_pairs={{0,1},{1,0},{2,3},{3,2},{4,5},{5,4},{6,7},{7,6},{8,9},{9,8},{10,11... | collective-permute-start | bytes 786440 | tf_op jit(solution)/shard_map/ppermute | solution.py:52
  27.2 4.0 %copy-start.1 = (bf16[128,1024]{1,0:T(8,128)(2,1)S(1)}, bf16[128,1024]{1,0:T(8,128)(2,1)}, u32[]{:S(2)}) copy-start(bf16[128,1024]{1,0:T(8,128)(2,1)} %refs_0_.4) | copy-start | bytes 786436
  29.6 6.0 %collective-permute-start.11 = (bf16[256,256]{1,0:T(8,128)(2,1)S(1)}, bf16[256,256]{1,0:T(8,128)(2,1)S(1)}, u32[]{:S(2)}, u32[]{:S(2)}) collective-permute-start(bf16[256,256]{1,0:T(8,128)(2,1)S(1)} %get-tuple-element.43), channel_id=1, source_target_pairs={{0,16},{8,24},{16,0},{24,8},{1,17},{9,25},{17,1},{25,9},{2,18},{10... | collective-permute-start | bytes 393224 | tf_op jit(solution)/shard_map/ppermute | solution.py:52
  31.2 4.4 %collective-permute-start.13 = (bf16[128,1024]{1,0:T(8,128)(2,1)S(1)}, bf16[128,1024]{1,0:T(8,128)(2,1)S(1)}, u32[]{:S(2)}, u32[]{:S(2)}) collective-permute-start(bf16[128,1024]{1,0:T(8,128)(2,1)S(1)} %collective-permute-done.12.refs_2_), channel_id=1, source_target_pairs={{0,1},{1,0},{2,3},{3,2},{4,5},{5,4},{6,7},{7,6},{8,9},{9,8},{10,11... | collective-permute-start | bytes 786440 | tf_op jit(solution)/shard_map/ppermute | solution.py:52
  36.3 18.3 %collective-permute-start.14 = (bf16[128,1024]{1,0:T(8,128)(2,1)S(1)}, bf16[128,1024]{1,0:T(8,128)(2,1)S(1)}, u32[]{:S(2)}, u32[]{:S(2)}) collective-permute-start(bf16[128,1024]{1,0:T(8,128)(2,1)S(1)} %get-tuple-element.45), channel_id=1, source_target_pairs={{0,8},{8,0},{16,24},{24,16},{1,9},{9,1},{17,25},{25,17},{2,10},{10... | collective-permute-start | bytes 786440 | tf_op jit(solution)/shard_map/ppermute | solution.py:52
  39.2 11.0 %collective-permute-start.10 = (bf16[384,256]{1,0:T(8,128)(2,1)S(1)}, bf16[384,256]{1,0:T(8,128)(2,1)S(1)}, u32[]{:S(2)}, u32[]{:S(2)}) collective-permute-start(bf16[384,256]{1,0:T(8,128)(2,1)S(1)} %get-tuple-element.41), channel_id=1, source_target_pairs={{0,24},{8,16},{16,8},{24,0},{1,25},{9,17},{17,9},{25,1},{2,26},{10... | collective-permute-start | bytes 589832 | tf_op jit(solution)/shard_map/ppermute | solution.py:52
  39.2 15.4 %collective-permute-start.8 = (bf16[384,256]{1,0:T(8,128)(2,1)S(1)}, bf16[384,256]{1,0:T(8,128)(2,1)S(1)}, u32[]{:S(2)}, u32[]{:S(2)}) collective-permute-start(bf16[384,256]{1,0:T(8,128)(2,1)S(1)} %get-tuple-element.39), channel_id=1, source_target_pairs={{0,8},{8,0},{16,24},{24,16},{1,9},{9,1},{17,25},{25,17},{2,10},{10... | collective-permute-start | bytes 589832 | tf_op jit(solution)/shard_map/ppermute | solution.py:52
  40.9 13.7 %collective-permute-start.9 = (bf16[384,256]{1,0:T(8,128)(2,1)S(1)}, bf16[384,256]{1,0:T(8,128)(2,1)S(1)}, u32[]{:S(2)}, u32[]{:S(2)}) collective-permute-start(bf16[384,256]{1,0:T(8,128)(2,1)S(1)} %get-tuple-element.40), channel_id=1, source_target_pairs={{0,16},{8,24},{16,0},{24,8},{1,17},{9,25},{17,1},{25,9},{2,18},{10... | collective-permute-start | bytes 589832 | tf_op jit(solution)/shard_map/ppermute | solution.py:52

commit v9 on v8

--- a/solution.py
+++ b/solution.py
@@ -398,36 +398,27 @@
     )(*upstreams, *halves, *after)
 
 
-def mix_kernel(near_ref, far_ref, *refs):
-    halves = refs[:4]
-    own, other = refs[-2:]
+def partial_kernel(att_ref, mine, other, own, *outs):
     rows = own.shape[0]
     _, _, core = my_place()
-    total = None
-    for group, ref in enumerate((near_ref, far_ref)):
-        for side in range(2):
-            term = dot_nn(
-                ref[:, half_columns(halves, core, side)], halves[2 * group + side][...]
-            )
-            total = term if total is None else total + term
-    own[...] = total[:rows, :]
-    other[...] = total[rows:, :].astype(bf16)
-
-
-def mix(near, far, halves, after):
-    rows, model = near.shape[0] // 2, halves[0].shape[1]
-    return pl.pallas_call(
-        mix_kernel,
-        out_shape=[
-            jax.ShapeDtypeStruct((rows, model), f32),
-            jax.ShapeDtypeStruct((rows, model), bf16),
-        ],
-        in_specs=[vmem()] * 6 + [unread()] * len(after),
-        out_specs=[vmem()] * 2,
-        compiler_params=params(8),
+    weight = both_halves((mine, other), core)
+    own[...] = dot_nn(att_ref[:rows, :], weight)
+    for block, out in enumerate(outs):
+        out[...] = dot_nn(att_ref[(block + 1) * rows:(block + 2) * rows, :], weight).astype(bf16)
+
+
+def partials(cycle, attended, halves):
+    rows, model = attended.shape[0] // cycle, halves[0].shape[1]
+    return pl.pallas_call(
+        partial_kernel,
+        out_shape=[jax.ShapeDtypeStruct((rows, model), f32)]
+        + [jax.ShapeDtypeStruct((rows, model), bf16)] * (cycle - 1),
+        in_specs=[vmem()] * 3,
+        out_specs=[vmem()] * cycle,
+        compiler_params=params(12),
         cost_estimate=cost(1),
-        name="mix",
-    )(near, far, *halves, *after)
+        name="partials",
+    )(attended, *halves)
 
 
 def grad_kernel(cycle, up_ref, *refs):
@@ -484,9 +475,11 @@
     mixed, *outs = refs[-5:-1]
     copies = place_columns(chunks, outs, refs[-1])
     rows = mixed.shape[0]
-    if len(refs) == cycle + 7:
-        mine, landed = refs[cycle:cycle + 2]
-        mixed[...] = (mine[...] + landed[...].astype(f32)).astype(bf16)
+    if len(refs) == 2 * cycle + 5:
+        total = refs[cycle][...]
+        for landed in refs[cycle + 1:2 * cycle]:
+            total = total + landed[...].astype(f32)
+        mixed[...] = total.astype(bf16)
     else:
         halves = refs[cycle:3 * cycle]
         _, _, core = my_place()
@@ -536,21 +529,18 @@
     next_x, next_y = exchange(upstream, "seq", 1), exchange(upstream, "seq", 2)
     chunks = swapped(list(pack(cycle, range(cycle), tensors)))
     (held_weight,) = hold((out_weight,), [next_x, next_y])
-    first = fetch_rows(held_weight, 0)
-    own_rows = with_other_core(first)
+    own_rows = with_other_core(fetch_rows(held_weight, 0))
     q_all, k_all, v_all, k_t, v_t, bias, word = gather(cycle, chunks)
     (held_y,) = hold((next_y,), [word])
     across = exchange(held_y, "seq", 1)
-    (near_att, far_att), att_t, lse = forward(cycle, 2, q_all, k_all, v_t, bias)
-    far_att = exchange(far_att, "seq", 2)
-    grads = [group_grads((upstream, next_x, next_y, across), own_rows, [lse])]
+    (attended,), att_t, lse = forward(cycle, cycle, q_all, k_all, v_t, bias)
+    mixed = list(partials(cycle, attended, own_rows))
+    grads = [group_grads((upstream, next_x, next_y, across), own_rows, mixed[:1])]
     inputs = (q_all, k_all, v_all, k_t, bias, att_t, lse)
-    terms = backward(cycle, inputs, grads, [], [])
-    (held_weight,) = hold((out_weight,), [first])
-    second = with_other_core(fetch_rows(held_weight, 2))
-    own_mixed, next_mixed = mix(near_att, far_att, own_rows + second, [terms[0]])
-    next_mixed = exchange(next_mixed, "seq", 1)
-    return tuple(finish(cycle, rows, swapped(terms), [own_mixed, next_mixed]))
+    mixed = swapped(mixed)
+    terms = list(backward(cycle, inputs, grads, [], []))
+    (terms[3],) = hold((terms[3],), mixed[1:])
+    return tuple(finish(cycle, rows, swapped(terms), mixed))
 
 
 def solution(mesh):

time: 56.5 us -> 50.5 us (0.89)
  starting transfers between devices: 21.5 us -> 17.8 us
  waiting for transfers between devices: 22.2 us -> 19.9 us
    ppermute x2 -> x1, starting transfers between devices: 5.17 us -> 0.68 us  [fetch_rows(): return lax.ppermute(out_weight, ('seq', 'mp'), pairs)]
    ppermute x2 -> x1, waiting for transfers between devices: 1.49 us -> 0.01 us  [fetch_rows(): return lax.ppermute(out_weight, ('seq', 'mp'), pairs)]
    ppermute x13, starting transfers between devices: 16.3 us -> 17.2 us  [exchange(): return lax.ppermute(value, axis, [(i, i ^ distance) for i in range(count)])]
    ppermute x13, waiting for transfers between devices: 20.8 us -> 19.9 us  [exchange(): return lax.ppermute(value, axis, [(i, i ^ distance) for i in range(count)])]
  transfers between devices with their start and end apart: 15 -> 14, of which waited for: 7 -> 7; matrix products, arithmetic and copies ran while one was open for 0% -> 0% of each run, Pallas kernels for 16% -> 19%
where the time goes in v9:
time: 50.5 us; the launch traced here: 50.3 us
  waiting for transfers between devices  19.9 us (39%)
  starting transfers between devices  17.8 us (35%)
  Pallas kernels  11.2 us (22%)
  between operations  1.4 us (3%)
    ppermute x13, waiting for transfers between devices, exchange(): return lax.ppermute(value, axis, [(i, i ^ distance) for i in range(count)])  19.9 us
    ppermute x13, starting transfers between devices, exchange(): return lax.ppermute(value, axis, [(i, i ^ distance) for i in range(count)])  17.2 us
    pallas_call x1, Pallas kernels, backward(): pl.pallas_call(functools.partial(backward_kernel, cycle, min(tokens, 512)...  3.06 us
    pallas_call x1, Pallas kernels, forward(): pl.pallas_call(functools.partial(forward_kernel, min(tokens, 512), parts)...  2.4 us
    pallas_call x1, Pallas kernels, pack(): pl.pallas_call(functools.partial(pack_kernel, cycle, places), out_shape=[...  2.24 us
    pallas_call x1, Pallas kernels, finish(): pl.pallas_call(functools.partial(finish_kernel, cycle), out_shape=[jax.Sh...  1.69 us
  transfers between devices with their start and end apart: 14, of which 7 were waited for; matrix products, arithmetic and copies ran while one was open for 0% of the time, Pallas kernels for 19%

profile of v9, /device:TPU:0, one launch (start us, length us, event | category | flops | bytes accessed | tf_op | source)
XLA Modules:
  0.0 50.3 jit_solution(9528033977977465438)
XLA Ops:
  0.6 3.0 %collective-permute-start.3 = (bf16[128,1024]{1,0:T(8,128)(2,1)}, bf16[128,1024]{1,0:T(8,128)(2,1)S(1)}, u32[]{:S(2)}, u32[]{:S(2)}) collective-permute-start(bf16[128,1024]{1,0:T(8,128)(2,1)} %refs_0_.3), channel_id=1, source_target_pairs={{0,8},{8,0},{16,24},{24,16},{1,9},{9,1},{17,25},{25,17},{2,10},{10... | collective-permute-start | bytes 786440 | tf_op jit(solution)/shard_map/ppermute | solution.py:52
  3.6 1.5 %collective-permute-start.4 = (bf16[128,1024]{1,0:T(8,128)(2,1)}, bf16[128,1024]{1,0:T(8,128)(2,1)S(1)}, u32[]{:S(2)}, u32[]{:S(2)}) collective-permute-start(bf16[128,1024]{1,0:T(8,128)(2,1)} %refs_0_.3), channel_id=1, source_target_pairs={{0,16},{8,24},{16,0},{24,8},{1,17},{9,25},{17,1},{25,9},{2,18},{10... | collective-permute-start | bytes 786440 | tf_op jit(solution)/shard_map/ppermute | solution.py:52
  5.8 2.2 %pack.1 = (bf16[416,256]{1,0:T(8,128)(2,1)}, bf16[416,256]{1,0:T(8,128)(2,1)}, bf16[416,256]{1,0:T(8,128)(2,1)}, bf16[416,256]{1,0:T(8,128)(2,1)}) custom-call(bf16[128,1024]{1,0:T(8,128)(2,1)} %q_ref.1, bf16[128,1024]{1,0:T(8,128)(2,1)} %k_ref.1, bf16[128,1024]{1,0:T(8,128)(2,1)} %v_ref.1, s32[1,4]{1,0:T(1,128)} %adj_any.1, s32[1,1]{1,0:T(1,128)} %bitcast.1.cnt_any), custom_call_target="tpu_custom_call" | custom-call | flops 5000000000 | tf_op jit(solution)/shard_map/pack/pallas_call | solution.py:157
  8.1 0.6 %collective-permute-start = (bf16[416,256]{1,0:T(8,128)(2,1)}, bf16[416,256]{1,0:T(8,128)(2,1)S(1)}, u32[]{:S(2)}, u32[]{:S(2)}) collective-permute-start(bf16[416,256]{1,0:T(8,128)(2,1)} %get-tuple-element.27), channel_id=1, source_target_pairs={{0,8},{8,0},{16,24},{24,16},{1,9},{9,1},{17,25},{25,17},{2,10},{10... | collective-permute-start | bytes 638984 | tf_op jit(solution)/shard_map/ppermute | solution.py:52
  8.7 2.9 %collective-permute-start.2 = (bf16[416,256]{1,0:T(8,128)(2,1)}, bf16[416,256]{1,0:T(8,128)(2,1)S(1)}, u32[]{:S(2)}, u32[]{:S(2)}) collective-permute-start(bf16[416,256]{1,0:T(8,128)(2,1)} %get-tuple-element.29), channel_id=1, source_target_pairs={{0,24},{8,16},{16,8},{24,0},{1,25},{9,17},{17,9},{25,1},{2,26},{10... | collective-permute-start | bytes 638984 | tf_op jit(solution)/shard_map/ppermute | solution.py:52
  11.6 1.1 %collective-permute-done.4.refs_0_.refs_2_ = bf16[128,1024]{1,0:T(8,128)(2,1)S(1)} collective-permute-done((bf16[128,1024]{1,0:T(8,128)(2,1)}, bf16[128,1024]{1,0:T(8,128)(2,1)S(1)}, u32[]{:S(2)}, u32[]{:S(2)}) %collective-permute-start.4) | collective-permute-done | bytes 262176 | tf_op jit(solution)/shard_map/ppermute | solution.py:52
  12.7 0.7 %collective-permute-start.6 = (bf16[128,1024]{1,0:T(8,128)(2,1)S(1)}, bf16[128,1024]{1,0:T(8,128)(2,1)S(1)}, u32[]{:S(2)}, u32[]{:S(2)}) collective-permute-start(bf16[128,1024]{1,0:T(8,128)(2,1)S(1)} %hold.4), channel_id=1, source_target_pairs={{0,0},{1,1},{4,2},{5,3},{2,4},{3,5},{6,6},{7,7},{12,8},{13,9},{10,... | collective-permute-start | bytes 786440 | tf_op jit(solution)/shard_map/ppermute | solution.py:357
  13.4 3.1 %collective-permute-done.refs_1_ = bf16[416,256]{1,0:T(8,128)(2,1)S(1)} collective-permute-done((bf16[416,256]{1,0:T(8,128)(2,1)}, bf16[416,256]{1,0:T(8,128)(2,1)S(1)}, u32[]{:S(2)}, u32[]{:S(2)}) %collective-permute-start) | collective-permute-done | bytes 213024 | tf_op jit(solution)/shard_map/ppermute | solution.py:52
  16.5 4.2 %collective-permute-done.1.refs_2_ = bf16[416,256]{1,0:T(8,128)(2,1)S(1)} collective-permute-done((bf16[416,256]{1,0:T(8,128)(2,1)}, bf16[416,256]{1,0:T(8,128)(2,1)S(1)}, u32[]{:S(2)}, u32[]{:S(2)}) %collective-permute-start.1) | collective-permute-done | bytes 213024 | tf_op jit(solution)/shard_map/ppermute | solution.py:52
  21.1 1.3 %collective-permute-start.5 = (bf16[128,1024]{1,0:T(8,128)(2,1)S(1)}, bf16[128,1024]{1,0:T(8,128)(2,1)S(1)}, u32[]{:S(2)}, u32[]{:S(2)}) collective-permute-start(bf16[128,1024]{1,0:T(8,128)(2,1)S(1)} %hold.3), channel_id=1, source_target_pairs={{0,8},{8,0},{16,24},{24,16},{1,9},{9,1},{17,25},{25,17},{2,10},{10... | collective-permute-start | bytes 786440 | tf_op jit(solution)/shard_map/ppermute | solution.py:52
  22.4 2.4 %forward.1 = (bf16[512,256]{1,0:T(8,128)(2,1)S(1)}, f32[256,512]{1,0:T(8,128)S(1)}, f32[8,512]{1,0:T(8,128)S(1)}) custom-call(bf16[512,256]{1,0:T(8,128)(2,1)S(1)} %get-tuple-element.30.q_all.refs_0_, bf16[512,256]{1,0:T(8,128)(2,1)S(1)} %get-tuple-element.31.k_all.refs_1_, bf16[256,512]{1,0:T(8,128)(2,1)S(1)} %get-tuple-element.35.v_t, ...), custom_call_target="tpu_custom_call" | custom-call | flops 3000000000 | tf_op jit(solution)/shard_map/forward/pallas_call | solution.py:260
  24.8 0.5 partials.1
  25.3 0.9 %collective-permute-start.10 = (bf16[128,1024]{1,0:T(8,128)(2,1)S(1)}, bf16[128,1024]{1,0:T(8,128)(2,1)S(1)}, u32[]{:S(2)}, u32[]{:S(2)}) collective-permute-start(bf16[128,1024]{1,0:T(8,128)(2,1)S(1)} %get-tuple-element.45), channel_id=1, source_target_pairs={{0,8},{8,0},{16,24},{24,16},{1,9},{9,1},{17,25},{25,17},{2,10},{10... | collective-permute-start | bytes 786440 | tf_op jit(solution)/shard_map/ppermute | solution.py:52
  26.2 1.7 %collective-permute-start.11 = (bf16[128,1024]{1,0:T(8,128)(2,1)S(1)}, bf16[128,1024]{1,0:T(8,128)(2,1)S(1)}, u32[]{:S(2)}, u32[]{:S(2)}) collective-permute-start(bf16[128,1024]{1,0:T(8,128)(2,1)S(1)} %get-tuple-element.46), channel_id=1, source_target_pairs={{0,16},{8,24},{16,0},{24,8},{1,17},{9,25},{17,1},{25,9},{2,18},{10... | collective-permute-start | bytes 786440 | tf_op jit(solution)/shard_map/ppermute | solution.py:52
  27.9 1.0 %collective-permute-start.12 = (bf16[128,1024]{1,0:T(8,128)(2,1)S(1)}, bf16[128,1024]{1,0:T(8,128)(2,1)S(1)}, u32[]{:S(2)}, u32[]{:S(2)}) collective-permute-start(bf16[128,1024]{1,0:T(8,128)(2,1)S(1)} %get-tuple-element.47), channel_id=1, source_target_pairs={{0,24},{8,16},{16,8},{24,0},{1,25},{9,17},{17,9},{25,1},{2,26},{10... | collective-permute-start | bytes 786440 | tf_op jit(solution)/shard_map/ppermute | solution.py:52
  28.8 0.7 %group_grads.1.refs_7_ = bf16[512,256]{1,0:T(8,128)(2,1)S(1)} custom-call(bf16[128,1024]{1,0:T(8,128)(2,1)S(1)} %copy-done.1, bf16[128,1024]{1,0:T(8,128)(2,1)S(1)} %collective-permute-done.3.refs_1_, bf16[128,1024]{1,0:T(8,128)(2,1)S(1)} %collective-permute-done.4.refs_0_.refs_2_, bf16[128,1024]{1,0:T(8,128)(2,1)S(1)} %collective-permute-done.5.refs_3_, ...), custom_call_target="tpu_custom_call" | custom-call | flops 1000000000 | tf_op jit(solution)/shard_map/group_grads/pallas_call | solution.py:390
  29.6 3.1 %backward.1 = (bf16[384,256]{1,0:T(8,128)(2,1)S(1)}, bf16[384,256]{1,0:T(8,128)(2,1)S(1)}, bf16[384,256]{1,0:T(8,128)(2,1)S(1)}, bf16[384,256]{1,0:T(8,128)(2,1)S(1)}) custom-call(bf16[512,256]{1,0:T(8,128)(2,1)S(1)} %get-tuple-element.30.q_all.refs_0_, bf16[512,256]{1,0:T(8,128)(2,1)S(1)} %get-tuple-element.31.k_all.refs_1_, ...), custom_call_target="tpu_custom_call" | custom-call | flops 3000000000 | tf_op jit(solution)/shard_map/backward/pallas_call | solution.py:333
  32.6 1.0 %collective-permute-start.8 = (bf16[384,256]{1,0:T(8,128)(2,1)S(1)}, bf16[384,256]{1,0:T(8,128)(2,1)S(1)}, u32[]{:S(2)}, u32[]{:S(2)}) collective-permute-start(bf16[384,256]{1,0:T(8,128)(2,1)S(1)} %get-tuple-element.42), channel_id=1, source_target_pairs={{0,8},{8,0},{16,24},{24,16},{1,9},{9,1},{17,25},{25,17},{2,10},{10... | collective-permute-start | bytes 589832 | tf_op jit(solution)/shard_map/ppermute | solution.py:52
  33.6 1.6 %collective-permute-start.9 = (bf16[384,256]{1,0:T(8,128)(2,1)S(1)}, bf16[384,256]{1,0:T(8,128)(2,1)S(1)}, u32[]{:S(2)}, u32[]{:S(2)}) collective-permute-start(bf16[384,256]{1,0:T(8,128)(2,1)S(1)} %get-tuple-element.43), channel_id=1, source_target_pairs={{0,16},{8,24},{16,0},{24,8},{1,17},{9,25},{17,1},{25,9},{2,18},{10... | collective-permute-start | bytes 589832 | tf_op jit(solution)/shard_map/ppermute | solution.py:52
  35.2 5.0 %collective-permute-done.11.refs_2_.refs_6_ = bf16[128,1024]{1,0:T(8,128)(2,1)S(1)} collective-permute-done((bf16[128,1024]{1,0:T(8,128)(2,1)S(1)}, bf16[128,1024]{1,0:T(8,128)(2,1)S(1)}, u32[]{:S(2)}, u32[]{:S(2)}) %collective-permute-start.11) | collective-permute-done | bytes 262176 | tf_op jit(solution)/shard_map/ppermute | solution.py:52
  40.6 1.7 %collective-permute-start.13 = (bf16[384,256]{1,0:T(8,128)(2,1)S(1)}, bf16[384,256]{1,0:T(8,128)(2,1)S(1)}, u32[]{:S(2)}, u32[]{:S(2)}) collective-permute-start(bf16[384,256]{1,0:T(8,128)(2,1)S(1)} %hold.5), channel_id=1, source_target_pairs={{0,24},{8,16},{16,8},{24,0},{1,25},{9,17},{17,9},{25,1},{2,26},{10... | collective-permute-start | bytes 589832 | tf_op jit(solution)/shard_map/ppermute | solution.py:52
  42.3 2.1 %collective-permute-done.8.refs_1_ = bf16[384,256]{1,0:T(8,128)(2,1)S(1)} collective-permute-done((bf16[384,256]{1,0:T(8,128)(2,1)S(1)}, bf16[384,256]{1,0:T(8,128)(2,1)S(1)}, u32[]{:S(2)}, u32[]{:S(2)}) %collective-permute-start.8) | collective-permute-done | bytes 196640 | tf_op jit(solution)/shard_map/ppermute | solution.py:52
  44.3 4.3 %collective-permute-done.9.refs_2_ = bf16[384,256]{1,0:T(8,128)(2,1)S(1)} collective-permute-done((bf16[384,256]{1,0:T(8,128)(2,1)S(1)}, bf16[384,256]{1,0:T(8,128)(2,1)S(1)}, u32[]{:S(2)}, u32[]{:S(2)}) %collective-permute-start.9) | collective-permute-done | bytes 196640 | tf_op jit(solution)/shard_map/ppermute | solution.py:52
  48.6 1.7 %finish.1 = (bf16[128,1024]{1,0:T(8,128)(2,1)}, bf16[128,1024]{1,0:T(8,128)(2,1)}, bf16[128,1024]{1,0:T(8,128)(2,1)}, bf16[128,1024]{1,0:T(8,128)(2,1)}) custom-call(bf16[384,256]{1,0:T(8,128)(2,1)S(1)} %get-tuple-element.41.refs_0_, bf16[384,256]{1,0:T(8,128)(2,1)S(1)} %collective-permute-done.8.refs_1_, ...), custom_call_target="tpu_custom_call" | custom-call | tf_op jit(solution)/shard_map/finish/pallas_call | solution.py:499
  (20 shorter events, 0.8 us)
Async XLA Ops:
  0.6 11.0 %collective-permute-start.3 = (bf16[128,1024]{1,0:T(8,128)(2,1)}, bf16[128,1024]{1,0:T(8,128)(2,1)S(1)}, u32[]{:S(2)}, u32[]{:S(2)}) collective-permute-start(bf16[128,1024]{1,0:T(8,128)(2,1)} %refs_0_.3), channel_id=1, source_target_pairs={{0,8},{8,0},{16,24},{24,16},{1,9},{9,1},{17,25},{25,17},{2,10},{10... | collective-permute-start | bytes 786440 | tf_op jit(solution)/shard_map/ppermute | solution.py:52
  3.6 9.1 %collective-permute-start.4 = (bf16[128,1024]{1,0:T(8,128)(2,1)}, bf16[128,1024]{1,0:T(8,128)(2,1)S(1)}, u32[]{:S(2)}, u32[]{:S(2)}) collective-permute-start(bf16[128,1024]{1,0:T(8,128)(2,1)} %refs_0_.3), channel_id=1, source_target_pairs={{0,16},{8,24},{16,0},{24,8},{1,17},{9,25},{17,1},{25,9},{2,18},{10... | collective-permute-start | bytes 786440 | tf_op jit(solution)/shard_map/ppermute | solution.py:52
  5.8 6.9 %copy-start = (bf16[128,1024]{1,0:T(8,128)(2,1)S(1)}, bf16[128,1024]{1,0:T(8,128)(2,1)}, u32[]{:S(2)}) copy-start(bf16[128,1024]{1,0:T(8,128)(2,1)} %refs_0_.2) | copy-start | bytes 786436
  8.1 8.5 %collective-permute-start = (bf16[416,256]{1,0:T(8,128)(2,1)}, bf16[416,256]{1,0:T(8,128)(2,1)S(1)}, u32[]{:S(2)}, u32[]{:S(2)}) collective-permute-start(bf16[416,256]{1,0:T(8,128)(2,1)} %get-tuple-element.27), channel_id=1, source_target_pairs={{0,8},{8,0},{16,24},{24,16},{1,9},{9,1},{17,25},{25,17},{2,10},{10... | collective-permute-start | bytes 638984 | tf_op jit(solution)/shard_map/ppermute | solution.py:52
  8.7 12.1 %collective-permute-start.1 = (bf16[416,256]{1,0:T(8,128)(2,1)}, bf16[416,256]{1,0:T(8,128)(2,1)S(1)}, u32[]{:S(2)}, u32[]{:S(2)}) collective-permute-start(bf16[416,256]{1,0:T(8,128)(2,1)} %get-tuple-element.28), channel_id=1, source_target_pairs={{0,16},{8,24},{16,0},{24,8},{1,17},{9,25},{17,1},{25,9},{2,18},{10... | collective-permute-start | bytes 638984 | tf_op jit(solution)/shard_map/ppermute | solution.py:52
  8.7 12.0 %copy-start.2 = (bf16[416,256]{1,0:T(8,128)(2,1)S(1)}, bf16[416,256]{1,0:T(8,128)(2,1)}, u32[]{:S(2)}) copy-start(bf16[416,256]{1,0:T(8,128)(2,1)} %get-tuple-element.26.refs_0_) | copy-start | bytes 638980
  8.7 12.0 %collective-permute-start.2 = (bf16[416,256]{1,0:T(8,128)(2,1)}, bf16[416,256]{1,0:T(8,128)(2,1)S(1)}, u32[]{:S(2)}, u32[]{:S(2)}) collective-permute-start(bf16[416,256]{1,0:T(8,128)(2,1)} %get-tuple-element.29), channel_id=1, source_target_pairs={{0,24},{8,16},{16,8},{24,0},{1,25},{9,17},{17,9},{25,1},{2,26},{10... | collective-permute-start | bytes 638984 | tf_op jit(solution)/shard_map/ppermute | solution.py:52
  12.7 9.6 %collective-permute-start.6 = (bf16[128,1024]{1,0:T(8,128)(2,1)S(1)}, bf16[128,1024]{1,0:T(8,128)(2,1)S(1)}, u32[]{:S(2)}, u32[]{:S(2)}) collective-permute-start(bf16[128,1024]{1,0:T(8,128)(2,1)S(1)} %hold.4), channel_id=1, source_target_pairs={{0,0},{1,1},{4,2},{5,3},{2,4},{3,5},{6,6},{7,7},{12,8},{13,9},{10,... | collective-permute-start | bytes 786440 | tf_op jit(solution)/shard_map/ppermute | solution.py:357
  21.1 7.8 %collective-permute-start.5 = (bf16[128,1024]{1,0:T(8,128)(2,1)S(1)}, bf16[128,1024]{1,0:T(8,128)(2,1)S(1)}, u32[]{:S(2)}, u32[]{:S(2)}) collective-permute-start(bf16[128,1024]{1,0:T(8,128)(2,1)S(1)} %hold.3), channel_id=1, source_target_pairs={{0,8},{8,0},{16,24},{24,16},{1,9},{9,1},{17,25},{25,17},{2,10},{10... | collective-permute-start | bytes 786440 | tf_op jit(solution)/shard_map/ppermute | solution.py:52
  22.4 2.4 %collective-permute-start.7 = (bf16[128,1024]{1,0:T(8,128)(2,1)S(1)}, bf16[128,1024]{1,0:T(8,128)(2,1)S(1)}, u32[]{:S(2)}, u32[]{:S(2)}) collective-permute-start(bf16[128,1024]{1,0:T(8,128)(2,1)S(1)} %collective-permute-done.6.mine.refs_4_), channel_id=1, source_target_pairs={{0,1},{1,0},{2,3},{3,2},{4,5},{5,4},{6,7},{7,6},{8,9},{9,8},{10,11... | collective-permute-start | bytes 786440 | tf_op jit(solution)/shard_map/ppermute | solution.py:52
  24.8 4.0 %copy-start.1 = (bf16[128,1024]{1,0:T(8,128)(2,1)S(1)}, bf16[128,1024]{1,0:T(8,128)(2,1)}, u32[]{:S(2)}) copy-start(bf16[128,1024]{1,0:T(8,128)(2,1)} %refs_0_.3) | copy-start | bytes 786436
  25.3 9.9 %collective-permute-start.10 = (bf16[128,1024]{1,0:T(8,128)(2,1)S(1)}, bf16[128,1024]{1,0:T(8,128)(2,1)S(1)}, u32[]{:S(2)}, u32[]{:S(2)}) collective-permute-start(bf16[128,1024]{1,0:T(8,128)(2,1)S(1)} %get-tuple-element.45), channel_id=1, source_target_pairs={{0,8},{8,0},{16,24},{24,16},{1,9},{9,1},{17,25},{25,17},{2,10},{10... | collective-permute-start | bytes 786440 | tf_op jit(solution)/shard_map/ppermute | solution.py:52
  26.2 14.1 %collective-permute-start.11 = (bf16[128,1024]{1,0:T(8,128)(2,1)S(1)}, bf16[128,1024]{1,0:T(8,128)(2,1)S(1)}, u32[]{:S(2)}, u32[]{:S(2)}) collective-permute-start(bf16[128,1024]{1,0:T(8,128)(2,1)S(1)} %get-tuple-element.46), channel_id=1, source_target_pairs={{0,16},{8,24},{16,0},{24,8},{1,17},{9,25},{17,1},{25,9},{2,18},{10... | collective-permute-start | bytes 786440 | tf_op jit(solution)/shard_map/ppermute | solution.py:52
  27.9 12.5 %collective-permute-start.12 = (bf16[128,1024]{1,0:T(8,128)(2,1)S(1)}, bf16[128,1024]{1,0:T(8,128)(2,1)S(1)}, u32[]{:S(2)}, u32[]{:S(2)}) collective-permute-start(bf16[128,1024]{1,0:T(8,128)(2,1)S(1)} %get-tuple-element.47), channel_id=1, source_target_pairs={{0,24},{8,16},{16,8},{24,0},{1,25},{9,17},{17,9},{25,1},{2,26},{10... | collective-permute-start | bytes 786440 | tf_op jit(solution)/shard_map/ppermute | solution.py:52
  32.6 11.7 %collective-permute-start.8 = (bf16[384,256]{1,0:T(8,128)(2,1)S(1)}, bf16[384,256]{1,0:T(8,128)(2,1)S(1)}, u32[]{:S(2)}, u32[]{:S(2)}) collective-permute-start(bf16[384,256]{1,0:T(8,128)(2,1)S(1)} %get-tuple-element.42), channel_id=1, source_target_pairs={{0,8},{8,0},{16,24},{24,16},{1,9},{9,1},{17,25},{25,17},{2,10},{10... | collective-permute-start | bytes 589832 | tf_op jit(solution)/shard_map/ppermute | solution.py:52
  33.6 15.0 %collective-permute-start.9 = (bf16[384,256]{1,0:T(8,128)(2,1)S(1)}, bf16[384,256]{1,0:T(8,128)(2,1)S(1)}, u32[]{:S(2)}, u32[]{:S(2)}) collective-permute-start(bf16[384,256]{1,0:T(8,128)(2,1)S(1)} %get-tuple-element.43), channel_id=1, source_target_pairs={{0,16},{8,24},{16,0},{24,8},{1,17},{9,25},{17,1},{25,9},{2,18},{10... | collective-permute-start | bytes 589832 | tf_op jit(solution)/shard_map/ppermute | solution.py:52
  40.6 8.0 %collective-permute-start.13 = (bf16[384,256]{1,0:T(8,128)(2,1)S(1)}, bf16[384,256]{1,0:T(8,128)(2,1)S(1)}, u32[]{:S(2)}, u32[]{:S(2)}) collective-permute-start(bf16[384,256]{1,0:T(8,128)(2,1)S(1)} %hold.5), channel_id=1, source_target_pairs={{0,24},{8,16},{16,8},{24,0},{1,25},{9,17},{17,9},{25,1},{2,26},{10... | collective-permute-start | bytes 589832 | tf_op jit(solution)/shard_map/ppermute | solution.py:52

commit v10 on v9

--- a/solution.py
+++ b/solution.py
@@ -54,6 +54,16 @@
 
 def turned(distance):
     return distance ^ (((distance ^ (distance >> 1)) & 1) * 3)
+
+
+def exchange_by_core(value, distances):
+    count = lax.axis_size("mp")
+    pairs = [
+        (member * count + rank, (member ^ distances[rank % 2]) * count + rank)
+        for member in range(lax.axis_size("seq"))
+        for rank in range(count)
+    ]
+    return lax.ppermute(value, ("seq", "mp"), pairs)
 
 
 def is_square():
@@ -398,27 +408,71 @@
     )(*upstreams, *halves, *after)
 
 
-def partial_kernel(att_ref, mine, other, own, *outs):
+def partial_kernel(att_ref, mine, other, own, kept, sent):
     rows = own.shape[0]
     _, _, core = my_place()
     weight = both_halves((mine, other), core)
-    own[...] = dot_nn(att_ref[:rows, :], weight)
-    for block, out in enumerate(outs):
-        out[...] = dot_nn(att_ref[(block + 1) * rows:(block + 2) * rows, :], weight).astype(bf16)
-
-
-def partials(cycle, attended, halves):
-    rows, model = attended.shape[0] // cycle, halves[0].shape[1]
+
+    def product(block):
+        return dot_nn(att_ref[pl.ds(pl.multiple_of(block * rows, rows), rows), :], weight)
+
+    own[...] = product(0)
+    kept[...] = product(1 + core)
+    sent[:rows, :] = product(2 - core).astype(bf16)
+    sent[rows:, :] = product(3).astype(bf16)
+
+
+def partials(attended, halves):
+    rows, model = attended.shape[0] // 4, halves[0].shape[1]
     return pl.pallas_call(
         partial_kernel,
-        out_shape=[jax.ShapeDtypeStruct((rows, model), f32)]
-        + [jax.ShapeDtypeStruct((rows, model), bf16)] * (cycle - 1),
+        out_shape=[jax.ShapeDtypeStruct((rows, model), f32)] * 2
+        + [jax.ShapeDtypeStruct((2 * rows, model), bf16)],
         in_specs=[vmem()] * 3,
-        out_specs=[vmem()] * cycle,
+        out_specs=[vmem()] * 3,
         compiler_params=params(12),
         cost_estimate=cost(1),
         name="partials",
     )(attended, *halves)
+
+
+def combine_kernel(own, kept, landed, total, sent):
+    rows = own.shape[0]
+    total[...] = own[...] + landed[:rows, :].astype(f32)
+    sent[...] = (kept[...] + landed[rows:, :].astype(f32)).astype(bf16)
+
+
+def combine(own, kept, landed):
+    return pl.pallas_call(
+        combine_kernel,
+        out_shape=[jax.ShapeDtypeStruct(own.shape, f32), jax.ShapeDtypeStruct(own.shape, bf16)],
+        in_specs=[vmem()] * 3,
+        out_specs=[vmem()] * 2,
+        compiler_params=params(8),
+        cost_estimate=cost(1),
+        name="combine",
+    )(own, kept, landed)
+
+
+def turn_kernel(w_ref, next_x, next_y, weight, passed, sem):
+    copy = pltpu.make_async_copy(w_ref, weight, sem)
+    copy.start()
+    _, _, core = my_place()
+    passed[...] = jnp.where(core == 0, next_y[...], next_x[...])
+    copy.wait()
+
+
+def turn(out_weight, next_x, next_y):
+    return pl.pallas_call(
+        turn_kernel,
+        out_shape=[jax.ShapeDtypeStruct(array.shape, bf16) for array in (out_weight, next_y)],
+        in_specs=[unread()] + [vmem()] * 2,
+        out_specs=[vmem()] * 2,
+        scratch_shapes=[pltpu.SemaphoreType.DMA],
+        compiler_params=params(4),
+        cost_estimate=cost(1),
+        name="turn",
+    )(out_weight, next_x, next_y)
 
 
 def grad_kernel(cycle, up_ref, *refs):
@@ -475,11 +529,8 @@
     mixed, *outs = refs[-5:-1]
     copies = place_columns(chunks, outs, refs[-1])
     rows = mixed.shape[0]
-    if len(refs) == 2 * cycle + 5:
-        total = refs[cycle][...]
-        for landed in refs[cycle + 1:2 * cycle]:
-            total = total + landed[...].astype(f32)
-        mixed[...] = total.astype(bf16)
+    if len(refs) == cycle + 7:
+        mixed[...] = (refs[cycle][...] + refs[cycle + 1][...].astype(f32)).astype(bf16)
     else:
         halves = refs[cycle:3 * cycle]
         _, _, core = my_place()
@@ -528,19 +579,20 @@
 def square(cycle, rows, tensors, out_weight, upstream):
     next_x, next_y = exchange(upstream, "seq", 1), exchange(upstream, "seq", 2)
     chunks = swapped(list(pack(cycle, range(cycle), tensors)))
-    (held_weight,) = hold((out_weight,), [next_x, next_y])
+    held_weight, passed = turn(out_weight, next_x, next_y)
+    across = exchange_by_core(passed, (1, 2))
     own_rows = with_other_core(fetch_rows(held_weight, 0))
     q_all, k_all, v_all, k_t, v_t, bias, word = gather(cycle, chunks)
-    (held_y,) = hold((next_y,), [word])
-    across = exchange(held_y, "seq", 1)
-    (attended,), att_t, lse = forward(cycle, cycle, q_all, k_all, v_t, bias)
-    mixed = list(partials(cycle, attended, own_rows))
-    grads = [group_grads((upstream, next_x, next_y, across), own_rows, mixed[:1])]
+    (attended,), att_t, lse = forward(cycle, cycle, q_all, k_all, v_t, bias, [across])
+    own_mixed, kept, sent = partials(attended, own_rows)
+    landed = exchange_by_core(sent, (2, 1))
+    grads = [group_grads((upstream, next_x, next_y, across), own_rows, [kept])]
     inputs = (q_all, k_all, v_all, k_t, bias, att_t, lse)
-    mixed = swapped(mixed)
     terms = list(backward(cycle, inputs, grads, [], []))
-    (terms[3],) = hold((terms[3],), mixed[1:])
-    return tuple(finish(cycle, rows, swapped(terms), mixed))
+    own_mixed, next_mixed = combine(own_mixed, kept, landed)
+    (terms[3],) = hold((terms[3],), [own_mixed])
+    next_mixed = exchange_by_core(next_mixed, (1, 2))
+    return tuple(finish(cycle, rows, swapped(terms), [own_mixed, next_mixed]))
 
 
 def solution(mesh):

time: 50.5 us -> 49.8 us (0.986)
  waiting for transfers between devices: 19.9 us -> 18.1 us
  Pallas kernels: 11.2 us -> 11.8 us
  starting transfers between devices: 17.8 us -> 18.4 us
    ppermute x0 -> x3, starting transfers between devices: none -> 4.99 us  [exchange_by_core(): return lax.ppermute(value, ('seq', 'mp'), pairs)]
    ppermute x13 -> x9, starting transfers between devices: 17.2 us -> 12.7 us  [exchange(): return lax.ppermute(value, axis, [(i, i ^ distance) for i in range(count)])]
    ppermute x13 -> x9, waiting for transfers between devices: 19.9 us -> 17.3 us  [exchange(): return lax.ppermute(value, axis, [(i, i ^ distance) for i in range(count)])]
    ppermute x0 -> x3, waiting for transfers between devices: none -> 0.73 us  [exchange_by_core(): return lax.ppermute(value, ('seq', 'mp'), pairs)]
    pallas_call x1, Pallas kernels: 0.28 us -> 0.88 us  [gather(): pl.pallas_call(functools.partial(gather_kernel, cycle), out_shape=[jax.Sh...]
  transfers between devices with their start and end apart: 14 -> 13, of which waited for: 7 -> 5; matrix products, arithmetic and copies ran while one was open for 0% -> 0% of each run, Pallas kernels for 19% -> 19%
where the time goes in v10:
time: 49.8 us; the launch traced here: 49.6 us
  starting transfers between devices  18.4 us (37%)
  waiting for transfers between devices  18.1 us (36%)
  Pallas kernels  11.8 us (24%)
  between operations  1.39 us (3%)
    ppermute x9, waiting for transfers between devices, exchange(): return lax.ppermute(value, axis, [(i, i ^ distance) for i in range(count)])  17.3 us
    ppermute x9, starting transfers between devices, exchange(): return lax.ppermute(value, axis, [(i, i ^ distance) for i in range(count)])  12.7 us
    ppermute x3, starting transfers between devices, exchange_by_core(): return lax.ppermute(value, ('seq', 'mp'), pairs)  4.99 us
    pallas_call x1, Pallas kernels, backward(): pl.pallas_call(functools.partial(backward_kernel, cycle, min(tokens, 512)...  3.06 us
    pallas_call x1, Pallas kernels, forward(): pl.pallas_call(functools.partial(forward_kernel, min(tokens, 512), parts)...  2.41 us
    pallas_call x1, Pallas kernels, pack(): pl.pallas_call(functools.partial(pack_kernel, cycle, places), out_shape=[...  2.24 us
    pallas_call x1, Pallas kernels, finish(): pl.pallas_call(functools.partial(finish_kernel, cycle), out_shape=[jax.Sh...  1.69 us
  transfers between devices with their start and end apart: 13, of which 5 were waited for; matrix products, arithmetic and copies ran while one was open for 0% of the time, Pallas kernels for 19%

profile of v10, /device:TPU:0, one launch (start us, length us, event | category | flops | bytes accessed | tf_op | source)
XLA Modules:
  0.0 49.6 jit_solution(3630173301671505889)
XLA Ops:
  0.6 3.0 %collective-permute-start.3 = (bf16[128,1024]{1,0:T(8,128)(2,1)}, bf16[128,1024]{1,0:T(8,128)(2,1)S(1)}, u32[]{:S(2)}, u32[]{:S(2)}) collective-permute-start(bf16[128,1024]{1,0:T(8,128)(2,1)} %refs_0_.1), channel_id=1, source_target_pairs={{0,8},{8,0},{16,24},{24,16},{1,9},{9,1},{17,25},{25,17},{2,10},{10... | collective-permute-start | bytes 786440 | tf_op jit(solution)/shard_map/ppermute | solution.py:52
  3.6 1.5 %collective-permute-start.4 = (bf16[128,1024]{1,0:T(8,128)(2,1)}, bf16[128,1024]{1,0:T(8,128)(2,1)S(1)}, u32[]{:S(2)}, u32[]{:S(2)}) collective-permute-start(bf16[128,1024]{1,0:T(8,128)(2,1)} %refs_0_.1), channel_id=1, source_target_pairs={{0,16},{8,24},{16,0},{24,8},{1,17},{9,25},{17,1},{25,9},{2,18},{10... | collective-permute-start | bytes 786440 | tf_op jit(solution)/shard_map/ppermute | solution.py:52
  5.8 2.2 %pack.1 = (bf16[416,256]{1,0:T(8,128)(2,1)}, bf16[416,256]{1,0:T(8,128)(2,1)}, bf16[416,256]{1,0:T(8,128)(2,1)}, bf16[416,256]{1,0:T(8,128)(2,1)}) custom-call(bf16[128,1024]{1,0:T(8,128)(2,1)} %q_ref.1, bf16[128,1024]{1,0:T(8,128)(2,1)} %k_ref.1, bf16[128,1024]{1,0:T(8,128)(2,1)} %v_ref.1, s32[1,4]{1,0:T(1,128)} %adj_any.1, s32[1,1]{1,0:T(1,128)} %bitcast.1.cnt_any), custom_call_target="tpu_custom_call" | custom-call | flops 5000000000 | tf_op jit(solution)/shard_map/pack/pallas_call | solution.py:167
  8.1 0.6 %collective-permute-start = (bf16[416,256]{1,0:T(8,128)(2,1)}, bf16[416,256]{1,0:T(8,128)(2,1)S(1)}, u32[]{:S(2)}, u32[]{:S(2)}) collective-permute-start(bf16[416,256]{1,0:T(8,128)(2,1)} %get-tuple-element.29), channel_id=1, source_target_pairs={{0,8},{8,0},{16,24},{24,16},{1,9},{9,1},{17,25},{25,17},{2,10},{10... | collective-permute-start | bytes 638984 | tf_op jit(solution)/shard_map/ppermute | solution.py:52
  8.7 2.9 %collective-permute-start.2 = (bf16[416,256]{1,0:T(8,128)(2,1)}, bf16[416,256]{1,0:T(8,128)(2,1)S(1)}, u32[]{:S(2)}, u32[]{:S(2)}) collective-permute-start(bf16[416,256]{1,0:T(8,128)(2,1)} %get-tuple-element.31), channel_id=1, source_target_pairs={{0,24},{8,16},{16,8},{24,0},{1,25},{9,17},{17,9},{25,1},{2,26},{10... | collective-permute-start | bytes 638984 | tf_op jit(solution)/shard_map/ppermute | solution.py:52
  11.6 1.1 %collective-permute-done.4.next_y.refs_2_ = bf16[128,1024]{1,0:T(8,128)(2,1)S(1)} collective-permute-done((bf16[128,1024]{1,0:T(8,128)(2,1)}, bf16[128,1024]{1,0:T(8,128)(2,1)S(1)}, u32[]{:S(2)}, u32[]{:S(2)}) %collective-permute-start.4) | collective-permute-done | bytes 262176 | tf_op jit(solution)/shard_map/ppermute | solution.py:52
  12.8 0.3 collective-permute-start.5
  13.1 0.7 %collective-permute-start.6 = (bf16[128,1024]{1,0:T(8,128)(2,1)S(1)}, bf16[128,1024]{1,0:T(8,128)(2,1)S(1)}, u32[]{:S(2)}, u32[]{:S(2)}) collective-permute-start(bf16[128,1024]{1,0:T(8,128)(2,1)S(1)} %get-tuple-element.41), channel_id=1, source_target_pairs={{0,0},{1,1},{4,2},{5,3},{2,4},{3,5},{6,6},{7,7},{12,8},{13,9},{10,... | collective-permute-start | bytes 786440 | tf_op jit(solution)/shard_map/ppermute | solution.py:367
  13.8 2.8 %collective-permute-done.refs_1_ = bf16[416,256]{1,0:T(8,128)(2,1)S(1)} collective-permute-done((bf16[416,256]{1,0:T(8,128)(2,1)}, bf16[416,256]{1,0:T(8,128)(2,1)S(1)}, u32[]{:S(2)}, u32[]{:S(2)}) %collective-permute-start) | collective-permute-done | bytes 213024 | tf_op jit(solution)/shard_map/ppermute | solution.py:52
  16.5 5.3 %collective-permute-done.1.refs_2_ = bf16[416,256]{1,0:T(8,128)(2,1)S(1)} collective-permute-done((bf16[416,256]{1,0:T(8,128)(2,1)}, bf16[416,256]{1,0:T(8,128)(2,1)S(1)}, u32[]{:S(2)}, u32[]{:S(2)}) %collective-permute-start.1) | collective-permute-done | bytes 213024 | tf_op jit(solution)/shard_map/ppermute | solution.py:52
  21.8 0.9 %gather.1 = (bf16[512,256]{1,0:T(8,128)(2,1)S(1)}, bf16[512,256]{1,0:T(8,128)(2,1)S(1)}, bf16[512,256]{1,0:T(8,128)(2,1)S(1)}, bf16[256,512]{1,0:T(8,128)(2,1)S(...) custom-call(bf16[416,256]{1,0:T(8,128)(2,1)S(1)} %copy-done.2, ...), custom_call_target="tpu_custom_call" | custom-call | flops 5000000000 | tf_op jit(solution)/shard_map/gather/pallas_call | solution.py:214
  22.7 2.4 %forward.1 = (bf16[512,256]{1,0:T(8,128)(2,1)S(1)}, f32[256,512]{1,0:T(8,128)S(1)}, f32[8,512]{1,0:T(8,128)S(1)}) custom-call(bf16[512,256]{1,0:T(8,128)(2,1)S(1)} %get-tuple-element.32.q_all.refs_0_, bf16[512,256]{1,0:T(8,128)(2,1)S(1)} %get-tuple-element.33.k_all.refs_1_, bf16[256,512]{1,0:T(8,128)(2,1)S(1)} %get-tuple-element.37.v_t, ...), custom_call_target="tpu_custom_call" | custom-call | flops 3000000000 | tf_op jit(solution)/shard_map/forward/pallas_call | solution.py:270
  25.2 0.5 partials.1
  25.6 2.0 %collective-permute-start.10 = (bf16[256,1024]{1,0:T(8,128)(2,1)S(1)}, bf16[256,1024]{1,0:T(8,128)(2,1)S(1)}, u32[]{:S(2)}, u32[]{:S(2)}) collective-permute-start(bf16[256,1024]{1,0:T(8,128)(2,1)S(1)} %get-tuple-element.49), channel_id=1, source_target_pairs={{0,16},{1,9},{2,18},{3,11},{4,20},{5,13},{6,22},{7,15},{8,24},{9,1... | collective-permute-start | bytes 1572872 | tf_op jit(solution)/shard_map/ppermute | solution.py:66
  27.6 0.7 %group_grads.1.refs_7_ = bf16[512,256]{1,0:T(8,128)(2,1)S(1)} custom-call(bf16[128,1024]{1,0:T(8,128)(2,1)S(1)} %copy-done.1, bf16[128,1024]{1,0:T(8,128)(2,1)S(1)} %collective-permute-done.3.next_x.refs_1_, bf16[128,1024]{1,0:T(8,128)(2,1)S(1)} %collective-permute-done.4.next_y.refs_2_, bf16[128,1024]{1,0:T(8,128)(2,1)S(1)} %collective-permute-done.5.refs_0_.refs_3_, ...), custom_call_target="tpu_custom_call" | custom-call | flops 1000000000 | tf_op jit(solution)/shard_map/group_grads/pallas_call | solution.py:400
  28.3 3.1 %backward.1 = (bf16[384,256]{1,0:T(8,128)(2,1)S(1)}, bf16[384,256]{1,0:T(8,128)(2,1)S(1)}, bf16[384,256]{1,0:T(8,128)(2,1)S(1)}, bf16[384,256]{1,0:T(8,128)(2,1)S(1)}) custom-call(bf16[512,256]{1,0:T(8,128)(2,1)S(1)} %get-tuple-element.32.q_all.refs_0_, bf16[512,256]{1,0:T(8,128)(2,1)S(1)} %get-tuple-element.33.k_all.refs_1_, ...), custom_call_target="tpu_custom_call" | custom-call | flops 3000000000 | tf_op jit(solution)/shard_map/backward/pallas_call | solution.py:343
  31.4 2.4 %collective-permute-start.8 = (bf16[384,256]{1,0:T(8,128)(2,1)S(1)}, bf16[384,256]{1,0:T(8,128)(2,1)S(1)}, u32[]{:S(2)}, u32[]{:S(2)}) collective-permute-start(bf16[384,256]{1,0:T(8,128)(2,1)S(1)} %get-tuple-element.45), channel_id=1, source_target_pairs={{0,8},{8,0},{16,24},{24,16},{1,9},{9,1},{17,25},{25,17},{2,10},{10... | collective-permute-start | bytes 589832 | tf_op jit(solution)/shard_map/ppermute | solution.py:52
  33.7 0.4 collective-permute-start.9
  34.2 0.7 %collective-permute-done.10.landed = bf16[256,1024]{1,0:T(8,128)(2,1)S(1)} collective-permute-done((bf16[256,1024]{1,0:T(8,128)(2,1)S(1)}, bf16[256,1024]{1,0:T(8,128)(2,1)S(1)}, u32[]{:S(2)}, u32[]{:S(2)}) %collective-permute-start.10) | collective-permute-done | bytes 524320 | tf_op jit(solution)/shard_map/ppermute | solution.py:66
  35.0 2.7 %collective-permute-start.12 = (bf16[128,1024]{1,0:T(8,128)(2,1)S(1)}, bf16[128,1024]{1,0:T(8,128)(2,1)S(1)}, u32[]{:S(2)}, u32[]{:S(2)}) collective-permute-start(bf16[128,1024]{1,0:T(8,128)(2,1)S(1)} %get-tuple-element.51), channel_id=1, source_target_pairs={{0,8},{1,17},{2,10},{3,19},{4,12},{5,21},{6,14},{7,23},{8,0},{9,25... | collective-permute-start | bytes 786440 | tf_op jit(solution)/shard_map/ppermute | solution.py:66
  37.7 0.2 hold.1
  37.9 1.8 %collective-permute-start.11 = (bf16[384,256]{1,0:T(8,128)(2,1)S(1)}, bf16[384,256]{1,0:T(8,128)(2,1)S(1)}, u32[]{:S(2)}, u32[]{:S(2)}) collective-permute-start(bf16[384,256]{1,0:T(8,128)(2,1)S(1)} %hold.1), channel_id=1, source_target_pairs={{0,24},{8,16},{16,8},{24,0},{1,25},{9,17},{17,9},{25,1},{2,26},{10... | collective-permute-start | bytes 589832 | tf_op jit(solution)/shard_map/ppermute | solution.py:52
  39.7 8.2 %collective-permute-done.11.refs_3_ = bf16[384,256]{1,0:T(8,128)(2,1)S(1)} collective-permute-done((bf16[384,256]{1,0:T(8,128)(2,1)S(1)}, bf16[384,256]{1,0:T(8,128)(2,1)S(1)}, u32[]{:S(2)}, u32[]{:S(2)}) %collective-permute-start.11) | collective-permute-done | bytes 196640 | tf_op jit(solution)/shard_map/ppermute | solution.py:52
  48.0 1.7 %finish.1 = (bf16[128,1024]{1,0:T(8,128)(2,1)}, bf16[128,1024]{1,0:T(8,128)(2,1)}, bf16[128,1024]{1,0:T(8,128)(2,1)}, bf16[128,1024]{1,0:T(8,128)(2,1)}) custom-call(bf16[384,256]{1,0:T(8,128)(2,1)S(1)} %get-tuple-element.44.refs_0_, bf16[384,256]{1,0:T(8,128)(2,1)S(1)} %collective-permute-done.8.refs_1_, ...), custom_call_target="tpu_custom_call" | custom-call | tf_op jit(solution)/shard_map/finish/pallas_call | solution.py:550
  (18 shorter events, 0.2 us)
Async XLA Ops:
  0.6 11.0 %collective-permute-start.3 = (bf16[128,1024]{1,0:T(8,128)(2,1)}, bf16[128,1024]{1,0:T(8,128)(2,1)S(1)}, u32[]{:S(2)}, u32[]{:S(2)}) collective-permute-start(bf16[128,1024]{1,0:T(8,128)(2,1)} %refs_0_.1), channel_id=1, source_target_pairs={{0,8},{8,0},{16,24},{24,16},{1,9},{9,1},{17,25},{25,17},{2,10},{10... | collective-permute-start | bytes 786440 | tf_op jit(solution)/shard_map/ppermute | solution.py:52
  3.6 9.1 %collective-permute-start.4 = (bf16[128,1024]{1,0:T(8,128)(2,1)}, bf16[128,1024]{1,0:T(8,128)(2,1)S(1)}, u32[]{:S(2)}, u32[]{:S(2)}) collective-permute-start(bf16[128,1024]{1,0:T(8,128)(2,1)} %refs_0_.1), channel_id=1, source_target_pairs={{0,16},{8,24},{16,0},{24,8},{1,17},{9,25},{17,1},{25,9},{2,18},{10... | collective-permute-start | bytes 786440 | tf_op jit(solution)/shard_map/ppermute | solution.py:52
  5.8 6.9 %copy-start = (bf16[128,1024]{1,0:T(8,128)(2,1)S(1)}, bf16[128,1024]{1,0:T(8,128)(2,1)}, u32[]{:S(2)}) copy-start(bf16[128,1024]{1,0:T(8,128)(2,1)} %w_ref.1) | copy-start | bytes 786436
  8.1 8.5 %collective-permute-start = (bf16[416,256]{1,0:T(8,128)(2,1)}, bf16[416,256]{1,0:T(8,128)(2,1)S(1)}, u32[]{:S(2)}, u32[]{:S(2)}) collective-permute-start(bf16[416,256]{1,0:T(8,128)(2,1)} %get-tuple-element.29), channel_id=1, source_target_pairs={{0,8},{8,0},{16,24},{24,16},{1,9},{9,1},{17,25},{25,17},{2,10},{10... | collective-permute-start | bytes 638984 | tf_op jit(solution)/shard_map/ppermute | solution.py:52
  8.7 13.2 %collective-permute-start.1 = (bf16[416,256]{1,0:T(8,128)(2,1)}, bf16[416,256]{1,0:T(8,128)(2,1)S(1)}, u32[]{:S(2)}, u32[]{:S(2)}) collective-permute-start(bf16[416,256]{1,0:T(8,128)(2,1)} %get-tuple-element.30), channel_id=1, source_target_pairs={{0,16},{8,24},{16,0},{24,8},{1,17},{9,25},{17,1},{25,9},{2,18},{10... | collective-permute-start | bytes 638984 | tf_op jit(solution)/shard_map/ppermute | solution.py:52
  8.7 13.1 %copy-start.2 = (bf16[416,256]{1,0:T(8,128)(2,1)S(1)}, bf16[416,256]{1,0:T(8,128)(2,1)}, u32[]{:S(2)}) copy-start(bf16[416,256]{1,0:T(8,128)(2,1)} %get-tuple-element.28.refs_0_) | copy-start | bytes 638980
  8.7 13.1 %collective-permute-start.2 = (bf16[416,256]{1,0:T(8,128)(2,1)}, bf16[416,256]{1,0:T(8,128)(2,1)S(1)}, u32[]{:S(2)}, u32[]{:S(2)}) collective-permute-start(bf16[416,256]{1,0:T(8,128)(2,1)} %get-tuple-element.31), channel_id=1, source_target_pairs={{0,24},{8,16},{16,8},{24,0},{1,25},{9,17},{17,9},{25,1},{2,26},{10... | collective-permute-start | bytes 638984 | tf_op jit(solution)/shard_map/ppermute | solution.py:52
  12.8 10.0 %collective-permute-start.5 = (bf16[128,1024]{1,0:T(8,128)(2,1)S(1)}, bf16[128,1024]{1,0:T(8,128)(2,1)S(1)}, u32[]{:S(2)}, u32[]{:S(2)}) collective-permute-start(bf16[128,1024]{1,0:T(8,128)(2,1)S(1)} %get-tuple-element.38), channel_id=1, source_target_pairs={{0,8},{1,17},{2,10},{3,19},{4,12},{5,21},{6,14},{7,23},{8,0},{9,25... | collective-permute-start | bytes 786440 | tf_op jit(solution)/shard_map/ppermute | solution.py:66
  13.1 9.6 %collective-permute-start.6 = (bf16[128,1024]{1,0:T(8,128)(2,1)S(1)}, bf16[128,1024]{1,0:T(8,128)(2,1)S(1)}, u32[]{:S(2)}, u32[]{:S(2)}) collective-permute-start(bf16[128,1024]{1,0:T(8,128)(2,1)S(1)} %get-tuple-element.41), channel_id=1, source_target_pairs={{0,0},{1,1},{4,2},{5,3},{2,4},{3,5},{6,6},{7,7},{12,8},{13,9},{10,... | collective-permute-start | bytes 786440 | tf_op jit(solution)/shard_map/ppermute | solution.py:367
  22.7 2.4 %collective-permute-start.7 = (bf16[128,1024]{1,0:T(8,128)(2,1)S(1)}, bf16[128,1024]{1,0:T(8,128)(2,1)S(1)}, u32[]{:S(2)}, u32[]{:S(2)}) collective-permute-start(bf16[128,1024]{1,0:T(8,128)(2,1)S(1)} %collective-permute-done.6.mine.refs_4_), channel_id=1, source_target_pairs={{0,1},{1,0},{2,3},{3,2},{4,5},{5,4},{6,7},{7,6},{8,9},{9,8},{10,11... | collective-permute-start | bytes 786440 | tf_op jit(solution)/shard_map/ppermute | solution.py:52
  25.1 2.5 %copy-start.1 = (bf16[128,1024]{1,0:T(8,128)(2,1)S(1)}, bf16[128,1024]{1,0:T(8,128)(2,1)}, u32[]{:S(2)}) copy-start(bf16[128,1024]{1,0:T(8,128)(2,1)} %refs_0_.1) | copy-start | bytes 786436
  25.6 9.2 %collective-permute-start.10 = (bf16[256,1024]{1,0:T(8,128)(2,1)S(1)}, bf16[256,1024]{1,0:T(8,128)(2,1)S(1)}, u32[]{:S(2)}, u32[]{:S(2)}) collective-permute-start(bf16[256,1024]{1,0:T(8,128)(2,1)S(1)} %get-tuple-element.49), channel_id=1, source_target_pairs={{0,16},{1,9},{2,18},{3,11},{4,20},{5,13},{6,22},{7,15},{8,24},{9,1... | collective-permute-start | bytes 1572872 | tf_op jit(solution)/shard_map/ppermute | solution.py:66
  31.4 8.4 %collective-permute-start.8 = (bf16[384,256]{1,0:T(8,128)(2,1)S(1)}, bf16[384,256]{1,0:T(8,128)(2,1)S(1)}, u32[]{:S(2)}, u32[]{:S(2)}) collective-permute-start(bf16[384,256]{1,0:T(8,128)(2,1)S(1)} %get-tuple-element.45), channel_id=1, source_target_pairs={{0,8},{8,0},{16,24},{24,16},{1,9},{9,1},{17,25},{25,17},{2,10},{10... | collective-permute-start | bytes 589832 | tf_op jit(solution)/shard_map/ppermute | solution.py:52
  33.7 6.0 %collective-permute-start.9 = (bf16[384,256]{1,0:T(8,128)(2,1)S(1)}, bf16[384,256]{1,0:T(8,128)(2,1)S(1)}, u32[]{:S(2)}, u32[]{:S(2)}) collective-permute-start(bf16[384,256]{1,0:T(8,128)(2,1)S(1)} %get-tuple-element.46), channel_id=1, source_target_pairs={{0,16},{8,24},{16,0},{24,8},{1,17},{9,25},{17,1},{25,9},{2,18},{10... | collective-permute-start | bytes 589832 | tf_op jit(solution)/shard_map/ppermute | solution.py:52
  35.0 13.0 %collective-permute-start.12 = (bf16[128,1024]{1,0:T(8,128)(2,1)S(1)}, bf16[128,1024]{1,0:T(8,128)(2,1)S(1)}, u32[]{:S(2)}, u32[]{:S(2)}) collective-permute-start(bf16[128,1024]{1,0:T(8,128)(2,1)S(1)} %get-tuple-element.51), channel_id=1, source_target_pairs={{0,8},{1,17},{2,10},{3,19},{4,12},{5,21},{6,14},{7,23},{8,0},{9,25... | collective-permute-start | bytes 786440 | tf_op jit(solution)/shard_map/ppermute | solution.py:66
  37.9 10.1 %collective-permute-start.11 = (bf16[384,256]{1,0:T(8,128)(2,1)S(1)}, bf16[384,256]{1,0:T(8,128)(2,1)S(1)}, u32[]{:S(2)}, u32[]{:S(2)}) collective-permute-start(bf16[384,256]{1,0:T(8,128)(2,1)S(1)} %hold.1), channel_id=1, source_target_pairs={{0,24},{8,16},{16,8},{24,0},{1,25},{9,17},{17,9},{25,1},{2,26},{10... | collective-permute-start | bytes 589832 | tf_op jit(solution)/shard_map/ppermute | solution.py:52

commit v11 on v10

--- a/solution.py
+++ b/solution.py
@@ -72,6 +72,10 @@
 
 def swapped(chunks):
     return [chunks[0]] + [exchange(chunks[k], "seq", k) for k in range(1, len(chunks))]
+
+
+def longest_first(chunks):
+    return [chunks[0]] + [chunks[len(chunks) - k] for k in range(1, len(chunks))]
 
 
 def group_of(cycle, member, chip):
@@ -183,9 +187,8 @@
 
 
 def gather_kernel(cycle, *refs):
-    chunks = refs[:cycle]
-    q_all, k_all, v_all, k_t, v_t, bias, word = refs[-7:]
-    word[...] = jnp.zeros(word.shape, word.dtype)
+    chunks = longest_first(refs[:cycle])
+    q_all, k_all, v_all, k_t, v_t, bias = refs[-6:]
     rows = q_all.shape[0] // cycle
     for place in range(cycle):
         for at, part in enumerate((q_all, k_all, v_all)):
@@ -215,13 +218,13 @@
         functools.partial(gather_kernel, cycle),
         out_shape=[jax.ShapeDtypeStruct((tokens, width), bf16)] * 3
         + [jax.ShapeDtypeStruct((width, tokens), bf16)] * 2
-        + [jax.ShapeDtypeStruct((tokens, tokens), f32), jax.ShapeDtypeStruct((16, 128), bf16)],
+        + [jax.ShapeDtypeStruct((tokens, tokens), f32)],
         in_specs=[vmem()] * cycle + [unread()] * len(after),
-        out_specs=[vmem()] * 7,
+        out_specs=[vmem()] * 6,
         compiler_params=params(8 if tokens <= 512 else 40),
         cost_estimate=cost(5),
         name="gather",
-    )(*chunks, *after)
+    )(*longest_first(chunks), *after)
 
 
 def head_tile(width):
@@ -408,7 +411,8 @@
     )(*upstreams, *halves, *after)
 
 
-def partial_kernel(att_ref, mine, other, own, kept, sent):
+def partial_kernel(att_ref, mine, other, *refs):
+    own, kept, sent = refs[-3:]
     rows = own.shape[0]
     _, _, core = my_place()
     weight = both_halves((mine, other), core)
@@ -422,32 +426,38 @@
     sent[rows:, :] = product(3).astype(bf16)
 
 
-def partials(attended, halves):
+def partials(attended, halves, after):
     rows, model = attended.shape[0] // 4, halves[0].shape[1]
     return pl.pallas_call(
         partial_kernel,
         out_shape=[jax.ShapeDtypeStruct((rows, model), f32)] * 2
         + [jax.ShapeDtypeStruct((2 * rows, model), bf16)],
-        in_specs=[vmem()] * 3,
+        in_specs=[vmem()] * 3 + [unread()] * len(after),
         out_specs=[vmem()] * 3,
         compiler_params=params(12),
         cost_estimate=cost(1),
         name="partials",
-    )(attended, *halves)
-
-
-def combine_kernel(own, kept, landed, total, sent):
+    )(attended, *halves, *after)
+
+
+def combine_kernel(own, kept, landed, total, *sent):
     rows = own.shape[0]
     total[...] = own[...] + landed[:rows, :].astype(f32)
-    sent[...] = (kept[...] + landed[rows:, :].astype(f32)).astype(bf16)
+    part = rows // len(sent)
+    for at, out in enumerate(sent):
+        span = slice(at * part, (at + 1) * part)
+        out[...] = (
+            kept[span, :] + landed[rows + at * part:rows + (at + 1) * part, :].astype(f32)
+        ).astype(bf16)
 
 
 def combine(own, kept, landed):
     return pl.pallas_call(
         combine_kernel,
-        out_shape=[jax.ShapeDtypeStruct(own.shape, f32), jax.ShapeDtypeStruct(own.shape, bf16)],
+        out_shape=[jax.ShapeDtypeStruct(own.shape, f32)]
+        + [jax.ShapeDtypeStruct((own.shape[0] // 2, own.shape[1]), bf16)] * 2,
         in_specs=[vmem()] * 3,
-        out_specs=[vmem()] * 2,
+        out_specs=[vmem()] * 3,
         compiler_params=params(8),
         cost_estimate=cost(1),
         name="combine",
@@ -525,12 +535,16 @@
 
 
 def finish_kernel(cycle, *refs):
-    chunks = refs[:cycle]
+    chunks = longest_first(refs[:cycle])
     mixed, *outs = refs[-5:-1]
     copies = place_columns(chunks, outs, refs[-1])
     rows = mixed.shape[0]
-    if len(refs) == cycle + 7:
-        mixed[...] = (refs[cycle][...] + refs[cycle + 1][...].astype(f32)).astype(bf16)
+    if len(refs) == cycle + 8:
+        for at in range(2):
+            span = slice(at * rows // 2, (at + 1) * rows // 2)
+            mixed[span, :] = (
+                refs[cycle][span, :] + refs[cycle + 1 + at][...].astype(f32)
+            ).astype(bf16)
     else:
         halves = refs[cycle:3 * cycle]
         _, _, core = my_place()
@@ -555,7 +569,7 @@
         scratch_shapes=[pltpu.SemaphoreType.DMA((cycle, 3))],
         compiler_params=params(8),
         name="finish",
-    )(*chunks, *others)
+    )(*longest_first(chunks), *others)
 
 
 def local(queries, keys, values, out_weight, upstream, adjacency, counts):
@@ -568,7 +582,7 @@
     halves = []
     for place in range(cycle):
         halves += with_other_core(fetch_rows(out_weight, place))
-    q_all, k_all, v_all, k_t, v_t, bias, _ = gather(cycle, chunks)
+    q_all, k_all, v_all, k_t, v_t, bias = gather(cycle, chunks)
     attended, att_t, lse = forward(cycle, 1, q_all, k_all, v_t, bias)
     grads = swapped(project_grad(cycle, upstream, halves))
     inputs = (q_all, k_all, v_all, k_t, bias, att_t, lse)
@@ -582,17 +596,16 @@
     held_weight, passed = turn(out_weight, next_x, next_y)
     across = exchange_by_core(passed, (1, 2))
     own_rows = with_other_core(fetch_rows(held_weight, 0))
-    q_all, k_all, v_all, k_t, v_t, bias, word = gather(cycle, chunks)
+    q_all, k_all, v_all, k_t, v_t, bias = gather(cycle, chunks)
     (attended,), att_t, lse = forward(cycle, cycle, q_all, k_all, v_t, bias, [across])
-    own_mixed, kept, sent = partials(attended, own_rows)
+    own_mixed, kept, sent = partials(attended, own_rows, [])
     landed = exchange_by_core(sent, (2, 1))
     grads = [group_grads((upstream, next_x, next_y, across), own_rows, [kept])]
     inputs = (q_all, k_all, v_all, k_t, bias, att_t, lse)
     terms = list(backward(cycle, inputs, grads, [], []))
-    own_mixed, next_mixed = combine(own_mixed, kept, landed)
-    (terms[3],) = hold((terms[3],), [own_mixed])
-    next_mixed = exchange_by_core(next_mixed, (1, 2))
-    return tuple(finish(cycle, rows, swapped(terms), [own_mixed, next_mixed]))
+    own_mixed, *next_mixed = combine(own_mixed, kept, landed)
+    next_mixed = [exchange_by_core(part, (1, 2)) for part in next_mixed]
+    return tuple(finish(cycle, rows, swapped(terms), [own_mixed] + next_mixed))
 
 
 def solution(mesh):

time: 49.8 us -> 53.1 us (1.066)
  starting transfers between devices: 18.4 us -> 24.5 us
  waiting for transfers between devices: 18.1 us -> 16 us
  Pallas kernels: 11.8 us -> 11 us
    ppermute x3 -> x4, starting transfers between devices: 4.99 us -> 10.4 us  [exchange_by_core(): return lax.ppermute(value, ('seq', 'mp'), pairs)]
    ppermute x9, waiting for transfers between devices: 17.3 us -> 12.1 us  [exchange(): return lax.ppermute(value, axis, [(i, i ^ distance) for i in range(count)])]
    ppermute x3 -> x4, waiting for transfers between devices: 0.73 us -> 3.92 us  [exchange_by_core(): return lax.ppermute(value, ('seq', 'mp'), pairs)]
    ppermute x9, starting transfers between devices: 12.7 us -> 13.5 us  [exchange(): return lax.ppermute(value, axis, [(i, i ^ distance) for i in range(count)])]
    pallas_call x1, Pallas kernels: 0.88 us -> 0.28 us  [gather(): pl.pallas_call(functools.partial(gather_kernel, cycle), out_shape=[jax.Sh...]
  transfers between devices with their start and end apart: 13 -> 14, of which waited for: 5 -> 6; matrix products, arithmetic and copies ran while one was open for 0% -> 0% of each run, Pallas kernels for 19% -> 17%
where the time goes in v11:
time: 53.1 us; the launch traced here: 52.9 us
  starting transfers between devices  24.5 us (46%)
  waiting for transfers between devices  16 us (30%)
  Pallas kernels  11 us (21%)
  between operations  1.42 us (3%)
    ppermute x9, starting transfers between devices, exchange(): return lax.ppermute(value, axis, [(i, i ^ distance) for i in range(count)])  13.5 us
    ppermute x9, waiting for transfers between devices, exchange(): return lax.ppermute(value, axis, [(i, i ^ distance) for i in range(count)])  12.1 us
    ppermute x4, starting transfers between devices, exchange_by_core(): return lax.ppermute(value, ('seq', 'mp'), pairs)  10.4 us
    ppermute x4, waiting for transfers between devices, exchange_by_core(): return lax.ppermute(value, ('seq', 'mp'), pairs)  3.92 us
    pallas_call x1, Pallas kernels, backward(): pl.pallas_call(functools.partial(backward_kernel, cycle, min(tokens, 512)...  3.06 us
    pallas_call x1, Pallas kernels, forward(): pl.pallas_call(functools.partial(forward_kernel, min(tokens, 512), parts)...  2.4 us
    pallas_call x1, Pallas kernels, pack(): pl.pallas_call(functools.partial(pack_kernel, cycle, places), out_shape=[...  2.24 us
    pallas_call x1, Pallas kernels, finish(): pl.pallas_call(functools.partial(finish_kernel, cycle), out_shape=[jax.Sh...  1.69 us
  transfers between devices with their start and end apart: 14, of which 6 were waited for; matrix products, arithmetic and copies ran while one was open for 0% of the time, Pallas kernels for 17%

profile of v11, /device:TPU:0, one launch (start us, length us, event | category | flops | bytes accessed | tf_op | source)
XLA Modules:
  0.0 52.9 jit_solution(15396223894980036166)
XLA Ops:
  0.6 3.0 %collective-permute-start.3 = (bf16[128,1024]{1,0:T(8,128)(2,1)}, bf16[128,1024]{1,0:T(8,128)(2,1)S(1)}, u32[]{:S(2)}, u32[]{:S(2)}) collective-permute-start(bf16[128,1024]{1,0:T(8,128)(2,1)} %refs_0_.1), channel_id=1, source_target_pairs={{0,8},{8,0},{16,24},{24,16},{1,9},{9,1},{17,25},{25,17},{2,10},{10... | collective-permute-start | bytes 786440 | tf_op jit(solution)/shard_map/ppermute | solution.py:52
  3.6 1.5 %collective-permute-start.4 = (bf16[128,1024]{1,0:T(8,128)(2,1)}, bf16[128,1024]{1,0:T(8,128)(2,1)S(1)}, u32[]{:S(2)}, u32[]{:S(2)}) collective-permute-start(bf16[128,1024]{1,0:T(8,128)(2,1)} %refs_0_.1), channel_id=1, source_target_pairs={{0,16},{8,24},{16,0},{24,8},{1,17},{9,25},{17,1},{25,9},{2,18},{10... | collective-permute-start | bytes 786440 | tf_op jit(solution)/shard_map/ppermute | solution.py:52
  5.8 2.2 %pack.1 = (bf16[416,256]{1,0:T(8,128)(2,1)}, bf16[416,256]{1,0:T(8,128)(2,1)}, bf16[416,256]{1,0:T(8,128)(2,1)}, bf16[416,256]{1,0:T(8,128)(2,1)}) custom-call(bf16[128,1024]{1,0:T(8,128)(2,1)} %q_ref.1, bf16[128,1024]{1,0:T(8,128)(2,1)} %k_ref.1, bf16[128,1024]{1,0:T(8,128)(2,1)} %v_ref.1, s32[1,4]{1,0:T(1,128)} %adj_any.1, s32[1,1]{1,0:T(1,128)} %bitcast.1.cnt_any), custom_call_target="tpu_custom_call" | custom-call | flops 5000000000 | tf_op jit(solution)/shard_map/pack/pallas_call | solution.py:171
  8.1 0.1 collective-permute-start
  8.2 2.0 %collective-permute-start.1 = (bf16[416,256]{1,0:T(8,128)(2,1)}, bf16[416,256]{1,0:T(8,128)(2,1)S(1)}, u32[]{:S(2)}, u32[]{:S(2)}) collective-permute-start(bf16[416,256]{1,0:T(8,128)(2,1)} %get-tuple-element.31), channel_id=1, source_target_pairs={{0,16},{8,24},{16,0},{24,8},{1,17},{9,25},{17,1},{25,9},{2,18},{10... | collective-permute-start | bytes 638984 | tf_op jit(solution)/shard_map/ppermute | solution.py:52
  10.1 1.5 %collective-permute-start.2 = (bf16[416,256]{1,0:T(8,128)(2,1)}, bf16[416,256]{1,0:T(8,128)(2,1)S(1)}, u32[]{:S(2)}, u32[]{:S(2)}) collective-permute-start(bf16[416,256]{1,0:T(8,128)(2,1)} %get-tuple-element.32), channel_id=1, source_target_pairs={{0,8},{8,0},{16,24},{24,16},{1,9},{9,1},{17,25},{25,17},{2,10},{10... | collective-permute-start | bytes 638984 | tf_op jit(solution)/shard_map/ppermute | solution.py:52
  11.6 5.8 %collective-permute-done.4.next_y.refs_2_ = bf16[128,1024]{1,0:T(8,128)(2,1)S(1)} collective-permute-done((bf16[128,1024]{1,0:T(8,128)(2,1)}, bf16[128,1024]{1,0:T(8,128)(2,1)S(1)}, u32[]{:S(2)}, u32[]{:S(2)}) %collective-permute-start.4) | collective-permute-done | bytes 262176 | tf_op jit(solution)/shard_map/ppermute | solution.py:52
  17.6 0.7 %collective-permute-start.6 = (bf16[128,1024]{1,0:T(8,128)(2,1)S(1)}, bf16[128,1024]{1,0:T(8,128)(2,1)S(1)}, u32[]{:S(2)}, u32[]{:S(2)}) collective-permute-start(bf16[128,1024]{1,0:T(8,128)(2,1)S(1)} %get-tuple-element.42), channel_id=1, source_target_pairs={{0,0},{1,1},{4,2},{5,3},{2,4},{3,5},{6,6},{7,7},{12,8},{13,9},{10,... | collective-permute-start | bytes 786440 | tf_op jit(solution)/shard_map/ppermute | solution.py:370
  18.3 3.7 %collective-permute-done.1.refs_2_ = bf16[416,256]{1,0:T(8,128)(2,1)S(1)} collective-permute-done((bf16[416,256]{1,0:T(8,128)(2,1)}, bf16[416,256]{1,0:T(8,128)(2,1)S(1)}, u32[]{:S(2)}, u32[]{:S(2)}) %collective-permute-start.1) | collective-permute-done | bytes 213024 | tf_op jit(solution)/shard_map/ppermute | solution.py:52
  22.0 0.3 gather.1
  22.4 1.6 %collective-permute-done.5.refs_0_.refs_3_ = bf16[128,1024]{1,0:T(8,128)(2,1)S(1)} collective-permute-done((bf16[128,1024]{1,0:T(8,128)(2,1)S(1)}, bf16[128,1024]{1,0:T(8,128)(2,1)S(1)}, u32[]{:S(2)}, u32[]{:S(2)}) %collective-permute-start.5) | collective-permute-done | bytes 262176 | tf_op jit(solution)/shard_map/ppermute | solution.py:66
  23.9 2.4 %forward.1 = (bf16[512,256]{1,0:T(8,128)(2,1)S(1)}, f32[256,512]{1,0:T(8,128)S(1)}, f32[8,512]{1,0:T(8,128)S(1)}) custom-call(bf16[512,256]{1,0:T(8,128)(2,1)S(1)} %get-tuple-element.33.q_all.refs_0_, bf16[512,256]{1,0:T(8,128)(2,1)S(1)} %get-tuple-element.34.k_all.refs_1_, bf16[256,512]{1,0:T(8,128)(2,1)S(1)} %get-tuple-element.38.v_t, ...), custom_call_target="tpu_custom_call" | custom-call | flops 3000000000 | tf_op jit(solution)/shard_map/forward/pallas_call | solution.py:273
  26.4 0.5 partials.1
  26.8 3.6 %collective-permute-start.11 = (bf16[256,1024]{1,0:T(8,128)(2,1)S(1)}, bf16[256,1024]{1,0:T(8,128)(2,1)S(1)}, u32[]{:S(2)}, u32[]{:S(2)}) collective-permute-start(bf16[256,1024]{1,0:T(8,128)(2,1)S(1)} %get-tuple-element.50), channel_id=1, source_target_pairs={{0,16},{1,9},{2,18},{3,11},{4,20},{5,13},{6,22},{7,15},{8,24},{9,1... | collective-permute-start | bytes 1572872 | tf_op jit(solution)/shard_map/ppermute | solution.py:66
  30.5 0.7 %group_grads.1.refs_7_ = bf16[512,256]{1,0:T(8,128)(2,1)S(1)} custom-call(bf16[128,1024]{1,0:T(8,128)(2,1)S(1)} %copy-done.1, bf16[128,1024]{1,0:T(8,128)(2,1)S(1)} %collective-permute-done.3.next_x.refs_1_, bf16[128,1024]{1,0:T(8,128)(2,1)S(1)} %collective-permute-done.4.next_y.refs_2_, bf16[128,1024]{1,0:T(8,128)(2,1)S(1)} %collective-permute-done.5.refs_0_.refs_3_, ...), custom_call_target="tpu_custom_call" | custom-call | flops 1000000000 | tf_op jit(solution)/shard_map/group_grads/pallas_call | solution.py:403
  31.2 3.1 %backward.1 = (bf16[384,256]{1,0:T(8,128)(2,1)S(1)}, bf16[384,256]{1,0:T(8,128)(2,1)S(1)}, bf16[384,256]{1,0:T(8,128)(2,1)S(1)}, bf16[384,256]{1,0:T(8,128)(2,1)S(1)}) custom-call(bf16[512,256]{1,0:T(8,128)(2,1)S(1)} %get-tuple-element.33.q_all.refs_0_, bf16[512,256]{1,0:T(8,128)(2,1)S(1)} %get-tuple-element.34.k_all.refs_1_, ...), custom_call_target="tpu_custom_call" | custom-call | flops 3000000000 | tf_op jit(solution)/shard_map/backward/pallas_call | solution.py:346
  34.2 3.7 %collective-permute-start.8 = (bf16[384,256]{1,0:T(8,128)(2,1)S(1)}, bf16[384,256]{1,0:T(8,128)(2,1)S(1)}, u32[]{:S(2)}, u32[]{:S(2)}) collective-permute-start(bf16[384,256]{1,0:T(8,128)(2,1)S(1)} %get-tuple-element.46), channel_id=1, source_target_pairs={{0,24},{8,16},{16,8},{24,0},{1,25},{9,17},{17,9},{25,1},{2,26},{10... | collective-permute-start | bytes 589832 | tf_op jit(solution)/shard_map/ppermute | solution.py:52
  37.9 1.6 %collective-permute-start.9 = (bf16[384,256]{1,0:T(8,128)(2,1)S(1)}, bf16[384,256]{1,0:T(8,128)(2,1)S(1)}, u32[]{:S(2)}, u32[]{:S(2)}) collective-permute-start(bf16[384,256]{1,0:T(8,128)(2,1)S(1)} %get-tuple-element.47), channel_id=1, source_target_pairs={{0,16},{8,24},{16,0},{24,8},{1,17},{9,25},{17,1},{25,9},{2,18},{10... | collective-permute-start | bytes 589832 | tf_op jit(solution)/shard_map/ppermute | solution.py:52
  39.6 0.1 combine.1
  39.6 6.6 %collective-permute-start.12 = (bf16[64,1024]{1,0:T(8,128)(2,1)S(1)}, bf16[64,1024]{1,0:T(8,128)(2,1)S(1)}, u32[]{:S(2)}, u32[]{:S(2)}) collective-permute-start(bf16[64,1024]{1,0:T(8,128)(2,1)S(1)} %get-tuple-element.52), channel_id=1, source_target_pairs={{0,8},{1,17},{2,10},{3,19},{4,12},{5,21},{6,14},{7,23},{8,0},{9,25... | collective-permute-start | bytes 393224 | tf_op jit(solution)/shard_map/ppermute | solution.py:66
  46.4 2.5 %collective-permute-done.9.refs_2_ = bf16[384,256]{1,0:T(8,128)(2,1)S(1)} collective-permute-done((bf16[384,256]{1,0:T(8,128)(2,1)S(1)}, bf16[384,256]{1,0:T(8,128)(2,1)S(1)}, u32[]{:S(2)}, u32[]{:S(2)}) %collective-permute-start.9) | collective-permute-done | bytes 196640 | tf_op jit(solution)/shard_map/ppermute | solution.py:52
  48.9 0.6 %collective-permute-done.12.refs_5_ = bf16[64,1024]{1,0:T(8,128)(2,1)S(1)} collective-permute-done((bf16[64,1024]{1,0:T(8,128)(2,1)S(1)}, bf16[64,1024]{1,0:T(8,128)(2,1)S(1)}, u32[]{:S(2)}, u32[]{:S(2)}) %collective-permute-start.12) | collective-permute-done | bytes 131104 | tf_op jit(solution)/shard_map/ppermute | solution.py:66
  49.5 1.7 %collective-permute-done.13.refs_6_ = bf16[64,1024]{1,0:T(8,128)(2,1)S(1)} collective-permute-done((bf16[64,1024]{1,0:T(8,128)(2,1)S(1)}, bf16[64,1024]{1,0:T(8,128)(2,1)S(1)}, u32[]{:S(2)}, u32[]{:S(2)}) %collective-permute-start.13) | collective-permute-done | bytes 131104 | tf_op jit(solution)/shard_map/ppermute | solution.py:66
  51.3 1.7 %finish.1 = (bf16[128,1024]{1,0:T(8,128)(2,1)}, bf16[128,1024]{1,0:T(8,128)(2,1)}, bf16[128,1024]{1,0:T(8,128)(2,1)}, bf16[128,1024]{1,0:T(8,128)(2,1)}) custom-call(bf16[384,256]{1,0:T(8,128)(2,1)S(1)} %get-tuple-element.45.refs_0_, bf16[384,256]{1,0:T(8,128)(2,1)S(1)} %collective-permute-done.8.refs_1_, ...), custom_call_target="tpu_custom_call" | custom-call | tf_op jit(solution)/shard_map/finish/pallas_call | solution.py:564
  (19 shorter events, 0.3 us)
Async XLA Ops:
  0.6 11.0 %collective-permute-start.3 = (bf16[128,1024]{1,0:T(8,128)(2,1)}, bf16[128,1024]{1,0:T(8,128)(2,1)S(1)}, u32[]{:S(2)}, u32[]{:S(2)}) collective-permute-start(bf16[128,1024]{1,0:T(8,128)(2,1)} %refs_0_.1), channel_id=1, source_target_pairs={{0,8},{8,0},{16,24},{24,16},{1,9},{9,1},{17,25},{25,17},{2,10},{10... | collective-permute-start | bytes 786440 | tf_op jit(solution)/shard_map/ppermute | solution.py:52
  3.6 13.8 %collective-permute-start.4 = (bf16[128,1024]{1,0:T(8,128)(2,1)}, bf16[128,1024]{1,0:T(8,128)(2,1)S(1)}, u32[]{:S(2)}, u32[]{:S(2)}) collective-permute-start(bf16[128,1024]{1,0:T(8,128)(2,1)} %refs_0_.1), channel_id=1, source_target_pairs={{0,16},{8,24},{16,0},{24,8},{1,17},{9,25},{17,1},{25,9},{2,18},{10... | collective-permute-start | bytes 786440 | tf_op jit(solution)/shard_map/ppermute | solution.py:52
  5.8 11.6 %copy-start = (bf16[128,1024]{1,0:T(8,128)(2,1)S(1)}, bf16[128,1024]{1,0:T(8,128)(2,1)}, u32[]{:S(2)}) copy-start(bf16[128,1024]{1,0:T(8,128)(2,1)} %w_ref.1) | copy-start | bytes 786436
  8.1 10.2 %collective-permute-start = (bf16[416,256]{1,0:T(8,128)(2,1)}, bf16[416,256]{1,0:T(8,128)(2,1)S(1)}, u32[]{:S(2)}, u32[]{:S(2)}) collective-permute-start(bf16[416,256]{1,0:T(8,128)(2,1)} %get-tuple-element.30), channel_id=1, source_target_pairs={{0,24},{8,16},{16,8},{24,0},{1,25},{9,17},{17,9},{25,1},{2,26},{10... | collective-permute-start | bytes 638984 | tf_op jit(solution)/shard_map/ppermute | solution.py:52
  8.2 13.8 %collective-permute-start.1 = (bf16[416,256]{1,0:T(8,128)(2,1)}, bf16[416,256]{1,0:T(8,128)(2,1)S(1)}, u32[]{:S(2)}, u32[]{:S(2)}) collective-permute-start(bf16[416,256]{1,0:T(8,128)(2,1)} %get-tuple-element.31), channel_id=1, source_target_pairs={{0,16},{8,24},{16,0},{24,8},{1,17},{9,25},{17,1},{25,9},{2,18},{10... | collective-permute-start | bytes 638984 | tf_op jit(solution)/shard_map/ppermute | solution.py:52
  10.1 11.9 %copy-start.2 = (bf16[416,256]{1,0:T(8,128)(2,1)S(1)}, bf16[416,256]{1,0:T(8,128)(2,1)}, u32[]{:S(2)}) copy-start(bf16[416,256]{1,0:T(8,128)(2,1)} %get-tuple-element.29.refs_0_) | copy-start | bytes 638980
  10.1 11.9 %collective-permute-start.2 = (bf16[416,256]{1,0:T(8,128)(2,1)}, bf16[416,256]{1,0:T(8,128)(2,1)S(1)}, u32[]{:S(2)}, u32[]{:S(2)}) collective-permute-start(bf16[416,256]{1,0:T(8,128)(2,1)} %get-tuple-element.32), channel_id=1, source_target_pairs={{0,8},{8,0},{16,24},{24,16},{1,9},{9,1},{17,25},{25,17},{2,10},{10... | collective-permute-start | bytes 638984 | tf_op jit(solution)/shard_map/ppermute | solution.py:52
  17.5 6.4 %collective-permute-start.5 = (bf16[128,1024]{1,0:T(8,128)(2,1)S(1)}, bf16[128,1024]{1,0:T(8,128)(2,1)S(1)}, u32[]{:S(2)}, u32[]{:S(2)}) collective-permute-start(bf16[128,1024]{1,0:T(8,128)(2,1)S(1)} %get-tuple-element.39), channel_id=1, source_target_pairs={{0,8},{1,17},{2,10},{3,19},{4,12},{5,21},{6,14},{7,23},{8,0},{9,25... | collective-permute-start | bytes 786440 | tf_op jit(solution)/shard_map/ppermute | solution.py:66
  17.6 4.7 %collective-permute-start.6 = (bf16[128,1024]{1,0:T(8,128)(2,1)S(1)}, bf16[128,1024]{1,0:T(8,128)(2,1)S(1)}, u32[]{:S(2)}, u32[]{:S(2)}) collective-permute-start(bf16[128,1024]{1,0:T(8,128)(2,1)S(1)} %get-tuple-element.42), channel_id=1, source_target_pairs={{0,0},{1,1},{4,2},{5,3},{2,4},{3,5},{6,6},{7,7},{12,8},{13,9},{10,... | collective-permute-start | bytes 786440 | tf_op jit(solution)/shard_map/ppermute | solution.py:370
  22.3 4.1 %collective-permute-start.7 = (bf16[128,1024]{1,0:T(8,128)(2,1)S(1)}, bf16[128,1024]{1,0:T(8,128)(2,1)S(1)}, u32[]{:S(2)}, u32[]{:S(2)}) collective-permute-start(bf16[128,1024]{1,0:T(8,128)(2,1)S(1)} %collective-permute-done.6.mine.refs_4_), channel_id=1, source_target_pairs={{0,1},{1,0},{2,3},{3,2},{4,5},{5,4},{6,7},{7,6},{8,9},{9,8},{10,11... | collective-permute-start | bytes 786440 | tf_op jit(solution)/shard_map/ppermute | solution.py:52
  26.4 4.1 %copy-start.1 = (bf16[128,1024]{1,0:T(8,128)(2,1)S(1)}, bf16[128,1024]{1,0:T(8,128)(2,1)}, u32[]{:S(2)}) copy-start(bf16[128,1024]{1,0:T(8,128)(2,1)} %refs_0_.1) | copy-start | bytes 786436
  26.8 12.7 %collective-permute-start.11 = (bf16[256,1024]{1,0:T(8,128)(2,1)S(1)}, bf16[256,1024]{1,0:T(8,128)(2,1)S(1)}, u32[]{:S(2)}, u32[]{:S(2)}) collective-permute-start(bf16[256,1024]{1,0:T(8,128)(2,1)S(1)} %get-tuple-element.50), channel_id=1, source_target_pairs={{0,16},{1,9},{2,18},{3,11},{4,20},{5,13},{6,22},{7,15},{8,24},{9,1... | collective-permute-start | bytes 1572872 | tf_op jit(solution)/shard_map/ppermute | solution.py:66
  34.2 12.1 %collective-permute-start.8 = (bf16[384,256]{1,0:T(8,128)(2,1)S(1)}, bf16[384,256]{1,0:T(8,128)(2,1)S(1)}, u32[]{:S(2)}, u32[]{:S(2)}) collective-permute-start(bf16[384,256]{1,0:T(8,128)(2,1)S(1)} %get-tuple-element.46), channel_id=1, source_target_pairs={{0,24},{8,16},{16,8},{24,0},{1,25},{9,17},{17,9},{25,1},{2,26},{10... | collective-permute-start | bytes 589832 | tf_op jit(solution)/shard_map/ppermute | solution.py:52
  37.9 11.0 %collective-permute-start.9 = (bf16[384,256]{1,0:T(8,128)(2,1)S(1)}, bf16[384,256]{1,0:T(8,128)(2,1)S(1)}, u32[]{:S(2)}, u32[]{:S(2)}) collective-permute-start(bf16[384,256]{1,0:T(8,128)(2,1)S(1)} %get-tuple-element.47), channel_id=1, source_target_pairs={{0,16},{8,24},{16,0},{24,8},{1,17},{9,25},{17,1},{25,9},{2,18},{10... | collective-permute-start | bytes 589832 | tf_op jit(solution)/shard_map/ppermute | solution.py:52
  39.5 9.3 %collective-permute-start.10 = (bf16[384,256]{1,0:T(8,128)(2,1)S(1)}, bf16[384,256]{1,0:T(8,128)(2,1)S(1)}, u32[]{:S(2)}, u32[]{:S(2)}) collective-permute-start(bf16[384,256]{1,0:T(8,128)(2,1)S(1)} %get-tuple-element.48), channel_id=1, source_target_pairs={{0,8},{8,0},{16,24},{24,16},{1,9},{9,1},{17,25},{25,17},{2,10},{10... | collective-permute-start | bytes 589832 | tf_op jit(solution)/shard_map/ppermute | solution.py:52
  39.6 9.9 %collective-permute-start.12 = (bf16[64,1024]{1,0:T(8,128)(2,1)S(1)}, bf16[64,1024]{1,0:T(8,128)(2,1)S(1)}, u32[]{:S(2)}, u32[]{:S(2)}) collective-permute-start(bf16[64,1024]{1,0:T(8,128)(2,1)S(1)} %get-tuple-element.52), channel_id=1, source_target_pairs={{0,8},{1,17},{2,10},{3,19},{4,12},{5,21},{6,14},{7,23},{8,0},{9,25... | collective-permute-start | bytes 393224 | tf_op jit(solution)/shard_map/ppermute | solution.py:66
  46.3 5.0 %collective-permute-start.13 = (bf16[64,1024]{1,0:T(8,128)(2,1)S(1)}, bf16[64,1024]{1,0:T(8,128)(2,1)S(1)}, u32[]{:S(2)}, u32[]{:S(2)}) collective-permute-start(bf16[64,1024]{1,0:T(8,128)(2,1)S(1)} %get-tuple-element.53), channel_id=1, source_target_pairs={{0,8},{1,17},{2,10},{3,19},{4,12},{5,21},{6,14},{7,23},{8,0},{9,25... | collective-permute-start | bytes 393224 | tf_op jit(solution)/shard_map/ppermute | solution.py:66

commit v12 on v11

--- a/solution.py
+++ b/solution.py
@@ -70,12 +70,18 @@
     return lax.axis_size("seq") == 4 and lax.axis_size("mp") == 8
 
 
+def distance_of(slot):
+    if is_square():
+        return jnp.where(lax.rem(lax.axis_index("mp"), 2) == 0, slot, turned(slot))
+    return slot
+
+
 def swapped(chunks):
+    if is_square():
+        return [chunks[0]] + [
+            exchange_by_core(chunks[k], (k, turned(k))) for k in range(1, len(chunks))
+        ]
     return [chunks[0]] + [exchange(chunks[k], "seq", k) for k in range(1, len(chunks))]
-
-
-def longest_first(chunks):
-    return [chunks[0]] + [chunks[len(chunks) - k] for k in range(1, len(chunks))]
 
 
 def group_of(cycle, member, chip):
@@ -107,7 +113,7 @@
     copies = []
     if width % 128 == 0:
         for place, out in zip(places, outs):
-            group = group_of(cycle, lax.bitwise_xor(own, place), chip)
+            group = group_of(cycle, lax.bitwise_xor(own, distance_of(place)), chip)
             for at, ref in enumerate((q_ref, k_ref, v_ref)):
                 copies.append(
                     pltpu.make_async_copy(
@@ -124,13 +130,13 @@
     for column, offset in enumerate(cycle_offsets):
         named = lax.rem(own - offset + 2 * cycle, cycle)
         meta = meta + jnp.where(
-            (lines == lax.bitwise_xor(own, named)) & (adj_ref[0, column] > 0), 1, 0
+            (lines == distance_of(lax.bitwise_xor(own, named))) & (adj_ref[0, column] > 0), 1, 0
         )
     meta = jnp.where(lines == META - 1, cnt_ref[0, 0], meta).astype(f32).astype(bf16)
     for place, out in zip(places, outs):
         out[3 * rows:, :] = meta
         if width % 128:
-            group = group_of(cycle, lax.bitwise_xor(own, place), chip)
+            group = group_of(cycle, lax.bitwise_xor(own, distance_of(place)), chip)
             for other in range(cycle):
                 @pl.when(group == other)
                 def _():
@@ -187,7 +193,7 @@
 
 
 def gather_kernel(cycle, *refs):
-    chunks = longest_first(refs[:cycle])
+    chunks = refs[:cycle]
     q_all, k_all, v_all, k_t, v_t, bias = refs[-6:]
     rows = q_all.shape[0] // cycle
     for place in range(cycle):
@@ -224,7 +230,7 @@
         compiler_params=params(8 if tokens <= 512 else 40),
         cost_estimate=cost(5),
         name="gather",
-    )(*longest_first(chunks), *after)
+    )(*chunks, *after)
 
 
 def head_tile(width):
@@ -374,32 +380,29 @@
     return [half, exchange(half, "mp", 1)]
 
 
+def rows_in_order(mine, others, core):
+    first = core == 0
+    mine, other = mine[...], jnp.concatenate([ref[...] for ref in others], axis=0)
+    return jnp.concatenate([jnp.where(first, mine, other), jnp.where(first, other, mine)], axis=0)
+
+
 def both_halves(halves, core):
     mine, other = halves[0][...], halves[1][...]
     first = core == 0
     return jnp.concatenate([jnp.where(first, mine, other), jnp.where(first, other, mine)], axis=0)
 
 
-def half_columns(halves, core, side):
-    half = halves[0].shape[0]
-    return columns_at((core if side == 0 else 1 - core) * half, half)
-
-
 def group_kernel(count, *refs):
-    ups, halves = refs[:count], refs[count:count + 2]
-    out = refs[-1]
+    ups, out = refs[:count], refs[-1]
     rows = ups[0].shape[0]
     _, _, core = my_place()
-    for side in range(2):
-        weight = halves[side][...]
-        for block, ref in enumerate(ups):
-            out[block * rows:(block + 1) * rows, half_columns(halves, core, side)] = dot_nt(
-                ref[...], weight
-            ).astype(bf16)
-
-
-def group_grads(upstreams, halves, after):
-    rows, width = upstreams[0].shape[0], 2 * halves[0].shape[0]
+    weight = rows_in_order(refs[count], refs[count + 1:count + 2], core)
+    for block, ref in enumerate(ups):
+        out[block * rows:(block + 1) * rows, :] = dot_nt(ref[...], weight).astype(bf16)
+
+
+def group_grads(upstreams, pieces, after):
+    rows, width = upstreams[0].shape[0], 2 * pieces[0].shape[0]
     return pl.pallas_call(
         functools.partial(group_kernel, len(upstreams)),
         out_shape=jax.ShapeDtypeStruct((len(upstreams) * rows, width), bf16),
@@ -408,26 +411,21 @@
         compiler_params=params(8),
         cost_estimate=cost(1),
         name="group_grads",
-    )(*upstreams, *halves, *after)
-
-
-def partial_kernel(att_ref, mine, other, *refs):
+    )(*upstreams, *pieces, *after)
+
+
+def partial_kernel(att_ref, mine, *refs):
     own, kept, sent = refs[-3:]
     rows = own.shape[0]
     _, _, core = my_place()
-    weight = both_halves((mine, other), core)
-
-    def product(block):
-        return dot_nn(att_ref[pl.ds(pl.multiple_of(block * rows, rows), rows), :], weight)
-
-    own[...] = product(0)
-    kept[...] = product(1 + core)
-    sent[:rows, :] = product(2 - core).astype(bf16)
-    sent[rows:, :] = product(3).astype(bf16)
-
-
-def partials(attended, halves, after):
-    rows, model = attended.shape[0] // 4, halves[0].shape[1]
+    weight = rows_in_order(mine, refs[:1], core)
+    own[...] = dot_nn(att_ref[:rows, :], weight)
+    kept[...] = dot_nn(att_ref[rows:2 * rows, :], weight)
+    sent[...] = dot_nn(att_ref[2 * rows:, :], weight).astype(bf16)
+
+
+def partials(attended, pieces, after):
+    rows, model = attended.shape[0] // 4, pieces[0].shape[1]
     return pl.pallas_call(
         partial_kernel,
         out_shape=[jax.ShapeDtypeStruct((rows, model), f32)] * 2
@@ -437,7 +435,7 @@
         compiler_params=params(12),
         cost_estimate=cost(1),
         name="partials",
-    )(attended, *halves, *after)
+    )(attended, *pieces, *after)
 
 
 def combine_kernel(own, kept, landed, total, *sent):
@@ -464,27 +462,6 @@
     )(own, kept, landed)
 
 
-def turn_kernel(w_ref, next_x, next_y, weight, passed, sem):
-    copy = pltpu.make_async_copy(w_ref, weight, sem)
-    copy.start()
-    _, _, core = my_place()
-    passed[...] = jnp.where(core == 0, next_y[...], next_x[...])
-    copy.wait()
-
-
-def turn(out_weight, next_x, next_y):
-    return pl.pallas_call(
-        turn_kernel,
-        out_shape=[jax.ShapeDtypeStruct(array.shape, bf16) for array in (out_weight, next_y)],
-        in_specs=[unread()] + [vmem()] * 2,
-        out_specs=[vmem()] * 2,
-        scratch_shapes=[pltpu.SemaphoreType.DMA],
-        compiler_params=params(4),
-        cost_estimate=cost(1),
-        name="turn",
-    )(out_weight, next_x, next_y)
-
-
 def grad_kernel(cycle, up_ref, *refs):
     _, _, core = my_place()
     outs = refs[2 * cycle:]
@@ -512,7 +489,7 @@
     own, chip, _ = my_place()
     copies = []
     for place in range(cycle):
-        group = group_of(cycle, lax.bitwise_xor(own, place), chip)
+        group = group_of(cycle, lax.bitwise_xor(own, distance_of(place)), chip)
         if width % 128 == 0:
             for at, out in enumerate(outs):
                 copies.append(
@@ -535,7 +512,7 @@
 
 
 def finish_kernel(cycle, *refs):
-    chunks = longest_first(refs[:cycle])
+    chunks = refs[:cycle]
     mixed, *outs = refs[-5:-1]
     copies = place_columns(chunks, outs, refs[-1])
     rows = mixed.shape[0]
@@ -569,7 +546,7 @@
         scratch_shapes=[pltpu.SemaphoreType.DMA((cycle, 3))],
         compiler_params=params(8),
         name="finish",
-    )(*longest_first(chunks), *others)
+    )(*chunks, *others)
 
 
 def local(queries, keys, values, out_weight, upstream, adjacency, counts):
@@ -591,21 +568,21 @@
 
 
 def square(cycle, rows, tensors, out_weight, upstream):
-    next_x, next_y = exchange(upstream, "seq", 1), exchange(upstream, "seq", 2)
+    nexts = swapped([upstream] * 3)[1:]
     chunks = swapped(list(pack(cycle, range(cycle), tensors)))
-    held_weight, passed = turn(out_weight, next_x, next_y)
+    held_weight, passed = hold((out_weight, nexts[1]), [nexts[0]])
     across = exchange_by_core(passed, (1, 2))
     own_rows = with_other_core(fetch_rows(held_weight, 0))
     q_all, k_all, v_all, k_t, v_t, bias = gather(cycle, chunks)
     (attended,), att_t, lse = forward(cycle, cycle, q_all, k_all, v_t, bias, [across])
     own_mixed, kept, sent = partials(attended, own_rows, [])
     landed = exchange_by_core(sent, (2, 1))
-    grads = [group_grads((upstream, next_x, next_y, across), own_rows, [kept])]
+    grads = [group_grads((upstream, *nexts, across), own_rows, [kept])]
     inputs = (q_all, k_all, v_all, k_t, bias, att_t, lse)
-    terms = list(backward(cycle, inputs, grads, [], []))
+    terms = swapped(list(backward(cycle, inputs, grads, [], [])))
     own_mixed, *next_mixed = combine(own_mixed, kept, landed)
     next_mixed = [exchange_by_core(part, (1, 2)) for part in next_mixed]
-    return tuple(finish(cycle, rows, swapped(terms), [own_mixed] + next_mixed))
+    return tuple(finish(cycle, rows, terms, [own_mixed] + next_mixed))
 
 
 def solution(mesh):

time: 53.1 us -> 47.6 us (0.90)
  starting transfers between devices: 24.5 us -> 18 us
  waiting for transfers between devices: 16 us -> 16.9 us
    ppermute x9 -> x1, starting transfers between devices: 13.5 us -> 0.07 us  [exchange(): return lax.ppermute(value, axis, [(i, i ^ distance) for i in range(count)])]
    ppermute x4 -> x12, waiting for transfers between devices: 3.92 us -> 16.9 us  [exchange_by_core(): return lax.ppermute(value, ('seq', 'mp'), pairs)]
    ppermute x9 -> x1, waiting for transfers between devices: 12.1 us -> 0.01 us  [exchange(): return lax.ppermute(value, axis, [(i, i ^ distance) for i in range(count)])]
    ppermute x4 -> x12, starting transfers between devices: 10.4 us -> 17.3 us  [exchange_by_core(): return lax.ppermute(value, ('seq', 'mp'), pairs)]
  transfers between devices with their start and end apart: 14 -> 14, of which waited for: 6 -> 9; matrix products, arithmetic and copies ran while one was open for 0% -> 0% of each run, Pallas kernels for 17% -> 19%
where the time goes in v12:
time: 47.6 us; the launch traced here: 47.4 us
  starting transfers between devices  18 us (38%)
  waiting for transfers between devices  16.9 us (36%)
  Pallas kernels  11.1 us (23%)
  between operations  1.41 us (3%)
    ppermute x12, starting transfers between devices, exchange_by_core(): return lax.ppermute(value, ('seq', 'mp'), pairs)  17.3 us
    ppermute x12, waiting for transfers between devices, exchange_by_core(): return lax.ppermute(value, ('seq', 'mp'), pairs)  16.9 us
    pallas_call x1, Pallas kernels, backward(): pl.pallas_call(functools.partial(backward_kernel, cycle, min(tokens, 512)...  3.06 us
    pallas_call x1, Pallas kernels, forward(): pl.pallas_call(functools.partial(forward_kernel, min(tokens, 512), parts)...  2.4 us
    pallas_call x1, Pallas kernels, pack(): pl.pallas_call(functools.partial(pack_kernel, cycle, places), out_shape=[...  2.24 us
    pallas_call x1, Pallas kernels, finish(): pl.pallas_call(functools.partial(finish_kernel, cycle), out_shape=[jax.Sh...  1.69 us
  transfers between devices with their start and end apart: 14, of which 9 were waited for; matrix products, arithmetic and copies ran while one was open for 0% of the time, Pallas kernels for 19%

profile of v12, /device:TPU:0, one launch (start us, length us, event | category | flops | bytes accessed | tf_op | source)
XLA Modules:
  0.0 47.4 jit_solution(3065516185573774332)
XLA Ops:
  0.6 3.0 %collective-permute-start.3 = (bf16[128,1024]{1,0:T(8,128)(2,1)}, bf16[128,1024]{1,0:T(8,128)(2,1)S(1)}, u32[]{:S(2)}, u32[]{:S(2)}) collective-permute-start(bf16[128,1024]{1,0:T(8,128)(2,1)} %refs_0_.3), channel_id=1, source_target_pairs={{0,16},{1,9},{2,18},{3,11},{4,20},{5,13},{6,22},{7,15},{8,24},{9,1... | collective-permute-start | bytes 786440 | tf_op jit(solution)/shard_map/ppermute | solution.py:66
  3.7 1.5 %collective-permute-start.4 = (bf16[128,1024]{1,0:T(8,128)(2,1)}, bf16[128,1024]{1,0:T(8,128)(2,1)S(1)}, u32[]{:S(2)}, u32[]{:S(2)}) collective-permute-start(bf16[128,1024]{1,0:T(8,128)(2,1)} %refs_0_.3), channel_id=1, source_target_pairs={{0,8},{1,17},{2,10},{3,19},{4,12},{5,21},{6,14},{7,23},{8,0},{9,25... | collective-permute-start | bytes 786440 | tf_op jit(solution)/shard_map/ppermute | solution.py:66
  5.8 2.2 %pack.1 = (bf16[416,256]{1,0:T(8,128)(2,1)}, bf16[416,256]{1,0:T(8,128)(2,1)}, bf16[416,256]{1,0:T(8,128)(2,1)}, bf16[416,256]{1,0:T(8,128)(2,1)}) custom-call(bf16[128,1024]{1,0:T(8,128)(2,1)} %q_ref.1, bf16[128,1024]{1,0:T(8,128)(2,1)} %k_ref.1, bf16[128,1024]{1,0:T(8,128)(2,1)} %v_ref.1, s32[1,4]{1,0:T(1,128)} %adj_any.1, s32[1,1]{1,0:T(1,128)} %bitcast.1.cnt_any), custom_call_target="tpu_custom_call" | custom-call | flops 5000000000 | tf_op jit(solution)/shard_map/pack/pallas_call | solution.py:177
  8.1 0.6 %collective-permute-start = (bf16[416,256]{1,0:T(8,128)(2,1)}, bf16[416,256]{1,0:T(8,128)(2,1)S(1)}, u32[]{:S(2)}, u32[]{:S(2)}) collective-permute-start(bf16[416,256]{1,0:T(8,128)(2,1)} %get-tuple-element.30), channel_id=1, source_target_pairs={{0,8},{1,17},{2,10},{3,19},{4,12},{5,21},{6,14},{7,23},{8,0},{9,25... | collective-permute-start | bytes 638984 | tf_op jit(solution)/shard_map/ppermute | solution.py:66
  8.8 2.9 %collective-permute-start.2 = (bf16[416,256]{1,0:T(8,128)(2,1)}, bf16[416,256]{1,0:T(8,128)(2,1)S(1)}, u32[]{:S(2)}, u32[]{:S(2)}) collective-permute-start(bf16[416,256]{1,0:T(8,128)(2,1)} %get-tuple-element.32), channel_id=1, source_target_pairs={{0,24},{1,25},{2,26},{3,27},{4,28},{5,29},{6,30},{7,31},{8,16},{9,... | collective-permute-start | bytes 638984 | tf_op jit(solution)/shard_map/ppermute | solution.py:66
  11.7 1.5 %collective-permute-start.5 = (bf16[128,1024]{1,0:T(8,128)(2,1)S(1)}, bf16[128,1024]{1,0:T(8,128)(2,1)S(1)}, u32[]{:S(2)}, u32[]{:S(2)}) collective-permute-start(bf16[128,1024]{1,0:T(8,128)(2,1)S(1)} %get-tuple-element.39), channel_id=1, source_target_pairs={{0,8},{1,17},{2,10},{3,19},{4,12},{5,21},{6,14},{7,23},{8,0},{9,25... | collective-permute-start | bytes 786440 | tf_op jit(solution)/shard_map/ppermute | solution.py:66
  13.2 0.7 %collective-permute-start.6 = (bf16[128,1024]{1,0:T(8,128)(2,1)S(1)}, bf16[128,1024]{1,0:T(8,128)(2,1)S(1)}, u32[]{:S(2)}, u32[]{:S(2)}) collective-permute-start(bf16[128,1024]{1,0:T(8,128)(2,1)S(1)} %get-tuple-element.42), channel_id=1, source_target_pairs={{0,0},{1,1},{4,2},{5,3},{2,4},{3,5},{6,6},{7,7},{12,8},{13,9},{10,... | collective-permute-start | bytes 786440 | tf_op jit(solution)/shard_map/ppermute | solution.py:376
  13.8 2.7 %collective-permute-done.refs_1_ = bf16[416,256]{1,0:T(8,128)(2,1)S(1)} collective-permute-done((bf16[416,256]{1,0:T(8,128)(2,1)}, bf16[416,256]{1,0:T(8,128)(2,1)S(1)}, u32[]{:S(2)}, u32[]{:S(2)}) %collective-permute-start) | collective-permute-done | bytes 213024 | tf_op jit(solution)/shard_map/ppermute | solution.py:66
  16.5 4.9 %collective-permute-done.1.refs_2_ = bf16[416,256]{1,0:T(8,128)(2,1)S(1)} collective-permute-done((bf16[416,256]{1,0:T(8,128)(2,1)}, bf16[416,256]{1,0:T(8,128)(2,1)S(1)}, u32[]{:S(2)}, u32[]{:S(2)}) %collective-permute-start.1) | collective-permute-done | bytes 213024 | tf_op jit(solution)/shard_map/ppermute | solution.py:66
  21.9 0.6 %collective-permute-done.5.refs_0_.refs_3_ = bf16[128,1024]{1,0:T(8,128)(2,1)S(1)} collective-permute-done((bf16[128,1024]{1,0:T(8,128)(2,1)S(1)}, bf16[128,1024]{1,0:T(8,128)(2,1)S(1)}, u32[]{:S(2)}, u32[]{:S(2)}) %collective-permute-start.5) | collective-permute-done | bytes 262176 | tf_op jit(solution)/shard_map/ppermute | solution.py:66
  22.4 2.4 %forward.1 = (bf16[512,256]{1,0:T(8,128)(2,1)S(1)}, f32[256,512]{1,0:T(8,128)S(1)}, f32[8,512]{1,0:T(8,128)S(1)}) custom-call(bf16[512,256]{1,0:T(8,128)(2,1)S(1)} %get-tuple-element.33.q_all.refs_0_, bf16[512,256]{1,0:T(8,128)(2,1)S(1)} %get-tuple-element.34.k_all.refs_1_, bf16[256,512]{1,0:T(8,128)(2,1)S(1)} %get-tuple-element.38.v_t, ...), custom_call_target="tpu_custom_call" | custom-call | flops 3000000000 | tf_op jit(solution)/shard_map/forward/pallas_call | solution.py:279
  25.3 1.6 %collective-permute-start.11 = (bf16[256,1024]{1,0:T(8,128)(2,1)S(1)}, bf16[256,1024]{1,0:T(8,128)(2,1)S(1)}, u32[]{:S(2)}, u32[]{:S(2)}) collective-permute-start(bf16[256,1024]{1,0:T(8,128)(2,1)S(1)} %get-tuple-element.50), channel_id=1, source_target_pairs={{0,16},{1,9},{2,18},{3,11},{4,20},{5,13},{6,22},{7,15},{8,24},{9,1... | collective-permute-start | bytes 1572872 | tf_op jit(solution)/shard_map/ppermute | solution.py:66
  26.9 0.8 %group_grads.1.refs_7_ = bf16[512,256]{1,0:T(8,128)(2,1)S(1)} custom-call(bf16[128,1024]{1,0:T(8,128)(2,1)S(1)} %copy-done.1, bf16[128,1024]{1,0:T(8,128)(2,1)S(1)} %collective-permute-done.4.refs_2_.refs_1_, bf16[128,1024]{1,0:T(8,128)(2,1)S(1)} %collective-permute-done.3.refs_1_.refs_2_, bf16[128,1024]{1,0:T(8,128)(2,1)S(1)} %collective-permute-done.5.refs_0_.refs_3_, ...), custom_call_target="tpu_custom_call" | custom-call | flops 1000000000 | tf_op jit(solution)/shard_map/group_grads/pallas_call | solution.py:406
  27.7 3.1 %backward.1 = (bf16[384,256]{1,0:T(8,128)(2,1)S(1)}, bf16[384,256]{1,0:T(8,128)(2,1)S(1)}, bf16[384,256]{1,0:T(8,128)(2,1)S(1)}, bf16[384,256]{1,0:T(8,128)(2,1)S(1)}) custom-call(bf16[512,256]{1,0:T(8,128)(2,1)S(1)} %get-tuple-element.33.q_all.refs_0_, bf16[512,256]{1,0:T(8,128)(2,1)S(1)} %get-tuple-element.34.k_all.refs_1_, ...), custom_call_target="tpu_custom_call" | custom-call | flops 3000000000 | tf_op jit(solution)/shard_map/backward/pallas_call | solution.py:352
  30.8 1.5 %collective-permute-start.8 = (bf16[384,256]{1,0:T(8,128)(2,1)S(1)}, bf16[384,256]{1,0:T(8,128)(2,1)S(1)}, u32[]{:S(2)}, u32[]{:S(2)}) collective-permute-start(bf16[384,256]{1,0:T(8,128)(2,1)S(1)} %get-tuple-element.46), channel_id=1, source_target_pairs={{0,8},{1,17},{2,10},{3,19},{4,12},{5,21},{6,14},{7,23},{8,0},{9,25... | collective-permute-start | bytes 589832 | tf_op jit(solution)/shard_map/ppermute | solution.py:66
  32.3 0.6 %collective-permute-start.9 = (bf16[384,256]{1,0:T(8,128)(2,1)S(1)}, bf16[384,256]{1,0:T(8,128)(2,1)S(1)}, u32[]{:S(2)}, u32[]{:S(2)}) collective-permute-start(bf16[384,256]{1,0:T(8,128)(2,1)S(1)} %get-tuple-element.47), channel_id=1, source_target_pairs={{0,16},{1,9},{2,18},{3,11},{4,20},{5,13},{6,22},{7,15},{8,24},{9,1... | collective-permute-start | bytes 589832 | tf_op jit(solution)/shard_map/ppermute | solution.py:66
  32.9 1.4 %collective-permute-start.10 = (bf16[384,256]{1,0:T(8,128)(2,1)S(1)}, bf16[384,256]{1,0:T(8,128)(2,1)S(1)}, u32[]{:S(2)}, u32[]{:S(2)}) collective-permute-start(bf16[384,256]{1,0:T(8,128)(2,1)S(1)} %get-tuple-element.48), channel_id=1, source_target_pairs={{0,24},{1,25},{2,26},{3,27},{4,28},{5,29},{6,30},{7,31},{8,16},{9,... | collective-permute-start | bytes 589832 | tf_op jit(solution)/shard_map/ppermute | solution.py:66
  34.4 1.0 %collective-permute-done.11.landed = bf16[256,1024]{1,0:T(8,128)(2,1)S(1)} collective-permute-done((bf16[256,1024]{1,0:T(8,128)(2,1)S(1)}, bf16[256,1024]{1,0:T(8,128)(2,1)S(1)}, u32[]{:S(2)}, u32[]{:S(2)}) %collective-permute-start.11) | collective-permute-done | bytes 524320 | tf_op jit(solution)/shard_map/ppermute | solution.py:66
  35.4 2.5 %collective-permute-start.12 = (bf16[64,1024]{1,0:T(8,128)(2,1)S(1)}, bf16[64,1024]{1,0:T(8,128)(2,1)S(1)}, u32[]{:S(2)}, u32[]{:S(2)}) collective-permute-start(bf16[64,1024]{1,0:T(8,128)(2,1)S(1)} %get-tuple-element.52), channel_id=1, source_target_pairs={{0,8},{1,17},{2,10},{3,19},{4,12},{5,21},{6,14},{7,23},{8,0},{9,25... | collective-permute-start | bytes 393224 | tf_op jit(solution)/shard_map/ppermute | solution.py:66
  38.4 3.9 %collective-permute-done.9.refs_2_ = bf16[384,256]{1,0:T(8,128)(2,1)S(1)} collective-permute-done((bf16[384,256]{1,0:T(8,128)(2,1)S(1)}, bf16[384,256]{1,0:T(8,128)(2,1)S(1)}, u32[]{:S(2)}, u32[]{:S(2)}) %collective-permute-start.9) | collective-permute-done | bytes 196640 | tf_op jit(solution)/shard_map/ppermute | solution.py:66
  42.2 0.7 %collective-permute-done.10.refs_3_ = bf16[384,256]{1,0:T(8,128)(2,1)S(1)} collective-permute-done((bf16[384,256]{1,0:T(8,128)(2,1)S(1)}, bf16[384,256]{1,0:T(8,128)(2,1)S(1)}, u32[]{:S(2)}, u32[]{:S(2)}) %collective-permute-start.10) | collective-permute-done | bytes 196640 | tf_op jit(solution)/shard_map/ppermute | solution.py:66
  43.0 1.3 %collective-permute-done.12.refs_5_ = bf16[64,1024]{1,0:T(8,128)(2,1)S(1)} collective-permute-done((bf16[64,1024]{1,0:T(8,128)(2,1)S(1)}, bf16[64,1024]{1,0:T(8,128)(2,1)S(1)}, u32[]{:S(2)}, u32[]{:S(2)}) %collective-permute-start.12) | collective-permute-done | bytes 131104 | tf_op jit(solution)/shard_map/ppermute | solution.py:66
  44.3 1.4 %collective-permute-done.13.refs_6_ = bf16[64,1024]{1,0:T(8,128)(2,1)S(1)} collective-permute-done((bf16[64,1024]{1,0:T(8,128)(2,1)S(1)}, bf16[64,1024]{1,0:T(8,128)(2,1)S(1)}, u32[]{:S(2)}, u32[]{:S(2)}) %collective-permute-start.13) | collective-permute-done | bytes 131104 | tf_op jit(solution)/shard_map/ppermute | solution.py:66
  45.7 1.7 %finish.1 = (bf16[128,1024]{1,0:T(8,128)(2,1)}, bf16[128,1024]{1,0:T(8,128)(2,1)}, bf16[128,1024]{1,0:T(8,128)(2,1)}, bf16[128,1024]{1,0:T(8,128)(2,1)}) custom-call(bf16[384,256]{1,0:T(8,128)(2,1)S(1)} %get-tuple-element.45.refs_0_, bf16[384,256]{1,0:T(8,128)(2,1)S(1)} %collective-permute-done.8.refs_1_, ...), custom_call_target="tpu_custom_call" | custom-call | tf_op jit(solution)/shard_map/finish/pallas_call | solution.py:541
  (19 shorter events, 1.5 us)
Async XLA Ops:
  0.6 11.0 %collective-permute-start.3 = (bf16[128,1024]{1,0:T(8,128)(2,1)}, bf16[128,1024]{1,0:T(8,128)(2,1)S(1)}, u32[]{:S(2)}, u32[]{:S(2)}) collective-permute-start(bf16[128,1024]{1,0:T(8,128)(2,1)} %refs_0_.3), channel_id=1, source_target_pairs={{0,16},{1,9},{2,18},{3,11},{4,20},{5,13},{6,22},{7,15},{8,24},{9,1... | collective-permute-start | bytes 786440 | tf_op jit(solution)/shard_map/ppermute | solution.py:66
  3.7 8.0 %collective-permute-start.4 = (bf16[128,1024]{1,0:T(8,128)(2,1)}, bf16[128,1024]{1,0:T(8,128)(2,1)S(1)}, u32[]{:S(2)}, u32[]{:S(2)}) collective-permute-start(bf16[128,1024]{1,0:T(8,128)(2,1)} %refs_0_.3), channel_id=1, source_target_pairs={{0,8},{1,17},{2,10},{3,19},{4,12},{5,21},{6,14},{7,23},{8,0},{9,25... | collective-permute-start | bytes 786440 | tf_op jit(solution)/shard_map/ppermute | solution.py:66
  5.8 5.8 %copy-start = (bf16[128,1024]{1,0:T(8,128)(2,1)S(1)}, bf16[128,1024]{1,0:T(8,128)(2,1)}, u32[]{:S(2)}) copy-start(bf16[128,1024]{1,0:T(8,128)(2,1)} %refs_0_.2) | copy-start | bytes 786436
  8.1 8.5 %collective-permute-start = (bf16[416,256]{1,0:T(8,128)(2,1)}, bf16[416,256]{1,0:T(8,128)(2,1)S(1)}, u32[]{:S(2)}, u32[]{:S(2)}) collective-permute-start(bf16[416,256]{1,0:T(8,128)(2,1)} %get-tuple-element.30), channel_id=1, source_target_pairs={{0,8},{1,17},{2,10},{3,19},{4,12},{5,21},{6,14},{7,23},{8,0},{9,25... | collective-permute-start | bytes 638984 | tf_op jit(solution)/shard_map/ppermute | solution.py:66
  8.7 12.8 %collective-permute-start.1 = (bf16[416,256]{1,0:T(8,128)(2,1)}, bf16[416,256]{1,0:T(8,128)(2,1)S(1)}, u32[]{:S(2)}, u32[]{:S(2)}) collective-permute-start(bf16[416,256]{1,0:T(8,128)(2,1)} %get-tuple-element.31), channel_id=1, source_target_pairs={{0,16},{1,9},{2,18},{3,11},{4,20},{5,13},{6,22},{7,15},{8,24},{9,1... | collective-permute-start | bytes 638984 | tf_op jit(solution)/shard_map/ppermute | solution.py:66
  8.7 12.7 %copy-start.2 = (bf16[416,256]{1,0:T(8,128)(2,1)S(1)}, bf16[416,256]{1,0:T(8,128)(2,1)}, u32[]{:S(2)}) copy-start(bf16[416,256]{1,0:T(8,128)(2,1)} %get-tuple-element.29.refs_0_) | copy-start | bytes 638980
  8.8 12.7 %collective-permute-start.2 = (bf16[416,256]{1,0:T(8,128)(2,1)}, bf16[416,256]{1,0:T(8,128)(2,1)S(1)}, u32[]{:S(2)}, u32[]{:S(2)}) collective-permute-start(bf16[416,256]{1,0:T(8,128)(2,1)} %get-tuple-element.32), channel_id=1, source_target_pairs={{0,24},{1,25},{2,26},{3,27},{4,28},{5,29},{6,30},{7,31},{8,16},{9,... | collective-permute-start | bytes 638984 | tf_op jit(solution)/shard_map/ppermute | solution.py:66
  11.7 10.7 %collective-permute-start.5 = (bf16[128,1024]{1,0:T(8,128)(2,1)S(1)}, bf16[128,1024]{1,0:T(8,128)(2,1)S(1)}, u32[]{:S(2)}, u32[]{:S(2)}) collective-permute-start(bf16[128,1024]{1,0:T(8,128)(2,1)S(1)} %get-tuple-element.39), channel_id=1, source_target_pairs={{0,8},{1,17},{2,10},{3,19},{4,12},{5,21},{6,14},{7,23},{8,0},{9,25... | collective-permute-start | bytes 786440 | tf_op jit(solution)/shard_map/ppermute | solution.py:66
  13.2 8.6 %collective-permute-start.6 = (bf16[128,1024]{1,0:T(8,128)(2,1)S(1)}, bf16[128,1024]{1,0:T(8,128)(2,1)S(1)}, u32[]{:S(2)}, u32[]{:S(2)}) collective-permute-start(bf16[128,1024]{1,0:T(8,128)(2,1)S(1)} %get-tuple-element.42), channel_id=1, source_target_pairs={{0,0},{1,1},{4,2},{5,3},{2,4},{3,5},{6,6},{7,7},{12,8},{13,9},{10,... | collective-permute-start | bytes 786440 | tf_op jit(solution)/shard_map/ppermute | solution.py:376
  21.8 3.1 %collective-permute-start.7 = (bf16[128,1024]{1,0:T(8,128)(2,1)S(1)}, bf16[128,1024]{1,0:T(8,128)(2,1)S(1)}, u32[]{:S(2)}, u32[]{:S(2)}) collective-permute-start(bf16[128,1024]{1,0:T(8,128)(2,1)S(1)} %collective-permute-done.6.mine.refs_4_), channel_id=1, source_target_pairs={{0,1},{1,0},{2,3},{3,2},{4,5},{5,4},{6,7},{7,6},{8,9},{9,8},{10,11... | collective-permute-start | bytes 786440 | tf_op jit(solution)/shard_map/ppermute | solution.py:52
  24.8 2.1 %copy-start.1 = (bf16[128,1024]{1,0:T(8,128)(2,1)S(1)}, bf16[128,1024]{1,0:T(8,128)(2,1)}, u32[]{:S(2)}) copy-start(bf16[128,1024]{1,0:T(8,128)(2,1)} %refs_0_.3) | copy-start | bytes 786436
  25.3 10.0 %collective-permute-start.11 = (bf16[256,1024]{1,0:T(8,128)(2,1)S(1)}, bf16[256,1024]{1,0:T(8,128)(2,1)S(1)}, u32[]{:S(2)}, u32[]{:S(2)}) collective-permute-start(bf16[256,1024]{1,0:T(8,128)(2,1)S(1)} %get-tuple-element.50), channel_id=1, source_target_pairs={{0,16},{1,9},{2,18},{3,11},{4,20},{5,13},{6,22},{7,15},{8,24},{9,1... | collective-permute-start | bytes 1572872 | tf_op jit(solution)/shard_map/ppermute | solution.py:66
  30.8 7.6 %collective-permute-start.8 = (bf16[384,256]{1,0:T(8,128)(2,1)S(1)}, bf16[384,256]{1,0:T(8,128)(2,1)S(1)}, u32[]{:S(2)}, u32[]{:S(2)}) collective-permute-start(bf16[384,256]{1,0:T(8,128)(2,1)S(1)} %get-tuple-element.46), channel_id=1, source_target_pairs={{0,8},{1,17},{2,10},{3,19},{4,12},{5,21},{6,14},{7,23},{8,0},{9,25... | collective-permute-start | bytes 589832 | tf_op jit(solution)/shard_map/ppermute | solution.py:66
  32.3 9.9 %collective-permute-start.9 = (bf16[384,256]{1,0:T(8,128)(2,1)S(1)}, bf16[384,256]{1,0:T(8,128)(2,1)S(1)}, u32[]{:S(2)}, u32[]{:S(2)}) collective-permute-start(bf16[384,256]{1,0:T(8,128)(2,1)S(1)} %get-tuple-element.47), channel_id=1, source_target_pairs={{0,16},{1,9},{2,18},{3,11},{4,20},{5,13},{6,22},{7,15},{8,24},{9,1... | collective-permute-start | bytes 589832 | tf_op jit(solution)/shard_map/ppermute | solution.py:66
  32.9 10.0 %collective-permute-start.10 = (bf16[384,256]{1,0:T(8,128)(2,1)S(1)}, bf16[384,256]{1,0:T(8,128)(2,1)S(1)}, u32[]{:S(2)}, u32[]{:S(2)}) collective-permute-start(bf16[384,256]{1,0:T(8,128)(2,1)S(1)} %get-tuple-element.48), channel_id=1, source_target_pairs={{0,24},{1,25},{2,26},{3,27},{4,28},{5,29},{6,30},{7,31},{8,16},{9,... | collective-permute-start | bytes 589832 | tf_op jit(solution)/shard_map/ppermute | solution.py:66
  35.4 8.9 %collective-permute-start.12 = (bf16[64,1024]{1,0:T(8,128)(2,1)S(1)}, bf16[64,1024]{1,0:T(8,128)(2,1)S(1)}, u32[]{:S(2)}, u32[]{:S(2)}) collective-permute-start(bf16[64,1024]{1,0:T(8,128)(2,1)S(1)} %get-tuple-element.52), channel_id=1, source_target_pairs={{0,8},{1,17},{2,10},{3,19},{4,12},{5,21},{6,14},{7,23},{8,0},{9,25... | collective-permute-start | bytes 393224 | tf_op jit(solution)/shard_map/ppermute | solution.py:66
  38.0 7.7 %collective-permute-start.13 = (bf16[64,1024]{1,0:T(8,128)(2,1)S(1)}, bf16[64,1024]{1,0:T(8,128)(2,1)S(1)}, u32[]{:S(2)}, u32[]{:S(2)}) collective-permute-start(bf16[64,1024]{1,0:T(8,128)(2,1)S(1)} %get-tuple-element.53), channel_id=1, source_target_pairs={{0,8},{1,17},{2,10},{3,19},{4,12},{5,21},{6,14},{7,23},{8,0},{9,25... | collective-permute-start | bytes 393224 | tf_op jit(solution)/shard_map/ppermute | solution.py:66

commit v13 on v12

--- a/solution.py
+++ b/solution.py
@@ -260,11 +260,10 @@
             largest = jnp.max(scores, axis=0, keepdims=True)
             expo = jnp.exp2(scores - largest)
             total = jnp.sum(expo, axis=0, keepdims=True)
-            probs = (expo * (1.0 / total)).astype(bf16)
             lse[head:head + 1, span] = largest + jnp.log2(total)
             att_t[head * HEAD_DIM:(head + 1) * HEAD_DIM, span] = dot_nn(
-                v_t[head * HEAD_DIM:(head + 1) * HEAD_DIM, :], probs
-            )
+                v_t[head * HEAD_DIM:(head + 1) * HEAD_DIM, :], expo.astype(bf16)
+            ) * (1.0 / total)
     attended = att_t[...].T.astype(bf16)
     filled = 0
     for out in outs:
@@ -513,16 +512,11 @@
 
 def finish_kernel(cycle, *refs):
     chunks = refs[:cycle]
-    mixed, *outs = refs[-5:-1]
+    outs, word = refs[-5:-2], refs[-2]
+    word[...] = jnp.zeros(word.shape, word.dtype)
+    rows = outs[0].shape[0]
     copies = place_columns(chunks, outs, refs[-1])
-    rows = mixed.shape[0]
-    if len(refs) == cycle + 8:
-        for at in range(2):
-            span = slice(at * rows // 2, (at + 1) * rows // 2)
-            mixed[span, :] = (
-                refs[cycle][span, :] + refs[cycle + 1 + at][...].astype(f32)
-            ).astype(bf16)
-    else:
+    if len(refs) > cycle + 5:
         halves = refs[cycle:3 * cycle]
         _, _, core = my_place()
         total = None
@@ -530,7 +524,7 @@
             weight = both_halves(halves[2 * place:2 * place + 2], core)
             term = dot_nn(chunks[place][3 * rows:, :], weight)
             total = term if total is None else total + term
-        mixed[...] = total.astype(bf16)
+        refs[-6][...] = total.astype(bf16)
     for copy in copies:
         copy.wait()
 
@@ -540,13 +534,35 @@
     aligned = model // cycle % 128 == 0
     return pl.pallas_call(
         functools.partial(finish_kernel, cycle),
-        out_shape=[jax.ShapeDtypeStruct((rows, model), bf16)] * 4,
+        out_shape=[jax.ShapeDtypeStruct((rows, model), bf16)] * (4 if others else 3)
+        + [jax.ShapeDtypeStruct((16, 128), bf16)],
         in_specs=[vmem()] * (cycle + len(others)),
-        out_specs=[vmem()] + [anywhere() if aligned else vmem()] * 3,
+        out_specs=[vmem()] * (1 if others else 0)
+        + [anywhere() if aligned else vmem()] * 3
+        + [vmem()],
         scratch_shapes=[pltpu.SemaphoreType.DMA((cycle, 3))],
         compiler_params=params(8),
         name="finish",
     )(*chunks, *others)
+
+
+def sum_kernel(own, *refs):
+    out = refs[-1]
+    part = own.shape[0] // 2
+    for at in range(2):
+        span = slice(at * part, (at + 1) * part)
+        out[span, :] = (own[span, :] + refs[at][...].astype(f32)).astype(bf16)
+
+
+def last_sum(own, landed, after):
+    return pl.pallas_call(
+        sum_kernel,
+        out_shape=jax.ShapeDtypeStruct(own.shape, bf16),
+        in_specs=[vmem()] * 3 + [unread()] * len(after),
+        out_specs=vmem(),
+        compiler_params=params(8),
+        name="last_sum",
+    )(own, *landed, *after)
 
 
 def local(queries, keys, values, out_weight, upstream, adjacency, counts):
@@ -564,7 +580,7 @@
     grads = swapped(project_grad(cycle, upstream, halves))
     inputs = (q_all, k_all, v_all, k_t, bias, att_t, lse)
     terms = swapped(backward(cycle, inputs, grads, attended, []))
-    return tuple(finish(cycle, rows, terms, halves))
+    return tuple(finish(cycle, rows, terms, halves)[:4])
 
 
 def square(cycle, rows, tensors, out_weight, upstream):
@@ -574,15 +590,16 @@
     across = exchange_by_core(passed, (1, 2))
     own_rows = with_other_core(fetch_rows(held_weight, 0))
     q_all, k_all, v_all, k_t, v_t, bias = gather(cycle, chunks)
-    (attended,), att_t, lse = forward(cycle, cycle, q_all, k_all, v_t, bias, [across])
-    own_mixed, kept, sent = partials(attended, own_rows, [])
+    (attended,), att_t, lse = forward(cycle, cycle, q_all, k_all, v_t, bias)
+    own_mixed, kept, sent = partials(attended, own_rows, [across])
     landed = exchange_by_core(sent, (2, 1))
     grads = [group_grads((upstream, *nexts, across), own_rows, [kept])]
     inputs = (q_all, k_all, v_all, k_t, bias, att_t, lse)
     terms = swapped(list(backward(cycle, inputs, grads, [], [])))
     own_mixed, *next_mixed = combine(own_mixed, kept, landed)
     next_mixed = [exchange_by_core(part, (1, 2)) for part in next_mixed]
-    return tuple(finish(cycle, rows, terms, [own_mixed] + next_mixed))
+    *grads, word = finish(cycle, rows, terms, [])
+    return (last_sum(own_mixed, next_mixed, [word]), *grads)
 
 
 def solution(mesh):

time: 47.6 us -> 51.8 us (1.088)
  starting transfers between devices: 18 us -> 21.1 us
  waiting for transfers between devices: 16.9 us -> 18.3 us
    ppermute x12, starting transfers between devices: 17.3 us -> 20.4 us  [exchange_by_core(): return lax.ppermute(value, ('seq', 'mp'), pairs)]
    ppermute x12, waiting for transfers between devices: 16.9 us -> 18.3 us  [exchange_by_core(): return lax.ppermute(value, ('seq', 'mp'), pairs)]
    pallas_call x0 -> x1, Pallas kernels: none -> 0.76 us  [last_sum(): pl.pallas_call(sum_kernel, out_shape=jax.ShapeDtypeStruct(own.shape, bf16...]
    pallas_call x1, Pallas kernels: 1.69 us -> 0.97 us  [finish(): pl.pallas_call(functools.partial(finish_kernel, cycle), out_shape=[jax.Sh...]
  transfers between devices with their start and end apart: 14 -> 14, of which waited for: 9 -> 7; matrix products, arithmetic and copies ran while one was open for 0% -> 0% of each run, Pallas kernels for 19% -> 19%
where the time goes in v13:
time: 51.8 us; the launch traced here: 51.6 us
  starting transfers between devices  21.1 us (41%)
  waiting for transfers between devices  18.3 us (35%)
  Pallas kernels  10.8 us (21%)
  between operations  1.39 us (3%)
    ppermute x12, starting transfers between devices, exchange_by_core(): return lax.ppermute(value, ('seq', 'mp'), pairs)  20.4 us
    ppermute x12, waiting for transfers between devices, exchange_by_core(): return lax.ppermute(value, ('seq', 'mp'), pairs)  18.3 us
    pallas_call x1, Pallas kernels, backward(): pl.pallas_call(functools.partial(backward_kernel, cycle, min(tokens, 512)...  3.06 us
    pallas_call x1, Pallas kernels, pack(): pl.pallas_call(functools.partial(pack_kernel, cycle, places), out_shape=[...  2.24 us
    pallas_call x1, Pallas kernels, forward(): pl.pallas_call(functools.partial(forward_kernel, min(tokens, 512), parts)...  2.08 us
  transfers between devices with their start and end apart: 14, of which 7 were waited for; matrix products, arithmetic and copies ran while one was open for 0% of the time, Pallas kernels for 19%

profile of v13, /device:TPU:0, one launch (start us, length us, event | category | flops | bytes accessed | tf_op | source)
XLA Modules:
  0.0 51.6 jit_solution(18279114780996124431)
XLA Ops:
  0.6 3.0 %collective-permute-start.3 = (bf16[128,1024]{1,0:T(8,128)(2,1)}, bf16[128,1024]{1,0:T(8,128)(2,1)S(1)}, u32[]{:S(2)}, u32[]{:S(2)}) collective-permute-start(bf16[128,1024]{1,0:T(8,128)(2,1)} %refs_0_.3), channel_id=1, source_target_pairs={{0,16},{1,9},{2,18},{3,11},{4,20},{5,13},{6,22},{7,15},{8,24},{9,1... | collective-permute-start | bytes 786440 | tf_op jit(solution)/shard_map/ppermute | solution.py:66
  3.7 1.5 %collective-permute-start.4 = (bf16[128,1024]{1,0:T(8,128)(2,1)}, bf16[128,1024]{1,0:T(8,128)(2,1)S(1)}, u32[]{:S(2)}, u32[]{:S(2)}) collective-permute-start(bf16[128,1024]{1,0:T(8,128)(2,1)} %refs_0_.3), channel_id=1, source_target_pairs={{0,8},{1,17},{2,10},{3,19},{4,12},{5,21},{6,14},{7,23},{8,0},{9,25... | collective-permute-start | bytes 786440 | tf_op jit(solution)/shard_map/ppermute | solution.py:66
  5.8 2.2 %pack.1 = (bf16[416,256]{1,0:T(8,128)(2,1)}, bf16[416,256]{1,0:T(8,128)(2,1)}, bf16[416,256]{1,0:T(8,128)(2,1)}, bf16[416,256]{1,0:T(8,128)(2,1)}) custom-call(bf16[128,1024]{1,0:T(8,128)(2,1)} %q_ref.1, bf16[128,1024]{1,0:T(8,128)(2,1)} %k_ref.1, bf16[128,1024]{1,0:T(8,128)(2,1)} %v_ref.1, s32[1,4]{1,0:T(1,128)} %adj_any.1, s32[1,1]{1,0:T(1,128)} %bitcast.1.cnt_any), custom_call_target="tpu_custom_call" | custom-call | flops 5000000000 | tf_op jit(solution)/shard_map/pack/pallas_call | solution.py:177
  8.1 0.6 %collective-permute-start = (bf16[416,256]{1,0:T(8,128)(2,1)}, bf16[416,256]{1,0:T(8,128)(2,1)S(1)}, u32[]{:S(2)}, u32[]{:S(2)}) collective-permute-start(bf16[416,256]{1,0:T(8,128)(2,1)} %get-tuple-element.34), channel_id=1, source_target_pairs={{0,8},{1,17},{2,10},{3,19},{4,12},{5,21},{6,14},{7,23},{8,0},{9,25... | collective-permute-start | bytes 638984 | tf_op jit(solution)/shard_map/ppermute | solution.py:66
  8.8 2.9 %collective-permute-start.2 = (bf16[416,256]{1,0:T(8,128)(2,1)}, bf16[416,256]{1,0:T(8,128)(2,1)S(1)}, u32[]{:S(2)}, u32[]{:S(2)}) collective-permute-start(bf16[416,256]{1,0:T(8,128)(2,1)} %get-tuple-element.36), channel_id=1, source_target_pairs={{0,24},{1,25},{2,26},{3,27},{4,28},{5,29},{6,30},{7,31},{8,16},{9,... | collective-permute-start | bytes 638984 | tf_op jit(solution)/shard_map/ppermute | solution.py:66
  11.7 0.7 %collective-permute-start.5 = (bf16[128,1024]{1,0:T(8,128)(2,1)S(1)}, bf16[128,1024]{1,0:T(8,128)(2,1)S(1)}, u32[]{:S(2)}, u32[]{:S(2)}) collective-permute-start(bf16[128,1024]{1,0:T(8,128)(2,1)S(1)} %get-tuple-element.42), channel_id=1, source_target_pairs={{0,0},{1,1},{4,2},{5,3},{2,4},{3,5},{6,6},{7,7},{12,8},{13,9},{10,... | collective-permute-start | bytes 786440 | tf_op jit(solution)/shard_map/ppermute | solution.py:375
  12.4 4.1 %collective-permute-done.refs_1_ = bf16[416,256]{1,0:T(8,128)(2,1)S(1)} collective-permute-done((bf16[416,256]{1,0:T(8,128)(2,1)}, bf16[416,256]{1,0:T(8,128)(2,1)S(1)}, u32[]{:S(2)}, u32[]{:S(2)}) %collective-permute-start) | collective-permute-done | bytes 213024 | tf_op jit(solution)/shard_map/ppermute | solution.py:66
  16.5 3.2 %collective-permute-done.1.refs_2_ = bf16[416,256]{1,0:T(8,128)(2,1)S(1)} collective-permute-done((bf16[416,256]{1,0:T(8,128)(2,1)}, bf16[416,256]{1,0:T(8,128)(2,1)S(1)}, u32[]{:S(2)}, u32[]{:S(2)}) %collective-permute-start.1) | collective-permute-done | bytes 213024 | tf_op jit(solution)/shard_map/ppermute | solution.py:66
  19.7 0.8 %collective-permute-done.2.refs_3_ = bf16[416,256]{1,0:T(8,128)(2,1)S(1)} collective-permute-done((bf16[416,256]{1,0:T(8,128)(2,1)}, bf16[416,256]{1,0:T(8,128)(2,1)S(1)}, u32[]{:S(2)}, u32[]{:S(2)}) %collective-permute-start.2) | collective-permute-done | bytes 213024 | tf_op jit(solution)/shard_map/ppermute | solution.py:66
  20.8 1.5 %collective-permute-start.7 = (bf16[128,1024]{1,0:T(8,128)(2,1)S(1)}, bf16[128,1024]{1,0:T(8,128)(2,1)S(1)}, u32[]{:S(2)}, u32[]{:S(2)}) collective-permute-start(bf16[128,1024]{1,0:T(8,128)(2,1)S(1)} %get-tuple-element.43), channel_id=1, source_target_pairs={{0,8},{1,17},{2,10},{3,19},{4,12},{5,21},{6,14},{7,23},{8,0},{9,25... | collective-permute-start | bytes 786440 | tf_op jit(solution)/shard_map/ppermute | solution.py:66
  22.4 2.1 %forward.1 = (bf16[512,256]{1,0:T(8,128)(2,1)S(1)}, f32[256,512]{1,0:T(8,128)S(1)}, f32[8,512]{1,0:T(8,128)S(1)}) custom-call(bf16[512,256]{1,0:T(8,128)(2,1)S(1)} %get-tuple-element.37.q_all.refs_0_, bf16[512,256]{1,0:T(8,128)(2,1)S(1)} %get-tuple-element.38.k_all.refs_1_, bf16[256,512]{1,0:T(8,128)(2,1)S(1)} %get-tuple-element.39.v_t, ...), custom_call_target="tpu_custom_call" | custom-call | flops 3000000000 | tf_op jit(solution)/shard_map/forward/pallas_call | solution.py:278
  24.5 2.8 %collective-permute-done.7.refs_1_.refs_3_ = bf16[128,1024]{1,0:T(8,128)(2,1)S(1)} collective-permute-done((bf16[128,1024]{1,0:T(8,128)(2,1)S(1)}, bf16[128,1024]{1,0:T(8,128)(2,1)S(1)}, u32[]{:S(2)}, u32[]{:S(2)}) %collective-permute-start.7) | collective-permute-done | bytes 262176 | tf_op jit(solution)/shard_map/ppermute | solution.py:66
  27.7 1.7 %collective-permute-start.8 = (bf16[256,1024]{1,0:T(8,128)(2,1)S(1)}, bf16[256,1024]{1,0:T(8,128)(2,1)S(1)}, u32[]{:S(2)}, u32[]{:S(2)}) collective-permute-start(bf16[256,1024]{1,0:T(8,128)(2,1)S(1)} %get-tuple-element.46), channel_id=1, source_target_pairs={{0,16},{1,9},{2,18},{3,11},{4,20},{5,13},{6,22},{7,15},{8,24},{9,1... | collective-permute-start | bytes 1572872 | tf_op jit(solution)/shard_map/ppermute | solution.py:66
  29.4 0.8 %group_grads.1.refs_7_ = bf16[512,256]{1,0:T(8,128)(2,1)S(1)} custom-call(bf16[128,1024]{1,0:T(8,128)(2,1)S(1)} %copy-done.1, bf16[128,1024]{1,0:T(8,128)(2,1)S(1)} %collective-permute-done.4.refs_2_.refs_1_, bf16[128,1024]{1,0:T(8,128)(2,1)S(1)} %collective-permute-done.3.refs_1_.refs_2_, bf16[128,1024]{1,0:T(8,128)(2,1)S(1)} %collective-permute-done.7.refs_1_.refs_3_, ...), custom_call_target="tpu_custom_call" | custom-call | flops 1000000000 | tf_op jit(solution)/shard_map/group_grads/pallas_call | solution.py:405
  30.2 3.1 %backward.1 = (bf16[384,256]{1,0:T(8,128)(2,1)S(1)}, bf16[384,256]{1,0:T(8,128)(2,1)S(1)}, bf16[384,256]{1,0:T(8,128)(2,1)S(1)}, bf16[384,256]{1,0:T(8,128)(2,1)S(1)}) custom-call(bf16[512,256]{1,0:T(8,128)(2,1)S(1)} %get-tuple-element.37.q_all.refs_0_, bf16[512,256]{1,0:T(8,128)(2,1)S(1)} %get-tuple-element.38.k_all.refs_1_, ...), custom_call_target="tpu_custom_call" | custom-call | flops 3000000000 | tf_op jit(solution)/shard_map/backward/pallas_call | solution.py:351
  33.3 0.8 %collective-permute-start.11 = (bf16[384,256]{1,0:T(8,128)(2,1)S(1)}, bf16[384,256]{1,0:T(8,128)(2,1)S(1)}, u32[]{:S(2)}, u32[]{:S(2)}) collective-permute-start(bf16[384,256]{1,0:T(8,128)(2,1)S(1)} %get-tuple-element.55), channel_id=1, source_target_pairs={{0,8},{1,17},{2,10},{3,19},{4,12},{5,21},{6,14},{7,23},{8,0},{9,25... | collective-permute-start | bytes 589832 | tf_op jit(solution)/shard_map/ppermute | solution.py:66
  34.0 1.2 %collective-permute-start.12 = (bf16[384,256]{1,0:T(8,128)(2,1)S(1)}, bf16[384,256]{1,0:T(8,128)(2,1)S(1)}, u32[]{:S(2)}, u32[]{:S(2)}) collective-permute-start(bf16[384,256]{1,0:T(8,128)(2,1)S(1)} %get-tuple-element.56), channel_id=1, source_target_pairs={{0,16},{1,9},{2,18},{3,11},{4,20},{5,13},{6,22},{7,15},{8,24},{9,1... | collective-permute-start | bytes 589832 | tf_op jit(solution)/shard_map/ppermute | solution.py:66
  35.2 1.6 %collective-permute-start.13 = (bf16[384,256]{1,0:T(8,128)(2,1)S(1)}, bf16[384,256]{1,0:T(8,128)(2,1)S(1)}, u32[]{:S(2)}, u32[]{:S(2)}) collective-permute-start(bf16[384,256]{1,0:T(8,128)(2,1)S(1)} %get-tuple-element.57), channel_id=1, source_target_pairs={{0,24},{1,25},{2,26},{3,27},{4,28},{5,29},{6,30},{7,31},{8,16},{9,... | collective-permute-start | bytes 589832 | tf_op jit(solution)/shard_map/ppermute | solution.py:66
  36.8 3.5 %collective-permute-done.8.landed = bf16[256,1024]{1,0:T(8,128)(2,1)S(1)} collective-permute-done((bf16[256,1024]{1,0:T(8,128)(2,1)S(1)}, bf16[256,1024]{1,0:T(8,128)(2,1)S(1)}, u32[]{:S(2)}, u32[]{:S(2)}) %collective-permute-start.8) | collective-permute-done | bytes 524320 | tf_op jit(solution)/shard_map/ppermute | solution.py:66
  40.4 5.5 %collective-permute-start.9 = (bf16[64,1024]{1,0:T(8,128)(2,1)S(1)}, bf16[64,1024]{1,0:T(8,128)(2,1)S(1)}, u32[]{:S(2)}, u32[]{:S(2)}) collective-permute-start(bf16[64,1024]{1,0:T(8,128)(2,1)S(1)} %get-tuple-element.48), channel_id=1, source_target_pairs={{0,8},{1,17},{2,10},{3,19},{4,12},{5,21},{6,14},{7,23},{8,0},{9,25... | collective-permute-start | bytes 393224 | tf_op jit(solution)/shard_map/ppermute | solution.py:66
  46.0 2.2 %collective-permute-done.12.refs_2_ = bf16[384,256]{1,0:T(8,128)(2,1)S(1)} collective-permute-done((bf16[384,256]{1,0:T(8,128)(2,1)S(1)}, bf16[384,256]{1,0:T(8,128)(2,1)S(1)}, u32[]{:S(2)}, u32[]{:S(2)}) %collective-permute-start.12) | collective-permute-done | bytes 196640 | tf_op jit(solution)/shard_map/ppermute | solution.py:66
  48.2 1.0 %finish.1 = (bf16[128,1024]{1,0:T(8,128)(2,1)}, bf16[128,1024]{1,0:T(8,128)(2,1)}, bf16[128,1024]{1,0:T(8,128)(2,1)}, bf16[16,128]{1,0:T(8,128)(2,1)S(1)}) custom-call(bf16[384,256]{1,0:T(8,128)(2,1)S(1)} %get-tuple-element.54.refs_0_, bf16[384,256]{1,0:T(8,128)(2,1)S(1)} %collective-permute-done.11.refs_1_, ...), custom_call_target="tpu_custom_call" | custom-call | tf_op jit(solution)/shard_map/finish/pallas_call | solution.py:535
  49.2 1.6 %collective-permute-done.10.refs_1_ = bf16[64,1024]{1,0:T(8,128)(2,1)S(1)} collective-permute-done((bf16[64,1024]{1,0:T(8,128)(2,1)S(1)}, bf16[64,1024]{1,0:T(8,128)(2,1)S(1)}, u32[]{:S(2)}, u32[]{:S(2)}) %collective-permute-start.10) | collective-permute-done | bytes 131104 | tf_op jit(solution)/shard_map/ppermute | solution.py:66
  50.9 0.8 %last_sum.1 = bf16[128,1024]{1,0:T(8,128)(2,1)} custom-call(f32[128,1024]{1,0:T(8,128)S(1)} %get-tuple-element.47.own, bf16[64,1024]{1,0:T(8,128)(2,1)S(1)} %collective-permute-done.9.refs_0_, bf16[64,1024]{1,0:T(8,128)(2,1)S(1)} %collective-permute-done.10.refs_1_, bf16[16,128]{1,0:T(8,128)(2,1)S(1)} %get-tuple-element.58.refs_2_), custom_call_target="tpu_custom_call" | custom-call | tf_op jit(solution)/shard_map/last_sum/pallas_call | solution.py:558
  (20 shorter events, 1.1 us)
Async XLA Ops:
  0.6 11.0 %collective-permute-start.3 = (bf16[128,1024]{1,0:T(8,128)(2,1)}, bf16[128,1024]{1,0:T(8,128)(2,1)S(1)}, u32[]{:S(2)}, u32[]{:S(2)}) collective-permute-start(bf16[128,1024]{1,0:T(8,128)(2,1)} %refs_0_.3), channel_id=1, source_target_pairs={{0,16},{1,9},{2,18},{3,11},{4,20},{5,13},{6,22},{7,15},{8,24},{9,1... | collective-permute-start | bytes 786440 | tf_op jit(solution)/shard_map/ppermute | solution.py:66
  3.7 8.0 %collective-permute-start.4 = (bf16[128,1024]{1,0:T(8,128)(2,1)}, bf16[128,1024]{1,0:T(8,128)(2,1)S(1)}, u32[]{:S(2)}, u32[]{:S(2)}) collective-permute-start(bf16[128,1024]{1,0:T(8,128)(2,1)} %refs_0_.3), channel_id=1, source_target_pairs={{0,8},{1,17},{2,10},{3,19},{4,12},{5,21},{6,14},{7,23},{8,0},{9,25... | collective-permute-start | bytes 786440 | tf_op jit(solution)/shard_map/ppermute | solution.py:66
  5.8 5.8 %copy-start = (bf16[128,1024]{1,0:T(8,128)(2,1)S(1)}, bf16[128,1024]{1,0:T(8,128)(2,1)}, u32[]{:S(2)}) copy-start(bf16[128,1024]{1,0:T(8,128)(2,1)} %refs_0_.2) | copy-start | bytes 786436
  8.1 8.5 %collective-permute-start = (bf16[416,256]{1,0:T(8,128)(2,1)}, bf16[416,256]{1,0:T(8,128)(2,1)S(1)}, u32[]{:S(2)}, u32[]{:S(2)}) collective-permute-start(bf16[416,256]{1,0:T(8,128)(2,1)} %get-tuple-element.34), channel_id=1, source_target_pairs={{0,8},{1,17},{2,10},{3,19},{4,12},{5,21},{6,14},{7,23},{8,0},{9,25... | collective-permute-start | bytes 638984 | tf_op jit(solution)/shard_map/ppermute | solution.py:66
  8.7 11.1 %collective-permute-start.1 = (bf16[416,256]{1,0:T(8,128)(2,1)}, bf16[416,256]{1,0:T(8,128)(2,1)S(1)}, u32[]{:S(2)}, u32[]{:S(2)}) collective-permute-start(bf16[416,256]{1,0:T(8,128)(2,1)} %get-tuple-element.35), channel_id=1, source_target_pairs={{0,16},{1,9},{2,18},{3,11},{4,20},{5,13},{6,22},{7,15},{8,24},{9,1... | collective-permute-start | bytes 638984 | tf_op jit(solution)/shard_map/ppermute | solution.py:66
  8.7 11.8 %copy-start.2 = (bf16[416,256]{1,0:T(8,128)(2,1)S(1)}, bf16[416,256]{1,0:T(8,128)(2,1)}, u32[]{:S(2)}) copy-start(bf16[416,256]{1,0:T(8,128)(2,1)} %get-tuple-element.33.refs_0_) | copy-start | bytes 638980
  8.8 11.8 %collective-permute-start.2 = (bf16[416,256]{1,0:T(8,128)(2,1)}, bf16[416,256]{1,0:T(8,128)(2,1)S(1)}, u32[]{:S(2)}, u32[]{:S(2)}) collective-permute-start(bf16[416,256]{1,0:T(8,128)(2,1)} %get-tuple-element.36), channel_id=1, source_target_pairs={{0,24},{1,25},{2,26},{3,27},{4,28},{5,29},{6,30},{7,31},{8,16},{9,... | collective-permute-start | bytes 638984 | tf_op jit(solution)/shard_map/ppermute | solution.py:66
  11.7 10.6 %collective-permute-start.5 = (bf16[128,1024]{1,0:T(8,128)(2,1)S(1)}, bf16[128,1024]{1,0:T(8,128)(2,1)S(1)}, u32[]{:S(2)}, u32[]{:S(2)}) collective-permute-start(bf16[128,1024]{1,0:T(8,128)(2,1)S(1)} %get-tuple-element.42), channel_id=1, source_target_pairs={{0,0},{1,1},{4,2},{5,3},{2,4},{3,5},{6,6},{7,7},{12,8},{13,9},{10,... | collective-permute-start | bytes 786440 | tf_op jit(solution)/shard_map/ppermute | solution.py:375
  20.8 6.4 %collective-permute-start.7 = (bf16[128,1024]{1,0:T(8,128)(2,1)S(1)}, bf16[128,1024]{1,0:T(8,128)(2,1)S(1)}, u32[]{:S(2)}, u32[]{:S(2)}) collective-permute-start(bf16[128,1024]{1,0:T(8,128)(2,1)S(1)} %get-tuple-element.43), channel_id=1, source_target_pairs={{0,8},{1,17},{2,10},{3,19},{4,12},{5,21},{6,14},{7,23},{8,0},{9,25... | collective-permute-start | bytes 786440 | tf_op jit(solution)/shard_map/ppermute | solution.py:66
  22.3 4.9 %collective-permute-start.6 = (bf16[128,1024]{1,0:T(8,128)(2,1)S(1)}, bf16[128,1024]{1,0:T(8,128)(2,1)S(1)}, u32[]{:S(2)}, u32[]{:S(2)}) collective-permute-start(bf16[128,1024]{1,0:T(8,128)(2,1)S(1)} %collective-permute-done.5.mine.refs_4_), channel_id=1, source_target_pairs={{0,1},{1,0},{2,3},{3,2},{4,5},{5,4},{6,7},{7,6},{8,9},{9,8},{10,11... | collective-permute-start | bytes 786440 | tf_op jit(solution)/shard_map/ppermute | solution.py:52
  27.3 2.1 %copy-start.1 = (bf16[128,1024]{1,0:T(8,128)(2,1)S(1)}, bf16[128,1024]{1,0:T(8,128)(2,1)}, u32[]{:S(2)}) copy-start(bf16[128,1024]{1,0:T(8,128)(2,1)} %refs_0_.3) | copy-start | bytes 786436
  27.7 12.6 %collective-permute-start.8 = (bf16[256,1024]{1,0:T(8,128)(2,1)S(1)}, bf16[256,1024]{1,0:T(8,128)(2,1)S(1)}, u32[]{:S(2)}, u32[]{:S(2)}) collective-permute-start(bf16[256,1024]{1,0:T(8,128)(2,1)S(1)} %get-tuple-element.46), channel_id=1, source_target_pairs={{0,16},{1,9},{2,18},{3,11},{4,20},{5,13},{6,22},{7,15},{8,24},{9,1... | collective-permute-start | bytes 1572872 | tf_op jit(solution)/shard_map/ppermute | solution.py:66
  33.3 12.7 %collective-permute-start.11 = (bf16[384,256]{1,0:T(8,128)(2,1)S(1)}, bf16[384,256]{1,0:T(8,128)(2,1)S(1)}, u32[]{:S(2)}, u32[]{:S(2)}) collective-permute-start(bf16[384,256]{1,0:T(8,128)(2,1)S(1)} %get-tuple-element.55), channel_id=1, source_target_pairs={{0,8},{1,17},{2,10},{3,19},{4,12},{5,21},{6,14},{7,23},{8,0},{9,25... | collective-permute-start | bytes 589832 | tf_op jit(solution)/shard_map/ppermute | solution.py:66
  34.0 14.2 %collective-permute-start.12 = (bf16[384,256]{1,0:T(8,128)(2,1)S(1)}, bf16[384,256]{1,0:T(8,128)(2,1)S(1)}, u32[]{:S(2)}, u32[]{:S(2)}) collective-permute-start(bf16[384,256]{1,0:T(8,128)(2,1)S(1)} %get-tuple-element.56), channel_id=1, source_target_pairs={{0,16},{1,9},{2,18},{3,11},{4,20},{5,13},{6,22},{7,15},{8,24},{9,1... | collective-permute-start | bytes 589832 | tf_op jit(solution)/shard_map/ppermute | solution.py:66
  35.2 13.0 %collective-permute-start.13 = (bf16[384,256]{1,0:T(8,128)(2,1)S(1)}, bf16[384,256]{1,0:T(8,128)(2,1)S(1)}, u32[]{:S(2)}, u32[]{:S(2)}) collective-permute-start(bf16[384,256]{1,0:T(8,128)(2,1)S(1)} %get-tuple-element.57), channel_id=1, source_target_pairs={{0,24},{1,25},{2,26},{3,27},{4,28},{5,29},{6,30},{7,31},{8,16},{9,... | collective-permute-start | bytes 589832 | tf_op jit(solution)/shard_map/ppermute | solution.py:66
  40.4 8.8 %collective-permute-start.9 = (bf16[64,1024]{1,0:T(8,128)(2,1)S(1)}, bf16[64,1024]{1,0:T(8,128)(2,1)S(1)}, u32[]{:S(2)}, u32[]{:S(2)}) collective-permute-start(bf16[64,1024]{1,0:T(8,128)(2,1)S(1)} %get-tuple-element.48), channel_id=1, source_target_pairs={{0,8},{1,17},{2,10},{3,19},{4,12},{5,21},{6,14},{7,23},{8,0},{9,25... | collective-permute-start | bytes 393224 | tf_op jit(solution)/shard_map/ppermute | solution.py:66
  45.9 5.0 %collective-permute-start.10 = (bf16[64,1024]{1,0:T(8,128)(2,1)S(1)}, bf16[64,1024]{1,0:T(8,128)(2,1)S(1)}, u32[]{:S(2)}, u32[]{:S(2)}) collective-permute-start(bf16[64,1024]{1,0:T(8,128)(2,1)S(1)} %get-tuple-element.49), channel_id=1, source_target_pairs={{0,8},{1,17},{2,10},{3,19},{4,12},{5,21},{6,14},{7,23},{8,0},{9,25... | collective-permute-start | bytes 393224 | tf_op jit(solution)/shard_map/ppermute | solution.py:66

commit v14 on v13

--- a/solution.py
+++ b/solution.py
@@ -393,11 +393,9 @@
 
 def group_kernel(count, *refs):
     ups, out = refs[:count], refs[-1]
-    rows = ups[0].shape[0]
     _, _, core = my_place()
     weight = rows_in_order(refs[count], refs[count + 1:count + 2], core)
-    for block, ref in enumerate(ups):
-        out[block * rows:(block + 1) * rows, :] = dot_nt(ref[...], weight).astype(bf16)
+    out[...] = dot_nt(jnp.concatenate([ref[...] for ref in ups], axis=0), weight).astype(bf16)
 
 
 def group_grads(upstreams, pieces, after):
@@ -418,9 +416,10 @@
     rows = own.shape[0]
     _, _, core = my_place()
     weight = rows_in_order(mine, refs[:1], core)
-    own[...] = dot_nn(att_ref[:rows, :], weight)
-    kept[...] = dot_nn(att_ref[rows:2 * rows, :], weight)
-    sent[...] = dot_nn(att_ref[2 * rows:, :], weight).astype(bf16)
+    product = dot_nn(att_ref[...], weight)
+    own[...] = product[:rows, :]
+    kept[...] = product[rows:2 * rows, :]
+    sent[...] = product[2 * rows:, :].astype(bf16)
 
 
 def partials(attended, pieces, after):
@@ -590,8 +589,8 @@
     across = exchange_by_core(passed, (1, 2))
     own_rows = with_other_core(fetch_rows(held_weight, 0))
     q_all, k_all, v_all, k_t, v_t, bias = gather(cycle, chunks)
-    (attended,), att_t, lse = forward(cycle, cycle, q_all, k_all, v_t, bias)
-    own_mixed, kept, sent = partials(attended, own_rows, [across])
+    (attended,), att_t, lse = forward(cycle, cycle, q_all, k_all, v_t, bias, [across])
+    own_mixed, kept, sent = partials(attended, own_rows, [])
     landed = exchange_by_core(sent, (2, 1))
     grads = [group_grads((upstream, *nexts, across), own_rows, [kept])]
     inputs = (q_all, k_all, v_all, k_t, bias, att_t, lse)

time: 51.8 us -> 46.2 us (0.89)
  starting transfers between devices: 21.1 us -> 18 us
  waiting for transfers between devices: 18.3 us -> 15.9 us
    ppermute x12, starting transfers between devices: 20.4 us -> 17.2 us  [exchange_by_core(): return lax.ppermute(value, ('seq', 'mp'), pairs)]
    ppermute x12, waiting for transfers between devices: 18.3 us -> 15.9 us  [exchange_by_core(): return lax.ppermute(value, ('seq', 'mp'), pairs)]
  transfers between devices with their start and end apart: 14 -> 14, of which waited for: 7 -> 8; matrix products, arithmetic and copies ran while one was open for 0% -> 0% of each run, Pallas kernels for 19% -> 20%
where the time goes in v14:
time: 46.2 us; the launch traced here: 45.8 us
  starting transfers between devices  18 us (39%)
  waiting for transfers between devices  15.9 us (34%)
  Pallas kernels  10.5 us (23%)
  between operations  1.41 us (3%)
    ppermute x12, starting transfers between devices, exchange_by_core(): return lax.ppermute(value, ('seq', 'mp'), pairs)  17.2 us
    ppermute x12, waiting for transfers between devices, exchange_by_core(): return lax.ppermute(value, ('seq', 'mp'), pairs)  15.9 us
    pallas_call x1, Pallas kernels, backward(): pl.pallas_call(functools.partial(backward_kernel, cycle, min(tokens, 512)...  3.06 us
    pallas_call x1, Pallas kernels, pack(): pl.pallas_call(functools.partial(pack_kernel, cycle, places), out_shape=[...  2.24 us
    pallas_call x1, Pallas kernels, forward(): pl.pallas_call(functools.partial(forward_kernel, min(tokens, 512), parts)...  2.07 us
    pallas_call x1, Pallas kernels, finish(): pl.pallas_call(functools.partial(finish_kernel, cycle), out_shape=[jax.Sh...  0.97 us
  transfers between devices with their start and end apart: 14, of which 8 were waited for; matrix products, arithmetic and copies ran while one was open for 0% of the time, Pallas kernels for 20%

profile of v14, /device:TPU:0, one launch (start us, length us, event | category | flops | bytes accessed | tf_op | source)
XLA Modules:
  0.0 45.8 jit_solution(9274003092447449387)
XLA Ops:
  0.6 3.0 %collective-permute-start.3 = (bf16[128,1024]{1,0:T(8,128)(2,1)}, bf16[128,1024]{1,0:T(8,128)(2,1)S(1)}, u32[]{:S(2)}, u32[]{:S(2)}) collective-permute-start(bf16[128,1024]{1,0:T(8,128)(2,1)} %refs_0_.3), channel_id=1, source_target_pairs={{0,16},{1,9},{2,18},{3,11},{4,20},{5,13},{6,22},{7,15},{8,24},{9,1... | collective-permute-start | bytes 786440 | tf_op jit(solution)/shard_map/ppermute | solution.py:66
  3.7 1.5 %collective-permute-start.4 = (bf16[128,1024]{1,0:T(8,128)(2,1)}, bf16[128,1024]{1,0:T(8,128)(2,1)S(1)}, u32[]{:S(2)}, u32[]{:S(2)}) collective-permute-start(bf16[128,1024]{1,0:T(8,128)(2,1)} %refs_0_.3), channel_id=1, source_target_pairs={{0,8},{1,17},{2,10},{3,19},{4,12},{5,21},{6,14},{7,23},{8,0},{9,25... | collective-permute-start | bytes 786440 | tf_op jit(solution)/shard_map/ppermute | solution.py:66
  5.8 2.2 %pack.1 = (bf16[416,256]{1,0:T(8,128)(2,1)}, bf16[416,256]{1,0:T(8,128)(2,1)}, bf16[416,256]{1,0:T(8,128)(2,1)}, bf16[416,256]{1,0:T(8,128)(2,1)}) custom-call(bf16[128,1024]{1,0:T(8,128)(2,1)} %q_ref.1, bf16[128,1024]{1,0:T(8,128)(2,1)} %k_ref.1, bf16[128,1024]{1,0:T(8,128)(2,1)} %v_ref.1, s32[1,4]{1,0:T(1,128)} %adj_any.1, s32[1,1]{1,0:T(1,128)} %bitcast.1.cnt_any), custom_call_target="tpu_custom_call" | custom-call | flops 5000000000 | tf_op jit(solution)/shard_map/pack/pallas_call | solution.py:177
  8.1 0.6 %collective-permute-start = (bf16[416,256]{1,0:T(8,128)(2,1)}, bf16[416,256]{1,0:T(8,128)(2,1)S(1)}, u32[]{:S(2)}, u32[]{:S(2)}) collective-permute-start(bf16[416,256]{1,0:T(8,128)(2,1)} %get-tuple-element.34), channel_id=1, source_target_pairs={{0,8},{1,17},{2,10},{3,19},{4,12},{5,21},{6,14},{7,23},{8,0},{9,25... | collective-permute-start | bytes 638984 | tf_op jit(solution)/shard_map/ppermute | solution.py:66
  8.8 2.9 %collective-permute-start.2 = (bf16[416,256]{1,0:T(8,128)(2,1)}, bf16[416,256]{1,0:T(8,128)(2,1)S(1)}, u32[]{:S(2)}, u32[]{:S(2)}) collective-permute-start(bf16[416,256]{1,0:T(8,128)(2,1)} %get-tuple-element.36), channel_id=1, source_target_pairs={{0,24},{1,25},{2,26},{3,27},{4,28},{5,29},{6,30},{7,31},{8,16},{9,... | collective-permute-start | bytes 638984 | tf_op jit(solution)/shard_map/ppermute | solution.py:66
  11.7 1.5 %collective-permute-start.5 = (bf16[128,1024]{1,0:T(8,128)(2,1)S(1)}, bf16[128,1024]{1,0:T(8,128)(2,1)S(1)}, u32[]{:S(2)}, u32[]{:S(2)}) collective-permute-start(bf16[128,1024]{1,0:T(8,128)(2,1)S(1)} %get-tuple-element.41), channel_id=1, source_target_pairs={{0,8},{1,17},{2,10},{3,19},{4,12},{5,21},{6,14},{7,23},{8,0},{9,25... | collective-permute-start | bytes 786440 | tf_op jit(solution)/shard_map/ppermute | solution.py:66
  13.2 0.7 %collective-permute-start.6 = (bf16[128,1024]{1,0:T(8,128)(2,1)S(1)}, bf16[128,1024]{1,0:T(8,128)(2,1)S(1)}, u32[]{:S(2)}, u32[]{:S(2)}) collective-permute-start(bf16[128,1024]{1,0:T(8,128)(2,1)S(1)} %get-tuple-element.43), channel_id=1, source_target_pairs={{0,0},{1,1},{4,2},{5,3},{2,4},{3,5},{6,6},{7,7},{12,8},{13,9},{10,... | collective-permute-start | bytes 786440 | tf_op jit(solution)/shard_map/ppermute | solution.py:375
  13.8 2.7 %collective-permute-done.refs_1_ = bf16[416,256]{1,0:T(8,128)(2,1)S(1)} collective-permute-done((bf16[416,256]{1,0:T(8,128)(2,1)}, bf16[416,256]{1,0:T(8,128)(2,1)S(1)}, u32[]{:S(2)}, u32[]{:S(2)}) %collective-permute-start) | collective-permute-done | bytes 213024 | tf_op jit(solution)/shard_map/ppermute | solution.py:66
  16.5 4.9 %collective-permute-done.1.refs_2_ = bf16[416,256]{1,0:T(8,128)(2,1)S(1)} collective-permute-done((bf16[416,256]{1,0:T(8,128)(2,1)}, bf16[416,256]{1,0:T(8,128)(2,1)S(1)}, u32[]{:S(2)}, u32[]{:S(2)}) %collective-permute-start.1) | collective-permute-done | bytes 213024 | tf_op jit(solution)/shard_map/ppermute | solution.py:66
  21.9 0.6 %collective-permute-done.5.refs_0_.refs_3_ = bf16[128,1024]{1,0:T(8,128)(2,1)S(1)} collective-permute-done((bf16[128,1024]{1,0:T(8,128)(2,1)S(1)}, bf16[128,1024]{1,0:T(8,128)(2,1)S(1)}, u32[]{:S(2)}, u32[]{:S(2)}) %collective-permute-start.5) | collective-permute-done | bytes 262176 | tf_op jit(solution)/shard_map/ppermute | solution.py:66
  22.4 2.1 %forward.1 = (bf16[512,256]{1,0:T(8,128)(2,1)S(1)}, f32[256,512]{1,0:T(8,128)S(1)}, f32[8,512]{1,0:T(8,128)S(1)}) custom-call(bf16[512,256]{1,0:T(8,128)(2,1)S(1)} %get-tuple-element.37.q_all.refs_0_, bf16[512,256]{1,0:T(8,128)(2,1)S(1)} %get-tuple-element.38.k_all.refs_1_, bf16[256,512]{1,0:T(8,128)(2,1)S(1)} %get-tuple-element.39.v_t, ...), custom_call_target="tpu_custom_call" | custom-call | flops 3000000000 | tf_op jit(solution)/shard_map/forward/pallas_call | solution.py:278
  24.5 0.4 partials.1
  25.0 1.6 %collective-permute-start.8 = (bf16[256,1024]{1,0:T(8,128)(2,1)S(1)}, bf16[256,1024]{1,0:T(8,128)(2,1)S(1)}, u32[]{:S(2)}, u32[]{:S(2)}) collective-permute-start(bf16[256,1024]{1,0:T(8,128)(2,1)S(1)} %get-tuple-element.46), channel_id=1, source_target_pairs={{0,16},{1,9},{2,18},{3,11},{4,20},{5,13},{6,22},{7,15},{8,24},{9,1... | collective-permute-start | bytes 1572872 | tf_op jit(solution)/shard_map/ppermute | solution.py:66
  26.6 0.5 %group_grads.1.refs_7_ = bf16[512,256]{1,0:T(8,128)(2,1)S(1)} custom-call(bf16[128,1024]{1,0:T(8,128)(2,1)S(1)} %copy-done.1, bf16[128,1024]{1,0:T(8,128)(2,1)S(1)} %collective-permute-done.4.refs_2_.refs_1_, bf16[128,1024]{1,0:T(8,128)(2,1)S(1)} %collective-permute-done.3.refs_1_.refs_2_, bf16[128,1024]{1,0:T(8,128)(2,1)S(1)} %collective-permute-done.5.refs_0_.refs_3_, ...), custom_call_target="tpu_custom_call" | custom-call | flops 1000000000 | tf_op jit(solution)/shard_map/group_grads/pallas_call | solution.py:403
  27.1 3.1 %backward.1 = (bf16[384,256]{1,0:T(8,128)(2,1)S(1)}, bf16[384,256]{1,0:T(8,128)(2,1)S(1)}, bf16[384,256]{1,0:T(8,128)(2,1)S(1)}, bf16[384,256]{1,0:T(8,128)(2,1)S(1)}) custom-call(bf16[512,256]{1,0:T(8,128)(2,1)S(1)} %get-tuple-element.37.q_all.refs_0_, bf16[512,256]{1,0:T(8,128)(2,1)S(1)} %get-tuple-element.38.k_all.refs_1_, ...), custom_call_target="tpu_custom_call" | custom-call | flops 3000000000 | tf_op jit(solution)/shard_map/backward/pallas_call | solution.py:351
  30.1 1.5 %collective-permute-start.11 = (bf16[384,256]{1,0:T(8,128)(2,1)S(1)}, bf16[384,256]{1,0:T(8,128)(2,1)S(1)}, u32[]{:S(2)}, u32[]{:S(2)}) collective-permute-start(bf16[384,256]{1,0:T(8,128)(2,1)S(1)} %get-tuple-element.55), channel_id=1, source_target_pairs={{0,8},{1,17},{2,10},{3,19},{4,12},{5,21},{6,14},{7,23},{8,0},{9,25... | collective-permute-start | bytes 589832 | tf_op jit(solution)/shard_map/ppermute | solution.py:66
  31.7 0.6 %collective-permute-start.12 = (bf16[384,256]{1,0:T(8,128)(2,1)S(1)}, bf16[384,256]{1,0:T(8,128)(2,1)S(1)}, u32[]{:S(2)}, u32[]{:S(2)}) collective-permute-start(bf16[384,256]{1,0:T(8,128)(2,1)S(1)} %get-tuple-element.56), channel_id=1, source_target_pairs={{0,16},{1,9},{2,18},{3,11},{4,20},{5,13},{6,22},{7,15},{8,24},{9,1... | collective-permute-start | bytes 589832 | tf_op jit(solution)/shard_map/ppermute | solution.py:66
  32.3 1.4 %collective-permute-start.13 = (bf16[384,256]{1,0:T(8,128)(2,1)S(1)}, bf16[384,256]{1,0:T(8,128)(2,1)S(1)}, u32[]{:S(2)}, u32[]{:S(2)}) collective-permute-start(bf16[384,256]{1,0:T(8,128)(2,1)S(1)} %get-tuple-element.57), channel_id=1, source_target_pairs={{0,24},{1,25},{2,26},{3,27},{4,28},{5,29},{6,30},{7,31},{8,16},{9,... | collective-permute-start | bytes 589832 | tf_op jit(solution)/shard_map/ppermute | solution.py:66
  33.7 1.6 %collective-permute-done.8.landed = bf16[256,1024]{1,0:T(8,128)(2,1)S(1)} collective-permute-done((bf16[256,1024]{1,0:T(8,128)(2,1)S(1)}, bf16[256,1024]{1,0:T(8,128)(2,1)S(1)}, u32[]{:S(2)}, u32[]{:S(2)}) %collective-permute-start.8) | collective-permute-done | bytes 524320 | tf_op jit(solution)/shard_map/ppermute | solution.py:66
  35.4 2.5 %collective-permute-start.9 = (bf16[64,1024]{1,0:T(8,128)(2,1)S(1)}, bf16[64,1024]{1,0:T(8,128)(2,1)S(1)}, u32[]{:S(2)}, u32[]{:S(2)}) collective-permute-start(bf16[64,1024]{1,0:T(8,128)(2,1)S(1)} %get-tuple-element.48), channel_id=1, source_target_pairs={{0,8},{1,17},{2,10},{3,19},{4,12},{5,21},{6,14},{7,23},{8,0},{9,25... | collective-permute-start | bytes 393224 | tf_op jit(solution)/shard_map/ppermute | solution.py:66
  38.0 3.9 %collective-permute-done.12.refs_2_ = bf16[384,256]{1,0:T(8,128)(2,1)S(1)} collective-permute-done((bf16[384,256]{1,0:T(8,128)(2,1)S(1)}, bf16[384,256]{1,0:T(8,128)(2,1)S(1)}, u32[]{:S(2)}, u32[]{:S(2)}) %collective-permute-start.12) | collective-permute-done | bytes 196640 | tf_op jit(solution)/shard_map/ppermute | solution.py:66
  42.3 1.0 %finish.1 = (bf16[128,1024]{1,0:T(8,128)(2,1)}, bf16[128,1024]{1,0:T(8,128)(2,1)}, bf16[128,1024]{1,0:T(8,128)(2,1)}, bf16[16,128]{1,0:T(8,128)(2,1)S(1)}) custom-call(bf16[384,256]{1,0:T(8,128)(2,1)S(1)} %get-tuple-element.54.refs_0_, bf16[384,256]{1,0:T(8,128)(2,1)S(1)} %collective-permute-done.11.refs_1_, ...), custom_call_target="tpu_custom_call" | custom-call | tf_op jit(solution)/shard_map/finish/pallas_call | solution.py:534
  43.6 1.4 %collective-permute-done.10.refs_1_ = bf16[64,1024]{1,0:T(8,128)(2,1)S(1)} collective-permute-done((bf16[64,1024]{1,0:T(8,128)(2,1)S(1)}, bf16[64,1024]{1,0:T(8,128)(2,1)S(1)}, u32[]{:S(2)}, u32[]{:S(2)}) %collective-permute-start.10) | collective-permute-done | bytes 131104 | tf_op jit(solution)/shard_map/ppermute | solution.py:66
  45.0 0.8 %last_sum.1 = bf16[128,1024]{1,0:T(8,128)(2,1)} custom-call(f32[128,1024]{1,0:T(8,128)S(1)} %get-tuple-element.47.own, bf16[64,1024]{1,0:T(8,128)(2,1)S(1)} %collective-permute-done.9.refs_0_, bf16[64,1024]{1,0:T(8,128)(2,1)S(1)} %collective-permute-done.10.refs_1_, bf16[16,128]{1,0:T(8,128)(2,1)S(1)} %get-tuple-element.58.refs_2_), custom_call_target="tpu_custom_call" | custom-call | tf_op jit(solution)/shard_map/last_sum/pallas_call | solution.py:557
  (20 shorter events, 1.4 us)
Async XLA Ops:
  0.6 11.0 %collective-permute-start.3 = (bf16[128,1024]{1,0:T(8,128)(2,1)}, bf16[128,1024]{1,0:T(8,128)(2,1)S(1)}, u32[]{:S(2)}, u32[]{:S(2)}) collective-permute-start(bf16[128,1024]{1,0:T(8,128)(2,1)} %refs_0_.3), channel_id=1, source_target_pairs={{0,16},{1,9},{2,18},{3,11},{4,20},{5,13},{6,22},{7,15},{8,24},{9,1... | collective-permute-start | bytes 786440 | tf_op jit(solution)/shard_map/ppermute | solution.py:66
  3.7 8.0 %collective-permute-start.4 = (bf16[128,1024]{1,0:T(8,128)(2,1)}, bf16[128,1024]{1,0:T(8,128)(2,1)S(1)}, u32[]{:S(2)}, u32[]{:S(2)}) collective-permute-start(bf16[128,1024]{1,0:T(8,128)(2,1)} %refs_0_.3), channel_id=1, source_target_pairs={{0,8},{1,17},{2,10},{3,19},{4,12},{5,21},{6,14},{7,23},{8,0},{9,25... | collective-permute-start | bytes 786440 | tf_op jit(solution)/shard_map/ppermute | solution.py:66
  5.8 5.8 %copy-start = (bf16[128,1024]{1,0:T(8,128)(2,1)S(1)}, bf16[128,1024]{1,0:T(8,128)(2,1)}, u32[]{:S(2)}) copy-start(bf16[128,1024]{1,0:T(8,128)(2,1)} %refs_0_.2) | copy-start | bytes 786436
  8.1 8.5 %collective-permute-start = (bf16[416,256]{1,0:T(8,128)(2,1)}, bf16[416,256]{1,0:T(8,128)(2,1)S(1)}, u32[]{:S(2)}, u32[]{:S(2)}) collective-permute-start(bf16[416,256]{1,0:T(8,128)(2,1)} %get-tuple-element.34), channel_id=1, source_target_pairs={{0,8},{1,17},{2,10},{3,19},{4,12},{5,21},{6,14},{7,23},{8,0},{9,25... | collective-permute-start | bytes 638984 | tf_op jit(solution)/shard_map/ppermute | solution.py:66
  8.7 12.8 %collective-permute-start.1 = (bf16[416,256]{1,0:T(8,128)(2,1)}, bf16[416,256]{1,0:T(8,128)(2,1)S(1)}, u32[]{:S(2)}, u32[]{:S(2)}) collective-permute-start(bf16[416,256]{1,0:T(8,128)(2,1)} %get-tuple-element.35), channel_id=1, source_target_pairs={{0,16},{1,9},{2,18},{3,11},{4,20},{5,13},{6,22},{7,15},{8,24},{9,1... | collective-permute-start | bytes 638984 | tf_op jit(solution)/shard_map/ppermute | solution.py:66
  8.7 12.7 %copy-start.2 = (bf16[416,256]{1,0:T(8,128)(2,1)S(1)}, bf16[416,256]{1,0:T(8,128)(2,1)}, u32[]{:S(2)}) copy-start(bf16[416,256]{1,0:T(8,128)(2,1)} %get-tuple-element.33.refs_0_) | copy-start | bytes 638980
  8.8 12.7 %collective-permute-start.2 = (bf16[416,256]{1,0:T(8,128)(2,1)}, bf16[416,256]{1,0:T(8,128)(2,1)S(1)}, u32[]{:S(2)}, u32[]{:S(2)}) collective-permute-start(bf16[416,256]{1,0:T(8,128)(2,1)} %get-tuple-element.36), channel_id=1, source_target_pairs={{0,24},{1,25},{2,26},{3,27},{4,28},{5,29},{6,30},{7,31},{8,16},{9,... | collective-permute-start | bytes 638984 | tf_op jit(solution)/shard_map/ppermute | solution.py:66
  11.7 10.7 %collective-permute-start.5 = (bf16[128,1024]{1,0:T(8,128)(2,1)S(1)}, bf16[128,1024]{1,0:T(8,128)(2,1)S(1)}, u32[]{:S(2)}, u32[]{:S(2)}) collective-permute-start(bf16[128,1024]{1,0:T(8,128)(2,1)S(1)} %get-tuple-element.41), channel_id=1, source_target_pairs={{0,8},{1,17},{2,10},{3,19},{4,12},{5,21},{6,14},{7,23},{8,0},{9,25... | collective-permute-start | bytes 786440 | tf_op jit(solution)/shard_map/ppermute | solution.py:66
  13.2 8.6 %collective-permute-start.6 = (bf16[128,1024]{1,0:T(8,128)(2,1)S(1)}, bf16[128,1024]{1,0:T(8,128)(2,1)S(1)}, u32[]{:S(2)}, u32[]{:S(2)}) collective-permute-start(bf16[128,1024]{1,0:T(8,128)(2,1)S(1)} %get-tuple-element.43), channel_id=1, source_target_pairs={{0,0},{1,1},{4,2},{5,3},{2,4},{3,5},{6,6},{7,7},{12,8},{13,9},{10,... | collective-permute-start | bytes 786440 | tf_op jit(solution)/shard_map/ppermute | solution.py:375
  21.8 2.7 %collective-permute-start.7 = (bf16[128,1024]{1,0:T(8,128)(2,1)S(1)}, bf16[128,1024]{1,0:T(8,128)(2,1)S(1)}, u32[]{:S(2)}, u32[]{:S(2)}) collective-permute-start(bf16[128,1024]{1,0:T(8,128)(2,1)S(1)} %collective-permute-done.6.mine.refs_4_), channel_id=1, source_target_pairs={{0,1},{1,0},{2,3},{3,2},{4,5},{5,4},{6,7},{7,6},{8,9},{9,8},{10,11... | collective-permute-start | bytes 786440 | tf_op jit(solution)/shard_map/ppermute | solution.py:52
  24.5 2.1 %copy-start.1 = (bf16[128,1024]{1,0:T(8,128)(2,1)S(1)}, bf16[128,1024]{1,0:T(8,128)(2,1)}, u32[]{:S(2)}) copy-start(bf16[128,1024]{1,0:T(8,128)(2,1)} %refs_0_.3) | copy-start | bytes 786436
  25.0 10.3 %collective-permute-start.8 = (bf16[256,1024]{1,0:T(8,128)(2,1)S(1)}, bf16[256,1024]{1,0:T(8,128)(2,1)S(1)}, u32[]{:S(2)}, u32[]{:S(2)}) collective-permute-start(bf16[256,1024]{1,0:T(8,128)(2,1)S(1)} %get-tuple-element.46), channel_id=1, source_target_pairs={{0,16},{1,9},{2,18},{3,11},{4,20},{5,13},{6,22},{7,15},{8,24},{9,1... | collective-permute-start | bytes 1572872 | tf_op jit(solution)/shard_map/ppermute | solution.py:66
  30.1 7.9 %collective-permute-start.11 = (bf16[384,256]{1,0:T(8,128)(2,1)S(1)}, bf16[384,256]{1,0:T(8,128)(2,1)S(1)}, u32[]{:S(2)}, u32[]{:S(2)}) collective-permute-start(bf16[384,256]{1,0:T(8,128)(2,1)S(1)} %get-tuple-element.55), channel_id=1, source_target_pairs={{0,8},{1,17},{2,10},{3,19},{4,12},{5,21},{6,14},{7,23},{8,0},{9,25... | collective-permute-start | bytes 589832 | tf_op jit(solution)/shard_map/ppermute | solution.py:66
  31.7 10.3 %collective-permute-start.12 = (bf16[384,256]{1,0:T(8,128)(2,1)S(1)}, bf16[384,256]{1,0:T(8,128)(2,1)S(1)}, u32[]{:S(2)}, u32[]{:S(2)}) collective-permute-start(bf16[384,256]{1,0:T(8,128)(2,1)S(1)} %get-tuple-element.56), channel_id=1, source_target_pairs={{0,16},{1,9},{2,18},{3,11},{4,20},{5,13},{6,22},{7,15},{8,24},{9,1... | collective-permute-start | bytes 589832 | tf_op jit(solution)/shard_map/ppermute | solution.py:66
  32.3 10.0 %collective-permute-start.13 = (bf16[384,256]{1,0:T(8,128)(2,1)S(1)}, bf16[384,256]{1,0:T(8,128)(2,1)S(1)}, u32[]{:S(2)}, u32[]{:S(2)}) collective-permute-start(bf16[384,256]{1,0:T(8,128)(2,1)S(1)} %get-tuple-element.57), channel_id=1, source_target_pairs={{0,24},{1,25},{2,26},{3,27},{4,28},{5,29},{6,30},{7,31},{8,16},{9,... | collective-permute-start | bytes 589832 | tf_op jit(solution)/shard_map/ppermute | solution.py:66
  35.4 8.2 %collective-permute-start.9 = (bf16[64,1024]{1,0:T(8,128)(2,1)S(1)}, bf16[64,1024]{1,0:T(8,128)(2,1)S(1)}, u32[]{:S(2)}, u32[]{:S(2)}) collective-permute-start(bf16[64,1024]{1,0:T(8,128)(2,1)S(1)} %get-tuple-element.48), channel_id=1, source_target_pairs={{0,8},{1,17},{2,10},{3,19},{4,12},{5,21},{6,14},{7,23},{8,0},{9,25... | collective-permute-start | bytes 393224 | tf_op jit(solution)/shard_map/ppermute | solution.py:66
  37.9 7.1 %collective-permute-start.10 = (bf16[64,1024]{1,0:T(8,128)(2,1)S(1)}, bf16[64,1024]{1,0:T(8,128)(2,1)S(1)}, u32[]{:S(2)}, u32[]{:S(2)}) collective-permute-start(bf16[64,1024]{1,0:T(8,128)(2,1)S(1)} %get-tuple-element.49), channel_id=1, source_target_pairs={{0,8},{1,17},{2,10},{3,19},{4,12},{5,21},{6,14},{7,23},{8,0},{9,25... | collective-permute-start | bytes 393224 | tf_op jit(solution)/shard_map/ppermute | solution.py:66

commit v15 on v14

--- a/solution.py
+++ b/solution.py
@@ -244,8 +244,8 @@
 
 
 def forward_kernel(query_tile, parts, q_all, k_all, v_t, bias, *refs):
-    outs = refs[-2 - parts:-2]
-    att_t, lse = refs[-2:]
+    outs = refs[-3 - parts:-3]
+    att_t, inverse, weights = refs[-3:]
     tokens, width = q_all.shape
     tile = head_tile(width)
     for start in range(0, tokens, query_tile):
@@ -260,10 +260,13 @@
             largest = jnp.max(scores, axis=0, keepdims=True)
             expo = jnp.exp2(scores - largest)
             total = jnp.sum(expo, axis=0, keepdims=True)
-            lse[head:head + 1, span] = largest + jnp.log2(total)
-            att_t[head * HEAD_DIM:(head + 1) * HEAD_DIM, span] = dot_nn(
-                v_t[head * HEAD_DIM:(head + 1) * HEAD_DIM, :], expo.astype(bf16)
-            ) * (1.0 / total)
+            share = 1.0 / total
+            expo = expo.astype(bf16)
+            inverse[head:head + 1, span] = share
+            weights[head * tokens:(head + 1) * tokens, span] = expo
+            att_t[head * HEAD_DIM:(head + 1) * HEAD_DIM, span] = (
+                dot_nn(v_t[head * HEAD_DIM:(head + 1) * HEAD_DIM, :], expo) * share
+            )
     attended = att_t[...].T.astype(bf16)
     filled = 0
     for out in outs:
@@ -281,33 +284,41 @@
         + [
             jax.ShapeDtypeStruct((width, tokens), f32),
             jax.ShapeDtypeStruct((8, tokens), f32),
+            jax.ShapeDtypeStruct((width // HEAD_DIM * tokens, tokens), bf16),
         ],
         in_specs=[vmem()] * 4 + [unread()] * len(after),
-        out_specs=[vmem()] * (parts + 2),
+        out_specs=[vmem()] * (parts + 3),
         compiler_params=params(16 if tokens <= 512 else 60),
         cost_estimate=cost(3),
         name="forward",
     )(q_all, k_all, v_t, bias, *after)
-    return outs[:parts], outs[parts], outs[parts + 1]
+    return outs[:parts], *outs[parts:]
 
 
 def backward_kernel(cycle, query_tile, grad_count, att_count, *refs):
-    q_all, k_all, v_all, k_t, bias, att_t, lse = refs[:7]
+    q_all, k_all, v_all, k_t, att_t, inverse, weights = refs[:7]
     refs = refs[7:]
     grads = refs[:grad_count]
     attended = refs[grad_count:grad_count + att_count]
-    outs = refs[-4 - cycle:-4]
-    g_all, dq_t, dk, dv = refs[-4:]
-    width = q_all.shape[1]
-    tokens = q_all.shape[0]
+    outs = refs[-5 - cycle:-5]
+    g_all, g_t, dq_t, dk, dv = refs[-5:]
+    tokens, width = q_all.shape
     rows = tokens // cycle
-    filled = 0
-    for grad in grads:
-        g_all[filled:filled + grad.shape[0], :] = grad[...]
-        filled += grad.shape[0]
+    if grad_count == 1:
+        turned_grad = grads[0][...].astype(f32)
+    else:
+        for place, grad in enumerate(grads):
+            g_all[place * rows:(place + 1) * rows, :] = grad[...]
+        turned_grad = g_all[...].astype(f32).T
+    shares = [
+        turned_grad[low:low + HEAD_DIM, :] * inverse[low // HEAD_DIM:low // HEAD_DIM + 1, :]
+        for low in range(0, width, HEAD_DIM)
+    ]
+    g_t[...] = jnp.concatenate(shares, axis=0).astype(bf16)
+    g_wide = g_t[...].astype(f32)
+    g_all[...] = g_wide.T.astype(bf16)
+    product = g_wide * att_t[...].astype(bf16).astype(f32)
     tile = head_tile(width)
-    g_t = g_all[...].astype(f32).T
-    product = g_t * att_t[...].astype(bf16).astype(f32)
     for start in range(0, tokens, query_tile):
         span = slice(start, start + query_tile)
         for at in range(0, width, tile):
@@ -316,19 +327,17 @@
                 low = at + which * HEAD_DIM
                 head = low // HEAD_DIM
                 delta = jnp.sum(product[low:low + HEAD_DIM, span], axis=0, keepdims=True)
-                q_head = only_head(q_all[span, at:at + tile], which)
-                g_head = only_head(g_all[span, at:at + tile], which)
-                scores = dot_nt(k_all[:, at:at + tile], q_head)
-                probs = jnp.exp2(
-                    scores * log2_scale + bias[:, span] - lse[head:head + 1, span]
+                grad_probs = dot_nn(
+                    only_head(v_all[:, at:at + tile], which), g_t[at:at + tile, span]
                 )
-                grad_probs = dot_nt(v_all[:, at:at + tile], g_head)
-                grad_scores = (probs * (grad_probs - delta)).astype(bf16)
-                dk_head = dot_nn(grad_scores, q_head)
-                dv_head = dot_nn(probs.astype(bf16), g_head)
+                expo = weights[head * tokens:(head + 1) * tokens, span]
+                grad_scores = (expo.astype(f32) * (grad_probs - delta)).astype(bf16)
+                dk_head = dot_nn(grad_scores, only_head(q_all[span, at:at + tile], which))
+                dv_head = dot_nn(expo, only_head(g_all[span, at:at + tile], which))
                 dk_tile = dk_head if dk_tile is None else dk_tile + dk_head
                 dv_tile = dv_head if dv_tile is None else dv_tile + dv_head
-                dq_t[low:low + HEAD_DIM, span] = dot_nn(k_t[low:low + HEAD_DIM, :], grad_scores)
+                dq_head = dot_nn(k_t[low:low + HEAD_DIM, :], grad_scores)
+                dq_t[low:low + HEAD_DIM, span] = dq_head
             if start == 0:
                 dk[:, at:at + tile] = dk_tile
                 dv[:, at:at + tile] = dv_tile
@@ -345,16 +354,17 @@
             outs[place][3 * rows:, :] = attended[place][...]
 
 
-def backward(cycle, inputs, grads, attended, after):
+def backward(cycle, inputs, grads, attended):
     tokens, width = inputs[0].shape
     rows = tokens // cycle
     return pl.pallas_call(
         functools.partial(backward_kernel, cycle, min(tokens, 512), len(grads), len(attended)),
         out_shape=[jax.ShapeDtypeStruct(((4 if attended else 3) * rows, width), bf16)] * cycle,
-        in_specs=[vmem()] * (len(inputs) + len(grads) + len(attended)) + [unread()] * len(after),
+        in_specs=[vmem()] * (len(inputs) + len(grads) + len(attended)),
         out_specs=[vmem()] * cycle,
         scratch_shapes=[
             pltpu.VMEM((tokens, width), bf16),
+            pltpu.VMEM((width, tokens), bf16),
             pltpu.VMEM((width, tokens), f32),
             pltpu.VMEM((tokens, width), f32),
             pltpu.VMEM((tokens, width), f32),
@@ -362,7 +372,7 @@
         compiler_params=params(16 if tokens <= 512 else 60),
         cost_estimate=cost(3),
         name="backward",
-    )(*inputs, *grads, *attended, *after)
+    )(*inputs, *grads, *attended)
 
 
 def fetch_rows(out_weight, place):
@@ -395,14 +405,14 @@
     ups, out = refs[:count], refs[-1]
     _, _, core = my_place()
     weight = rows_in_order(refs[count], refs[count + 1:count + 2], core)
-    out[...] = dot_nt(jnp.concatenate([ref[...] for ref in ups], axis=0), weight).astype(bf16)
+    out[...] = dot_nt(weight, jnp.concatenate([ref[...] for ref in ups], axis=0)).astype(bf16)
 
 
 def group_grads(upstreams, pieces, after):
     rows, width = upstreams[0].shape[0], 2 * pieces[0].shape[0]
     return pl.pallas_call(
         functools.partial(group_kernel, len(upstreams)),
-        out_shape=jax.ShapeDtypeStruct((len(upstreams) * rows, width), bf16),
+        out_shape=jax.ShapeDtypeStruct((width, len(upstreams) * rows), bf16),
         in_specs=[vmem()] * (len(upstreams) + 2) + [unread()] * len(after),
         out_specs=vmem(),
         compiler_params=params(8),
@@ -575,10 +585,10 @@
     for place in range(cycle):
         halves += with_other_core(fetch_rows(out_weight, place))
     q_all, k_all, v_all, k_t, v_t, bias = gather(cycle, chunks)
-    attended, att_t, lse = forward(cycle, 1, q_all, k_all, v_t, bias)
+    attended, att_t, inverse, weights = forward(cycle, 1, q_all, k_all, v_t, bias)
     grads = swapped(project_grad(cycle, upstream, halves))
-    inputs = (q_all, k_all, v_all, k_t, bias, att_t, lse)
-    terms = swapped(backward(cycle, inputs, grads, attended, []))
+    inputs = (q_all, k_all, v_all, k_t, att_t, inverse, weights)
+    terms = swapped(backward(cycle, inputs, grads, attended))
     return tuple(finish(cycle, rows, terms, halves)[:4])
 
 
@@ -589,12 +599,14 @@
     across = exchange_by_core(passed, (1, 2))
     own_rows = with_other_core(fetch_rows(held_weight, 0))
     q_all, k_all, v_all, k_t, v_t, bias = gather(cycle, chunks)
-    (attended,), att_t, lse = forward(cycle, cycle, q_all, k_all, v_t, bias, [across])
+    (attended,), att_t, inverse, weights = forward(
+        cycle, cycle, q_all, k_all, v_t, bias, [across]
+    )
     own_mixed, kept, sent = partials(attended, own_rows, [])
     landed = exchange_by_core(sent, (2, 1))
     grads = [group_grads((upstream, *nexts, across), own_rows, [kept])]
-    inputs = (q_all, k_all, v_all, k_t, bias, att_t, lse)
-    terms = swapped(list(backward(cycle, inputs, grads, [], [])))
+    inputs = (q_all, k_all, v_all, k_t, att_t, inverse, weights)
+    terms = swapped(list(backward(cycle, inputs, grads, [])))
     own_mixed, *next_mixed = combine(own_mixed, kept, landed)
     next_mixed = [exchange_by_core(part, (1, 2)) for part in next_mixed]
     *grads, word = finish(cycle, rows, terms, [])

time: 46.2 us -> 46.9 us (1.015)
  the two profiles are of different devices: /device:TPU:0 before, /device:TPU:1 now
where the time goes in v15:
time: 46.9 us; the launch traced here: 46.8 us
  starting transfers between devices  18.2 us (39%)
  waiting for transfers between devices  17.2 us (37%)
  Pallas kernels  9.87 us (21%)
  between operations  1.42 us (3%)
    ppermute x12, waiting for transfers between devices, exchange_by_core(): return lax.ppermute(value, ('seq', 'mp'), pairs)  17.2 us
    ppermute x12, starting transfers between devices, exchange_by_core(): return lax.ppermute(value, ('seq', 'mp'), pairs)  15.8 us
    pallas_call x1, Pallas kernels, backward(): pl.pallas_call(functools.partial(backward_kernel, cycle, min(tokens, 512)...  2.36 us
    pallas_call x1, Pallas kernels, pack(): pl.pallas_call(functools.partial(pack_kernel, cycle, places), out_shape=[...  2.24 us
    pallas_call x1, Pallas kernels, forward(): pl.pallas_call(functools.partial(forward_kernel, min(tokens, 512), parts)...  2.19 us
    ppermute x1, starting transfers between devices, exchange(): return lax.ppermute(value, axis, [(i, i ^ distance) for i in range(count)])  1.73 us
    pallas_call x1, Pallas kernels, finish(): pl.pallas_call(functools.partial(finish_kernel, cycle), out_shape=[jax.Sh...  0.97 us
  transfers between devices with their start and end apart: 14, of which 7 were waited for; matrix products, arithmetic and copies ran while one was open for 0% of the time, Pallas kernels for 19%

profile of v15, /device:TPU:1, one launch (start us, length us, event | category | flops | bytes accessed | tf_op | source)
XLA Modules:
  0.0 46.8 jit_solution(8218456223630339999)
XLA Ops:
  0.6 2.1 %collective-permute-start.3 = (bf16[128,1024]{1,0:T(8,128)(2,1)}, bf16[128,1024]{1,0:T(8,128)(2,1)S(1)}, u32[]{:S(2)}, u32[]{:S(2)}) collective-permute-start(bf16[128,1024]{1,0:T(8,128)(2,1)} %refs_0_.3), channel_id=1, source_target_pairs={{0,16},{1,9},{2,18},{3,11},{4,20},{5,13},{6,22},{7,15},{8,24},{9,1... | collective-permute-start | bytes 786440 | tf_op jit(solution)/shard_map/ppermute | solution.py:66
  2.7 1.2 %collective-permute-start.4 = (bf16[128,1024]{1,0:T(8,128)(2,1)}, bf16[128,1024]{1,0:T(8,128)(2,1)S(1)}, u32[]{:S(2)}, u32[]{:S(2)}) collective-permute-start(bf16[128,1024]{1,0:T(8,128)(2,1)} %refs_0_.3), channel_id=1, source_target_pairs={{0,8},{1,17},{2,10},{3,19},{4,12},{5,21},{6,14},{7,23},{8,0},{9,25... | collective-permute-start | bytes 786440 | tf_op jit(solution)/shard_map/ppermute | solution.py:66
  4.6 2.2 %pack.1 = (bf16[416,256]{1,0:T(8,128)(2,1)}, bf16[416,256]{1,0:T(8,128)(2,1)}, bf16[416,256]{1,0:T(8,128)(2,1)}, bf16[416,256]{1,0:T(8,128)(2,1)}) custom-call(bf16[128,1024]{1,0:T(8,128)(2,1)} %q_ref.1, bf16[128,1024]{1,0:T(8,128)(2,1)} %k_ref.1, bf16[128,1024]{1,0:T(8,128)(2,1)} %v_ref.1, s32[1,4]{1,0:T(1,128)} %adj_any.1, s32[1,1]{1,0:T(1,128)} %bitcast.1.cnt_any), custom_call_target="tpu_custom_call" | custom-call | flops 5000000000 | tf_op jit(solution)/shard_map/pack/pallas_call | solution.py:177
  7.3 2.3 %collective-permute-start.2 = (bf16[416,256]{1,0:T(8,128)(2,1)}, bf16[416,256]{1,0:T(8,128)(2,1)S(1)}, u32[]{:S(2)}, u32[]{:S(2)}) collective-permute-start(bf16[416,256]{1,0:T(8,128)(2,1)} %get-tuple-element.37), channel_id=1, source_target_pairs={{0,24},{1,25},{2,26},{3,27},{4,28},{5,29},{6,30},{7,31},{8,16},{9,... | collective-permute-start | bytes 638984 | tf_op jit(solution)/shard_map/ppermute | solution.py:66
  9.6 0.8 %collective-permute-done.4.refs_2_.refs_1_ = bf16[128,1024]{1,0:T(8,128)(2,1)S(1)} collective-permute-done((bf16[128,1024]{1,0:T(8,128)(2,1)}, bf16[128,1024]{1,0:T(8,128)(2,1)S(1)}, u32[]{:S(2)}, u32[]{:S(2)}) %collective-permute-start.4) | collective-permute-done | bytes 262176 | tf_op jit(solution)/shard_map/ppermute | solution.py:66
  10.5 2.2 %collective-permute-start.5 = (bf16[128,1024]{1,0:T(8,128)(2,1)S(1)}, bf16[128,1024]{1,0:T(8,128)(2,1)S(1)}, u32[]{:S(2)}, u32[]{:S(2)}) collective-permute-start(bf16[128,1024]{1,0:T(8,128)(2,1)S(1)} %get-tuple-element.42), channel_id=1, source_target_pairs={{0,8},{1,17},{2,10},{3,19},{4,12},{5,21},{6,14},{7,23},{8,0},{9,25... | collective-permute-start | bytes 786440 | tf_op jit(solution)/shard_map/ppermute | solution.py:66
  12.6 0.7 %collective-permute-start.6 = (bf16[128,1024]{1,0:T(8,128)(2,1)S(1)}, bf16[128,1024]{1,0:T(8,128)(2,1)S(1)}, u32[]{:S(2)}, u32[]{:S(2)}) collective-permute-start(bf16[128,1024]{1,0:T(8,128)(2,1)S(1)} %get-tuple-element.44), channel_id=1, source_target_pairs={{0,0},{1,1},{4,2},{5,3},{2,4},{3,5},{6,6},{7,7},{12,8},{13,9},{10,... | collective-permute-start | bytes 786440 | tf_op jit(solution)/shard_map/ppermute | solution.py:385
  13.3 6.2 %collective-permute-done.refs_1_ = bf16[416,256]{1,0:T(8,128)(2,1)S(1)} collective-permute-done((bf16[416,256]{1,0:T(8,128)(2,1)}, bf16[416,256]{1,0:T(8,128)(2,1)S(1)}, u32[]{:S(2)}, u32[]{:S(2)}) %collective-permute-start) | collective-permute-done | bytes 213024 | tf_op jit(solution)/shard_map/ppermute | solution.py:66
  20.2 1.7 %collective-permute-start.7 = (bf16[128,1024]{1,0:T(8,128)(2,1)S(1)}, bf16[128,1024]{1,0:T(8,128)(2,1)S(1)}, u32[]{:S(2)}, u32[]{:S(2)}) collective-permute-start(bf16[128,1024]{1,0:T(8,128)(2,1)S(1)} %collective-permute-done.6.mine.refs_4_), channel_id=1, source_target_pairs={{0,1},{1,0},{2,3},{3,2},{4,5},{5,4},{6,7},{7,6},{8,9},{9,8},{10,11... | collective-permute-start | bytes 786440 | tf_op jit(solution)/shard_map/ppermute | solution.py:52
  21.9 0.4 collective-permute-done.5.refs_0_.refs_3_
  22.3 2.2 %forward.1 = (bf16[512,256]{1,0:T(8,128)(2,1)S(1)}, f32[256,512]{1,0:T(8,128)S(1)}, f32[8,512]{1,0:T(8,128)S(1)}, bf16[2048,512]{1,0:T(8,128)(2,1)S(1)}) custom-call(bf16[512,256]{1,0:T(8,128)(2,1)S(1)} %get-tuple-element.38.q_all.refs_0_, bf16[512,256]{1,0:T(8,128)(2,1)S(1)} %get-tuple-element.39.k_all.refs_1_, bf16[256,512]{1,0:T(8,128)(2,1)S(1)} %get-tuple-element.40.v_t, ...), custom_call_target="tpu_custom_call" | custom-call | flops 3000000000 | tf_op jit(solution)/shard_map/forward/pallas_call | solution.py:281
  24.6 0.4 partials.1
  25.0 1.5 %collective-permute-start.8 = (bf16[256,1024]{1,0:T(8,128)(2,1)S(1)}, bf16[256,1024]{1,0:T(8,128)(2,1)S(1)}, u32[]{:S(2)}, u32[]{:S(2)}) collective-permute-start(bf16[256,1024]{1,0:T(8,128)(2,1)S(1)} %get-tuple-element.47), channel_id=1, source_target_pairs={{0,16},{1,9},{2,18},{3,11},{4,20},{5,13},{6,22},{7,15},{8,24},{9,1... | collective-permute-start | bytes 1572872 | tf_op jit(solution)/shard_map/ppermute | solution.py:66
  26.5 0.5 %group_grads.1.refs_7_ = bf16[256,512]{1,0:T(8,128)(2,1)S(1)} custom-call(bf16[128,1024]{1,0:T(8,128)(2,1)S(1)} %copy-done.1, bf16[128,1024]{1,0:T(8,128)(2,1)S(1)} %collective-permute-done.4.refs_2_.refs_1_, bf16[128,1024]{1,0:T(8,128)(2,1)S(1)} %collective-permute-done.3.refs_1_.refs_2_, bf16[128,1024]{1,0:T(8,128)(2,1)S(1)} %collective-permute-done.5.refs_0_.refs_3_, ...), custom_call_target="tpu_custom_call" | custom-call | flops 1000000000 | tf_op jit(solution)/shard_map/group_grads/pallas_call | solution.py:413
  27.0 2.4 %backward.1 = (bf16[384,256]{1,0:T(8,128)(2,1)S(1)}, bf16[384,256]{1,0:T(8,128)(2,1)S(1)}, bf16[384,256]{1,0:T(8,128)(2,1)S(1)}, bf16[384,256]{1,0:T(8,128)(2,1)S(1)}) custom-call(bf16[512,256]{1,0:T(8,128)(2,1)S(1)} %get-tuple-element.38.q_all.refs_0_, bf16[512,256]{1,0:T(8,128)(2,1)S(1)} %get-tuple-element.39.k_all.refs_1_, ...), custom_call_target="tpu_custom_call" | custom-call | flops 3000000000 | tf_op jit(solution)/shard_map/backward/pallas_call | solution.py:360
  29.4 1.0 %collective-permute-start.11 = (bf16[384,256]{1,0:T(8,128)(2,1)S(1)}, bf16[384,256]{1,0:T(8,128)(2,1)S(1)}, u32[]{:S(2)}, u32[]{:S(2)}) collective-permute-start(bf16[384,256]{1,0:T(8,128)(2,1)S(1)} %get-tuple-element.57), channel_id=1, source_target_pairs={{0,8},{1,17},{2,10},{3,19},{4,12},{5,21},{6,14},{7,23},{8,0},{9,25... | collective-permute-start | bytes 589832 | tf_op jit(solution)/shard_map/ppermute | solution.py:66
  30.4 0.8 %collective-permute-start.12 = (bf16[384,256]{1,0:T(8,128)(2,1)S(1)}, bf16[384,256]{1,0:T(8,128)(2,1)S(1)}, u32[]{:S(2)}, u32[]{:S(2)}) collective-permute-start(bf16[384,256]{1,0:T(8,128)(2,1)S(1)} %get-tuple-element.58), channel_id=1, source_target_pairs={{0,16},{1,9},{2,18},{3,11},{4,20},{5,13},{6,22},{7,15},{8,24},{9,1... | collective-permute-start | bytes 589832 | tf_op jit(solution)/shard_map/ppermute | solution.py:66
  31.2 0.9 %collective-permute-start.13 = (bf16[384,256]{1,0:T(8,128)(2,1)S(1)}, bf16[384,256]{1,0:T(8,128)(2,1)S(1)}, u32[]{:S(2)}, u32[]{:S(2)}) collective-permute-start(bf16[384,256]{1,0:T(8,128)(2,1)S(1)} %get-tuple-element.59), channel_id=1, source_target_pairs={{0,24},{1,25},{2,26},{3,27},{4,28},{5,29},{6,30},{7,31},{8,16},{9,... | collective-permute-start | bytes 589832 | tf_op jit(solution)/shard_map/ppermute | solution.py:66
  32.1 1.8 %collective-permute-done.8.landed = bf16[256,1024]{1,0:T(8,128)(2,1)S(1)} collective-permute-done((bf16[256,1024]{1,0:T(8,128)(2,1)S(1)}, bf16[256,1024]{1,0:T(8,128)(2,1)S(1)}, u32[]{:S(2)}, u32[]{:S(2)}) %collective-permute-start.8) | collective-permute-done | bytes 524320 | tf_op jit(solution)/shard_map/ppermute | solution.py:66
  34.0 3.3 %collective-permute-start.9 = (bf16[64,1024]{1,0:T(8,128)(2,1)S(1)}, bf16[64,1024]{1,0:T(8,128)(2,1)S(1)}, u32[]{:S(2)}, u32[]{:S(2)}) collective-permute-start(bf16[64,1024]{1,0:T(8,128)(2,1)S(1)} %get-tuple-element.49), channel_id=1, source_target_pairs={{0,8},{1,17},{2,10},{3,19},{4,12},{5,21},{6,14},{7,23},{8,0},{9,25... | collective-permute-start | bytes 393224 | tf_op jit(solution)/shard_map/ppermute | solution.py:66
  37.4 0.7 %collective-permute-done.12.refs_2_ = bf16[384,256]{1,0:T(8,128)(2,1)S(1)} collective-permute-done((bf16[384,256]{1,0:T(8,128)(2,1)S(1)}, bf16[384,256]{1,0:T(8,128)(2,1)S(1)}, u32[]{:S(2)}, u32[]{:S(2)}) %collective-permute-start.12) | collective-permute-done | bytes 196640 | tf_op jit(solution)/shard_map/ppermute | solution.py:66
  38.1 6.9 %collective-permute-done.13.refs_3_ = bf16[384,256]{1,0:T(8,128)(2,1)S(1)} collective-permute-done((bf16[384,256]{1,0:T(8,128)(2,1)S(1)}, bf16[384,256]{1,0:T(8,128)(2,1)S(1)}, u32[]{:S(2)}, u32[]{:S(2)}) %collective-permute-start.13) | collective-permute-done | bytes 196640 | tf_op jit(solution)/shard_map/ppermute | solution.py:66
  45.0 1.0 %finish.1 = (bf16[128,1024]{1,0:T(8,128)(2,1)}, bf16[128,1024]{1,0:T(8,128)(2,1)}, bf16[128,1024]{1,0:T(8,128)(2,1)}, bf16[16,128]{1,0:T(8,128)(2,1)S(1)}) custom-call(bf16[384,256]{1,0:T(8,128)(2,1)S(1)} %get-tuple-element.56.refs_0_, bf16[384,256]{1,0:T(8,128)(2,1)S(1)} %collective-permute-done.11.refs_1_, ...), custom_call_target="tpu_custom_call" | custom-call | tf_op jit(solution)/shard_map/finish/pallas_call | solution.py:544
  46.0 0.8 %last_sum.1 = bf16[128,1024]{1,0:T(8,128)(2,1)} custom-call(f32[128,1024]{1,0:T(8,128)S(1)} %get-tuple-element.48.own, bf16[64,1024]{1,0:T(8,128)(2,1)S(1)} %collective-permute-done.9.refs_0_, bf16[64,1024]{1,0:T(8,128)(2,1)S(1)} %collective-permute-done.10.refs_1_, bf16[16,128]{1,0:T(8,128)(2,1)S(1)} %get-tuple-element.60.refs_2_), custom_call_target="tpu_custom_call" | custom-call | tf_op jit(solution)/shard_map/last_sum/pallas_call | solution.py:567
  (20 shorter events, 1.3 us)
Async XLA Ops:
  0.6 9.0 %collective-permute-start.3 = (bf16[128,1024]{1,0:T(8,128)(2,1)}, bf16[128,1024]{1,0:T(8,128)(2,1)S(1)}, u32[]{:S(2)}, u32[]{:S(2)}) collective-permute-start(bf16[128,1024]{1,0:T(8,128)(2,1)} %refs_0_.3), channel_id=1, source_target_pairs={{0,16},{1,9},{2,18},{3,11},{4,20},{5,13},{6,22},{7,15},{8,24},{9,1... | collective-permute-start | bytes 786440 | tf_op jit(solution)/shard_map/ppermute | solution.py:66
  2.7 7.7 %collective-permute-start.4 = (bf16[128,1024]{1,0:T(8,128)(2,1)}, bf16[128,1024]{1,0:T(8,128)(2,1)S(1)}, u32[]{:S(2)}, u32[]{:S(2)}) collective-permute-start(bf16[128,1024]{1,0:T(8,128)(2,1)} %refs_0_.3), channel_id=1, source_target_pairs={{0,8},{1,17},{2,10},{3,19},{4,12},{5,21},{6,14},{7,23},{8,0},{9,25... | collective-permute-start | bytes 786440 | tf_op jit(solution)/shard_map/ppermute | solution.py:66
  4.6 5.8 %copy-start = (bf16[128,1024]{1,0:T(8,128)(2,1)S(1)}, bf16[128,1024]{1,0:T(8,128)(2,1)}, u32[]{:S(2)}) copy-start(bf16[128,1024]{1,0:T(8,128)(2,1)} %refs_0_.2) | copy-start | bytes 786436
  6.9 13.0 %copy-start.2 = (bf16[416,256]{1,0:T(8,128)(2,1)S(1)}, bf16[416,256]{1,0:T(8,128)(2,1)}, u32[]{:S(2)}) copy-start(bf16[416,256]{1,0:T(8,128)(2,1)} %get-tuple-element.34.refs_0_) | copy-start | bytes 638980
  6.9 12.6 %collective-permute-start = (bf16[416,256]{1,0:T(8,128)(2,1)}, bf16[416,256]{1,0:T(8,128)(2,1)S(1)}, u32[]{:S(2)}, u32[]{:S(2)}) collective-permute-start(bf16[416,256]{1,0:T(8,128)(2,1)} %get-tuple-element.35), channel_id=1, source_target_pairs={{0,8},{1,17},{2,10},{3,19},{4,12},{5,21},{6,14},{7,23},{8,0},{9,25... | collective-permute-start | bytes 638984 | tf_op jit(solution)/shard_map/ppermute | solution.py:66
  7.2 12.3 %collective-permute-start.1 = (bf16[416,256]{1,0:T(8,128)(2,1)}, bf16[416,256]{1,0:T(8,128)(2,1)S(1)}, u32[]{:S(2)}, u32[]{:S(2)}) collective-permute-start(bf16[416,256]{1,0:T(8,128)(2,1)} %get-tuple-element.36), channel_id=1, source_target_pairs={{0,16},{1,9},{2,18},{3,11},{4,20},{5,13},{6,22},{7,15},{8,24},{9,1... | collective-permute-start | bytes 638984 | tf_op jit(solution)/shard_map/ppermute | solution.py:66
  7.3 12.6 %collective-permute-start.2 = (bf16[416,256]{1,0:T(8,128)(2,1)}, bf16[416,256]{1,0:T(8,128)(2,1)S(1)}, u32[]{:S(2)}, u32[]{:S(2)}) collective-permute-start(bf16[416,256]{1,0:T(8,128)(2,1)} %get-tuple-element.37), channel_id=1, source_target_pairs={{0,24},{1,25},{2,26},{3,27},{4,28},{5,29},{6,30},{7,31},{8,16},{9,... | collective-permute-start | bytes 638984 | tf_op jit(solution)/shard_map/ppermute | solution.py:66
  10.5 11.9 %collective-permute-start.5 = (bf16[128,1024]{1,0:T(8,128)(2,1)S(1)}, bf16[128,1024]{1,0:T(8,128)(2,1)S(1)}, u32[]{:S(2)}, u32[]{:S(2)}) collective-permute-start(bf16[128,1024]{1,0:T(8,128)(2,1)S(1)} %get-tuple-element.42), channel_id=1, source_target_pairs={{0,8},{1,17},{2,10},{3,19},{4,12},{5,21},{6,14},{7,23},{8,0},{9,25... | collective-permute-start | bytes 786440 | tf_op jit(solution)/shard_map/ppermute | solution.py:66
  12.6 7.5 %collective-permute-start.6 = (bf16[128,1024]{1,0:T(8,128)(2,1)S(1)}, bf16[128,1024]{1,0:T(8,128)(2,1)S(1)}, u32[]{:S(2)}, u32[]{:S(2)}) collective-permute-start(bf16[128,1024]{1,0:T(8,128)(2,1)S(1)} %get-tuple-element.44), channel_id=1, source_target_pairs={{0,0},{1,1},{4,2},{5,3},{2,4},{3,5},{6,6},{7,7},{12,8},{13,9},{10,... | collective-permute-start | bytes 786440 | tf_op jit(solution)/shard_map/ppermute | solution.py:385
  20.2 4.4 %collective-permute-start.7 = (bf16[128,1024]{1,0:T(8,128)(2,1)S(1)}, bf16[128,1024]{1,0:T(8,128)(2,1)S(1)}, u32[]{:S(2)}, u32[]{:S(2)}) collective-permute-start(bf16[128,1024]{1,0:T(8,128)(2,1)S(1)} %collective-permute-done.6.mine.refs_4_), channel_id=1, source_target_pairs={{0,1},{1,0},{2,3},{3,2},{4,5},{5,4},{6,7},{7,6},{8,9},{9,8},{10,11... | collective-permute-start | bytes 786440 | tf_op jit(solution)/shard_map/ppermute | solution.py:52
  24.5 2.0 %copy-start.1 = (bf16[128,1024]{1,0:T(8,128)(2,1)S(1)}, bf16[128,1024]{1,0:T(8,128)(2,1)}, u32[]{:S(2)}) copy-start(bf16[128,1024]{1,0:T(8,128)(2,1)} %refs_0_.3) | copy-start | bytes 786436
  25.0 8.9 %collective-permute-start.8 = (bf16[256,1024]{1,0:T(8,128)(2,1)S(1)}, bf16[256,1024]{1,0:T(8,128)(2,1)S(1)}, u32[]{:S(2)}, u32[]{:S(2)}) collective-permute-start(bf16[256,1024]{1,0:T(8,128)(2,1)S(1)} %get-tuple-element.47), channel_id=1, source_target_pairs={{0,16},{1,9},{2,18},{3,11},{4,20},{5,13},{6,22},{7,15},{8,24},{9,1... | collective-permute-start | bytes 1572872 | tf_op jit(solution)/shard_map/ppermute | solution.py:66
  29.4 8.1 %collective-permute-start.11 = (bf16[384,256]{1,0:T(8,128)(2,1)S(1)}, bf16[384,256]{1,0:T(8,128)(2,1)S(1)}, u32[]{:S(2)}, u32[]{:S(2)}) collective-permute-start(bf16[384,256]{1,0:T(8,128)(2,1)S(1)} %get-tuple-element.57), channel_id=1, source_target_pairs={{0,8},{1,17},{2,10},{3,19},{4,12},{5,21},{6,14},{7,23},{8,0},{9,25... | collective-permute-start | bytes 589832 | tf_op jit(solution)/shard_map/ppermute | solution.py:66
  30.4 7.7 %collective-permute-start.12 = (bf16[384,256]{1,0:T(8,128)(2,1)S(1)}, bf16[384,256]{1,0:T(8,128)(2,1)S(1)}, u32[]{:S(2)}, u32[]{:S(2)}) collective-permute-start(bf16[384,256]{1,0:T(8,128)(2,1)S(1)} %get-tuple-element.58), channel_id=1, source_target_pairs={{0,16},{1,9},{2,18},{3,11},{4,20},{5,13},{6,22},{7,15},{8,24},{9,1... | collective-permute-start | bytes 589832 | tf_op jit(solution)/shard_map/ppermute | solution.py:66
  31.2 13.8 %collective-permute-start.13 = (bf16[384,256]{1,0:T(8,128)(2,1)S(1)}, bf16[384,256]{1,0:T(8,128)(2,1)S(1)}, u32[]{:S(2)}, u32[]{:S(2)}) collective-permute-start(bf16[384,256]{1,0:T(8,128)(2,1)S(1)} %get-tuple-element.59), channel_id=1, source_target_pairs={{0,24},{1,25},{2,26},{3,27},{4,28},{5,29},{6,30},{7,31},{8,16},{9,... | collective-permute-start | bytes 589832 | tf_op jit(solution)/shard_map/ppermute | solution.py:66
  34.0 12.0 %collective-permute-start.9 = (bf16[64,1024]{1,0:T(8,128)(2,1)S(1)}, bf16[64,1024]{1,0:T(8,128)(2,1)S(1)}, u32[]{:S(2)}, u32[]{:S(2)}) collective-permute-start(bf16[64,1024]{1,0:T(8,128)(2,1)S(1)} %get-tuple-element.49), channel_id=1, source_target_pairs={{0,8},{1,17},{2,10},{3,19},{4,12},{5,21},{6,14},{7,23},{8,0},{9,25... | collective-permute-start | bytes 393224 | tf_op jit(solution)/shard_map/ppermute | solution.py:66
  37.3 8.7 %collective-permute-start.10 = (bf16[64,1024]{1,0:T(8,128)(2,1)S(1)}, bf16[64,1024]{1,0:T(8,128)(2,1)S(1)}, u32[]{:S(2)}, u32[]{:S(2)}) collective-permute-start(bf16[64,1024]{1,0:T(8,128)(2,1)S(1)} %get-tuple-element.50), channel_id=1, source_target_pairs={{0,8},{1,17},{2,10},{3,19},{4,12},{5,21},{6,14},{7,23},{8,0},{9,25... | collective-permute-start | bytes 393224 | tf_op jit(solution)/shard_map/ppermute | solution.py:66

commit v16 on v15

--- a/solution.py
+++ b/solution.py
@@ -595,13 +595,12 @@
 def square(cycle, rows, tensors, out_weight, upstream):
     nexts = swapped([upstream] * 3)[1:]
     chunks = swapped(list(pack(cycle, range(cycle), tensors)))
-    held_weight, passed = hold((out_weight, nexts[1]), [nexts[0]])
+    (held_weight,) = hold((out_weight,), nexts)
+    (passed,) = hold((nexts[1],), [chunks[1]])
     across = exchange_by_core(passed, (1, 2))
     own_rows = with_other_core(fetch_rows(held_weight, 0))
     q_all, k_all, v_all, k_t, v_t, bias = gather(cycle, chunks)
-    (attended,), att_t, inverse, weights = forward(
-        cycle, cycle, q_all, k_all, v_t, bias, [across]
-    )
+    (attended,), att_t, inverse, weights = forward(cycle, cycle, q_all, k_all, v_t, bias)
     own_mixed, kept, sent = partials(attended, own_rows, [])
     landed = exchange_by_core(sent, (2, 1))
     grads = [group_grads((upstream, *nexts, across), own_rows, [kept])]

time: 46.9 us -> 46.4 us (0.989)
  the two profiles are of different devices: /device:TPU:1 before, /device:TPU:0 now
where the time goes in v16:
time: 46.4 us; the launch traced here: 46.3 us
  starting transfers between devices  18.1 us (39%)
  waiting for transfers between devices  16.9 us (36%)
  Pallas kernels  9.89 us (21%)
  between operations  1.42 us (3%)
    ppermute x12, starting transfers between devices, exchange_by_core(): return lax.ppermute(value, ('seq', 'mp'), pairs)  17.4 us
    ppermute x12, waiting for transfers between devices, exchange_by_core(): return lax.ppermute(value, ('seq', 'mp'), pairs)  16.9 us
    pallas_call x1, Pallas kernels, backward(): pl.pallas_call(functools.partial(backward_kernel, cycle, min(tokens, 512)...  2.36 us
    pallas_call x1, Pallas kernels, pack(): pl.pallas_call(functools.partial(pack_kernel, cycle, places), out_shape=[...  2.24 us
    pallas_call x1, Pallas kernels, forward(): pl.pallas_call(functools.partial(forward_kernel, min(tokens, 512), parts)...  2.19 us
    pallas_call x1, Pallas kernels, finish(): pl.pallas_call(functools.partial(finish_kernel, cycle), out_shape=[jax.Sh...  0.97 us
  transfers between devices with their start and end apart: 14, of which 6 were waited for; matrix products, arithmetic and copies ran while one was open for 0% of the time, Pallas kernels for 20%

profile of v16, /device:TPU:0, one launch (start us, length us, event | category | flops | bytes accessed | tf_op | source)
XLA Modules:
  0.0 46.3 jit_solution(12884605955426818512)
XLA Ops:
  0.6 3.0 %collective-permute-start.3 = (bf16[128,1024]{1,0:T(8,128)(2,1)}, bf16[128,1024]{1,0:T(8,128)(2,1)S(1)}, u32[]{:S(2)}, u32[]{:S(2)}) collective-permute-start(bf16[128,1024]{1,0:T(8,128)(2,1)} %refs_0_.3), channel_id=1, source_target_pairs={{0,8},{1,17},{2,10},{3,19},{4,12},{5,21},{6,14},{7,23},{8,0},{9,25... | collective-permute-start | bytes 786440 | tf_op jit(solution)/shard_map/ppermute | solution.py:66
  3.6 1.5 %collective-permute-start.4 = (bf16[128,1024]{1,0:T(8,128)(2,1)}, bf16[128,1024]{1,0:T(8,128)(2,1)S(1)}, u32[]{:S(2)}, u32[]{:S(2)}) collective-permute-start(bf16[128,1024]{1,0:T(8,128)(2,1)} %refs_0_.3), channel_id=1, source_target_pairs={{0,16},{1,9},{2,18},{3,11},{4,20},{5,13},{6,22},{7,15},{8,24},{9,1... | collective-permute-start | bytes 786440 | tf_op jit(solution)/shard_map/ppermute | solution.py:66
  5.8 2.2 %pack.1 = (bf16[416,256]{1,0:T(8,128)(2,1)}, bf16[416,256]{1,0:T(8,128)(2,1)}, bf16[416,256]{1,0:T(8,128)(2,1)}, bf16[416,256]{1,0:T(8,128)(2,1)}) custom-call(bf16[128,1024]{1,0:T(8,128)(2,1)} %q_ref.1, bf16[128,1024]{1,0:T(8,128)(2,1)} %k_ref.1, bf16[128,1024]{1,0:T(8,128)(2,1)} %v_ref.1, s32[1,4]{1,0:T(1,128)} %adj_any.1, s32[1,1]{1,0:T(1,128)} %bitcast.1.cnt_any), custom_call_target="tpu_custom_call" | custom-call | flops 5000000000 | tf_op jit(solution)/shard_map/pack/pallas_call | solution.py:177
  8.1 0.6 %collective-permute-start = (bf16[416,256]{1,0:T(8,128)(2,1)}, bf16[416,256]{1,0:T(8,128)(2,1)S(1)}, u32[]{:S(2)}, u32[]{:S(2)}) collective-permute-start(bf16[416,256]{1,0:T(8,128)(2,1)} %get-tuple-element.33), channel_id=1, source_target_pairs={{0,8},{1,17},{2,10},{3,19},{4,12},{5,21},{6,14},{7,23},{8,0},{9,25... | collective-permute-start | bytes 638984 | tf_op jit(solution)/shard_map/ppermute | solution.py:66
  8.7 2.9 %collective-permute-start.2 = (bf16[416,256]{1,0:T(8,128)(2,1)}, bf16[416,256]{1,0:T(8,128)(2,1)S(1)}, u32[]{:S(2)}, u32[]{:S(2)}) collective-permute-start(bf16[416,256]{1,0:T(8,128)(2,1)} %get-tuple-element.35), channel_id=1, source_target_pairs={{0,24},{1,25},{2,26},{3,27},{4,28},{5,29},{6,30},{7,31},{8,16},{9,... | collective-permute-start | bytes 638984 | tf_op jit(solution)/shard_map/ppermute | solution.py:66
  11.7 0.7 %collective-permute-start.5 = (bf16[128,1024]{1,0:T(8,128)(2,1)S(1)}, bf16[128,1024]{1,0:T(8,128)(2,1)S(1)}, u32[]{:S(2)}, u32[]{:S(2)}) collective-permute-start(bf16[128,1024]{1,0:T(8,128)(2,1)S(1)} %hold.2), channel_id=1, source_target_pairs={{0,0},{1,1},{4,2},{5,3},{2,4},{3,5},{6,6},{7,7},{12,8},{13,9},{10,... | collective-permute-start | bytes 786440 | tf_op jit(solution)/shard_map/ppermute | solution.py:385
  12.4 4.2 %collective-permute-done.refs_1_ = bf16[416,256]{1,0:T(8,128)(2,1)S(1)} collective-permute-done((bf16[416,256]{1,0:T(8,128)(2,1)}, bf16[416,256]{1,0:T(8,128)(2,1)S(1)}, u32[]{:S(2)}, u32[]{:S(2)}) %collective-permute-start) | collective-permute-done | bytes 213024 | tf_op jit(solution)/shard_map/ppermute | solution.py:66
  16.5 4.0 %collective-permute-done.2.refs_3_ = bf16[416,256]{1,0:T(8,128)(2,1)S(1)} collective-permute-done((bf16[416,256]{1,0:T(8,128)(2,1)}, bf16[416,256]{1,0:T(8,128)(2,1)S(1)}, u32[]{:S(2)}, u32[]{:S(2)}) %collective-permute-start.2) | collective-permute-done | bytes 213024 | tf_op jit(solution)/shard_map/ppermute | solution.py:66
  20.9 1.7 %collective-permute-start.10 = (bf16[128,1024]{1,0:T(8,128)(2,1)S(1)}, bf16[128,1024]{1,0:T(8,128)(2,1)S(1)}, u32[]{:S(2)}, u32[]{:S(2)}) collective-permute-start(bf16[128,1024]{1,0:T(8,128)(2,1)S(1)} %hold.3), channel_id=1, source_target_pairs={{0,8},{1,17},{2,10},{3,19},{4,12},{5,21},{6,14},{7,23},{8,0},{9,25... | collective-permute-start | bytes 786440 | tf_op jit(solution)/shard_map/ppermute | solution.py:66
  22.6 2.2 %forward.1 = (bf16[512,256]{1,0:T(8,128)(2,1)S(1)}, f32[256,512]{1,0:T(8,128)S(1)}, f32[8,512]{1,0:T(8,128)S(1)}, bf16[2048,512]{1,0:T(8,128)(2,1)S(1)}) custom-call(bf16[512,256]{1,0:T(8,128)(2,1)S(1)} %get-tuple-element.36.q_all.refs_0_, bf16[512,256]{1,0:T(8,128)(2,1)S(1)} %get-tuple-element.37.k_all.refs_1_, bf16[256,512]{1,0:T(8,128)(2,1)S(1)} %get-tuple-element.38.v_t, ...), custom_call_target="tpu_custom_call" | custom-call | flops 3000000000 | tf_op jit(solution)/shard_map/forward/pallas_call | solution.py:281
  24.8 0.4 partials.1
  25.3 1.4 %collective-permute-start.7 = (bf16[256,1024]{1,0:T(8,128)(2,1)S(1)}, bf16[256,1024]{1,0:T(8,128)(2,1)S(1)}, u32[]{:S(2)}, u32[]{:S(2)}) collective-permute-start(bf16[256,1024]{1,0:T(8,128)(2,1)S(1)} %get-tuple-element.43), channel_id=1, source_target_pairs={{0,16},{1,9},{2,18},{3,11},{4,20},{5,13},{6,22},{7,15},{8,24},{9,1... | collective-permute-start | bytes 1572872 | tf_op jit(solution)/shard_map/ppermute | solution.py:66
  26.6 0.7 %collective-permute-done.10.refs_3_ = bf16[128,1024]{1,0:T(8,128)(2,1)S(1)} collective-permute-done((bf16[128,1024]{1,0:T(8,128)(2,1)S(1)}, bf16[128,1024]{1,0:T(8,128)(2,1)S(1)}, u32[]{:S(2)}, u32[]{:S(2)}) %collective-permute-start.10) | collective-permute-done | bytes 262176 | tf_op jit(solution)/shard_map/ppermute | solution.py:66
  27.3 0.5 %group_grads.1.refs_7_ = bf16[256,512]{1,0:T(8,128)(2,1)S(1)} custom-call(bf16[128,1024]{1,0:T(8,128)(2,1)S(1)} %copy-done.1, bf16[128,1024]{1,0:T(8,128)(2,1)S(1)} %collective-permute-done.3.refs_1_, bf16[128,1024]{1,0:T(8,128)(2,1)S(1)} %collective-permute-done.4.refs_2_.refs_0_, bf16[128,1024]{1,0:T(8,128)(2,1)S(1)} %collective-permute-done.10.refs_3_, ...), custom_call_target="tpu_custom_call" | custom-call | flops 1000000000 | tf_op jit(solution)/shard_map/group_grads/pallas_call | solution.py:413
  27.8 2.4 %backward.1 = (bf16[384,256]{1,0:T(8,128)(2,1)S(1)}, bf16[384,256]{1,0:T(8,128)(2,1)S(1)}, bf16[384,256]{1,0:T(8,128)(2,1)S(1)}, bf16[384,256]{1,0:T(8,128)(2,1)S(1)}) custom-call(bf16[512,256]{1,0:T(8,128)(2,1)S(1)} %get-tuple-element.36.q_all.refs_0_, bf16[512,256]{1,0:T(8,128)(2,1)S(1)} %get-tuple-element.37.k_all.refs_1_, ...), custom_call_target="tpu_custom_call" | custom-call | flops 3000000000 | tf_op jit(solution)/shard_map/backward/pallas_call | solution.py:360
  30.2 1.7 %collective-permute-start.11 = (bf16[384,256]{1,0:T(8,128)(2,1)S(1)}, bf16[384,256]{1,0:T(8,128)(2,1)S(1)}, u32[]{:S(2)}, u32[]{:S(2)}) collective-permute-start(bf16[384,256]{1,0:T(8,128)(2,1)S(1)} %get-tuple-element.53), channel_id=1, source_target_pairs={{0,8},{1,17},{2,10},{3,19},{4,12},{5,21},{6,14},{7,23},{8,0},{9,25... | collective-permute-start | bytes 589832 | tf_op jit(solution)/shard_map/ppermute | solution.py:66
  31.9 1.3 %collective-permute-start.12 = (bf16[384,256]{1,0:T(8,128)(2,1)S(1)}, bf16[384,256]{1,0:T(8,128)(2,1)S(1)}, u32[]{:S(2)}, u32[]{:S(2)}) collective-permute-start(bf16[384,256]{1,0:T(8,128)(2,1)S(1)} %get-tuple-element.54), channel_id=1, source_target_pairs={{0,16},{1,9},{2,18},{3,11},{4,20},{5,13},{6,22},{7,15},{8,24},{9,1... | collective-permute-start | bytes 589832 | tf_op jit(solution)/shard_map/ppermute | solution.py:66
  33.2 0.5 %collective-permute-start.13 = (bf16[384,256]{1,0:T(8,128)(2,1)S(1)}, bf16[384,256]{1,0:T(8,128)(2,1)S(1)}, u32[]{:S(2)}, u32[]{:S(2)}) collective-permute-start(bf16[384,256]{1,0:T(8,128)(2,1)S(1)} %get-tuple-element.55), channel_id=1, source_target_pairs={{0,24},{1,25},{2,26},{3,27},{4,28},{5,29},{6,30},{7,31},{8,16},{9,... | collective-permute-start | bytes 589832 | tf_op jit(solution)/shard_map/ppermute | solution.py:66
  33.7 2.3 %collective-permute-done.7.landed = bf16[256,1024]{1,0:T(8,128)(2,1)S(1)} collective-permute-done((bf16[256,1024]{1,0:T(8,128)(2,1)S(1)}, bf16[256,1024]{1,0:T(8,128)(2,1)S(1)}, u32[]{:S(2)}, u32[]{:S(2)}) %collective-permute-start.7) | collective-permute-done | bytes 524320 | tf_op jit(solution)/shard_map/ppermute | solution.py:66
  36.1 2.6 %collective-permute-start.8 = (bf16[64,1024]{1,0:T(8,128)(2,1)S(1)}, bf16[64,1024]{1,0:T(8,128)(2,1)S(1)}, u32[]{:S(2)}, u32[]{:S(2)}) collective-permute-start(bf16[64,1024]{1,0:T(8,128)(2,1)S(1)} %get-tuple-element.45), channel_id=1, source_target_pairs={{0,8},{1,17},{2,10},{3,19},{4,12},{5,21},{6,14},{7,23},{8,0},{9,25... | collective-permute-start | bytes 393224 | tf_op jit(solution)/shard_map/ppermute | solution.py:66
  38.8 5.4 %collective-permute-done.12.refs_2_ = bf16[384,256]{1,0:T(8,128)(2,1)S(1)} collective-permute-done((bf16[384,256]{1,0:T(8,128)(2,1)S(1)}, bf16[384,256]{1,0:T(8,128)(2,1)S(1)}, u32[]{:S(2)}, u32[]{:S(2)}) %collective-permute-start.12) | collective-permute-done | bytes 196640 | tf_op jit(solution)/shard_map/ppermute | solution.py:66
  44.2 1.0 %finish.1 = (bf16[128,1024]{1,0:T(8,128)(2,1)}, bf16[128,1024]{1,0:T(8,128)(2,1)}, bf16[128,1024]{1,0:T(8,128)(2,1)}, bf16[16,128]{1,0:T(8,128)(2,1)S(1)}) custom-call(bf16[384,256]{1,0:T(8,128)(2,1)S(1)} %get-tuple-element.52.refs_0_, bf16[384,256]{1,0:T(8,128)(2,1)S(1)} %collective-permute-done.11.refs_1_, ...), custom_call_target="tpu_custom_call" | custom-call | tf_op jit(solution)/shard_map/finish/pallas_call | solution.py:544
  45.2 0.3 collective-permute-done.9.refs_1_
  45.5 0.8 %last_sum.1 = bf16[128,1024]{1,0:T(8,128)(2,1)} custom-call(f32[128,1024]{1,0:T(8,128)S(1)} %get-tuple-element.44.own, bf16[64,1024]{1,0:T(8,128)(2,1)S(1)} %collective-permute-done.8.refs_0_, bf16[64,1024]{1,0:T(8,128)(2,1)S(1)} %collective-permute-done.9.refs_1_, bf16[16,128]{1,0:T(8,128)(2,1)S(1)} %get-tuple-element.56.refs_2_), custom_call_target="tpu_custom_call" | custom-call | tf_op jit(solution)/shard_map/last_sum/pallas_call | solution.py:567
  (21 shorter events, 0.6 us)
Async XLA Ops:
  0.6 11.0 %collective-permute-start.3 = (bf16[128,1024]{1,0:T(8,128)(2,1)}, bf16[128,1024]{1,0:T(8,128)(2,1)S(1)}, u32[]{:S(2)}, u32[]{:S(2)}) collective-permute-start(bf16[128,1024]{1,0:T(8,128)(2,1)} %refs_0_.3), channel_id=1, source_target_pairs={{0,8},{1,17},{2,10},{3,19},{4,12},{5,21},{6,14},{7,23},{8,0},{9,25... | collective-permute-start | bytes 786440 | tf_op jit(solution)/shard_map/ppermute | solution.py:66
  3.6 8.0 %collective-permute-start.4 = (bf16[128,1024]{1,0:T(8,128)(2,1)}, bf16[128,1024]{1,0:T(8,128)(2,1)S(1)}, u32[]{:S(2)}, u32[]{:S(2)}) collective-permute-start(bf16[128,1024]{1,0:T(8,128)(2,1)} %refs_0_.3), channel_id=1, source_target_pairs={{0,16},{1,9},{2,18},{3,11},{4,20},{5,13},{6,22},{7,15},{8,24},{9,1... | collective-permute-start | bytes 786440 | tf_op jit(solution)/shard_map/ppermute | solution.py:66
  5.8 5.8 %copy-start = (bf16[128,1024]{1,0:T(8,128)(2,1)S(1)}, bf16[128,1024]{1,0:T(8,128)(2,1)}, u32[]{:S(2)}) copy-start(bf16[128,1024]{1,0:T(8,128)(2,1)} %refs_0_.2) | copy-start | bytes 786436
  8.1 12.5 %copy-start.2 = (bf16[416,256]{1,0:T(8,128)(2,1)S(1)}, bf16[416,256]{1,0:T(8,128)(2,1)}, u32[]{:S(2)}) copy-start(bf16[416,256]{1,0:T(8,128)(2,1)} %get-tuple-element.32.refs_0_) | copy-start | bytes 638980
  8.1 8.5 %collective-permute-start = (bf16[416,256]{1,0:T(8,128)(2,1)}, bf16[416,256]{1,0:T(8,128)(2,1)S(1)}, u32[]{:S(2)}, u32[]{:S(2)}) collective-permute-start(bf16[416,256]{1,0:T(8,128)(2,1)} %get-tuple-element.33), channel_id=1, source_target_pairs={{0,8},{1,17},{2,10},{3,19},{4,12},{5,21},{6,14},{7,23},{8,0},{9,25... | collective-permute-start | bytes 638984 | tf_op jit(solution)/shard_map/ppermute | solution.py:66
  8.7 7.9 %collective-permute-start.1 = (bf16[416,256]{1,0:T(8,128)(2,1)}, bf16[416,256]{1,0:T(8,128)(2,1)S(1)}, u32[]{:S(2)}, u32[]{:S(2)}) collective-permute-start(bf16[416,256]{1,0:T(8,128)(2,1)} %get-tuple-element.34), channel_id=1, source_target_pairs={{0,16},{1,9},{2,18},{3,11},{4,20},{5,13},{6,22},{7,15},{8,24},{9,1... | collective-permute-start | bytes 638984 | tf_op jit(solution)/shard_map/ppermute | solution.py:66
  8.7 11.8 %collective-permute-start.2 = (bf16[416,256]{1,0:T(8,128)(2,1)}, bf16[416,256]{1,0:T(8,128)(2,1)S(1)}, u32[]{:S(2)}, u32[]{:S(2)}) collective-permute-start(bf16[416,256]{1,0:T(8,128)(2,1)} %get-tuple-element.35), channel_id=1, source_target_pairs={{0,24},{1,25},{2,26},{3,27},{4,28},{5,29},{6,30},{7,31},{8,16},{9,... | collective-permute-start | bytes 638984 | tf_op jit(solution)/shard_map/ppermute | solution.py:66
  11.7 10.9 %collective-permute-start.5 = (bf16[128,1024]{1,0:T(8,128)(2,1)S(1)}, bf16[128,1024]{1,0:T(8,128)(2,1)S(1)}, u32[]{:S(2)}, u32[]{:S(2)}) collective-permute-start(bf16[128,1024]{1,0:T(8,128)(2,1)S(1)} %hold.2), channel_id=1, source_target_pairs={{0,0},{1,1},{4,2},{5,3},{2,4},{3,5},{6,6},{7,7},{12,8},{13,9},{10,... | collective-permute-start | bytes 786440 | tf_op jit(solution)/shard_map/ppermute | solution.py:385
  20.9 6.4 %collective-permute-start.10 = (bf16[128,1024]{1,0:T(8,128)(2,1)S(1)}, bf16[128,1024]{1,0:T(8,128)(2,1)S(1)}, u32[]{:S(2)}, u32[]{:S(2)}) collective-permute-start(bf16[128,1024]{1,0:T(8,128)(2,1)S(1)} %hold.3), channel_id=1, source_target_pairs={{0,8},{1,17},{2,10},{3,19},{4,12},{5,21},{6,14},{7,23},{8,0},{9,25... | collective-permute-start | bytes 786440 | tf_op jit(solution)/shard_map/ppermute | solution.py:66
  22.6 2.2 %collective-permute-start.6 = (bf16[128,1024]{1,0:T(8,128)(2,1)S(1)}, bf16[128,1024]{1,0:T(8,128)(2,1)S(1)}, u32[]{:S(2)}, u32[]{:S(2)}) collective-permute-start(bf16[128,1024]{1,0:T(8,128)(2,1)S(1)} %collective-permute-done.5.mine.refs_4_), channel_id=1, source_target_pairs={{0,1},{1,0},{2,3},{3,2},{4,5},{5,4},{6,7},{7,6},{8,9},{9,8},{10,11... | collective-permute-start | bytes 786440 | tf_op jit(solution)/shard_map/ppermute | solution.py:52
  24.8 2.5 %copy-start.1 = (bf16[128,1024]{1,0:T(8,128)(2,1)S(1)}, bf16[128,1024]{1,0:T(8,128)(2,1)}, u32[]{:S(2)}) copy-start(bf16[128,1024]{1,0:T(8,128)(2,1)} %refs_0_.3) | copy-start | bytes 786436
  25.3 10.7 %collective-permute-start.7 = (bf16[256,1024]{1,0:T(8,128)(2,1)S(1)}, bf16[256,1024]{1,0:T(8,128)(2,1)S(1)}, u32[]{:S(2)}, u32[]{:S(2)}) collective-permute-start(bf16[256,1024]{1,0:T(8,128)(2,1)S(1)} %get-tuple-element.43), channel_id=1, source_target_pairs={{0,16},{1,9},{2,18},{3,11},{4,20},{5,13},{6,22},{7,15},{8,24},{9,1... | collective-permute-start | bytes 1572872 | tf_op jit(solution)/shard_map/ppermute | solution.py:66
  30.2 8.6 %collective-permute-start.11 = (bf16[384,256]{1,0:T(8,128)(2,1)S(1)}, bf16[384,256]{1,0:T(8,128)(2,1)S(1)}, u32[]{:S(2)}, u32[]{:S(2)}) collective-permute-start(bf16[384,256]{1,0:T(8,128)(2,1)S(1)} %get-tuple-element.53), channel_id=1, source_target_pairs={{0,8},{1,17},{2,10},{3,19},{4,12},{5,21},{6,14},{7,23},{8,0},{9,25... | collective-permute-start | bytes 589832 | tf_op jit(solution)/shard_map/ppermute | solution.py:66
  31.9 12.3 %collective-permute-start.12 = (bf16[384,256]{1,0:T(8,128)(2,1)S(1)}, bf16[384,256]{1,0:T(8,128)(2,1)S(1)}, u32[]{:S(2)}, u32[]{:S(2)}) collective-permute-start(bf16[384,256]{1,0:T(8,128)(2,1)S(1)} %get-tuple-element.54), channel_id=1, source_target_pairs={{0,16},{1,9},{2,18},{3,11},{4,20},{5,13},{6,22},{7,15},{8,24},{9,1... | collective-permute-start | bytes 589832 | tf_op jit(solution)/shard_map/ppermute | solution.py:66
  33.2 11.0 %collective-permute-start.13 = (bf16[384,256]{1,0:T(8,128)(2,1)S(1)}, bf16[384,256]{1,0:T(8,128)(2,1)S(1)}, u32[]{:S(2)}, u32[]{:S(2)}) collective-permute-start(bf16[384,256]{1,0:T(8,128)(2,1)S(1)} %get-tuple-element.55), channel_id=1, source_target_pairs={{0,24},{1,25},{2,26},{3,27},{4,28},{5,29},{6,30},{7,31},{8,16},{9,... | collective-permute-start | bytes 589832 | tf_op jit(solution)/shard_map/ppermute | solution.py:66
  36.1 9.1 %collective-permute-start.8 = (bf16[64,1024]{1,0:T(8,128)(2,1)S(1)}, bf16[64,1024]{1,0:T(8,128)(2,1)S(1)}, u32[]{:S(2)}, u32[]{:S(2)}) collective-permute-start(bf16[64,1024]{1,0:T(8,128)(2,1)S(1)} %get-tuple-element.45), channel_id=1, source_target_pairs={{0,8},{1,17},{2,10},{3,19},{4,12},{5,21},{6,14},{7,23},{8,0},{9,25... | collective-permute-start | bytes 393224 | tf_op jit(solution)/shard_map/ppermute | solution.py:66
  38.7 6.8 %collective-permute-start.9 = (bf16[64,1024]{1,0:T(8,128)(2,1)S(1)}, bf16[64,1024]{1,0:T(8,128)(2,1)S(1)}, u32[]{:S(2)}, u32[]{:S(2)}) collective-permute-start(bf16[64,1024]{1,0:T(8,128)(2,1)S(1)} %get-tuple-element.46), channel_id=1, source_target_pairs={{0,8},{1,17},{2,10},{3,19},{4,12},{5,21},{6,14},{7,23},{8,0},{9,25... | collective-permute-start | bytes 393224 | tf_op jit(solution)/shard_map/ppermute | solution.py:66

commit v17 on v16

--- a/solution.py
+++ b/solution.py
@@ -422,14 +422,15 @@
 
 
 def partial_kernel(att_ref, mine, *refs):
-    own, kept, sent = refs[-3:]
+    own, kept, near, across = refs[-4:]
     rows = own.shape[0]
     _, _, core = my_place()
     weight = rows_in_order(mine, refs[:1], core)
     product = dot_nn(att_ref[...], weight)
     own[...] = product[:rows, :]
     kept[...] = product[rows:2 * rows, :]
-    sent[...] = product[2 * rows:, :].astype(bf16)
+    near[...] = product[2 * rows:3 * rows, :].astype(bf16)
+    across[...] = product[3 * rows:, :].astype(bf16)
 
 
 def partials(attended, pieces, after):
@@ -437,37 +438,32 @@
     return pl.pallas_call(
         partial_kernel,
         out_shape=[jax.ShapeDtypeStruct((rows, model), f32)] * 2
-        + [jax.ShapeDtypeStruct((2 * rows, model), bf16)],
+        + [jax.ShapeDtypeStruct((rows, model), bf16)] * 2,
         in_specs=[vmem()] * 3 + [unread()] * len(after),
-        out_specs=[vmem()] * 3,
+        out_specs=[vmem()] * 4,
         compiler_params=params(12),
         cost_estimate=cost(1),
         name="partials",
     )(attended, *pieces, *after)
 
 
-def combine_kernel(own, kept, landed, total, *sent):
-    rows = own.shape[0]
-    total[...] = own[...] + landed[:rows, :].astype(f32)
-    part = rows // len(sent)
+def combine_kernel(kept, landed, *sent):
+    part = kept.shape[0] // len(sent)
     for at, out in enumerate(sent):
         span = slice(at * part, (at + 1) * part)
-        out[...] = (
-            kept[span, :] + landed[rows + at * part:rows + (at + 1) * part, :].astype(f32)
-        ).astype(bf16)
-
-
-def combine(own, kept, landed):
+        out[...] = (kept[span, :] + landed[span, :].astype(f32)).astype(bf16)
+
+
+def combine(kept, landed):
     return pl.pallas_call(
         combine_kernel,
-        out_shape=[jax.ShapeDtypeStruct(own.shape, f32)]
-        + [jax.ShapeDtypeStruct((own.shape[0] // 2, own.shape[1]), bf16)] * 2,
-        in_specs=[vmem()] * 3,
-        out_specs=[vmem()] * 3,
+        out_shape=[jax.ShapeDtypeStruct((kept.shape[0] // 2, kept.shape[1]), bf16)] * 2,
+        in_specs=[vmem()] * 2,
+        out_specs=[vmem()] * 2,
         compiler_params=params(8),
         cost_estimate=cost(1),
         name="combine",
-    )(own, kept, landed)
+    )(kept, landed)
 
 
 def grad_kernel(cycle, up_ref, *refs):
@@ -519,13 +515,12 @@
     return copies
 
 
-def finish_kernel(cycle, *refs):
+def finish_kernel(cycle, product, *refs):
     chunks = refs[:cycle]
-    outs, word = refs[-5:-2], refs[-2]
-    word[...] = jnp.zeros(word.shape, word.dtype)
+    outs = refs[-4:-1]
     rows = outs[0].shape[0]
     copies = place_columns(chunks, outs, refs[-1])
-    if len(refs) > cycle + 5:
+    if product:
         halves = refs[cycle:3 * cycle]
         _, _, core = my_place()
         total = None
@@ -533,45 +528,48 @@
             weight = both_halves(halves[2 * place:2 * place + 2], core)
             term = dot_nn(chunks[place][3 * rows:, :], weight)
             total = term if total is None else total + term
-        refs[-6][...] = total.astype(bf16)
+        refs[-5][...] = total.astype(bf16)
     for copy in copies:
         copy.wait()
 
 
-def finish(cycle, rows, chunks, others):
+def finish(cycle, rows, chunks, others, after=()):
     model = chunks[0].shape[1] * cycle
     aligned = model // cycle % 128 == 0
     return pl.pallas_call(
-        functools.partial(finish_kernel, cycle),
-        out_shape=[jax.ShapeDtypeStruct((rows, model), bf16)] * (4 if others else 3)
-        + [jax.ShapeDtypeStruct((16, 128), bf16)],
-        in_specs=[vmem()] * (cycle + len(others)),
+        functools.partial(finish_kernel, cycle, len(others) > 0),
+        out_shape=[jax.ShapeDtypeStruct((rows, model), bf16)] * (4 if others else 3),
+        in_specs=[vmem()] * (cycle + len(others)) + [unread()] * len(after),
         out_specs=[vmem()] * (1 if others else 0)
-        + [anywhere() if aligned else vmem()] * 3
-        + [vmem()],
+        + [anywhere() if aligned else vmem()] * 3,
         scratch_shapes=[pltpu.SemaphoreType.DMA((cycle, 3))],
         compiler_params=params(8),
         name="finish",
-    )(*chunks, *others)
+    )(*chunks, *others, *after)
 
 
 def sum_kernel(own, *refs):
-    out = refs[-1]
+    near, out, word = refs[-3:]
+    word[...] = jnp.zeros(word.shape, word.dtype)
     part = own.shape[0] // 2
     for at in range(2):
         span = slice(at * part, (at + 1) * part)
-        out[span, :] = (own[span, :] + refs[at][...].astype(f32)).astype(bf16)
-
-
-def last_sum(own, landed, after):
+        total = own[span, :] + near[span, :].astype(f32) + refs[at][...].astype(f32)
+        out[span, :] = total.astype(bf16)
+
+
+def last_sum(own, near, landed):
     return pl.pallas_call(
         sum_kernel,
-        out_shape=jax.ShapeDtypeStruct(own.shape, bf16),
-        in_specs=[vmem()] * 3 + [unread()] * len(after),
-        out_specs=vmem(),
+        out_shape=[
+            jax.ShapeDtypeStruct(own.shape, bf16),
+            jax.ShapeDtypeStruct((16, 128), bf16),
+        ],
+        in_specs=[vmem()] * 4,
+        out_specs=[vmem()] * 2,
         compiler_params=params(8),
         name="last_sum",
-    )(own, *landed, *after)
+    )(own, *landed, near)
 
 
 def local(queries, keys, values, out_weight, upstream, adjacency, counts):
@@ -589,7 +587,7 @@
     grads = swapped(project_grad(cycle, upstream, halves))
     inputs = (q_all, k_all, v_all, k_t, att_t, inverse, weights)
     terms = swapped(backward(cycle, inputs, grads, attended))
-    return tuple(finish(cycle, rows, terms, halves)[:4])
+    return tuple(finish(cycle, rows, terms, halves))
 
 
 def square(cycle, rows, tensors, out_weight, upstream):
@@ -601,15 +599,15 @@
     own_rows = with_other_core(fetch_rows(held_weight, 0))
     q_all, k_all, v_all, k_t, v_t, bias = gather(cycle, chunks)
     (attended,), att_t, inverse, weights = forward(cycle, cycle, q_all, k_all, v_t, bias)
-    own_mixed, kept, sent = partials(attended, own_rows, [])
-    landed = exchange_by_core(sent, (2, 1))
+    own_mixed, kept, near_mixed, passed_mixed = partials(attended, own_rows, [])
+    passed_mixed = exchange_by_core(passed_mixed, (2, 1))
+    near_mixed = exchange_by_core(near_mixed, (2, 1))
     grads = [group_grads((upstream, *nexts, across), own_rows, [kept])]
     inputs = (q_all, k_all, v_all, k_t, att_t, inverse, weights)
     terms = swapped(list(backward(cycle, inputs, grads, [])))
-    own_mixed, *next_mixed = combine(own_mixed, kept, landed)
-    next_mixed = [exchange_by_core(part, (1, 2)) for part in next_mixed]
-    *grads, word = finish(cycle, rows, terms, [])
-    return (last_sum(own_mixed, next_mixed, [word]), *grads)
+    next_mixed = [exchange_by_core(part, (1, 2)) for part in combine(kept, passed_mixed)]
+    mixed_out, word = last_sum(own_mixed, near_mixed, next_mixed)
+    return (mixed_out, *finish(cycle, rows, terms, [], [word]))
 
 
 def solution(mesh):

time: 46.4 us -> 47.5 us (1.024)
  starting transfers between devices: 18.1 us -> 20.2 us
  waiting for transfers between devices: 16.9 us -> 15.8 us
    ppermute x12 -> x13, starting transfers between devices: 17.4 us -> 19.6 us  [exchange_by_core(): return lax.ppermute(value, ('seq', 'mp'), pairs)]
    ppermute x12 -> x13, waiting for transfers between devices: 16.9 us -> 15.7 us  [exchange_by_core(): return lax.ppermute(value, ('seq', 'mp'), pairs)]
  transfers between devices with their start and end apart: 14 -> 15, of which waited for: 6 -> 5; matrix products, arithmetic and copies ran while one was open for 0% -> 0% of each run, Pallas kernels for 20% -> 19%
where the time goes in v17:
time: 47.5 us; the launch traced here: 47.3 us
  starting transfers between devices  20.2 us (43%)
  waiting for transfers between devices  15.8 us (33%)
  Pallas kernels  9.88 us (21%)
  between operations  1.41 us (3%)
    ppermute x13, starting transfers between devices, exchange_by_core(): return lax.ppermute(value, ('seq', 'mp'), pairs)  19.6 us
    ppermute x13, waiting for transfers between devices, exchange_by_core(): return lax.ppermute(value, ('seq', 'mp'), pairs)  15.7 us
    pallas_call x1, Pallas kernels, backward(): pl.pallas_call(functools.partial(backward_kernel, cycle, min(tokens, 512)...  2.36 us
    pallas_call x1, Pallas kernels, pack(): pl.pallas_call(functools.partial(pack_kernel, cycle, places), out_shape=[...  2.24 us
    pallas_call x1, Pallas kernels, forward(): pl.pallas_call(functools.partial(forward_kernel, min(tokens, 512), parts)...  2.19 us
    pallas_call x1, Pallas kernels, finish(): pl.pallas_call(functools.partial(finish_kernel, cycle, len(others) > 0),...  0.99 us
  transfers between devices with their start and end apart: 15, of which 5 were waited for; matrix products, arithmetic and copies ran while one was open for 0% of the time, Pallas kernels for 19%

profile of v17, /device:TPU:0, one launch (start us, length us, event | category | flops | bytes accessed | tf_op | source)
XLA Modules:
  0.0 47.3 jit_solution(17087214215289119017)
XLA Ops:
  0.6 3.0 %collective-permute-start.3 = (bf16[128,1024]{1,0:T(8,128)(2,1)}, bf16[128,1024]{1,0:T(8,128)(2,1)S(1)}, u32[]{:S(2)}, u32[]{:S(2)}) collective-permute-start(bf16[128,1024]{1,0:T(8,128)(2,1)} %refs_0_.3), channel_id=1, source_target_pairs={{0,8},{1,17},{2,10},{3,19},{4,12},{5,21},{6,14},{7,23},{8,0},{9,25... | collective-permute-start | bytes 786440 | tf_op jit(solution)/shard_map/ppermute | solution.py:66
  3.6 1.5 %collective-permute-start.4 = (bf16[128,1024]{1,0:T(8,128)(2,1)}, bf16[128,1024]{1,0:T(8,128)(2,1)S(1)}, u32[]{:S(2)}, u32[]{:S(2)}) collective-permute-start(bf16[128,1024]{1,0:T(8,128)(2,1)} %refs_0_.3), channel_id=1, source_target_pairs={{0,16},{1,9},{2,18},{3,11},{4,20},{5,13},{6,22},{7,15},{8,24},{9,1... | collective-permute-start | bytes 786440 | tf_op jit(solution)/shard_map/ppermute | solution.py:66
  5.8 2.2 %pack.1 = (bf16[416,256]{1,0:T(8,128)(2,1)}, bf16[416,256]{1,0:T(8,128)(2,1)}, bf16[416,256]{1,0:T(8,128)(2,1)}, bf16[416,256]{1,0:T(8,128)(2,1)}) custom-call(bf16[128,1024]{1,0:T(8,128)(2,1)} %q_ref.1, bf16[128,1024]{1,0:T(8,128)(2,1)} %k_ref.1, bf16[128,1024]{1,0:T(8,128)(2,1)} %v_ref.1, s32[1,4]{1,0:T(1,128)} %adj_any.1, s32[1,1]{1,0:T(1,128)} %bitcast.1.cnt_any), custom_call_target="tpu_custom_call" | custom-call | flops 5000000000 | tf_op jit(solution)/shard_map/pack/pallas_call | solution.py:177
  8.1 0.6 %collective-permute-start = (bf16[416,256]{1,0:T(8,128)(2,1)}, bf16[416,256]{1,0:T(8,128)(2,1)S(1)}, u32[]{:S(2)}, u32[]{:S(2)}) collective-permute-start(bf16[416,256]{1,0:T(8,128)(2,1)} %get-tuple-element.34), channel_id=1, source_target_pairs={{0,8},{1,17},{2,10},{3,19},{4,12},{5,21},{6,14},{7,23},{8,0},{9,25... | collective-permute-start | bytes 638984 | tf_op jit(solution)/shard_map/ppermute | solution.py:66
  8.7 2.9 %collective-permute-start.2 = (bf16[416,256]{1,0:T(8,128)(2,1)}, bf16[416,256]{1,0:T(8,128)(2,1)S(1)}, u32[]{:S(2)}, u32[]{:S(2)}) collective-permute-start(bf16[416,256]{1,0:T(8,128)(2,1)} %get-tuple-element.36), channel_id=1, source_target_pairs={{0,24},{1,25},{2,26},{3,27},{4,28},{5,29},{6,30},{7,31},{8,16},{9,... | collective-permute-start | bytes 638984 | tf_op jit(solution)/shard_map/ppermute | solution.py:66
  11.7 0.7 %collective-permute-start.5 = (bf16[128,1024]{1,0:T(8,128)(2,1)S(1)}, bf16[128,1024]{1,0:T(8,128)(2,1)S(1)}, u32[]{:S(2)}, u32[]{:S(2)}) collective-permute-start(bf16[128,1024]{1,0:T(8,128)(2,1)S(1)} %hold.2), channel_id=1, source_target_pairs={{0,0},{1,1},{4,2},{5,3},{2,4},{3,5},{6,6},{7,7},{12,8},{13,9},{10,... | collective-permute-start | bytes 786440 | tf_op jit(solution)/shard_map/ppermute | solution.py:385
  12.4 4.2 %collective-permute-done.refs_1_ = bf16[416,256]{1,0:T(8,128)(2,1)S(1)} collective-permute-done((bf16[416,256]{1,0:T(8,128)(2,1)}, bf16[416,256]{1,0:T(8,128)(2,1)S(1)}, u32[]{:S(2)}, u32[]{:S(2)}) %collective-permute-start) | collective-permute-done | bytes 213024 | tf_op jit(solution)/shard_map/ppermute | solution.py:66
  16.5 4.0 %collective-permute-done.2.refs_3_ = bf16[416,256]{1,0:T(8,128)(2,1)S(1)} collective-permute-done((bf16[416,256]{1,0:T(8,128)(2,1)}, bf16[416,256]{1,0:T(8,128)(2,1)S(1)}, u32[]{:S(2)}, u32[]{:S(2)}) %collective-permute-start.2) | collective-permute-done | bytes 213024 | tf_op jit(solution)/shard_map/ppermute | solution.py:66
  20.9 1.7 %collective-permute-start.11 = (bf16[128,1024]{1,0:T(8,128)(2,1)S(1)}, bf16[128,1024]{1,0:T(8,128)(2,1)S(1)}, u32[]{:S(2)}, u32[]{:S(2)}) collective-permute-start(bf16[128,1024]{1,0:T(8,128)(2,1)S(1)} %hold.3), channel_id=1, source_target_pairs={{0,8},{1,17},{2,10},{3,19},{4,12},{5,21},{6,14},{7,23},{8,0},{9,25... | collective-permute-start | bytes 786440 | tf_op jit(solution)/shard_map/ppermute | solution.py:66
  22.6 2.2 %forward.1 = (bf16[512,256]{1,0:T(8,128)(2,1)S(1)}, f32[256,512]{1,0:T(8,128)S(1)}, f32[8,512]{1,0:T(8,128)S(1)}, bf16[2048,512]{1,0:T(8,128)(2,1)S(1)}) custom-call(bf16[512,256]{1,0:T(8,128)(2,1)S(1)} %get-tuple-element.37.q_all.refs_0_, bf16[512,256]{1,0:T(8,128)(2,1)S(1)} %get-tuple-element.38.k_all.refs_1_, bf16[256,512]{1,0:T(8,128)(2,1)S(1)} %get-tuple-element.39.v_t, ...), custom_call_target="tpu_custom_call" | custom-call | flops 3000000000 | tf_op jit(solution)/shard_map/forward/pallas_call | solution.py:281
  24.8 0.4 partials.1
  25.3 1.4 %collective-permute-start.7 = (bf16[128,1024]{1,0:T(8,128)(2,1)S(1)}, bf16[128,1024]{1,0:T(8,128)(2,1)S(1)}, u32[]{:S(2)}, u32[]{:S(2)}) collective-permute-start(bf16[128,1024]{1,0:T(8,128)(2,1)S(1)} %get-tuple-element.44), channel_id=1, source_target_pairs={{0,16},{1,9},{2,18},{3,11},{4,20},{5,13},{6,22},{7,15},{8,24},{9,1... | collective-permute-start | bytes 786440 | tf_op jit(solution)/shard_map/ppermute | solution.py:66
  26.7 0.7 %collective-permute-start.10 = (bf16[128,1024]{1,0:T(8,128)(2,1)S(1)}, bf16[128,1024]{1,0:T(8,128)(2,1)S(1)}, u32[]{:S(2)}, u32[]{:S(2)}) collective-permute-start(bf16[128,1024]{1,0:T(8,128)(2,1)S(1)} %get-tuple-element.47), channel_id=1, source_target_pairs={{0,16},{1,9},{2,18},{3,11},{4,20},{5,13},{6,22},{7,15},{8,24},{9,1... | collective-permute-start | bytes 786440 | tf_op jit(solution)/shard_map/ppermute | solution.py:66
  27.4 0.5 %group_grads.1.refs_7_ = bf16[256,512]{1,0:T(8,128)(2,1)S(1)} custom-call(bf16[128,1024]{1,0:T(8,128)(2,1)S(1)} %copy-done.1, bf16[128,1024]{1,0:T(8,128)(2,1)S(1)} %collective-permute-done.3.refs_1_, bf16[128,1024]{1,0:T(8,128)(2,1)S(1)} %collective-permute-done.4.refs_2_.refs_0_, bf16[128,1024]{1,0:T(8,128)(2,1)S(1)} %collective-permute-done.11.refs_3_, ...), custom_call_target="tpu_custom_call" | custom-call | flops 1000000000 | tf_op jit(solution)/shard_map/group_grads/pallas_call | solution.py:413
  27.9 2.4 %backward.1 = (bf16[384,256]{1,0:T(8,128)(2,1)S(1)}, bf16[384,256]{1,0:T(8,128)(2,1)S(1)}, bf16[384,256]{1,0:T(8,128)(2,1)S(1)}, bf16[384,256]{1,0:T(8,128)(2,1)S(1)}) custom-call(bf16[512,256]{1,0:T(8,128)(2,1)S(1)} %get-tuple-element.37.q_all.refs_0_, bf16[512,256]{1,0:T(8,128)(2,1)S(1)} %get-tuple-element.38.k_all.refs_1_, ...), custom_call_target="tpu_custom_call" | custom-call | flops 3000000000 | tf_op jit(solution)/shard_map/backward/pallas_call | solution.py:360
  30.2 2.0 %collective-permute-start.12 = (bf16[384,256]{1,0:T(8,128)(2,1)S(1)}, bf16[384,256]{1,0:T(8,128)(2,1)S(1)}, u32[]{:S(2)}, u32[]{:S(2)}) collective-permute-start(bf16[384,256]{1,0:T(8,128)(2,1)S(1)} %get-tuple-element.55), channel_id=1, source_target_pairs={{0,8},{1,17},{2,10},{3,19},{4,12},{5,21},{6,14},{7,23},{8,0},{9,25... | collective-permute-start | bytes 589832 | tf_op jit(solution)/shard_map/ppermute | solution.py:66
  32.2 1.0 %collective-permute-start.13 = (bf16[384,256]{1,0:T(8,128)(2,1)S(1)}, bf16[384,256]{1,0:T(8,128)(2,1)S(1)}, u32[]{:S(2)}, u32[]{:S(2)}) collective-permute-start(bf16[384,256]{1,0:T(8,128)(2,1)S(1)} %get-tuple-element.56), channel_id=1, source_target_pairs={{0,16},{1,9},{2,18},{3,11},{4,20},{5,13},{6,22},{7,15},{8,24},{9,1... | collective-permute-start | bytes 589832 | tf_op jit(solution)/shard_map/ppermute | solution.py:66
  33.2 0.6 %collective-permute-start.14 = (bf16[384,256]{1,0:T(8,128)(2,1)S(1)}, bf16[384,256]{1,0:T(8,128)(2,1)S(1)}, u32[]{:S(2)}, u32[]{:S(2)}) collective-permute-start(bf16[384,256]{1,0:T(8,128)(2,1)S(1)} %get-tuple-element.57), channel_id=1, source_target_pairs={{0,24},{1,25},{2,26},{3,27},{4,28},{5,29},{6,30},{7,31},{8,16},{9,... | collective-permute-start | bytes 589832 | tf_op jit(solution)/shard_map/ppermute | solution.py:66
  33.8 2.0 %collective-permute-start.8 = (bf16[64,1024]{1,0:T(8,128)(2,1)S(1)}, bf16[64,1024]{1,0:T(8,128)(2,1)S(1)}, u32[]{:S(2)}, u32[]{:S(2)}) collective-permute-start(bf16[64,1024]{1,0:T(8,128)(2,1)S(1)} %get-tuple-element.45), channel_id=1, source_target_pairs={{0,8},{1,17},{2,10},{3,19},{4,12},{5,21},{6,14},{7,23},{8,0},{9,25... | collective-permute-start | bytes 393224 | tf_op jit(solution)/shard_map/ppermute | solution.py:66
  35.9 2.2 %collective-permute-start.9 = (bf16[64,1024]{1,0:T(8,128)(2,1)S(1)}, bf16[64,1024]{1,0:T(8,128)(2,1)S(1)}, u32[]{:S(2)}, u32[]{:S(2)}) collective-permute-start(bf16[64,1024]{1,0:T(8,128)(2,1)S(1)} %get-tuple-element.46), channel_id=1, source_target_pairs={{0,8},{1,17},{2,10},{3,19},{4,12},{5,21},{6,14},{7,23},{8,0},{9,25... | collective-permute-start | bytes 393224 | tf_op jit(solution)/shard_map/ppermute | solution.py:66
  38.1 6.0 %collective-permute-done.8.refs_0_ = bf16[64,1024]{1,0:T(8,128)(2,1)S(1)} collective-permute-done((bf16[64,1024]{1,0:T(8,128)(2,1)S(1)}, bf16[64,1024]{1,0:T(8,128)(2,1)S(1)}, u32[]{:S(2)}, u32[]{:S(2)}) %collective-permute-start.8) | collective-permute-done | bytes 131104 | tf_op jit(solution)/shard_map/ppermute | solution.py:66
  44.1 1.4 %collective-permute-done.9.refs_1_ = bf16[64,1024]{1,0:T(8,128)(2,1)S(1)} collective-permute-done((bf16[64,1024]{1,0:T(8,128)(2,1)S(1)}, bf16[64,1024]{1,0:T(8,128)(2,1)S(1)}, u32[]{:S(2)}, u32[]{:S(2)}) %collective-permute-start.9) | collective-permute-done | bytes 131104 | tf_op jit(solution)/shard_map/ppermute | solution.py:66
  45.5 0.8 %last_sum.1 = (bf16[128,1024]{1,0:T(8,128)(2,1)}, bf16[16,128]{1,0:T(8,128)(2,1)S(1)}) custom-call(f32[128,1024]{1,0:T(8,128)S(1)} %get-tuple-element.42.own, bf16[64,1024]{1,0:T(8,128)(2,1)S(1)} %collective-permute-done.8.refs_0_, bf16[64,1024]{1,0:T(8,128)(2,1)S(1)} %collective-permute-done.9.refs_1_, bf16[128,1024]{1,0:T(8,128)(2,1)S(1)} %collective-permute-done.10.refs_2_), custom_call_target="tpu_custom_call" | custom-call | tf_op jit(solution)/shard_map/last_sum/pallas_call | solution.py:562
  46.3 1.0 %finish.1 = (bf16[128,1024]{1,0:T(8,128)(2,1)}, bf16[128,1024]{1,0:T(8,128)(2,1)}, bf16[128,1024]{1,0:T(8,128)(2,1)}) custom-call(bf16[384,256]{1,0:T(8,128)(2,1)S(1)} %get-tuple-element.54.refs_0_, bf16[384,256]{1,0:T(8,128)(2,1)S(1)} %collective-permute-done.12.refs_1_, bf16[384,256]{1,0:T(8,128)(2,1)S(1)} %collective-permute-done.13.refs_2_, ...), custom_call_target="tpu_custom_call" | custom-call | tf_op jit(solution)/shard_map/finish/pallas_call | solution.py:539
  (23 shorter events, 0.6 us)
Async XLA Ops:
  0.6 11.0 %collective-permute-start.3 = (bf16[128,1024]{1,0:T(8,128)(2,1)}, bf16[128,1024]{1,0:T(8,128)(2,1)S(1)}, u32[]{:S(2)}, u32[]{:S(2)}) collective-permute-start(bf16[128,1024]{1,0:T(8,128)(2,1)} %refs_0_.3), channel_id=1, source_target_pairs={{0,8},{1,17},{2,10},{3,19},{4,12},{5,21},{6,14},{7,23},{8,0},{9,25... | collective-permute-start | bytes 786440 | tf_op jit(solution)/shard_map/ppermute | solution.py:66
  3.6 8.0 %collective-permute-start.4 = (bf16[128,1024]{1,0:T(8,128)(2,1)}, bf16[128,1024]{1,0:T(8,128)(2,1)S(1)}, u32[]{:S(2)}, u32[]{:S(2)}) collective-permute-start(bf16[128,1024]{1,0:T(8,128)(2,1)} %refs_0_.3), channel_id=1, source_target_pairs={{0,16},{1,9},{2,18},{3,11},{4,20},{5,13},{6,22},{7,15},{8,24},{9,1... | collective-permute-start | bytes 786440 | tf_op jit(solution)/shard_map/ppermute | solution.py:66
  5.8 5.8 %copy-start = (bf16[128,1024]{1,0:T(8,128)(2,1)S(1)}, bf16[128,1024]{1,0:T(8,128)(2,1)}, u32[]{:S(2)}) copy-start(bf16[128,1024]{1,0:T(8,128)(2,1)} %refs_0_.2) | copy-start | bytes 786436
  8.1 12.5 %copy-start.2 = (bf16[416,256]{1,0:T(8,128)(2,1)S(1)}, bf16[416,256]{1,0:T(8,128)(2,1)}, u32[]{:S(2)}) copy-start(bf16[416,256]{1,0:T(8,128)(2,1)} %get-tuple-element.33.refs_0_) | copy-start | bytes 638980
  8.1 8.5 %collective-permute-start = (bf16[416,256]{1,0:T(8,128)(2,1)}, bf16[416,256]{1,0:T(8,128)(2,1)S(1)}, u32[]{:S(2)}, u32[]{:S(2)}) collective-permute-start(bf16[416,256]{1,0:T(8,128)(2,1)} %get-tuple-element.34), channel_id=1, source_target_pairs={{0,8},{1,17},{2,10},{3,19},{4,12},{5,21},{6,14},{7,23},{8,0},{9,25... | collective-permute-start | bytes 638984 | tf_op jit(solution)/shard_map/ppermute | solution.py:66
  8.7 7.9 %collective-permute-start.1 = (bf16[416,256]{1,0:T(8,128)(2,1)}, bf16[416,256]{1,0:T(8,128)(2,1)S(1)}, u32[]{:S(2)}, u32[]{:S(2)}) collective-permute-start(bf16[416,256]{1,0:T(8,128)(2,1)} %get-tuple-element.35), channel_id=1, source_target_pairs={{0,16},{1,9},{2,18},{3,11},{4,20},{5,13},{6,22},{7,15},{8,24},{9,1... | collective-permute-start | bytes 638984 | tf_op jit(solution)/shard_map/ppermute | solution.py:66
  8.7 11.8 %collective-permute-start.2 = (bf16[416,256]{1,0:T(8,128)(2,1)}, bf16[416,256]{1,0:T(8,128)(2,1)S(1)}, u32[]{:S(2)}, u32[]{:S(2)}) collective-permute-start(bf16[416,256]{1,0:T(8,128)(2,1)} %get-tuple-element.36), channel_id=1, source_target_pairs={{0,24},{1,25},{2,26},{3,27},{4,28},{5,29},{6,30},{7,31},{8,16},{9,... | collective-permute-start | bytes 638984 | tf_op jit(solution)/shard_map/ppermute | solution.py:66
  11.7 10.9 %collective-permute-start.5 = (bf16[128,1024]{1,0:T(8,128)(2,1)S(1)}, bf16[128,1024]{1,0:T(8,128)(2,1)S(1)}, u32[]{:S(2)}, u32[]{:S(2)}) collective-permute-start(bf16[128,1024]{1,0:T(8,128)(2,1)S(1)} %hold.2), channel_id=1, source_target_pairs={{0,0},{1,1},{4,2},{5,3},{2,4},{3,5},{6,6},{7,7},{12,8},{13,9},{10,... | collective-permute-start | bytes 786440 | tf_op jit(solution)/shard_map/ppermute | solution.py:385
  20.9 6.5 %collective-permute-start.11 = (bf16[128,1024]{1,0:T(8,128)(2,1)S(1)}, bf16[128,1024]{1,0:T(8,128)(2,1)S(1)}, u32[]{:S(2)}, u32[]{:S(2)}) collective-permute-start(bf16[128,1024]{1,0:T(8,128)(2,1)S(1)} %hold.3), channel_id=1, source_target_pairs={{0,8},{1,17},{2,10},{3,19},{4,12},{5,21},{6,14},{7,23},{8,0},{9,25... | collective-permute-start | bytes 786440 | tf_op jit(solution)/shard_map/ppermute | solution.py:66
  22.6 2.2 %collective-permute-start.6 = (bf16[128,1024]{1,0:T(8,128)(2,1)S(1)}, bf16[128,1024]{1,0:T(8,128)(2,1)S(1)}, u32[]{:S(2)}, u32[]{:S(2)}) collective-permute-start(bf16[128,1024]{1,0:T(8,128)(2,1)S(1)} %collective-permute-done.5.mine.refs_4_), channel_id=1, source_target_pairs={{0,1},{1,0},{2,3},{3,2},{4,5},{5,4},{6,7},{7,6},{8,9},{9,8},{10,11... | collective-permute-start | bytes 786440 | tf_op jit(solution)/shard_map/ppermute | solution.py:52
  24.8 2.6 %copy-start.1 = (bf16[128,1024]{1,0:T(8,128)(2,1)S(1)}, bf16[128,1024]{1,0:T(8,128)(2,1)}, u32[]{:S(2)}) copy-start(bf16[128,1024]{1,0:T(8,128)(2,1)} %refs_0_.3) | copy-start | bytes 786436
  25.3 8.5 %collective-permute-start.7 = (bf16[128,1024]{1,0:T(8,128)(2,1)S(1)}, bf16[128,1024]{1,0:T(8,128)(2,1)S(1)}, u32[]{:S(2)}, u32[]{:S(2)}) collective-permute-start(bf16[128,1024]{1,0:T(8,128)(2,1)S(1)} %get-tuple-element.44), channel_id=1, source_target_pairs={{0,16},{1,9},{2,18},{3,11},{4,20},{5,13},{6,22},{7,15},{8,24},{9,1... | collective-permute-start | bytes 786440 | tf_op jit(solution)/shard_map/ppermute | solution.py:66
  26.7 9.3 %collective-permute-start.10 = (bf16[128,1024]{1,0:T(8,128)(2,1)S(1)}, bf16[128,1024]{1,0:T(8,128)(2,1)S(1)}, u32[]{:S(2)}, u32[]{:S(2)}) collective-permute-start(bf16[128,1024]{1,0:T(8,128)(2,1)S(1)} %get-tuple-element.47), channel_id=1, source_target_pairs={{0,16},{1,9},{2,18},{3,11},{4,20},{5,13},{6,22},{7,15},{8,24},{9,1... | collective-permute-start | bytes 786440 | tf_op jit(solution)/shard_map/ppermute | solution.py:66
  30.2 16.1 %collective-permute-start.12 = (bf16[384,256]{1,0:T(8,128)(2,1)S(1)}, bf16[384,256]{1,0:T(8,128)(2,1)S(1)}, u32[]{:S(2)}, u32[]{:S(2)}) collective-permute-start(bf16[384,256]{1,0:T(8,128)(2,1)S(1)} %get-tuple-element.55), channel_id=1, source_target_pairs={{0,8},{1,17},{2,10},{3,19},{4,12},{5,21},{6,14},{7,23},{8,0},{9,25... | collective-permute-start | bytes 589832 | tf_op jit(solution)/shard_map/ppermute | solution.py:66
  32.2 14.1 %collective-permute-start.13 = (bf16[384,256]{1,0:T(8,128)(2,1)S(1)}, bf16[384,256]{1,0:T(8,128)(2,1)S(1)}, u32[]{:S(2)}, u32[]{:S(2)}) collective-permute-start(bf16[384,256]{1,0:T(8,128)(2,1)S(1)} %get-tuple-element.56), channel_id=1, source_target_pairs={{0,16},{1,9},{2,18},{3,11},{4,20},{5,13},{6,22},{7,15},{8,24},{9,1... | collective-permute-start | bytes 589832 | tf_op jit(solution)/shard_map/ppermute | solution.py:66
  33.2 13.1 %collective-permute-start.14 = (bf16[384,256]{1,0:T(8,128)(2,1)S(1)}, bf16[384,256]{1,0:T(8,128)(2,1)S(1)}, u32[]{:S(2)}, u32[]{:S(2)}) collective-permute-start(bf16[384,256]{1,0:T(8,128)(2,1)S(1)} %get-tuple-element.57), channel_id=1, source_target_pairs={{0,24},{1,25},{2,26},{3,27},{4,28},{5,29},{6,30},{7,31},{8,16},{9,... | collective-permute-start | bytes 589832 | tf_op jit(solution)/shard_map/ppermute | solution.py:66
  33.8 10.3 %collective-permute-start.8 = (bf16[64,1024]{1,0:T(8,128)(2,1)S(1)}, bf16[64,1024]{1,0:T(8,128)(2,1)S(1)}, u32[]{:S(2)}, u32[]{:S(2)}) collective-permute-start(bf16[64,1024]{1,0:T(8,128)(2,1)S(1)} %get-tuple-element.45), channel_id=1, source_target_pairs={{0,8},{1,17},{2,10},{3,19},{4,12},{5,21},{6,14},{7,23},{8,0},{9,25... | collective-permute-start | bytes 393224 | tf_op jit(solution)/shard_map/ppermute | solution.py:66
  35.9 9.6 %collective-permute-start.9 = (bf16[64,1024]{1,0:T(8,128)(2,1)S(1)}, bf16[64,1024]{1,0:T(8,128)(2,1)S(1)}, u32[]{:S(2)}, u32[]{:S(2)}) collective-permute-start(bf16[64,1024]{1,0:T(8,128)(2,1)S(1)} %get-tuple-element.46), channel_id=1, source_target_pairs={{0,8},{1,17},{2,10},{3,19},{4,12},{5,21},{6,14},{7,23},{8,0},{9,25... | collective-permute-start | bytes 393224 | tf_op jit(solution)/shard_map/ppermute | solution.py:66

commit v18 on v17

--- a/solution.py
+++ b/solution.py
@@ -447,23 +447,20 @@
     )(attended, *pieces, *after)
 
 
-def combine_kernel(kept, landed, *sent):
-    part = kept.shape[0] // len(sent)
-    for at, out in enumerate(sent):
-        span = slice(at * part, (at + 1) * part)
-        out[...] = (kept[span, :] + landed[span, :].astype(f32)).astype(bf16)
-
-
-def combine(kept, landed):
+def combine_kernel(kept, landed, unused, sent):
+    sent[...] = (kept[...] + landed[...].astype(f32)).astype(bf16)
+
+
+def combine(kept, landed, after):
     return pl.pallas_call(
         combine_kernel,
-        out_shape=[jax.ShapeDtypeStruct((kept.shape[0] // 2, kept.shape[1]), bf16)] * 2,
-        in_specs=[vmem()] * 2,
-        out_specs=[vmem()] * 2,
+        out_shape=jax.ShapeDtypeStruct(kept.shape, bf16),
+        in_specs=[vmem()] * 2 + [unread()],
+        out_specs=vmem(),
         compiler_params=params(8),
         cost_estimate=cost(1),
         name="combine",
-    )(kept, landed)
+    )(kept, landed, after)
 
 
 def grad_kernel(cycle, up_ref, *refs):
@@ -548,14 +545,10 @@
     )(*chunks, *others, *after)
 
 
-def sum_kernel(own, *refs):
-    near, out, word = refs[-3:]
+def sum_kernel(own, landed, near, out, word):
     word[...] = jnp.zeros(word.shape, word.dtype)
-    part = own.shape[0] // 2
-    for at in range(2):
-        span = slice(at * part, (at + 1) * part)
-        total = own[span, :] + near[span, :].astype(f32) + refs[at][...].astype(f32)
-        out[span, :] = total.astype(bf16)
+    total = own[...] + near[...].astype(f32) + landed[...].astype(f32)
+    out[...] = total.astype(bf16)
 
 
 def last_sum(own, near, landed):
@@ -565,11 +558,11 @@
             jax.ShapeDtypeStruct(own.shape, bf16),
             jax.ShapeDtypeStruct((16, 128), bf16),
         ],
-        in_specs=[vmem()] * 4,
+        in_specs=[vmem()] * 3,
         out_specs=[vmem()] * 2,
         compiler_params=params(8),
         name="last_sum",
-    )(own, *landed, near)
+    )(own, landed, near)
 
 
 def local(queries, keys, values, out_weight, upstream, adjacency, counts):
@@ -605,7 +598,7 @@
     grads = [group_grads((upstream, *nexts, across), own_rows, [kept])]
     inputs = (q_all, k_all, v_all, k_t, att_t, inverse, weights)
     terms = swapped(list(backward(cycle, inputs, grads, [])))
-    next_mixed = [exchange_by_core(part, (1, 2)) for part in combine(kept, passed_mixed)]
+    next_mixed = exchange_by_core(combine(kept, passed_mixed, terms[0]), (1, 2))
     mixed_out, word = last_sum(own_mixed, near_mixed, next_mixed)
     return (mixed_out, *finish(cycle, rows, terms, [], [word]))
 

time: 47.5 us -> 48.5 us (1.021)
  waiting for transfers between devices: 15.8 us -> 19.1 us
  starting transfers between devices: 20.2 us -> 18 us
    ppermute x13 -> x12, waiting for transfers between devices: 15.7 us -> 19 us  [exchange_by_core(): return lax.ppermute(value, ('seq', 'mp'), pairs)]
    ppermute x13 -> x12, starting transfers between devices: 19.6 us -> 17.3 us  [exchange_by_core(): return lax.ppermute(value, ('seq', 'mp'), pairs)]
  transfers between devices with their start and end apart: 15 -> 14, of which waited for: 5 -> 6; matrix products, arithmetic and copies ran while one was open for 0% -> 0% of each run, Pallas kernels for 19% -> 18%
where the time goes in v18:
time: 48.5 us; the launch traced here: 48.3 us
  waiting for transfers between devices  19.1 us (39%)
  starting transfers between devices  18 us (37%)
  Pallas kernels  9.85 us (20%)
  between operations  1.4 us (3%)
    ppermute x12, waiting for transfers between devices, exchange_by_core(): return lax.ppermute(value, ('seq', 'mp'), pairs)  19 us
    ppermute x12, starting transfers between devices, exchange_by_core(): return lax.ppermute(value, ('seq', 'mp'), pairs)  17.3 us
    pallas_call x1, Pallas kernels, backward(): pl.pallas_call(functools.partial(backward_kernel, cycle, min(tokens, 512)...  2.36 us
    pallas_call x1, Pallas kernels, pack(): pl.pallas_call(functools.partial(pack_kernel, cycle, places), out_shape=[...  2.24 us
    pallas_call x1, Pallas kernels, forward(): pl.pallas_call(functools.partial(forward_kernel, min(tokens, 512), parts)...  2.19 us
  transfers between devices with their start and end apart: 14, of which 6 were waited for; matrix products, arithmetic and copies ran while one was open for 0% of the time, Pallas kernels for 18%

profile of v18, /device:TPU:0, one launch (start us, length us, event | category | flops | bytes accessed | tf_op | source)
XLA Modules:
  0.0 48.3 jit_solution(3894421705817014638)
XLA Ops:
  0.6 3.0 %collective-permute-start.3 = (bf16[128,1024]{1,0:T(8,128)(2,1)}, bf16[128,1024]{1,0:T(8,128)(2,1)S(1)}, u32[]{:S(2)}, u32[]{:S(2)}) collective-permute-start(bf16[128,1024]{1,0:T(8,128)(2,1)} %refs_0_.3), channel_id=1, source_target_pairs={{0,8},{1,17},{2,10},{3,19},{4,12},{5,21},{6,14},{7,23},{8,0},{9,25... | collective-permute-start | bytes 786440 | tf_op jit(solution)/shard_map/ppermute | solution.py:66
  3.6 1.5 %collective-permute-start.4 = (bf16[128,1024]{1,0:T(8,128)(2,1)}, bf16[128,1024]{1,0:T(8,128)(2,1)S(1)}, u32[]{:S(2)}, u32[]{:S(2)}) collective-permute-start(bf16[128,1024]{1,0:T(8,128)(2,1)} %refs_0_.3), channel_id=1, source_target_pairs={{0,16},{1,9},{2,18},{3,11},{4,20},{5,13},{6,22},{7,15},{8,24},{9,1... | collective-permute-start | bytes 786440 | tf_op jit(solution)/shard_map/ppermute | solution.py:66
  5.8 2.2 %pack.1 = (bf16[416,256]{1,0:T(8,128)(2,1)}, bf16[416,256]{1,0:T(8,128)(2,1)}, bf16[416,256]{1,0:T(8,128)(2,1)}, bf16[416,256]{1,0:T(8,128)(2,1)}) custom-call(bf16[128,1024]{1,0:T(8,128)(2,1)} %q_ref.1, bf16[128,1024]{1,0:T(8,128)(2,1)} %k_ref.1, bf16[128,1024]{1,0:T(8,128)(2,1)} %v_ref.1, s32[1,4]{1,0:T(1,128)} %adj_any.1, s32[1,1]{1,0:T(1,128)} %bitcast.1.cnt_any), custom_call_target="tpu_custom_call" | custom-call | flops 5000000000 | tf_op jit(solution)/shard_map/pack/pallas_call | solution.py:177
  8.1 0.6 %collective-permute-start = (bf16[416,256]{1,0:T(8,128)(2,1)}, bf16[416,256]{1,0:T(8,128)(2,1)S(1)}, u32[]{:S(2)}, u32[]{:S(2)}) collective-permute-start(bf16[416,256]{1,0:T(8,128)(2,1)} %get-tuple-element.32), channel_id=1, source_target_pairs={{0,8},{1,17},{2,10},{3,19},{4,12},{5,21},{6,14},{7,23},{8,0},{9,25... | collective-permute-start | bytes 638984 | tf_op jit(solution)/shard_map/ppermute | solution.py:66
  8.7 2.9 %collective-permute-start.2 = (bf16[416,256]{1,0:T(8,128)(2,1)}, bf16[416,256]{1,0:T(8,128)(2,1)S(1)}, u32[]{:S(2)}, u32[]{:S(2)}) collective-permute-start(bf16[416,256]{1,0:T(8,128)(2,1)} %get-tuple-element.34), channel_id=1, source_target_pairs={{0,24},{1,25},{2,26},{3,27},{4,28},{5,29},{6,30},{7,31},{8,16},{9,... | collective-permute-start | bytes 638984 | tf_op jit(solution)/shard_map/ppermute | solution.py:66
  11.7 0.7 %collective-permute-start.5 = (bf16[128,1024]{1,0:T(8,128)(2,1)S(1)}, bf16[128,1024]{1,0:T(8,128)(2,1)S(1)}, u32[]{:S(2)}, u32[]{:S(2)}) collective-permute-start(bf16[128,1024]{1,0:T(8,128)(2,1)S(1)} %hold.2), channel_id=1, source_target_pairs={{0,0},{1,1},{4,2},{5,3},{2,4},{3,5},{6,6},{7,7},{12,8},{13,9},{10,... | collective-permute-start | bytes 786440 | tf_op jit(solution)/shard_map/ppermute | solution.py:385
  12.4 4.2 %collective-permute-done.refs_1_ = bf16[416,256]{1,0:T(8,128)(2,1)S(1)} collective-permute-done((bf16[416,256]{1,0:T(8,128)(2,1)}, bf16[416,256]{1,0:T(8,128)(2,1)S(1)}, u32[]{:S(2)}, u32[]{:S(2)}) %collective-permute-start) | collective-permute-done | bytes 213024 | tf_op jit(solution)/shard_map/ppermute | solution.py:66
  16.5 4.0 %collective-permute-done.2.refs_3_ = bf16[416,256]{1,0:T(8,128)(2,1)S(1)} collective-permute-done((bf16[416,256]{1,0:T(8,128)(2,1)}, bf16[416,256]{1,0:T(8,128)(2,1)S(1)}, u32[]{:S(2)}, u32[]{:S(2)}) %collective-permute-start.2) | collective-permute-done | bytes 213024 | tf_op jit(solution)/shard_map/ppermute | solution.py:66
  20.9 1.7 %collective-permute-start.8 = (bf16[128,1024]{1,0:T(8,128)(2,1)S(1)}, bf16[128,1024]{1,0:T(8,128)(2,1)S(1)}, u32[]{:S(2)}, u32[]{:S(2)}) collective-permute-start(bf16[128,1024]{1,0:T(8,128)(2,1)S(1)} %hold.3), channel_id=1, source_target_pairs={{0,8},{1,17},{2,10},{3,19},{4,12},{5,21},{6,14},{7,23},{8,0},{9,25... | collective-permute-start | bytes 786440 | tf_op jit(solution)/shard_map/ppermute | solution.py:66
  22.6 2.2 %forward.1 = (bf16[512,256]{1,0:T(8,128)(2,1)S(1)}, f32[256,512]{1,0:T(8,128)S(1)}, f32[8,512]{1,0:T(8,128)S(1)}, bf16[2048,512]{1,0:T(8,128)(2,1)S(1)}) custom-call(bf16[512,256]{1,0:T(8,128)(2,1)S(1)} %get-tuple-element.35.q_all.refs_0_, bf16[512,256]{1,0:T(8,128)(2,1)S(1)} %get-tuple-element.36.k_all.refs_1_, bf16[256,512]{1,0:T(8,128)(2,1)S(1)} %get-tuple-element.37.v_t, ...), custom_call_target="tpu_custom_call" | custom-call | flops 3000000000 | tf_op jit(solution)/shard_map/forward/pallas_call | solution.py:281
  24.8 0.4 partials.1
  25.3 1.4 %collective-permute-start.7 = (bf16[128,1024]{1,0:T(8,128)(2,1)S(1)}, bf16[128,1024]{1,0:T(8,128)(2,1)S(1)}, u32[]{:S(2)}, u32[]{:S(2)}) collective-permute-start(bf16[128,1024]{1,0:T(8,128)(2,1)S(1)} %get-tuple-element.42), channel_id=1, source_target_pairs={{0,16},{1,9},{2,18},{3,11},{4,20},{5,13},{6,22},{7,15},{8,24},{9,1... | collective-permute-start | bytes 786440 | tf_op jit(solution)/shard_map/ppermute | solution.py:66
  26.7 0.7 %collective-permute-start.10 = (bf16[128,1024]{1,0:T(8,128)(2,1)S(1)}, bf16[128,1024]{1,0:T(8,128)(2,1)S(1)}, u32[]{:S(2)}, u32[]{:S(2)}) collective-permute-start(bf16[128,1024]{1,0:T(8,128)(2,1)S(1)} %get-tuple-element.49), channel_id=1, source_target_pairs={{0,16},{1,9},{2,18},{3,11},{4,20},{5,13},{6,22},{7,15},{8,24},{9,1... | collective-permute-start | bytes 786440 | tf_op jit(solution)/shard_map/ppermute | solution.py:66
  27.4 0.5 group_grads.1.refs_7_
  27.9 2.4 %backward.1 = (bf16[384,256]{1,0:T(8,128)(2,1)S(1)}, bf16[384,256]{1,0:T(8,128)(2,1)S(1)}, bf16[384,256]{1,0:T(8,128)(2,1)S(1)}, bf16[384,256]{1,0:T(8,128)(2,1)S(1)}) custom-call(bf16[512,256]{1,0:T(8,128)(2,1)S(1)} %get-tuple-element.35.q_all.refs_0_, bf16[512,256]{1,0:T(8,128)(2,1)S(1)} %get-tuple-element.36.k_all.refs_1_, ...), custom_call_target="tpu_custom_call" | custom-call | flops 3000000000 | tf_op jit(solution)/shard_map/backward/pallas_call | solution.py:360
  30.2 1.5 %collective-permute-done.7.landed = bf16[128,1024]{1,0:T(8,128)(2,1)S(1)} collective-permute-done((bf16[128,1024]{1,0:T(8,128)(2,1)S(1)}, bf16[128,1024]{1,0:T(8,128)(2,1)S(1)}, u32[]{:S(2)}, u32[]{:S(2)}) %collective-permute-start.7) | collective-permute-done | bytes 262176 | tf_op jit(solution)/shard_map/ppermute | solution.py:66
  31.8 2.0 %collective-permute-start.9 = (bf16[128,1024]{1,0:T(8,128)(2,1)S(1)}, bf16[128,1024]{1,0:T(8,128)(2,1)S(1)}, u32[]{:S(2)}, u32[]{:S(2)}) collective-permute-start(bf16[128,1024]{1,0:T(8,128)(2,1)S(1)} %combine.1), channel_id=1, source_target_pairs={{0,8},{1,17},{2,10},{3,19},{4,12},{5,21},{6,14},{7,23},{8,0},{9,25... | collective-permute-start | bytes 786440 | tf_op jit(solution)/shard_map/ppermute | solution.py:66
  33.9 1.3 %collective-permute-start.12 = (bf16[384,256]{1,0:T(8,128)(2,1)S(1)}, bf16[384,256]{1,0:T(8,128)(2,1)S(1)}, u32[]{:S(2)}, u32[]{:S(2)}) collective-permute-start(bf16[384,256]{1,0:T(8,128)(2,1)S(1)} %get-tuple-element.52), channel_id=1, source_target_pairs={{0,16},{1,9},{2,18},{3,11},{4,20},{5,13},{6,22},{7,15},{8,24},{9,1... | collective-permute-start | bytes 589832 | tf_op jit(solution)/shard_map/ppermute | solution.py:66
  35.2 2.1 %collective-permute-start.13 = (bf16[384,256]{1,0:T(8,128)(2,1)S(1)}, bf16[384,256]{1,0:T(8,128)(2,1)S(1)}, u32[]{:S(2)}, u32[]{:S(2)}) collective-permute-start(bf16[384,256]{1,0:T(8,128)(2,1)S(1)} %get-tuple-element.53), channel_id=1, source_target_pairs={{0,24},{1,25},{2,26},{3,27},{4,28},{5,29},{6,30},{7,31},{8,16},{9,... | collective-permute-start | bytes 589832 | tf_op jit(solution)/shard_map/ppermute | solution.py:66
  37.2 3.5 %collective-permute-done.9.landed = bf16[128,1024]{1,0:T(8,128)(2,1)S(1)} collective-permute-done((bf16[128,1024]{1,0:T(8,128)(2,1)S(1)}, bf16[128,1024]{1,0:T(8,128)(2,1)S(1)}, u32[]{:S(2)}, u32[]{:S(2)}) %collective-permute-start.9) | collective-permute-done | bytes 262176 | tf_op jit(solution)/shard_map/ppermute | solution.py:66
  40.7 0.8 %last_sum.1 = (bf16[128,1024]{1,0:T(8,128)(2,1)}, bf16[16,128]{1,0:T(8,128)(2,1)S(1)}) custom-call(f32[128,1024]{1,0:T(8,128)S(1)} %get-tuple-element.40.own, bf16[128,1024]{1,0:T(8,128)(2,1)S(1)} %collective-permute-done.9.landed, bf16[128,1024]{1,0:T(8,128)(2,1)S(1)} %collective-permute-done.10.near), custom_call_target="tpu_custom_call" | custom-call | tf_op jit(solution)/shard_map/last_sum/pallas_call | solution.py:555
  41.5 3.0 %collective-permute-done.11.refs_1_ = bf16[384,256]{1,0:T(8,128)(2,1)S(1)} collective-permute-done((bf16[384,256]{1,0:T(8,128)(2,1)S(1)}, bf16[384,256]{1,0:T(8,128)(2,1)S(1)}, u32[]{:S(2)}, u32[]{:S(2)}) %collective-permute-start.11) | collective-permute-done | bytes 196640 | tf_op jit(solution)/shard_map/ppermute | solution.py:66
  44.5 2.8 %collective-permute-done.13.refs_3_ = bf16[384,256]{1,0:T(8,128)(2,1)S(1)} collective-permute-done((bf16[384,256]{1,0:T(8,128)(2,1)S(1)}, bf16[384,256]{1,0:T(8,128)(2,1)S(1)}, u32[]{:S(2)}, u32[]{:S(2)}) %collective-permute-start.13) | collective-permute-done | bytes 196640 | tf_op jit(solution)/shard_map/ppermute | solution.py:66
  47.4 1.0 %finish.1 = (bf16[128,1024]{1,0:T(8,128)(2,1)}, bf16[128,1024]{1,0:T(8,128)(2,1)}, bf16[128,1024]{1,0:T(8,128)(2,1)}) custom-call(bf16[384,256]{1,0:T(8,128)(2,1)S(1)} %get-tuple-element.48.unused.refs_0_, bf16[384,256]{1,0:T(8,128)(2,1)S(1)} %collective-permute-done.11.refs_1_, bf16[384,256]{1,0:T(8,128)(2,1)S(1)} %collective-permute-done.12.refs_2_, ...), custom_call_target="tpu_custom_call" | custom-call | tf_op jit(solution)/shard_map/finish/pallas_call | solution.py:536
  (21 shorter events, 0.6 us)
Async XLA Ops:
  0.6 11.0 %collective-permute-start.3 = (bf16[128,1024]{1,0:T(8,128)(2,1)}, bf16[128,1024]{1,0:T(8,128)(2,1)S(1)}, u32[]{:S(2)}, u32[]{:S(2)}) collective-permute-start(bf16[128,1024]{1,0:T(8,128)(2,1)} %refs_0_.3), channel_id=1, source_target_pairs={{0,8},{1,17},{2,10},{3,19},{4,12},{5,21},{6,14},{7,23},{8,0},{9,25... | collective-permute-start | bytes 786440 | tf_op jit(solution)/shard_map/ppermute | solution.py:66
  3.6 8.0 %collective-permute-start.4 = (bf16[128,1024]{1,0:T(8,128)(2,1)}, bf16[128,1024]{1,0:T(8,128)(2,1)S(1)}, u32[]{:S(2)}, u32[]{:S(2)}) collective-permute-start(bf16[128,1024]{1,0:T(8,128)(2,1)} %refs_0_.3), channel_id=1, source_target_pairs={{0,16},{1,9},{2,18},{3,11},{4,20},{5,13},{6,22},{7,15},{8,24},{9,1... | collective-permute-start | bytes 786440 | tf_op jit(solution)/shard_map/ppermute | solution.py:66
  5.8 5.8 %copy-start = (bf16[128,1024]{1,0:T(8,128)(2,1)S(1)}, bf16[128,1024]{1,0:T(8,128)(2,1)}, u32[]{:S(2)}) copy-start(bf16[128,1024]{1,0:T(8,128)(2,1)} %refs_0_.2) | copy-start | bytes 786436
  8.1 12.5 %copy-start.2 = (bf16[416,256]{1,0:T(8,128)(2,1)S(1)}, bf16[416,256]{1,0:T(8,128)(2,1)}, u32[]{:S(2)}) copy-start(bf16[416,256]{1,0:T(8,128)(2,1)} %get-tuple-element.31.refs_0_) | copy-start | bytes 638980
  8.1 8.5 %collective-permute-start = (bf16[416,256]{1,0:T(8,128)(2,1)}, bf16[416,256]{1,0:T(8,128)(2,1)S(1)}, u32[]{:S(2)}, u32[]{:S(2)}) collective-permute-start(bf16[416,256]{1,0:T(8,128)(2,1)} %get-tuple-element.32), channel_id=1, source_target_pairs={{0,8},{1,17},{2,10},{3,19},{4,12},{5,21},{6,14},{7,23},{8,0},{9,25... | collective-permute-start | bytes 638984 | tf_op jit(solution)/shard_map/ppermute | solution.py:66
  8.7 7.9 %collective-permute-start.1 = (bf16[416,256]{1,0:T(8,128)(2,1)}, bf16[416,256]{1,0:T(8,128)(2,1)S(1)}, u32[]{:S(2)}, u32[]{:S(2)}) collective-permute-start(bf16[416,256]{1,0:T(8,128)(2,1)} %get-tuple-element.33), channel_id=1, source_target_pairs={{0,16},{1,9},{2,18},{3,11},{4,20},{5,13},{6,22},{7,15},{8,24},{9,1... | collective-permute-start | bytes 638984 | tf_op jit(solution)/shard_map/ppermute | solution.py:66
  8.7 11.8 %collective-permute-start.2 = (bf16[416,256]{1,0:T(8,128)(2,1)}, bf16[416,256]{1,0:T(8,128)(2,1)S(1)}, u32[]{:S(2)}, u32[]{:S(2)}) collective-permute-start(bf16[416,256]{1,0:T(8,128)(2,1)} %get-tuple-element.34), channel_id=1, source_target_pairs={{0,24},{1,25},{2,26},{3,27},{4,28},{5,29},{6,30},{7,31},{8,16},{9,... | collective-permute-start | bytes 638984 | tf_op jit(solution)/shard_map/ppermute | solution.py:66
  11.7 10.9 %collective-permute-start.5 = (bf16[128,1024]{1,0:T(8,128)(2,1)S(1)}, bf16[128,1024]{1,0:T(8,128)(2,1)S(1)}, u32[]{:S(2)}, u32[]{:S(2)}) collective-permute-start(bf16[128,1024]{1,0:T(8,128)(2,1)S(1)} %hold.2), channel_id=1, source_target_pairs={{0,0},{1,1},{4,2},{5,3},{2,4},{3,5},{6,6},{7,7},{12,8},{13,9},{10,... | collective-permute-start | bytes 786440 | tf_op jit(solution)/shard_map/ppermute | solution.py:385
  20.9 6.5 %collective-permute-start.8 = (bf16[128,1024]{1,0:T(8,128)(2,1)S(1)}, bf16[128,1024]{1,0:T(8,128)(2,1)S(1)}, u32[]{:S(2)}, u32[]{:S(2)}) collective-permute-start(bf16[128,1024]{1,0:T(8,128)(2,1)S(1)} %hold.3), channel_id=1, source_target_pairs={{0,8},{1,17},{2,10},{3,19},{4,12},{5,21},{6,14},{7,23},{8,0},{9,25... | collective-permute-start | bytes 786440 | tf_op jit(solution)/shard_map/ppermute | solution.py:66
  22.6 2.2 %collective-permute-start.6 = (bf16[128,1024]{1,0:T(8,128)(2,1)S(1)}, bf16[128,1024]{1,0:T(8,128)(2,1)S(1)}, u32[]{:S(2)}, u32[]{:S(2)}) collective-permute-start(bf16[128,1024]{1,0:T(8,128)(2,1)S(1)} %collective-permute-done.5.mine.refs_4_), channel_id=1, source_target_pairs={{0,1},{1,0},{2,3},{3,2},{4,5},{5,4},{6,7},{7,6},{8,9},{9,8},{10,11... | collective-permute-start | bytes 786440 | tf_op jit(solution)/shard_map/ppermute | solution.py:52
  24.8 2.6 %copy-start.1 = (bf16[128,1024]{1,0:T(8,128)(2,1)S(1)}, bf16[128,1024]{1,0:T(8,128)(2,1)}, u32[]{:S(2)}) copy-start(bf16[128,1024]{1,0:T(8,128)(2,1)} %refs_0_.3) | copy-start | bytes 786436
  25.3 6.4 %collective-permute-start.7 = (bf16[128,1024]{1,0:T(8,128)(2,1)S(1)}, bf16[128,1024]{1,0:T(8,128)(2,1)S(1)}, u32[]{:S(2)}, u32[]{:S(2)}) collective-permute-start(bf16[128,1024]{1,0:T(8,128)(2,1)S(1)} %get-tuple-element.42), channel_id=1, source_target_pairs={{0,16},{1,9},{2,18},{3,11},{4,20},{5,13},{6,22},{7,15},{8,24},{9,1... | collective-permute-start | bytes 786440 | tf_op jit(solution)/shard_map/ppermute | solution.py:66
  26.7 10.6 %collective-permute-start.10 = (bf16[128,1024]{1,0:T(8,128)(2,1)S(1)}, bf16[128,1024]{1,0:T(8,128)(2,1)S(1)}, u32[]{:S(2)}, u32[]{:S(2)}) collective-permute-start(bf16[128,1024]{1,0:T(8,128)(2,1)S(1)} %get-tuple-element.49), channel_id=1, source_target_pairs={{0,16},{1,9},{2,18},{3,11},{4,20},{5,13},{6,22},{7,15},{8,24},{9,1... | collective-permute-start | bytes 786440 | tf_op jit(solution)/shard_map/ppermute | solution.py:66
  31.8 8.9 %collective-permute-start.9 = (bf16[128,1024]{1,0:T(8,128)(2,1)S(1)}, bf16[128,1024]{1,0:T(8,128)(2,1)S(1)}, u32[]{:S(2)}, u32[]{:S(2)}) collective-permute-start(bf16[128,1024]{1,0:T(8,128)(2,1)S(1)} %combine.1), channel_id=1, source_target_pairs={{0,8},{1,17},{2,10},{3,19},{4,12},{5,21},{6,14},{7,23},{8,0},{9,25... | collective-permute-start | bytes 786440 | tf_op jit(solution)/shard_map/ppermute | solution.py:66
  33.7 10.8 %collective-permute-start.11 = (bf16[384,256]{1,0:T(8,128)(2,1)S(1)}, bf16[384,256]{1,0:T(8,128)(2,1)S(1)}, u32[]{:S(2)}, u32[]{:S(2)}) collective-permute-start(bf16[384,256]{1,0:T(8,128)(2,1)S(1)} %get-tuple-element.51), channel_id=1, source_target_pairs={{0,8},{1,17},{2,10},{3,19},{4,12},{5,21},{6,14},{7,23},{8,0},{9,25... | collective-permute-start | bytes 589832 | tf_op jit(solution)/shard_map/ppermute | solution.py:66
  33.9 10.7 %collective-permute-start.12 = (bf16[384,256]{1,0:T(8,128)(2,1)S(1)}, bf16[384,256]{1,0:T(8,128)(2,1)S(1)}, u32[]{:S(2)}, u32[]{:S(2)}) collective-permute-start(bf16[384,256]{1,0:T(8,128)(2,1)S(1)} %get-tuple-element.52), channel_id=1, source_target_pairs={{0,16},{1,9},{2,18},{3,11},{4,20},{5,13},{6,22},{7,15},{8,24},{9,1... | collective-permute-start | bytes 589832 | tf_op jit(solution)/shard_map/ppermute | solution.py:66
  35.2 12.2 %collective-permute-start.13 = (bf16[384,256]{1,0:T(8,128)(2,1)S(1)}, bf16[384,256]{1,0:T(8,128)(2,1)S(1)}, u32[]{:S(2)}, u32[]{:S(2)}) collective-permute-start(bf16[384,256]{1,0:T(8,128)(2,1)S(1)} %get-tuple-element.53), channel_id=1, source_target_pairs={{0,24},{1,25},{2,26},{3,27},{4,28},{5,29},{6,30},{7,31},{8,16},{9,... | collective-permute-start | bytes 589832 | tf_op jit(solution)/shard_map/ppermute | solution.py:66

commit v19 on v14

--- a/solution.py
+++ b/solution.py
@@ -545,23 +545,26 @@
     )(*chunks, *others)
 
 
-def sum_kernel(own, *refs):
-    out = refs[-1]
-    part = own.shape[0] // 2
-    for at in range(2):
-        span = slice(at * part, (at + 1) * part)
-        out[span, :] = (own[span, :] + refs[at][...].astype(f32)).astype(bf16)
-
-
-def last_sum(own, landed, after):
-    return pl.pallas_call(
-        sum_kernel,
+def sum_kernel(half, own, landed, unused, out, total, sem):
+    part = total.shape[0]
+    span = slice(half * part, (half + 1) * part)
+    total[...] = (own[span, :] + landed[...].astype(f32)).astype(bf16)
+    copy = pltpu.make_async_copy(total, out.at[span, :], sem)
+    copy.start()
+    copy.wait()
+
+
+def half_sum(half, own, landed, before):
+    return pl.pallas_call(
+        functools.partial(sum_kernel, half),
         out_shape=jax.ShapeDtypeStruct(own.shape, bf16),
-        in_specs=[vmem()] * 3 + [unread()] * len(after),
-        out_specs=vmem(),
+        in_specs=[vmem()] * 2 + [anywhere() if half else unread()],
+        out_specs=anywhere(),
+        scratch_shapes=[pltpu.VMEM(landed.shape, bf16), pltpu.SemaphoreType.DMA],
+        input_output_aliases={2: 0} if half else {},
         compiler_params=params(8),
-        name="last_sum",
-    )(own, *landed, *after)
+        name="half_sum",
+    )(own, landed, before)
 
 
 def local(queries, keys, values, out_weight, upstream, adjacency, counts):
@@ -598,7 +601,9 @@
     own_mixed, *next_mixed = combine(own_mixed, kept, landed)
     next_mixed = [exchange_by_core(part, (1, 2)) for part in next_mixed]
     *grads, word = finish(cycle, rows, terms, [])
-    return (last_sum(own_mixed, next_mixed, [word]), *grads)
+    mixed_out = half_sum(0, own_mixed, next_mixed[0], word)
+    mixed_out = half_sum(1, own_mixed, next_mixed[1], mixed_out)
+    return (mixed_out, *grads)
 
 
 def solution(mesh):

time: 46.2 us -> 46.8 us (1.013)
  the two profiles are of different devices: /device:TPU:0 before, /device:TPU:1 now
where the time goes in v19:
time: 46.8 us; the launch traced here: 46.6 us
  starting transfers between devices  18 us (38%)
  waiting for transfers between devices  16.1 us (34%)
  Pallas kernels  11.1 us (24%)
  between operations  1.42 us (3%)
    ppermute x12, waiting for transfers between devices, exchange_by_core(): return lax.ppermute(value, ('seq', 'mp'), pairs)  16.1 us
    ppermute x12, starting transfers between devices, exchange_by_core(): return lax.ppermute(value, ('seq', 'mp'), pairs)  15.6 us
    pallas_call x1, Pallas kernels, backward(): pl.pallas_call(functools.partial(backward_kernel, cycle, min(tokens, 512)...  3.06 us
    pallas_call x1, Pallas kernels, pack(): pl.pallas_call(functools.partial(pack_kernel, cycle, places), out_shape=[...  2.24 us
    pallas_call x1, Pallas kernels, forward(): pl.pallas_call(functools.partial(forward_kernel, min(tokens, 512), parts)...  2.08 us
    ppermute x1, starting transfers between devices, exchange(): return lax.ppermute(value, axis, [(i, i ^ distance) for i in range(count)])  1.75 us
    pallas_call x2, Pallas kernels, half_sum(): pl.pallas_call(functools.partial(sum_kernel, half), out_shape=jax.ShapeDt...  1.38 us
    pallas_call x1, Pallas kernels, finish(): pl.pallas_call(functools.partial(finish_kernel, cycle), out_shape=[jax.Sh...  0.97 us
  transfers between devices with their start and end apart: 14, of which 8 were waited for; matrix products, arithmetic and copies ran while one was open for 0% of the time, Pallas kernels for 21%

profile of v19, /device:TPU:1, one launch (start us, length us, event | category | flops | bytes accessed | tf_op | source)
XLA Modules:
  0.0 46.6 jit_solution(7322303450070518497)
XLA Ops:
  0.6 2.1 %collective-permute-start.3 = (bf16[128,1024]{1,0:T(8,128)(2,1)}, bf16[128,1024]{1,0:T(8,128)(2,1)S(1)}, u32[]{:S(2)}, u32[]{:S(2)}) collective-permute-start(bf16[128,1024]{1,0:T(8,128)(2,1)} %refs_0_.3), channel_id=1, source_target_pairs={{0,16},{1,9},{2,18},{3,11},{4,20},{5,13},{6,22},{7,15},{8,24},{9,1... | collective-permute-start | bytes 786440 | tf_op jit(solution)/shard_map/ppermute | solution.py:66
  2.7 1.2 %collective-permute-start.4 = (bf16[128,1024]{1,0:T(8,128)(2,1)}, bf16[128,1024]{1,0:T(8,128)(2,1)S(1)}, u32[]{:S(2)}, u32[]{:S(2)}) collective-permute-start(bf16[128,1024]{1,0:T(8,128)(2,1)} %refs_0_.3), channel_id=1, source_target_pairs={{0,8},{1,17},{2,10},{3,19},{4,12},{5,21},{6,14},{7,23},{8,0},{9,25... | collective-permute-start | bytes 786440 | tf_op jit(solution)/shard_map/ppermute | solution.py:66
  4.6 2.2 %pack.1 = (bf16[416,256]{1,0:T(8,128)(2,1)}, bf16[416,256]{1,0:T(8,128)(2,1)}, bf16[416,256]{1,0:T(8,128)(2,1)}, bf16[416,256]{1,0:T(8,128)(2,1)}) custom-call(bf16[128,1024]{1,0:T(8,128)(2,1)} %q_ref.1, bf16[128,1024]{1,0:T(8,128)(2,1)} %k_ref.1, bf16[128,1024]{1,0:T(8,128)(2,1)} %v_ref.1, s32[1,4]{1,0:T(1,128)} %adj_any.1, s32[1,1]{1,0:T(1,128)} %bitcast.1.cnt_any), custom_call_target="tpu_custom_call" | custom-call | flops 5000000000 | tf_op jit(solution)/shard_map/pack/pallas_call | solution.py:177
  7.3 2.3 %collective-permute-start.2 = (bf16[416,256]{1,0:T(8,128)(2,1)}, bf16[416,256]{1,0:T(8,128)(2,1)S(1)}, u32[]{:S(2)}, u32[]{:S(2)}) collective-permute-start(bf16[416,256]{1,0:T(8,128)(2,1)} %get-tuple-element.36), channel_id=1, source_target_pairs={{0,24},{1,25},{2,26},{3,27},{4,28},{5,29},{6,30},{7,31},{8,16},{9,... | collective-permute-start | bytes 638984 | tf_op jit(solution)/shard_map/ppermute | solution.py:66
  9.6 0.8 %collective-permute-done.4.refs_2_.refs_1_ = bf16[128,1024]{1,0:T(8,128)(2,1)S(1)} collective-permute-done((bf16[128,1024]{1,0:T(8,128)(2,1)}, bf16[128,1024]{1,0:T(8,128)(2,1)S(1)}, u32[]{:S(2)}, u32[]{:S(2)}) %collective-permute-start.4) | collective-permute-done | bytes 262176 | tf_op jit(solution)/shard_map/ppermute | solution.py:66
  10.5 2.2 %collective-permute-start.5 = (bf16[128,1024]{1,0:T(8,128)(2,1)S(1)}, bf16[128,1024]{1,0:T(8,128)(2,1)S(1)}, u32[]{:S(2)}, u32[]{:S(2)}) collective-permute-start(bf16[128,1024]{1,0:T(8,128)(2,1)S(1)} %get-tuple-element.41), channel_id=1, source_target_pairs={{0,8},{1,17},{2,10},{3,19},{4,12},{5,21},{6,14},{7,23},{8,0},{9,25... | collective-permute-start | bytes 786440 | tf_op jit(solution)/shard_map/ppermute | solution.py:66
  12.6 0.7 %collective-permute-start.6 = (bf16[128,1024]{1,0:T(8,128)(2,1)S(1)}, bf16[128,1024]{1,0:T(8,128)(2,1)S(1)}, u32[]{:S(2)}, u32[]{:S(2)}) collective-permute-start(bf16[128,1024]{1,0:T(8,128)(2,1)S(1)} %get-tuple-element.43), channel_id=1, source_target_pairs={{0,0},{1,1},{4,2},{5,3},{2,4},{3,5},{6,6},{7,7},{12,8},{13,9},{10,... | collective-permute-start | bytes 786440 | tf_op jit(solution)/shard_map/ppermute | solution.py:375
  13.3 6.2 %collective-permute-done.refs_1_ = bf16[416,256]{1,0:T(8,128)(2,1)S(1)} collective-permute-done((bf16[416,256]{1,0:T(8,128)(2,1)}, bf16[416,256]{1,0:T(8,128)(2,1)S(1)}, u32[]{:S(2)}, u32[]{:S(2)}) %collective-permute-start) | collective-permute-done | bytes 213024 | tf_op jit(solution)/shard_map/ppermute | solution.py:66
  20.1 1.7 %collective-permute-start.7 = (bf16[128,1024]{1,0:T(8,128)(2,1)S(1)}, bf16[128,1024]{1,0:T(8,128)(2,1)S(1)}, u32[]{:S(2)}, u32[]{:S(2)}) collective-permute-start(bf16[128,1024]{1,0:T(8,128)(2,1)S(1)} %collective-permute-done.6.mine.refs_4_), channel_id=1, source_target_pairs={{0,1},{1,0},{2,3},{3,2},{4,5},{5,4},{6,7},{7,6},{8,9},{9,8},{10,11... | collective-permute-start | bytes 786440 | tf_op jit(solution)/shard_map/ppermute | solution.py:52
  22.3 2.1 %forward.1 = (bf16[512,256]{1,0:T(8,128)(2,1)S(1)}, f32[256,512]{1,0:T(8,128)S(1)}, f32[8,512]{1,0:T(8,128)S(1)}) custom-call(bf16[512,256]{1,0:T(8,128)(2,1)S(1)} %get-tuple-element.37.q_all.refs_0_, bf16[512,256]{1,0:T(8,128)(2,1)S(1)} %get-tuple-element.38.k_all.refs_1_, bf16[256,512]{1,0:T(8,128)(2,1)S(1)} %get-tuple-element.39.v_t, ...), custom_call_target="tpu_custom_call" | custom-call | flops 3000000000 | tf_op jit(solution)/shard_map/forward/pallas_call | solution.py:278
  24.4 0.4 partials.1
  24.9 1.5 %collective-permute-start.8 = (bf16[256,1024]{1,0:T(8,128)(2,1)S(1)}, bf16[256,1024]{1,0:T(8,128)(2,1)S(1)}, u32[]{:S(2)}, u32[]{:S(2)}) collective-permute-start(bf16[256,1024]{1,0:T(8,128)(2,1)S(1)} %get-tuple-element.46), channel_id=1, source_target_pairs={{0,16},{1,9},{2,18},{3,11},{4,20},{5,13},{6,22},{7,15},{8,24},{9,1... | collective-permute-start | bytes 1572872 | tf_op jit(solution)/shard_map/ppermute | solution.py:66
  26.4 0.5 %group_grads.1.refs_7_ = bf16[512,256]{1,0:T(8,128)(2,1)S(1)} custom-call(bf16[128,1024]{1,0:T(8,128)(2,1)S(1)} %copy-done.1, bf16[128,1024]{1,0:T(8,128)(2,1)S(1)} %collective-permute-done.4.refs_2_.refs_1_, bf16[128,1024]{1,0:T(8,128)(2,1)S(1)} %collective-permute-done.3.refs_1_.refs_2_, bf16[128,1024]{1,0:T(8,128)(2,1)S(1)} %collective-permute-done.5.refs_0_.refs_3_, ...), custom_call_target="tpu_custom_call" | custom-call | flops 1000000000 | tf_op jit(solution)/shard_map/group_grads/pallas_call | solution.py:403
  26.9 3.1 %backward.1 = (bf16[384,256]{1,0:T(8,128)(2,1)S(1)}, bf16[384,256]{1,0:T(8,128)(2,1)S(1)}, bf16[384,256]{1,0:T(8,128)(2,1)S(1)}, bf16[384,256]{1,0:T(8,128)(2,1)S(1)}) custom-call(bf16[512,256]{1,0:T(8,128)(2,1)S(1)} %get-tuple-element.37.q_all.refs_0_, bf16[512,256]{1,0:T(8,128)(2,1)S(1)} %get-tuple-element.38.k_all.refs_1_, ...), custom_call_target="tpu_custom_call" | custom-call | flops 3000000000 | tf_op jit(solution)/shard_map/backward/pallas_call | solution.py:351
  30.0 1.0 %collective-permute-start.11 = (bf16[384,256]{1,0:T(8,128)(2,1)S(1)}, bf16[384,256]{1,0:T(8,128)(2,1)S(1)}, u32[]{:S(2)}, u32[]{:S(2)}) collective-permute-start(bf16[384,256]{1,0:T(8,128)(2,1)S(1)} %get-tuple-element.55), channel_id=1, source_target_pairs={{0,8},{1,17},{2,10},{3,19},{4,12},{5,21},{6,14},{7,23},{8,0},{9,25... | collective-permute-start | bytes 589832 | tf_op jit(solution)/shard_map/ppermute | solution.py:66
  31.0 0.8 %collective-permute-start.12 = (bf16[384,256]{1,0:T(8,128)(2,1)S(1)}, bf16[384,256]{1,0:T(8,128)(2,1)S(1)}, u32[]{:S(2)}, u32[]{:S(2)}) collective-permute-start(bf16[384,256]{1,0:T(8,128)(2,1)S(1)} %get-tuple-element.56), channel_id=1, source_target_pairs={{0,16},{1,9},{2,18},{3,11},{4,20},{5,13},{6,22},{7,15},{8,24},{9,1... | collective-permute-start | bytes 589832 | tf_op jit(solution)/shard_map/ppermute | solution.py:66
  31.8 0.9 %collective-permute-start.13 = (bf16[384,256]{1,0:T(8,128)(2,1)S(1)}, bf16[384,256]{1,0:T(8,128)(2,1)S(1)}, u32[]{:S(2)}, u32[]{:S(2)}) collective-permute-start(bf16[384,256]{1,0:T(8,128)(2,1)S(1)} %get-tuple-element.57), channel_id=1, source_target_pairs={{0,24},{1,25},{2,26},{3,27},{4,28},{5,29},{6,30},{7,31},{8,16},{9,... | collective-permute-start | bytes 589832 | tf_op jit(solution)/shard_map/ppermute | solution.py:66
  32.7 0.6 %collective-permute-done.8.landed = bf16[256,1024]{1,0:T(8,128)(2,1)S(1)} collective-permute-done((bf16[256,1024]{1,0:T(8,128)(2,1)S(1)}, bf16[256,1024]{1,0:T(8,128)(2,1)S(1)}, u32[]{:S(2)}, u32[]{:S(2)}) %collective-permute-start.8) | collective-permute-done | bytes 524320 | tf_op jit(solution)/shard_map/ppermute | solution.py:66
  33.4 3.1 %collective-permute-start.10 = (bf16[64,1024]{1,0:T(8,128)(2,1)S(1)}, bf16[64,1024]{1,0:T(8,128)(2,1)S(1)}, u32[]{:S(2)}, u32[]{:S(2)}) collective-permute-start(bf16[64,1024]{1,0:T(8,128)(2,1)S(1)} %get-tuple-element.49), channel_id=1, source_target_pairs={{0,8},{1,17},{2,10},{3,19},{4,12},{5,21},{6,14},{7,23},{8,0},{9,25... | collective-permute-start | bytes 393224 | tf_op jit(solution)/shard_map/ppermute | solution.py:66
  37.0 0.9 %collective-permute-done.12.refs_2_ = bf16[384,256]{1,0:T(8,128)(2,1)S(1)} collective-permute-done((bf16[384,256]{1,0:T(8,128)(2,1)S(1)}, bf16[384,256]{1,0:T(8,128)(2,1)S(1)}, u32[]{:S(2)}, u32[]{:S(2)}) %collective-permute-start.12) | collective-permute-done | bytes 196640 | tf_op jit(solution)/shard_map/ppermute | solution.py:66
  37.9 6.3 %collective-permute-done.13.refs_3_ = bf16[384,256]{1,0:T(8,128)(2,1)S(1)} collective-permute-done((bf16[384,256]{1,0:T(8,128)(2,1)S(1)}, bf16[384,256]{1,0:T(8,128)(2,1)S(1)}, u32[]{:S(2)}, u32[]{:S(2)}) %collective-permute-start.13) | collective-permute-done | bytes 196640 | tf_op jit(solution)/shard_map/ppermute | solution.py:66
  44.2 1.0 %finish.1 = (bf16[128,1024]{1,0:T(8,128)(2,1)}, bf16[128,1024]{1,0:T(8,128)(2,1)}, bf16[128,1024]{1,0:T(8,128)(2,1)}, bf16[16,128]{1,0:T(8,128)(2,1)S(1)}) custom-call(bf16[384,256]{1,0:T(8,128)(2,1)S(1)} %get-tuple-element.54.refs_0_, bf16[384,256]{1,0:T(8,128)(2,1)S(1)} %collective-permute-done.11.refs_1_, ...), custom_call_target="tpu_custom_call" | custom-call | tf_op jit(solution)/shard_map/finish/pallas_call | solution.py:534
  45.2 0.7 %half_sum.2.unused = bf16[128,1024]{1,0:T(8,128)(2,1)} custom-call(f32[128,1024]{1,0:T(8,128)S(1)} %get-tuple-element.47.own, bf16[64,1024]{1,0:T(8,128)(2,1)S(1)} %collective-permute-done.10.landed, bf16[16,128]{1,0:T(8,128)(2,1)S(1)} %get-tuple-element.58.unused), custom_call_target="tpu_custom_call" | custom-call | tf_op jit(solution)/shard_map/half_sum/pallas_call | solution.py:558
  45.9 0.7 %half_sum.3 = bf16[128,1024]{1,0:T(8,128)(2,1)} custom-call(f32[128,1024]{1,0:T(8,128)S(1)} %get-tuple-element.47.own, bf16[64,1024]{1,0:T(8,128)(2,1)S(1)} %collective-permute-done.9.landed, bf16[128,1024]{1,0:T(8,128)(2,1)} %half_sum.2.unused), custom_call_target="tpu_custom_call", output_to_operand_aliasing={{}: (2, {})} | custom-call | tf_op jit(solution)/shard_map/half_sum/pallas_call | solution.py:558
  (21 shorter events, 2.2 us)
Async XLA Ops:
  0.6 9.0 %collective-permute-start.3 = (bf16[128,1024]{1,0:T(8,128)(2,1)}, bf16[128,1024]{1,0:T(8,128)(2,1)S(1)}, u32[]{:S(2)}, u32[]{:S(2)}) collective-permute-start(bf16[128,1024]{1,0:T(8,128)(2,1)} %refs_0_.3), channel_id=1, source_target_pairs={{0,16},{1,9},{2,18},{3,11},{4,20},{5,13},{6,22},{7,15},{8,24},{9,1... | collective-permute-start | bytes 786440 | tf_op jit(solution)/shard_map/ppermute | solution.py:66
  2.7 7.7 %collective-permute-start.4 = (bf16[128,1024]{1,0:T(8,128)(2,1)}, bf16[128,1024]{1,0:T(8,128)(2,1)S(1)}, u32[]{:S(2)}, u32[]{:S(2)}) collective-permute-start(bf16[128,1024]{1,0:T(8,128)(2,1)} %refs_0_.3), channel_id=1, source_target_pairs={{0,8},{1,17},{2,10},{3,19},{4,12},{5,21},{6,14},{7,23},{8,0},{9,25... | collective-permute-start | bytes 786440 | tf_op jit(solution)/shard_map/ppermute | solution.py:66
  4.6 5.8 %copy-start = (bf16[128,1024]{1,0:T(8,128)(2,1)S(1)}, bf16[128,1024]{1,0:T(8,128)(2,1)}, u32[]{:S(2)}) copy-start(bf16[128,1024]{1,0:T(8,128)(2,1)} %refs_0_.2) | copy-start | bytes 786436
  6.9 12.6 %collective-permute-start = (bf16[416,256]{1,0:T(8,128)(2,1)}, bf16[416,256]{1,0:T(8,128)(2,1)S(1)}, u32[]{:S(2)}, u32[]{:S(2)}) collective-permute-start(bf16[416,256]{1,0:T(8,128)(2,1)} %get-tuple-element.34), channel_id=1, source_target_pairs={{0,8},{1,17},{2,10},{3,19},{4,12},{5,21},{6,14},{7,23},{8,0},{9,25... | collective-permute-start | bytes 638984 | tf_op jit(solution)/shard_map/ppermute | solution.py:66
  7.2 12.3 %collective-permute-start.1 = (bf16[416,256]{1,0:T(8,128)(2,1)}, bf16[416,256]{1,0:T(8,128)(2,1)S(1)}, u32[]{:S(2)}, u32[]{:S(2)}) collective-permute-start(bf16[416,256]{1,0:T(8,128)(2,1)} %get-tuple-element.35), channel_id=1, source_target_pairs={{0,16},{1,9},{2,18},{3,11},{4,20},{5,13},{6,22},{7,15},{8,24},{9,1... | collective-permute-start | bytes 638984 | tf_op jit(solution)/shard_map/ppermute | solution.py:66
  7.3 12.6 %copy-start.2 = (bf16[416,256]{1,0:T(8,128)(2,1)S(1)}, bf16[416,256]{1,0:T(8,128)(2,1)}, u32[]{:S(2)}) copy-start(bf16[416,256]{1,0:T(8,128)(2,1)} %get-tuple-element.33.refs_0_) | copy-start | bytes 638980
  7.3 12.6 %collective-permute-start.2 = (bf16[416,256]{1,0:T(8,128)(2,1)}, bf16[416,256]{1,0:T(8,128)(2,1)S(1)}, u32[]{:S(2)}, u32[]{:S(2)}) collective-permute-start(bf16[416,256]{1,0:T(8,128)(2,1)} %get-tuple-element.36), channel_id=1, source_target_pairs={{0,24},{1,25},{2,26},{3,27},{4,28},{5,29},{6,30},{7,31},{8,16},{9,... | collective-permute-start | bytes 638984 | tf_op jit(solution)/shard_map/ppermute | solution.py:66
  10.5 11.9 %collective-permute-start.5 = (bf16[128,1024]{1,0:T(8,128)(2,1)S(1)}, bf16[128,1024]{1,0:T(8,128)(2,1)S(1)}, u32[]{:S(2)}, u32[]{:S(2)}) collective-permute-start(bf16[128,1024]{1,0:T(8,128)(2,1)S(1)} %get-tuple-element.41), channel_id=1, source_target_pairs={{0,8},{1,17},{2,10},{3,19},{4,12},{5,21},{6,14},{7,23},{8,0},{9,25... | collective-permute-start | bytes 786440 | tf_op jit(solution)/shard_map/ppermute | solution.py:66
  12.6 7.5 %collective-permute-start.6 = (bf16[128,1024]{1,0:T(8,128)(2,1)S(1)}, bf16[128,1024]{1,0:T(8,128)(2,1)S(1)}, u32[]{:S(2)}, u32[]{:S(2)}) collective-permute-start(bf16[128,1024]{1,0:T(8,128)(2,1)S(1)} %get-tuple-element.43), channel_id=1, source_target_pairs={{0,0},{1,1},{4,2},{5,3},{2,4},{3,5},{6,6},{7,7},{12,8},{13,9},{10,... | collective-permute-start | bytes 786440 | tf_op jit(solution)/shard_map/ppermute | solution.py:375
  20.1 4.3 %collective-permute-start.7 = (bf16[128,1024]{1,0:T(8,128)(2,1)S(1)}, bf16[128,1024]{1,0:T(8,128)(2,1)S(1)}, u32[]{:S(2)}, u32[]{:S(2)}) collective-permute-start(bf16[128,1024]{1,0:T(8,128)(2,1)S(1)} %collective-permute-done.6.mine.refs_4_), channel_id=1, source_target_pairs={{0,1},{1,0},{2,3},{3,2},{4,5},{5,4},{6,7},{7,6},{8,9},{9,8},{10,11... | collective-permute-start | bytes 786440 | tf_op jit(solution)/shard_map/ppermute | solution.py:52
  24.4 2.0 %copy-start.1 = (bf16[128,1024]{1,0:T(8,128)(2,1)S(1)}, bf16[128,1024]{1,0:T(8,128)(2,1)}, u32[]{:S(2)}) copy-start(bf16[128,1024]{1,0:T(8,128)(2,1)} %refs_0_.3) | copy-start | bytes 786436
  24.9 8.4 %collective-permute-start.8 = (bf16[256,1024]{1,0:T(8,128)(2,1)S(1)}, bf16[256,1024]{1,0:T(8,128)(2,1)S(1)}, u32[]{:S(2)}, u32[]{:S(2)}) collective-permute-start(bf16[256,1024]{1,0:T(8,128)(2,1)S(1)} %get-tuple-element.46), channel_id=1, source_target_pairs={{0,16},{1,9},{2,18},{3,11},{4,20},{5,13},{6,22},{7,15},{8,24},{9,1... | collective-permute-start | bytes 1572872 | tf_op jit(solution)/shard_map/ppermute | solution.py:66
  30.0 7.0 %collective-permute-start.11 = (bf16[384,256]{1,0:T(8,128)(2,1)S(1)}, bf16[384,256]{1,0:T(8,128)(2,1)S(1)}, u32[]{:S(2)}, u32[]{:S(2)}) collective-permute-start(bf16[384,256]{1,0:T(8,128)(2,1)S(1)} %get-tuple-element.55), channel_id=1, source_target_pairs={{0,8},{1,17},{2,10},{3,19},{4,12},{5,21},{6,14},{7,23},{8,0},{9,25... | collective-permute-start | bytes 589832 | tf_op jit(solution)/shard_map/ppermute | solution.py:66
  31.0 6.9 %collective-permute-start.12 = (bf16[384,256]{1,0:T(8,128)(2,1)S(1)}, bf16[384,256]{1,0:T(8,128)(2,1)S(1)}, u32[]{:S(2)}, u32[]{:S(2)}) collective-permute-start(bf16[384,256]{1,0:T(8,128)(2,1)S(1)} %get-tuple-element.56), channel_id=1, source_target_pairs={{0,16},{1,9},{2,18},{3,11},{4,20},{5,13},{6,22},{7,15},{8,24},{9,1... | collective-permute-start | bytes 589832 | tf_op jit(solution)/shard_map/ppermute | solution.py:66
  31.8 12.4 %collective-permute-start.13 = (bf16[384,256]{1,0:T(8,128)(2,1)S(1)}, bf16[384,256]{1,0:T(8,128)(2,1)S(1)}, u32[]{:S(2)}, u32[]{:S(2)}) collective-permute-start(bf16[384,256]{1,0:T(8,128)(2,1)S(1)} %get-tuple-element.57), channel_id=1, source_target_pairs={{0,24},{1,25},{2,26},{3,27},{4,28},{5,29},{6,30},{7,31},{8,16},{9,... | collective-permute-start | bytes 589832 | tf_op jit(solution)/shard_map/ppermute | solution.py:66
  33.4 11.8 %collective-permute-start.10 = (bf16[64,1024]{1,0:T(8,128)(2,1)S(1)}, bf16[64,1024]{1,0:T(8,128)(2,1)S(1)}, u32[]{:S(2)}, u32[]{:S(2)}) collective-permute-start(bf16[64,1024]{1,0:T(8,128)(2,1)S(1)} %get-tuple-element.49), channel_id=1, source_target_pairs={{0,8},{1,17},{2,10},{3,19},{4,12},{5,21},{6,14},{7,23},{8,0},{9,25... | collective-permute-start | bytes 393224 | tf_op jit(solution)/shard_map/ppermute | solution.py:66
  36.5 9.4 %collective-permute-start.9 = (bf16[64,1024]{1,0:T(8,128)(2,1)S(1)}, bf16[64,1024]{1,0:T(8,128)(2,1)S(1)}, u32[]{:S(2)}, u32[]{:S(2)}) collective-permute-start(bf16[64,1024]{1,0:T(8,128)(2,1)S(1)} %get-tuple-element.48), channel_id=1, source_target_pairs={{0,8},{1,17},{2,10},{3,19},{4,12},{5,21},{6,14},{7,23},{8,0},{9,25... | collective-permute-start | bytes 393224 | tf_op jit(solution)/shard_map/ppermute | solution.py:66
